TPU v7x, 32 devices: a whole 2x2x4 slice. The times are simulated.
32 devices in a mesh: groups: 2 (over y), row: 8 (over z, core), col: 2 (over x).
Axes of the slice: x: 2, y: 2, z: 4, core: 2. Of those that a mesh axis runs over, the one named last changes fastest.
Arguments:
- pair_repr: bfloat16 [256, 128, 128], P(('groups', 'row'), 'col'), parts along dimension 0, may hold values from -6 to 6
- distance_bins: int32 [256, 128], P(('groups', 'row'), 'col'), parts along dimension 0, may hold values from 0 to 63
- chain_lengths: int32 [10], P('groups'), parts along dimension 0, may hold values from 1 to 64, 128 in all
- left_weight: bfloat16 [128, 128], replicated, may hold values from -0.5 to 0.5
- left_gate_weight: bfloat16 [128, 128], replicated, may hold values from -0.5 to 0.5
- right_weight: bfloat16 [128, 128], replicated, may hold values from -0.5 to 0.5
- right_gate_weight: bfloat16 [128, 128], replicated, may hold values from -0.5 to 0.5
- out_weight: bfloat16 [128, 128], replicated, may hold values from -0.5 to 0.5
- out_gate_weight: bfloat16 [128, 128], replicated, may hold values from -0.5 to 0.5
- dist_weight: bfloat16 [128, 64], replicated, may hold values from -1.59375 to 1.59375
Outputs:
- pair_out: bfloat16 [256, 128, 128], P(('groups', 'row'), 'col'), parts along dimension 0
- loss_value: float32 [2], P('groups'), parts along dimension 0
There are 2 independent parts, one for each index of `groups`. A program takes and returns all parts, laid end to end along the dimension named above; an argument that names none is the same for every part. Nothing has to cross between parts.
Inputs may be any that keep to these rules, and one draw needn't show every extreme that they name: chain_lengths holds 4 chain lengths followed by the count of padding residues at the end of the complex; the entries sum to 128.
All inputs are finite; a program needn't handle non-finite values.
Results may differ from a plain program's by a relative error of at most 0.0048.
Values may be sent and summed in bfloat16 or wider, within the bound.
No kernel may reach another device: no remote copies, remote signals or barrier semaphores. Data moves between devices by JAX's collectives and lax.ppermute only.
A program may use at most 64 MiB of HBM per device.

v0:
```python
import jax
import jax.numpy as jnp
from jax import lax
from jax.sharding import PartitionSpec as P

CG = 32


def layer_norm(values):
    average = jnp.mean(values, axis=-1, keepdims=True)
    centred = values - average
    spread = jnp.mean(centred * centred, axis=-1, keepdims=True)
    return centred * lax.rsqrt(spread + 1e-05)


def on_device(
    pair_repr,
    distance_bins,
    chain_lengths,
    left_weight,
    left_gate_weight,
    right_weight,
    right_gate_weight,
    out_weight,
    out_gate_weight,
    dist_weight,
):
    tile_rows, tile_cols, channels = pair_repr.shape
    residues = tile_rows * lax.axis_size("row")
    live_count = residues - chain_lengths[chain_lengths.shape[0] - 1]
    row_place = lax.axis_index("row") * tile_rows + jnp.arange(tile_rows, dtype=jnp.int32)
    col_place = lax.axis_index("col") * tile_cols + jnp.arange(tile_cols, dtype=jnp.int32)
    live_rows = (row_place < live_count).astype(jnp.float32)
    live_cols = (col_place < live_count).astype(jnp.float32)
    pair_mask = live_rows[:, None] * live_cols[None, :]
    normed = layer_norm(pair_repr.astype(jnp.float32)).astype(jnp.bfloat16).reshape(-1, channels)

    def project(weight):
        return jnp.dot(normed, weight, preferred_element_type=jnp.float32).reshape(
            tile_rows, tile_cols, -1
        )

    left = (
        jax.nn.sigmoid(project(left_gate_weight)) * project(left_weight) * pair_mask[:, :, None]
    ).astype(jnp.bfloat16)
    right = (
        jax.nn.sigmoid(project(right_gate_weight)) * project(right_weight) * pair_mask[:, :, None]
    ).astype(jnp.bfloat16)
    left_major = left.transpose(2, 0, 1)
    right_major = right.transpose(2, 0, 1)
    products = []
    for first in range(0, channels, CG):
        left_block = left_major[first : first + CG]
        right_block = right_major[first : first + CG]
        right_cols = lax.all_gather(right_block, "row", axis=1, tiled=True)
        right_turned = lax.all_to_all(right_cols, "col", split_axis=1, concat_axis=2, tiled=True)
        left_whole = lax.all_gather(left_block, "col", axis=2, tiled=True)
        product = jnp.einsum(
            "cik,cjk->cij", left_whole, right_turned, preferred_element_type=jnp.float32
        )
        products.append(product)
    tri = jnp.concatenate(products, axis=0).transpose(1, 2, 0)
    tri_normed = layer_norm(tri).astype(jnp.bfloat16).reshape(-1, channels)
    out_gate = jax.nn.sigmoid(project(out_gate_weight))
    update = out_gate * jnp.dot(tri_normed, out_weight, preferred_element_type=jnp.float32).reshape(
        tile_rows, tile_cols, -1
    )
    pair_out = (pair_repr.astype(jnp.float32) + update).astype(jnp.bfloat16)
    logits = jnp.dot(
        pair_out.reshape(-1, channels), dist_weight, preferred_element_type=jnp.float32
    )
    log_total = jnp.log(jnp.sum(jnp.exp(logits), axis=-1))
    bin_ids = jnp.arange(logits.shape[1], dtype=jnp.int32)
    picked = jnp.sum(
        jnp.where(bin_ids[None, :] == distance_bins.reshape(-1, 1), logits, 0.0), axis=-1
    )
    cross_entropy = log_total - picked
    flat_mask = pair_mask.reshape(-1)
    loss_sum, pair_count = lax.psum(
        (jnp.sum(flat_mask * cross_entropy), jnp.sum(flat_mask)), ("row", "col")
    )
    loss_value = (loss_sum / pair_count).reshape(1)
    return (pair_out, loss_value)


def solution(mesh):
    in_specs = (
        P(("groups", "row"), "col", None),
        P(("groups", "row"), "col"),
        P("groups"),
        P(),
        P(),
        P(),
        P(),
        P(),
        P(),
        P(),
    )
    out_specs = (P(("groups", "row"), "col", None), P("groups"))
    return jax.shard_map(
        on_device, mesh=mesh, in_specs=in_specs, out_specs=out_specs, check_vma=False
    )
```

profile of v0, /device:TPU:0, one launch (start us, length us, event | category | flops | bytes accessed | tf_op | source)
XLA Modules:
  0.0 203.9 jit_solution(16318219181328306431)
XLA Ops:
  0.7 1.3 slice.27
  2.6 1.2 convert_reduce_fusion
  3.8 0.4 fusion.19
  4.2 0.7 fusion.29
  4.9 0.7 fusion.2
  5.6 0.5 fusion.16
  6.1 0.9 fusion.35
  7.0 0.1 copy.24
  7.2 18.4 %all_gather.27 = bf16[32,128,64]{2,0,1:T(8,128)(2,1)S(1)} all-gather(bf16[32,16,64]{2,0,1:T(8,128)(2,1)S(1)} %copy.24), channel_id=1, replica_groups=mesh['groups'=2,'row'=8,'col'=2] {'row'}, dimensions={1}, use_global_device_ids=true | all-gather | bytes 589824 | tf_op jit(solution)/shard_map/all_gather | solution.py:55
  25.6 1.5 reshape.121
  27.1 3.5 %all-to-all-start.1 = ((bf16[2,2,65536]{2,1,0:T(2,128)(2,1)}), bf16[2,2,65536]{2,1,0:T(2,128)(2,1)S(1)}, u32[]{:S(2)}, u32[]{:S(2)}) async-start(bf16[2,2,65536]{2,1,0:T(2,128)(2,1)} %reshape.121), calls=%async_computation.1 | async-start | bytes 1048576 | tf_op jit(solution)/shard_map/all_to_all | solution.py:56
  30.6 0.8 copy.30
  31.5 17.6 %all_gather.29 = bf16[32,128,64]{2,0,1:T(8,128)(2,1)S(1)} all-gather(bf16[32,16,64]{2,0,1:T(8,128)(2,1)S(1)} %copy.27), channel_id=1, replica_groups=mesh['groups'=2,'row'=8,'col'=2] {'row'}, dimensions={1}, use_global_device_ids=true | all-gather | bytes 589824 | tf_op jit(solution)/shard_map/all_gather | solution.py:55
  49.1 17.5 %all_gather.31 = bf16[32,128,64]{2,0,1:T(8,128)(2,1)S(1)} all-gather(bf16[32,16,64]{2,0,1:T(8,128)(2,1)S(1)} %copy-done.12), channel_id=1, replica_groups=mesh['groups'=2,'row'=8,'col'=2] {'row'}, dimensions={1}, use_global_device_ids=true | all-gather | bytes 589824 | tf_op jit(solution)/shard_map/all_gather | solution.py:55
  66.6 0.8 copy.21
  67.4 1.5 reshape.119
  68.9 1.3 fusion.5
  70.2 3.5 %all-to-all-start.2 = ((bf16[2,2,65536]{2,1,0:T(2,128)(2,1)}), bf16[2,2,65536]{2,1,0:T(2,128)(2,1)S(1)}, u32[]{:S(2)}, u32[]{:S(2)}) async-start(bf16[2,2,65536]{2,1,0:T(2,128)(2,1)} %reshape.119), calls=%async_computation.2 | async-start | bytes 1048576 | tf_op jit(solution)/shard_map/all_to_all | solution.py:56
  73.7 17.6 %all_gather.25 = bf16[32,128,64]{2,0,1:T(8,128)(2,1)S(1)} all-gather(bf16[32,16,64]{2,0,1:T(8,128)(2,1)} %copy.21), channel_id=1, replica_groups=mesh['groups'=2,'row'=8,'col'=2] {'row'}, dimensions={1}, use_global_device_ids=true | all-gather | bytes 589824 | tf_op jit(solution)/shard_map/all_gather | solution.py:55
  91.2 1.5 reshape.117
  92.8 1.5 reshape.123
  94.3 0.5 fusion.15
  94.8 3.5 %all-to-all-start.3 = ((bf16[2,2,65536]{2,1,0:T(2,128)(2,1)}), bf16[2,2,65536]{2,1,0:T(2,128)(2,1)S(1)}, u32[]{:S(2)}, u32[]{:S(2)}) async-start(bf16[2,2,65536]{2,1,0:T(2,128)(2,1)} %reshape.117), calls=%async_computation.3 | async-start | bytes 1048576 | tf_op jit(solution)/shard_map/all_to_all | solution.py:56
  98.3 0.3 fusion.36
  98.6 14.3 %all_gather.24 = bf16[32,16,128]{0,2,1:T(8,128)(2,1)S(1)} all-gather(bf16[32,16,64]{0,2,1:T(8,128)(2,1)S(1)} %get-tuple-element.10), channel_id=1, replica_groups=mesh['groups'=2,'row'=8,'col'=2] {'col'}, dimensions={2}, use_global_device_ids=true | all-gather | bytes 196608 | tf_op jit(solution)/shard_map/all_gather | solution.py:57
  112.9 8.6 %all_gather.30 = bf16[32,16,128]{0,2,1:T(8,128)(2,1)S(1)} all-gather(bf16[32,16,64]{0,2,1:T(8,128)(2,1)S(1)} %get-tuple-element.11), channel_id=1, replica_groups=mesh['groups'=2,'row'=8,'col'=2] {'col'}, dimensions={2}, use_global_device_ids=true | all-gather | bytes 196608 | tf_op jit(solution)/shard_map/all_gather | solution.py:57
  121.5 7.9 %all_gather.28 = bf16[32,16,128]{0,2,1:T(8,128)(2,1)} all-gather(bf16[32,16,64]{0,2,1:T(8,128)(2,1)S(1)} %get-tuple-element.12), channel_id=1, replica_groups=mesh['groups'=2,'row'=8,'col'=2] {'col'}, dimensions={2}, use_global_device_ids=true | all-gather | bytes 196608 | tf_op jit(solution)/shard_map/all_gather | solution.py:57
  129.4 0.8 copy-done.3
  130.2 4.2 %all-to-all-start = ((bf16[2,2,65536]{2,1,0:T(2,128)(2,1)}), bf16[2,2,65536]{2,1,0:T(2,128)(2,1)}, u32[]{:S(2)}, u32[]{:S(2)}) async-start(bf16[2,2,65536]{2,1,0:T(2,128)(2,1)} %reshape.123), calls=%async_computation | async-start | bytes 1048576 | tf_op jit(solution)/shard_map/all_to_all | solution.py:56
  134.4 12.1 %all_gather.26 = bf16[32,16,128]{0,2,1:T(8,128)(2,1)} all-gather(bf16[32,16,64]{0,2,1:T(8,128)(2,1)S(1)} %get-tuple-element.13), channel_id=1, replica_groups=mesh['groups'=2,'row'=8,'col'=2] {'col'}, dimensions={2}, use_global_device_ids=true | all-gather | bytes 196608 | tf_op jit(solution)/shard_map/all_gather | solution.py:57
  146.6 0.6 copy-done.18
  147.3 0.9 copy.23
  148.1 0.9 copy.32
  149.0 0.9 copy.29
  149.9 0.9 copy.26
  150.8 1.3 fusion.8
  152.0 0.7 reshape.122
  152.8 1.1 copy.42
  153.9 0.5 all_to_all.59
  154.3 0.7 reshape.120
  155.1 1.1 copy.41
  156.2 0.5 all_to_all.63
  156.7 1.7 reshape.118
  158.4 1.1 copy.40
  159.5 1.3 all_to_all.67
  160.8 1.7 reshape.124
  162.5 1.1 copy.43
  163.6 0.5 all_to_all.55
  164.1 0.4 copy-done.11
  164.5 0.4 fusion.38
  164.9 0.5 copy-done.10
  165.4 0.4 fusion.39
  165.8 0.7 copy-done.2
  166.5 0.4 fusion.40
  166.9 0.5 copy-done.8
  167.4 0.4 fusion.37
  167.8 0.2 fusion.22
  168.0 0.2 multiply_reduce_fusion
  168.4 0.9 copy-done.7
  169.2 0.3 fusion.14
  169.6 0.4 copy-done.21
  170.0 0.2 exponential_reduce_fusion
  170.3 0.7 multiply_reduce_fusion.1
  170.9 30.5 %all-reduce = (f32[]{:T(128)}, f32[]{:T(128)}) all-reduce(f32[]{:T(128)} %multiply_reduce_fusion.1, f32[]{:T(128)} %get-tuple-element.14), channel_id=1, replica_groups=mesh['groups'=2,'row'=8,'col'=2] {'row','col'}, use_global_device_ids=true, to_apply=%region_7.8 | all-reduce | flops 2 | bytes 16 | tf_op jit(solution)/shard_map/psum | solution.py:79
  (49 shorter events, 0.7 us)
Async XLA Ops:
  0.6 4.2 %copy-start = (bf16[128,128]{1,0:T(8,128)(2,1)S(1)}, bf16[128,128]{1,0:T(8,128)(2,1)}, u32[]{:S(2)}) copy-start(bf16[128,128]{1,0:T(8,128)(2,1)} %param.16) | copy-start | bytes 98308
  0.6 3.2 %copy-start.1 = (bf16[16,64,128]{2,1,0:T(8,128)(2,1)S(1)}, bf16[16,64,128]{2,1,0:T(8,128)(2,1)}, u32[]{:S(2)}) copy-start(bf16[16,64,128]{2,1,0:T(8,128)(2,1)} %param.10) | copy-start | bytes 786436
  4.9 0.8 copy-start.15
  27.1 43.1 %all-to-all-start.1 = ((bf16[2,2,65536]{2,1,0:T(2,128)(2,1)}), bf16[2,2,65536]{2,1,0:T(2,128)(2,1)S(1)}, u32[]{:S(2)}, u32[]{:S(2)}) async-start(bf16[2,2,65536]{2,1,0:T(2,128)(2,1)} %reshape.121), calls=%async_computation.1 | async-start | bytes 1048576 | tf_op jit(solution)/shard_map/all_to_all | solution.py:56
  31.5 17.6 %copy-start.12 = (bf16[32,16,64]{2,0,1:T(8,128)(2,1)S(1)}, bf16[32,16,64]{2,0,1:T(8,128)(2,1)}, u32[]{:S(2)}) copy-start(bf16[32,16,64]{2,0,1:T(8,128)(2,1)} %copy.30) | copy-start | bytes 196612
  49.1 17.5 %copy-start.6 = (bf16[32,16,64]{0,2,1:T(8,128)(2,1)S(1)}, bf16[32,16,64]{0,2,1:T(8,128)(2,1)}, u32[]{:S(2)}) copy-start(bf16[32,16,64]{0,2,1:T(8,128)(2,1)} %get-tuple-element.6) | copy-start | bytes 196612
  67.4 1.5 copy-start.19
  70.2 24.6 %all-to-all-start.2 = ((bf16[2,2,65536]{2,1,0:T(2,128)(2,1)}), bf16[2,2,65536]{2,1,0:T(2,128)(2,1)S(1)}, u32[]{:S(2)}, u32[]{:S(2)}) async-start(bf16[2,2,65536]{2,1,0:T(2,128)(2,1)} %reshape.119), calls=%async_computation.2 | async-start | bytes 1048576 | tf_op jit(solution)/shard_map/all_to_all | solution.py:56
  92.8 1.5 copy-start.13
  92.8 1.5 copy-start.16
  94.8 34.6 %all-to-all-start.3 = ((bf16[2,2,65536]{2,1,0:T(2,128)(2,1)}), bf16[2,2,65536]{2,1,0:T(2,128)(2,1)S(1)}, u32[]{:S(2)}, u32[]{:S(2)}) async-start(bf16[2,2,65536]{2,1,0:T(2,128)(2,1)} %reshape.117), calls=%async_computation.3 | async-start | bytes 1048576 | tf_op jit(solution)/shard_map/all_to_all | solution.py:56
  129.4 0.8 copy-start.3
  130.2 30.6 %all-to-all-start = ((bf16[2,2,65536]{2,1,0:T(2,128)(2,1)}), bf16[2,2,65536]{2,1,0:T(2,128)(2,1)}, u32[]{:S(2)}, u32[]{:S(2)}) async-start(bf16[2,2,65536]{2,1,0:T(2,128)(2,1)} %reshape.123), calls=%async_computation | async-start | bytes 1048576 | tf_op jit(solution)/shard_map/all_to_all | solution.py:56
  146.5 0.7 copy-start.18
  147.3 1.7 copy-start.4
  148.1 1.7 copy-start.5
  149.9 0.9 copy-start.20
  163.6 0.9 copy-start.11
  164.5 0.9 copy-start.10
  165.4 1.0 copy-start.2
  165.4 1.1 copy-start.9
  166.5 0.9 copy-start.8
  168.2 1.0 copy-start.7
  168.2 1.0 copy-start.17
  169.2 0.7 copy-start.21
  169.6 0.7 copy-start.14
where the time goes:
time: 205 us; the launch traced here: 204 us
  blocking collectives  144 us (70%)
  local copies, waits for them, and re-layouts  31.1 us (15%)
  starting transfers between devices  14.7 us (7%)
  matrix products  6.25 us (3%)
  between operations  4.11 us (2%)
  other arithmetic  3.45 us (2%)
    all_gather x4, blocking collectives, on_device(): right_cols = lax.all_gather(right_block, 'row', axis=1, tiled=True)  70.9 us
    all_gather x4, blocking collectives, on_device(): left_whole = lax.all_gather(left_block, 'col', axis=2, tiled=True)  42.9 us
    psum x1, blocking collectives, on_device(): lax.psum((jnp.sum(flat_mask * cross_entropy), jnp.sum(flat_mask)), ('row'...  30.5 us
    unnamed x52, local copies, waits for them, and re-layouts  16.1 us
    all_to_all x4, starting transfers between devices, on_device(): lax.all_to_all(right_cols, 'col', split_axis=1, concat_axis=2, tiled=True)  14.7 us
    all_to_all x8, local copies, waits for them, and re-layouts, on_device(): lax.all_to_all(right_cols, 'col', split_axis=1, concat_axis=2, tiled=True)  7.04 us
    dot_general x5, matrix products, project(): jnp.dot(normed, weight, preferred_element_type=jnp.float32)  4.2 us
  transfers between devices with their start and end apart: 4, of which 0 were waited for; matrix products, arithmetic and copies ran while one was open for 10% of the time, Pallas kernels for 0%

commit v1 on v0

v1 whole, which is shorter than its diff:
```python
import jax
import jax.numpy as jnp
from jax import lax
from jax.sharding import PartitionSpec as P

AXES = ("row", "col")


def layer_norm(values, axis):
    average = jnp.mean(values, axis=axis, keepdims=True)
    centred = values - average
    spread = jnp.mean(centred * centred, axis=axis, keepdims=True)
    return centred * lax.rsqrt(spread + 1e-05)


def on_device(
    pair_repr,
    distance_bins,
    chain_lengths,
    left_weight,
    left_gate_weight,
    right_weight,
    right_gate_weight,
    out_weight,
    out_gate_weight,
    dist_weight,
):
    tile_rows, tile_cols, channels = pair_repr.shape
    rows, cols = lax.axis_size("row"), lax.axis_size("col")
    peers = rows * cols
    share = channels // peers
    residues = tile_rows * rows
    spots = tile_rows * tile_cols
    live_count = residues - chain_lengths[chain_lengths.shape[0] - 1]
    row_place = lax.axis_index("row") * tile_rows + jnp.arange(tile_rows, dtype=jnp.int32)
    col_place = lax.axis_index("col") * tile_cols + jnp.arange(tile_cols, dtype=jnp.int32)
    live_rows = (row_place < live_count).astype(jnp.float32)
    live_cols = (col_place < live_count).astype(jnp.float32)
    flat_mask = (live_rows[:, None] * live_cols[None, :]).reshape(-1)
    normed = layer_norm(pair_repr.astype(jnp.float32), -1).astype(jnp.bfloat16)
    normed = normed.reshape(spots, channels)

    def project_turned(weight):
        return lax.dot_general(
            weight, normed, (((0,), (1,)), ((), ())), preferred_element_type=jnp.float32
        )

    def gated(gate_weight, weight):
        values = jax.nn.sigmoid(project_turned(gate_weight)) * project_turned(weight)
        return (values * flat_mask[None, :]).astype(jnp.bfloat16)

    left = gated(left_gate_weight, left_weight).reshape(peers, share, tile_rows, tile_cols)
    right = gated(right_gate_weight, right_weight).reshape(peers, share, tile_rows, tile_cols)
    both = jnp.concatenate([left, right], axis=3).reshape(peers, share * tile_rows, 2 * tile_cols)
    owned = lax.all_to_all(both, AXES, split_axis=0, concat_axis=0, tiled=True)
    owned = owned.reshape(rows, cols, share, tile_rows, 2, tile_cols)
    owned = owned.transpose(4, 2, 0, 3, 1, 5).reshape(2, share, residues, residues)
    tri = jnp.einsum(
        "cik,cjk->cij", owned[0], owned[1], preferred_element_type=jnp.float32
    ).astype(jnp.bfloat16)
    tri = tri.reshape(share, rows, tile_rows, cols, tile_cols).transpose(1, 3, 0, 2, 4)
    tri = tri.reshape(peers, share, spots)
    tri = lax.all_to_all(tri, AXES, split_axis=0, concat_axis=0, tiled=True)
    tri = tri.reshape(channels, spots).astype(jnp.float32)
    tri_normed = layer_norm(tri, 0).astype(jnp.bfloat16)
    out_gate = jax.nn.sigmoid(jnp.dot(normed, out_gate_weight, preferred_element_type=jnp.float32))
    update = out_gate * lax.dot_general(
        tri_normed, out_weight, (((0,), (0,)), ((), ())), preferred_element_type=jnp.float32
    )
    pair_out = (pair_repr.astype(jnp.float32).reshape(spots, channels) + update).astype(
        jnp.bfloat16
    )
    logits = jnp.dot(pair_out, dist_weight, preferred_element_type=jnp.float32)
    log_total = jnp.log(jnp.sum(jnp.exp(logits), axis=-1))
    bin_ids = jnp.arange(logits.shape[1], dtype=jnp.int32)
    picked = jnp.sum(
        jnp.where(bin_ids[None, :] == distance_bins.reshape(-1, 1), logits, 0.0), axis=-1
    )
    loss_sum = jnp.sum(flat_mask * (log_total - picked))
    sums = lax.all_to_all(
        jnp.full((peers, 1, 128), loss_sum), AXES, split_axis=0, concat_axis=0, tiled=True
    )
    pair_count = (live_count * live_count).astype(jnp.float32)
    loss_value = (jnp.sum(sums[:, 0, 0]) / pair_count).reshape(1)
    return (pair_out.reshape(pair_repr.shape), loss_value)


def solution(mesh):
    in_specs = (
        P(("groups", "row"), "col", None),
        P(("groups", "row"), "col"),
        P("groups"),
        P(),
        P(),
        P(),
        P(),
        P(),
        P(),
        P(),
    )
    out_specs = (P(("groups", "row"), "col", None), P("groups"))
    return jax.shard_map(
        on_device, mesh=mesh, in_specs=in_specs, out_specs=out_specs, check_vma=False
    )
```

time: 205 us -> 67.1 us (0.33)
  blocking collectives: 144 us -> 21.7 us
  local copies, waits for them, and re-layouts: 31.1 us -> 11.9 us
  waiting for transfers between devices: 0.01 us -> 15.9 us
  starting transfers between devices: 14.7 us -> 7.72 us
  matrix products: 6.25 us -> 2.1 us
    all_gather x8 -> x0, blocking collectives: 114 us -> none  [the longest x4 70.9 us: on_device(): right_cols = lax.all_gather(right_block, 'row', axis=1, tiled=True)]
    psum x1 -> x0, blocking collectives: 30.5 us -> none  [on_device(): lax.psum((jnp.sum(flat_mask * cross_entropy), jnp.sum(flat_mask)), ('row'...]
    all_to_all x0 -> x1, blocking collectives: none -> 21.7 us  [on_device(): owned = lax.all_to_all(both, AXES, split_axis=0, concat_axis=0, tiled=True)]
    all_to_all x4 -> x2, waiting for transfers between devices: 0.01 us -> 15.9 us  [the longest x1 9.59 us: on_device(): tri = lax.all_to_all(tri, AXES, split_axis=0, concat_axis=0, tiled=True)]
    unnamed x52 -> x20, local copies, waits for them, and re-layouts: 16.1 us -> 2.91 us
    all_to_all x8 -> x0, local copies, waits for them, and re-layouts: 7.04 us -> none  [on_device(): lax.all_to_all(right_cols, 'col', split_axis=1, concat_axis=2, tiled=True)]
    all_to_all x4 -> x2, starting transfers between devices: 14.7 us -> 7.72 us  [the longest x1 4.23 us: on_device(): tri = lax.all_to_all(tri, AXES, split_axis=0, concat_axis=0, tiled=True)]
    dot_general x11 -> x8, matrix products: 6.25 us -> 2.1 us  [the longest x4 1.02 us: project_turned(): lax.dot_general(weight, normed, (((0,), (1,)), ((), ())), preferred_eleme...]
  transfers between devices with their start and end apart: 4 -> 2, of which waited for: 0 -> 2; matrix products, arithmetic and copies ran while one was open for 10% -> 1% of each run, Pallas kernels for 0% -> 0%
where the time goes in v1:
time: 67.1 us; the launch traced here: 66.4 us
  blocking collectives  21.7 us (32%)
  waiting for transfers between devices  15.9 us (24%)
  local copies, waits for them, and re-layouts  11.9 us (18%)
  starting transfers between devices  7.72 us (12%)
  other arithmetic  3.64 us (5%)
  between operations  3.37 us (5%)
  matrix products  2.1 us (3%)
    all_to_all x1, blocking collectives, on_device(): owned = lax.all_to_all(both, AXES, split_axis=0, concat_axis=0, tiled=True)  21.7 us
    all_to_all x1, waiting for transfers between devices, on_device(): tri = lax.all_to_all(tri, AXES, split_axis=0, concat_axis=0, tiled=True)  9.59 us
    all_to_all x1, waiting for transfers between devices, on_device(): lax.all_to_all(jnp.full((peers, 1, 128), loss_sum), AXES, split_axis=0, c...  6.33 us
    all_to_all x1, starting transfers between devices, on_device(): tri = lax.all_to_all(tri, AXES, split_axis=0, concat_axis=0, tiled=True)  4.23 us
    all_to_all x1, starting transfers between devices, on_device(): lax.all_to_all(jnp.full((peers, 1, 128), loss_sum), AXES, split_axis=0, c...  3.49 us
    unnamed x20, local copies, waits for them, and re-layouts  2.91 us
    slice x2, local copies, waits for them, and re-layouts, on_device(): owned[1]  2.35 us
  transfers between devices with their start and end apart: 2, of which 2 were waited for; matrix products, arithmetic and copies ran while one was open for 1% of the time, Pallas kernels for 0%

profile of v1, /device:TPU:0, one launch (start us, length us, event | category | flops | bytes accessed | tf_op | source)
XLA Modules:
  0.0 66.4 jit_solution(3146784136004772347)
XLA Ops:
  0.6 0.0 copy-start
  0.6 0.0 copy-start.1
  0.7 1.3 %slice.14 = s32[1]{0:T(128)} slice(s32[5]{0:T(128)} %param.12), slice={[4:5]} | slice | bytes 8 | tf_op jit(solution)/shard_map/slice | solution.py:34
  2.6 0.1 broadcast_multiply_fusion
  2.7 0.1 mul.96
  2.8 1.2 %convert_reduce_fusion.1 = f32[16,64]{1,0:T(8,128)S(1)} fusion(bf16[16,64,128]{2,1,0:T(8,128)(2,1)} %param.10), kind=kLoop, calls=%fused_computation.36 | loop fusion | flops 261120 | bytes 266240 | tf_op jit(solution)/shard_map/reduce_sum | solution.py:10
  3.9 0.0 copy-done.1
  4.0 0.4 multiply_reduce_fusion
  4.4 0.3 multiply_convert_fusion
  4.7 0.0 copy-done
  4.7 0.0 copy-start.3
  4.7 0.3 fusion.5
  5.0 0.5 copy-done.3
  5.5 0.2 fusion.15
  5.7 0.1 copy.22
  5.9 0.0 copy-start.7
  5.9 0.3 concatenate.8
  6.2 0.4 copy-done.7
  6.6 0.0 copy-start.4
  6.6 0.3 fusion.2
  6.9 0.5 copy-done.4
  7.4 0.2 fusion.16
  7.6 0.1 copy.23
  7.8 0.3 concatenate.9
  8.1 0.3 pad_maximum_fusion
  8.4 21.7 %all_to_all.15 = bf16[16,128,128]{2,1,0:T(8,128)(2,1)S(1)} all-to-all(bf16[16,128,128]{2,1,0:T(8,128)(2,1)S(1)} %pad_maximum_fusion), channel_id=1, replica_groups=mesh['groups'=2,'row'=8,'col'=2] {'row','col'}, dimensions={0} | all-to-all | bytes 1048576 | tf_op jit(solution)/shard_map/all_to_all | solution.py:55
  30.1 0.4 reshape.112
  30.5 1.5 %fusion.25 = (bf16[1,8,8,16,2,64]{5,0,3,1,4,2:T(2,128)(2,1)S(1)}, bf16[1,8,8,16,2,64]{5,0,3,1,4,2:T(2,128)(2,1)S(1)}) fusion(bf16[2,8,8,16,2,64]{5,0,3,1,4,2:T(2,128)(2,1)S(1)} %bitcast.40), kind=kLoop, calls=%fused_computation.51 | loop fusion | bytes 1048576 | tf_op jit(solution)/shard_map/slice | solution.py:59
  32.1 0.8 %copy.24 = bf16[1,8,8,16,2,64]{5,4,3,2,1,0:T(2,128)(2,1)S(1)} copy(bf16[1,8,8,16,2,64]{5,0,3,1,4,2:T(2,128)(2,1)S(1)} %get-tuple-element.5) | data formatting | bytes 524288 | tf_op jit(solution)/shard_map/slice | solution.py:59
  32.9 0.2 squeeze.8
  33.1 0.8 %copy.25 = bf16[1,8,8,16,2,64]{5,4,3,2,1,0:T(2,128)(2,1)S(1)} copy(bf16[1,8,8,16,2,64]{5,0,3,1,4,2:T(2,128)(2,1)S(1)} %get-tuple-element.4) | data formatting | bytes 524288 | tf_op jit(solution)/shard_map/slice | solution.py:59
  34.0 0.2 squeeze.9
  34.2 0.3 convolution_convert_fusion
  34.5 0.2 reshape.113
  34.8 0.1 copy.30
  34.9 1.1 %reshape.114 = bf16[16,8,1024]{2,1,0:T(8,128)(2,1)} reshape(bf16[8,2,8,16,64]{4,3,2,1,0:T(8,128)(2,1)S(1)} %bitcast.47) | data formatting | bytes 524288 | tf_op jit(solution)/shard_map/reshape | solution.py:62
  35.9 0.0 copy-start.6
  35.9 0.0 copy-start.8
  35.9 4.2 %all-to-all-start.1 = ((bf16[16,8,1024]{2,1,0:T(8,128)(2,1)}), bf16[16,8,1024]{2,1,0:T(8,128)(2,1)S(1)}, u32[]{:S(2)}, u32[]{:S(2)}) async-start(bf16[16,8,1024]{2,1,0:T(8,128)(2,1)} %reshape.114), calls=%async_computation.1 | async-start | bytes 524288 | tf_op jit(solution)/shard_map/all_to_all | solution.py:63
  40.2 0.0 copy-done.6
  40.2 0.1 eq.16
  40.2 0.0 copy-done.8
  40.2 0.3 fusion.8
  40.5 9.6 %all-to-all-done.1 = bf16[16,8,1024]{2,1,0:T(8,128)(2,1)S(1)} async-done(((bf16[16,8,1024]{2,1,0:T(8,128)(2,1)}), bf16[16,8,1024]{2,1,0:T(8,128)(2,1)S(1)}, u32[]{:S(2)}, u32[]{:S(2)}) %all-to-all-start.1) | async-done | bytes 262176 | tf_op jit(solution)/shard_map/all_to_all | solution.py:63
  50.1 0.1 convert_reduce_fusion
  50.2 0.0 copy-start.5
  50.2 0.1 fusion.21
  50.3 0.6 copy-done.5
  51.0 0.0 copy-start.9
  51.0 0.3 fusion.12
  51.2 0.4 copy-done.9
  51.7 0.0 copy-start.2
  51.7 0.2 exponential_reduce_fusion
  51.9 0.5 copy-done.2
  52.4 0.6 multiply_reduce_fusion.1
  53.0 1.2 %broadcast_in_dim.6 = f32[16,1,128]{2,1,0:T(1,128)} broadcast(f32[]{:T(128)} %multiply_reduce_fusion.1), dimensions={} | broadcast | bytes 8196 | tf_op jit(solution)/shard_map/broadcast_in_dim | solution.py:81
  54.1 3.5 %all-to-all-start.2 = ((f32[16,1,128]{2,1,0:T(1,128)}), f32[16,1,128]{2,1,0:T(1,128)S(1)}, u32[]{:S(2)}, u32[]{:S(2)}) async-start(f32[16,1,128]{2,1,0:T(1,128)} %broadcast_in_dim.6), calls=%async_computation.2 | async-start | bytes 16384 | tf_op jit(solution)/shard_map/all_to_all | solution.py:80
  57.6 6.3 %all-to-all-done.2 = f32[16,1,128]{2,1,0:T(1,128)S(1)} async-done(((f32[16,1,128]{2,1,0:T(1,128)}), f32[16,1,128]{2,1,0:T(1,128)S(1)}, u32[]{:S(2)}, u32[]{:S(2)}) %all-to-all-start.2) | async-done | bytes 8224 | tf_op jit(solution)/shard_map/all_to_all | solution.py:80
  64.0 0.6 slice_reduce_fusion
  (6 shorter events, 0.0 us)
Async XLA Ops:
  0.6 4.1 %copy-start = (bf16[128,128]{1,0:T(8,128)(2,1)S(1)}, bf16[128,128]{1,0:T(8,128)(2,1)}, u32[]{:S(2)}) copy-start(bf16[128,128]{1,0:T(8,128)(2,1)} %param.14) | copy-start | bytes 98308
  0.6 3.3 %copy-start.1 = (bf16[16,64,128]{2,1,0:T(8,128)(2,1)S(1)}, bf16[16,64,128]{2,1,0:T(8,128)(2,1)}, u32[]{:S(2)}) copy-start(bf16[16,64,128]{2,1,0:T(8,128)(2,1)} %param.10) | copy-start | bytes 786436
  4.7 0.8 %copy-start.3 = (bf16[128,128]{1,0:T(8,128)(2,1)S(1)}, bf16[128,128]{1,0:T(8,128)(2,1)}, u32[]{:S(2)}) copy-start(bf16[128,128]{1,0:T(8,128)(2,1)} %param.13) | copy-start | bytes 98308
  5.9 0.8 %copy-start.7 = (bf16[128,128]{1,0:T(8,128)(2,1)S(1)}, bf16[128,128]{1,0:T(8,128)(2,1)}, u32[]{:S(2)}) copy-start(bf16[128,128]{1,0:T(8,128)(2,1)} %param.16) | copy-start | bytes 98308
  6.6 0.8 %copy-start.4 = (bf16[128,128]{1,0:T(8,128)(2,1)S(1)}, bf16[128,128]{1,0:T(8,128)(2,1)}, u32[]{:S(2)}) copy-start(bf16[128,128]{1,0:T(8,128)(2,1)} %param.15) | copy-start | bytes 98308
  35.9 4.2 %copy-start.6 = (s32[16,64]{1,0:T(8,128)S(1)}, s32[16,64]{1,0:T(8,128)}, u32[]{:S(2)}) copy-start(s32[16,64]{1,0:T(8,128)} %param.11) | copy-start | bytes 12292
  35.9 4.3 %copy-start.8 = (bf16[128,128]{1,0:T(8,128)(2,1)S(1)}, bf16[128,128]{1,0:T(8,128)(2,1)}, u32[]{:S(2)}) copy-start(bf16[128,128]{1,0:T(8,128)(2,1)} %param.18) | copy-start | bytes 98308
  35.9 14.2 %all-to-all-start.1 = ((bf16[16,8,1024]{2,1,0:T(8,128)(2,1)}), bf16[16,8,1024]{2,1,0:T(8,128)(2,1)S(1)}, u32[]{:S(2)}, u32[]{:S(2)}) async-start(bf16[16,8,1024]{2,1,0:T(8,128)(2,1)} %reshape.114), calls=%async_computation.1 | async-start | bytes 524288 | tf_op jit(solution)/shard_map/all_to_all | solution.py:63
  50.2 0.8 %copy-start.5 = (bf16[128,128]{1,0:T(8,128)(2,1)S(1)}, bf16[128,128]{1,0:T(8,128)(2,1)}, u32[]{:S(2)}) copy-start(bf16[128,128]{1,0:T(8,128)(2,1)} %param.17) | copy-start | bytes 98308
  51.0 0.7 %copy-start.9 = (bf16[128,64]{0,1:T(8,128)(2,1)S(1)}, bf16[128,64]{0,1:T(8,128)(2,1)}, u32[]{:S(2)}) copy-start(bf16[128,64]{0,1:T(8,128)(2,1)} %param.19) | copy-start | bytes 49156
  51.7 0.7 %copy-start.2 = (bf16[1024,128]{1,0:T(8,128)(2,1)}, bf16[1024,128]{1,0:T(8,128)(2,1)S(1)}, u32[]{:S(2)}) copy-start(bf16[1024,128]{1,0:T(8,128)(2,1)S(1)} %fusion.12) | copy-start | bytes 786436
  54.1 9.8 %all-to-all-start.2 = ((f32[16,1,128]{2,1,0:T(1,128)}), f32[16,1,128]{2,1,0:T(1,128)S(1)}, u32[]{:S(2)}, u32[]{:S(2)}) async-start(f32[16,1,128]{2,1,0:T(1,128)} %broadcast_in_dim.6), calls=%async_computation.2 | async-start | bytes 16384 | tf_op jit(solution)/shard_map/all_to_all | solution.py:80

commit v2 on v1

--- a/solution.py
+++ b/solution.py
@@ -77,11 +77,14 @@
         jnp.where(bin_ids[None, :] == distance_bins.reshape(-1, 1), logits, 0.0), axis=-1
     )
     loss_sum = jnp.sum(flat_mask * (log_total - picked))
-    sums = lax.all_to_all(
-        jnp.full((peers, 1, 128), loss_sum), AXES, split_axis=0, concat_axis=0, tiled=True
-    )
+    total = jnp.full((1, 128), loss_sum)
+    for axis, size in (("col", cols), ("row", rows)):
+        step = 1
+        while step < size:
+            total = total + lax.ppermute(total, axis, [(at, at ^ step) for at in range(size)])
+            step *= 2
     pair_count = (live_count * live_count).astype(jnp.float32)
-    loss_value = (jnp.sum(sums[:, 0, 0]) / pair_count).reshape(1)
+    loss_value = total[0, :1] / pair_count
     return (pair_out.reshape(pair_repr.shape), loss_value)
 
 

time: 67.1 us -> 69.9 us (1.042)
  waiting for transfers between devices: 15.9 us -> 20.1 us
  starting transfers between devices: 7.72 us -> 6.51 us
  other arithmetic: 3.64 us -> 4.5 us
    ppermute x0 -> x4, waiting for transfers between devices: none -> 10.5 us  [on_device(): lax.ppermute(total, axis, [(at, at ^ step) for at in range(size)])]
    all_to_all x1 -> x0, waiting for transfers between devices: 6.33 us -> none  [on_device(): lax.all_to_all(jnp.full((peers, 1, 128), loss_sum), AXES, split_axis=0, c...]
    all_to_all x1 -> x0, starting transfers between devices: 3.49 us -> none  [on_device(): lax.all_to_all(jnp.full((peers, 1, 128), loss_sum), AXES, split_axis=0, c...]
    ppermute x0 -> x4, starting transfers between devices: none -> 2.28 us  [on_device(): lax.ppermute(total, axis, [(at, at ^ step) for at in range(size)])]
    add x0 -> x4, other arithmetic: none -> 1.39 us  [on_device(): total + lax.ppermute(total, axis, [(at, at ^ step) for at in range(size)])]
  transfers between devices with their start and end apart: 2 -> 5, of which waited for: 2 -> 5; matrix products, arithmetic and copies ran while one was open for 1% -> 1% of each run, Pallas kernels for 0% -> 0%
where the time goes in v2:
time: 69.9 us; the launch traced here: 69.2 us
  blocking collectives  21.7 us (31%)
  waiting for transfers between devices  20.1 us (29%)
  local copies, waits for them, and re-layouts  11.4 us (16%)
  starting transfers between devices  6.51 us (9%)
  other arithmetic  4.5 us (6%)
  between operations  2.79 us (4%)
  matrix products  2.1 us (3%)
    all_to_all x1, blocking collectives, on_device(): owned = lax.all_to_all(both, AXES, split_axis=0, concat_axis=0, tiled=True)  21.7 us
    ppermute x4, waiting for transfers between devices, on_device(): lax.ppermute(total, axis, [(at, at ^ step) for at in range(size)])  10.5 us
    all_to_all x1, waiting for transfers between devices, on_device(): tri = lax.all_to_all(tri, AXES, split_axis=0, concat_axis=0, tiled=True)  9.59 us
    all_to_all x1, starting transfers between devices, on_device(): tri = lax.all_to_all(tri, AXES, split_axis=0, concat_axis=0, tiled=True)  4.23 us
    unnamed x20, local copies, waits for them, and re-layouts  2.91 us
    slice x2, local copies, waits for them, and re-layouts, on_device(): owned[1]  2.35 us
    ppermute x4, starting transfers between devices, on_device(): lax.ppermute(total, axis, [(at, at ^ step) for at in range(size)])  2.28 us
  transfers between devices with their start and end apart: 5, of which 5 were waited for; matrix products, arithmetic and copies ran while one was open for 1% of the time, Pallas kernels for 0%

profile of v2, /device:TPU:0, one launch (start us, length us, event | category | flops | bytes accessed | tf_op | source)
XLA Modules:
  0.0 69.2 jit_solution(12422037854530407781)
XLA Ops:
  0.6 0.0 copy-start
  0.6 0.0 copy-start.1
  0.7 1.3 %slice.14 = s32[1]{0:T(128)} slice(s32[5]{0:T(128)} %param.12), slice={[4:5]} | slice | bytes 8 | tf_op jit(solution)/shard_map/slice | solution.py:34
  2.6 0.1 broadcast_multiply_fusion
  2.7 0.1 mul.96
  2.8 1.2 %convert_reduce_fusion.1 = f32[16,64]{1,0:T(8,128)S(1)} fusion(bf16[16,64,128]{2,1,0:T(8,128)(2,1)} %param.10), kind=kLoop, calls=%fused_computation.36 | loop fusion | flops 261120 | bytes 266240 | tf_op jit(solution)/shard_map/reduce_sum | solution.py:10
  3.9 0.0 copy-done.1
  4.0 0.4 multiply_reduce_fusion
  4.4 0.3 multiply_convert_fusion
  4.7 0.0 copy-done
  4.7 0.0 copy-start.3
  4.7 0.3 fusion.5
  5.0 0.5 copy-done.3
  5.5 0.2 fusion.15
  5.7 0.1 copy.12
  5.9 0.0 copy-start.7
  5.9 0.3 concatenate.8
  6.2 0.4 copy-done.7
  6.6 0.0 copy-start.4
  6.6 0.3 fusion.2
  6.9 0.5 copy-done.4
  7.4 0.2 fusion.16
  7.6 0.1 copy.13
  7.8 0.3 concatenate.9
  8.1 0.3 pad_maximum_fusion
  8.4 21.7 %all_to_all.10 = bf16[16,128,128]{2,1,0:T(8,128)(2,1)S(1)} all-to-all(bf16[16,128,128]{2,1,0:T(8,128)(2,1)S(1)} %pad_maximum_fusion), channel_id=1, replica_groups=mesh['groups'=2,'row'=8,'col'=2] {'row','col'}, dimensions={0} | all-to-all | bytes 1048576 | tf_op jit(solution)/shard_map/all_to_all | solution.py:55
  30.1 0.4 reshape.109
  30.5 1.5 %fusion.25 = (bf16[1,8,8,16,2,64]{5,0,3,1,4,2:T(2,128)(2,1)S(1)}, bf16[1,8,8,16,2,64]{5,0,3,1,4,2:T(2,128)(2,1)S(1)}) fusion(bf16[2,8,8,16,2,64]{5,0,3,1,4,2:T(2,128)(2,1)S(1)} %bitcast.42), kind=kLoop, calls=%fused_computation.51 | loop fusion | bytes 1048576 | tf_op jit(solution)/shard_map/slice | solution.py:59
  32.1 0.8 %copy.14 = bf16[1,8,8,16,2,64]{5,4,3,2,1,0:T(2,128)(2,1)S(1)} copy(bf16[1,8,8,16,2,64]{5,0,3,1,4,2:T(2,128)(2,1)S(1)} %get-tuple-element.5) | data formatting | bytes 524288 | tf_op jit(solution)/shard_map/slice | solution.py:59
  32.9 0.2 squeeze.10
  33.1 0.8 %copy.15 = bf16[1,8,8,16,2,64]{5,4,3,2,1,0:T(2,128)(2,1)S(1)} copy(bf16[1,8,8,16,2,64]{5,0,3,1,4,2:T(2,128)(2,1)S(1)} %get-tuple-element.4) | data formatting | bytes 524288 | tf_op jit(solution)/shard_map/slice | solution.py:59
  34.0 0.2 squeeze.11
  34.2 0.3 convolution_convert_fusion
  34.5 0.2 reshape.110
  34.8 0.1 copy.18
  34.9 1.1 %reshape.111 = bf16[16,8,1024]{2,1,0:T(8,128)(2,1)} reshape(bf16[8,2,8,16,64]{4,3,2,1,0:T(8,128)(2,1)S(1)} %bitcast.49) | data formatting | bytes 524288 | tf_op jit(solution)/shard_map/reshape | solution.py:62
  35.9 0.0 copy-start.8
  35.9 4.2 %all-to-all-start.1 = ((bf16[16,8,1024]{2,1,0:T(8,128)(2,1)}), bf16[16,8,1024]{2,1,0:T(8,128)(2,1)S(1)}, u32[]{:S(2)}, u32[]{:S(2)}) async-start(bf16[16,8,1024]{2,1,0:T(8,128)(2,1)} %reshape.111), calls=%async_computation.1 | async-start | bytes 524288 | tf_op jit(solution)/shard_map/all_to_all | solution.py:63
  40.2 0.0 copy-done.6
  40.2 0.1 eq.16
  40.2 0.0 copy-done.8
  40.2 0.3 fusion.8
  40.5 9.6 %all-to-all-done.1 = bf16[16,8,1024]{2,1,0:T(8,128)(2,1)S(1)} async-done(((bf16[16,8,1024]{2,1,0:T(8,128)(2,1)}), bf16[16,8,1024]{2,1,0:T(8,128)(2,1)S(1)}, u32[]{:S(2)}, u32[]{:S(2)}) %all-to-all-start.1) | async-done | bytes 262176 | tf_op jit(solution)/shard_map/all_to_all | solution.py:63
  50.1 0.1 convert_reduce_fusion
  50.2 0.0 copy-start.5
  50.2 0.1 fusion.21
  50.3 0.6 copy-done.5
  51.0 0.0 copy-start.9
  51.0 0.3 fusion.12
  51.2 0.4 copy-done.9
  51.7 0.2 exponential_reduce_fusion
  51.9 0.5 copy-done.2
  52.4 0.7 multiply_reduce_fusion.1
  53.1 0.7 broadcast_in_dim.6
  53.8 0.6 collective-permute-start
  54.4 3.0 %collective-permute-done = f32[1,128]{1,0:T(1,128)S(1)} collective-permute-done((f32[1,128]{1,0:T(1,128)S(1)}, f32[1,128]{1,0:T(1,128)S(1)}, u32[]{:S(2)}, u32[]{:S(2)}) %collective-permute-start) | collective-permute-done | bytes 544 | tf_op jit(solution)/shard_map/ppermute | solution.py:84
  57.4 0.7 broadcast_add_fusion
  58.1 0.1 collective-permute-start.1
  58.1 1.1 %collective-permute-done.1 = f32[1,128]{1,0:T(1,128)S(1)} collective-permute-done((f32[1,128]{1,0:T(1,128)S(1)}, f32[1,128]{1,0:T(1,128)S(1)}, u32[]{:S(2)}, u32[]{:S(2)}) %collective-permute-start.1) | collective-permute-done | bytes 544 | tf_op jit(solution)/shard_map/ppermute | solution.py:84
  59.2 0.7 %fusion.41 = f32[1,128]{1,0:T(1,128)S(1)} fusion(f32[1,128]{1,0:T(1,128)S(1)} %collective-permute-done.1, f32[1,128]{1,0:T(1,128)S(1)} %collective-permute-done, f32[]{:T(128)} %multiply_reduce_fusion.1), kind=kLoop, calls=%fused_computation.52 | loop fusion | flops 256 | bytes 1540 | tf_op jit(solution)/shard_map/add | solution.py:84
  59.9 1.0 %collective-permute-start.2 = (f32[1,128]{1,0:T(1,128)S(1)}, f32[1,128]{1,0:T(1,128)S(1)}, u32[]{:S(2)}, u32[]{:S(2)}) collective-permute-start(f32[1,128]{1,0:T(1,128)S(1)} %fusion.41), channel_id=1, source_target_pairs={{0,4},{2,6},{4,0},{6,2},{8,12},{10,14},{12,8},{14,10},{1,5},{3,7},... | collective-permute-start | bytes 1544 | tf_op jit(solution)/shard_map/ppermute | solution.py:84
  61.0 2.6 %collective-permute-done.2 = f32[1,128]{1,0:T(1,128)S(1)} collective-permute-done((f32[1,128]{1,0:T(1,128)S(1)}, f32[1,128]{1,0:T(1,128)S(1)}, u32[]{:S(2)}, u32[]{:S(2)}) %collective-permute-start.2) | collective-permute-done | bytes 544 | tf_op jit(solution)/shard_map/ppermute | solution.py:84
  63.6 0.6 collective-permute-start.3
  64.1 3.9 %collective-permute-done.3 = f32[1,128]{1,0:T(1,128)S(1)} collective-permute-done((f32[1,128]{1,0:T(1,128)S(1)}, f32[1,128]{1,0:T(1,128)S(1)}, u32[]{:S(2)}, u32[]{:S(2)}) %collective-permute-start.3) | collective-permute-done | bytes 544 | tf_op jit(solution)/shard_map/ppermute | solution.py:84
  (10 shorter events, 0.0 us)
Async XLA Ops:
  0.6 4.1 %copy-start = (bf16[128,128]{1,0:T(8,128)(2,1)S(1)}, bf16[128,128]{1,0:T(8,128)(2,1)}, u32[]{:S(2)}) copy-start(bf16[128,128]{1,0:T(8,128)(2,1)} %param.14) | copy-start | bytes 98308
  0.6 3.3 %copy-start.1 = (bf16[16,64,128]{2,1,0:T(8,128)(2,1)S(1)}, bf16[16,64,128]{2,1,0:T(8,128)(2,1)}, u32[]{:S(2)}) copy-start(bf16[16,64,128]{2,1,0:T(8,128)(2,1)} %param.10) | copy-start | bytes 786436
  4.7 0.8 %copy-start.3 = (bf16[128,128]{1,0:T(8,128)(2,1)S(1)}, bf16[128,128]{1,0:T(8,128)(2,1)}, u32[]{:S(2)}) copy-start(bf16[128,128]{1,0:T(8,128)(2,1)} %param.13) | copy-start | bytes 98308
  5.9 0.8 %copy-start.7 = (bf16[128,128]{1,0:T(8,128)(2,1)S(1)}, bf16[128,128]{1,0:T(8,128)(2,1)}, u32[]{:S(2)}) copy-start(bf16[128,128]{1,0:T(8,128)(2,1)} %param.16) | copy-start | bytes 98308
  6.6 0.8 %copy-start.4 = (bf16[128,128]{1,0:T(8,128)(2,1)S(1)}, bf16[128,128]{1,0:T(8,128)(2,1)}, u32[]{:S(2)}) copy-start(bf16[128,128]{1,0:T(8,128)(2,1)} %param.15) | copy-start | bytes 98308
  35.9 4.2 %copy-start.6 = (s32[16,64]{1,0:T(8,128)S(1)}, s32[16,64]{1,0:T(8,128)}, u32[]{:S(2)}) copy-start(s32[16,64]{1,0:T(8,128)} %param.11) | copy-start | bytes 12292
  35.9 4.3 %copy-start.8 = (bf16[128,128]{1,0:T(8,128)(2,1)S(1)}, bf16[128,128]{1,0:T(8,128)(2,1)}, u32[]{:S(2)}) copy-start(bf16[128,128]{1,0:T(8,128)(2,1)} %param.18) | copy-start | bytes 98308
  35.9 14.2 %all-to-all-start.1 = ((bf16[16,8,1024]{2,1,0:T(8,128)(2,1)}), bf16[16,8,1024]{2,1,0:T(8,128)(2,1)S(1)}, u32[]{:S(2)}, u32[]{:S(2)}) async-start(bf16[16,8,1024]{2,1,0:T(8,128)(2,1)} %reshape.111), calls=%async_computation.1 | async-start | bytes 524288 | tf_op jit(solution)/shard_map/all_to_all | solution.py:63
  50.2 0.8 %copy-start.5 = (bf16[128,128]{1,0:T(8,128)(2,1)S(1)}, bf16[128,128]{1,0:T(8,128)(2,1)}, u32[]{:S(2)}) copy-start(bf16[128,128]{1,0:T(8,128)(2,1)} %param.17) | copy-start | bytes 98308
  51.0 0.7 %copy-start.9 = (bf16[128,64]{0,1:T(8,128)(2,1)S(1)}, bf16[128,64]{0,1:T(8,128)(2,1)}, u32[]{:S(2)}) copy-start(bf16[128,64]{0,1:T(8,128)(2,1)} %param.19) | copy-start | bytes 49156
  51.7 0.7 %copy-start.2 = (bf16[1024,128]{1,0:T(8,128)(2,1)}, bf16[1024,128]{1,0:T(8,128)(2,1)S(1)}, u32[]{:S(2)}) copy-start(bf16[1024,128]{1,0:T(8,128)(2,1)S(1)} %fusion.12) | copy-start | bytes 786436
  53.8 3.6 %collective-permute-start = (f32[1,128]{1,0:T(1,128)S(1)}, f32[1,128]{1,0:T(1,128)S(1)}, u32[]{:S(2)}, u32[]{:S(2)}) collective-permute-start(f32[1,128]{1,0:T(1,128)S(1)} %broadcast_in_dim.6), channel_id=1, source_target_pairs={{0,1},{1,0},{2,3},{3,2},{4,5},{5,4},{6,7},{7,6},{8,9},{9,8},{10,11... | collective-permute-start | bytes 1544 | tf_op jit(solution)/shard_map/ppermute | solution.py:84
  58.1 1.2 %collective-permute-start.1 = (f32[1,128]{1,0:T(1,128)S(1)}, f32[1,128]{1,0:T(1,128)S(1)}, u32[]{:S(2)}, u32[]{:S(2)}) collective-permute-start(f32[1,128]{1,0:T(1,128)S(1)} %broadcast_add_fusion), channel_id=1, source_target_pairs={{0,2},{2,0},{4,6},{6,4},{8,10},{10,8},{12,14},{14,12},{1,3},{3,1},... | collective-permute-start | bytes 1544 | tf_op jit(solution)/shard_map/ppermute | solution.py:84
  59.9 3.6 %collective-permute-start.2 = (f32[1,128]{1,0:T(1,128)S(1)}, f32[1,128]{1,0:T(1,128)S(1)}, u32[]{:S(2)}, u32[]{:S(2)}) collective-permute-start(f32[1,128]{1,0:T(1,128)S(1)} %fusion.41), channel_id=1, source_target_pairs={{0,4},{2,6},{4,0},{6,2},{8,12},{10,14},{12,8},{14,10},{1,5},{3,7},... | collective-permute-start | bytes 1544 | tf_op jit(solution)/shard_map/ppermute | solution.py:84
  63.6 4.4 %collective-permute-start.3 = (f32[1,128]{1,0:T(1,128)S(1)}, f32[1,128]{1,0:T(1,128)S(1)}, u32[]{:S(2)}, u32[]{:S(2)}) collective-permute-start(f32[1,128]{1,0:T(1,128)S(1)} %add.82), channel_id=1, source_target_pairs={{0,8},{2,10},{4,12},{6,14},{8,0},{10,2},{12,4},{14,6},{1,9},{3,11}... | collective-permute-start | bytes 1544 | tf_op jit(solution)/shard_map/ppermute | solution.py:84

commit v3 on v1

--- a/solution.py
+++ b/solution.py
@@ -1,9 +1,15 @@
 import jax
 import jax.numpy as jnp
 from jax import lax
+from jax.experimental import pallas as pl
+from jax.experimental.pallas import tpu as pltpu
 from jax.sharding import PartitionSpec as P
 
 AXES = ("row", "col")
+OWNERS = 4
+VMEM = pl.BlockSpec(memory_space=pltpu.VMEM)
+SMEM = pl.BlockSpec(memory_space=pltpu.SMEM)
+PARAMS = pltpu.CompilerParams(vmem_limit_bytes=24 * 1024 * 1024)
 
 
 def layer_norm(values, axis):
@@ -13,7 +19,278 @@
     return centred * lax.rsqrt(spread + 1e-05)
 
 
-def on_device(
+def sigmoid(values):
+    return 0.5 * jnp.tanh(0.5 * values) + 0.5
+
+
+def nt_dot(a, b):
+    return lax.dot_general(a, b, (((1,), (1,)), ((), ())), preferred_element_type=jnp.float32)
+
+
+def tn_dot(a, b):
+    return lax.dot_general(a, b, (((0,), (0,)), ((), ())), preferred_element_type=jnp.float32)
+
+
+def lanes_of(shape):
+    return lax.broadcasted_iota(jnp.int32, shape, 1)
+
+
+def pair_mask(lens_ref, tile_rows, tile_cols, first):
+    live = tile_rows * lax.axis_size("row") - lens_ref[lens_ref.shape[0] - 1]
+    lane = lanes_of((1, 2 * tile_cols))
+    row = lax.axis_index("row") * tile_rows + first + (lane >= tile_cols).astype(jnp.int32)
+    col = lax.axis_index("col") * tile_cols + lane % tile_cols
+    return ((row < live) & (col < live)).astype(jnp.float32)
+
+
+def project_kernel(lens_ref, x_ref, lw_ref, lg_ref, rw_ref, rg_ref, *refs):
+    normed_ref, outs, (turned, held_left, held_right) = refs[0], refs[1:-3], refs[-3:]
+    tile_rows, tile_cols, channels = x_ref.shape
+    share = channels // OWNERS
+    half = share // 2
+    packed = OWNERS * half
+    for at, w_ref in enumerate((lw_ref, lg_ref, rw_ref, rg_ref)):
+        w = w_ref[...].astype(jnp.float32).T
+        blocks = [
+            w[o * share + g * half : o * share + (g + 1) * half] for g in (0, 1) for o in range(OWNERS)
+        ]
+        turned[at * channels : (at + 1) * channels] = jnp.concatenate(blocks, 0).astype(jnp.bfloat16)
+    low = lanes_of((packed, 2 * tile_cols)) < tile_cols
+    for first in range(0, tile_rows, 2):
+        x = x_ref[first : first + 2].astype(jnp.float32).reshape(2 * tile_cols, channels)
+        normed = layer_norm(x, -1).astype(jnp.bfloat16)
+        normed_ref[first * tile_cols : (first + 2) * tile_cols] = normed
+        flat = nt_dot(turned[...], normed)
+        mask = pair_mask(lens_ref, tile_rows, tile_cols, first)
+        for at, held in ((0, held_left), (2, held_right)):
+            value = flat[at * channels : (at + 1) * channels]
+            gate = flat[(at + 1) * channels : (at + 2) * channels]
+            value = sigmoid(gate) * value * mask
+            a, b = value[:packed], value[packed:]
+            held[pl.ds(first, packed, stride=tile_rows), :] = jnp.where(
+                low, a, pltpu.roll(b, tile_cols, 1)
+            )
+            held[pl.ds(first + 1, packed, stride=tile_rows), :] = jnp.where(
+                low, pltpu.roll(a, tile_cols, 1), b
+            )
+    me = lax.axis_index("row") % OWNERS
+    size = half * tile_rows
+    for d in range(OWNERS):
+        at = pl.multiple_of((me ^ d) * size, size)
+        right = held_right[pl.ds(at, size)].astype(jnp.bfloat16)
+        outs[d][:size] = held_left[pl.ds(at, size)].astype(jnp.bfloat16)
+        outs[d][size:] = right
+        outs[OWNERS + d][...] = right
+
+
+def gate_kernel(normed_ref, w_ref, gate_ref):
+    gate_ref[...] = sigmoid(jnp.dot(normed_ref[...], w_ref[...], preferred_element_type=jnp.float32))
+
+
+def tri_kernel(*refs):
+    near, far, outs = refs[:OWNERS], refs[OWNERS : 2 * OWNERS], refs[2 * OWNERS : -1]
+    rights = refs[-1]
+    size, width = far[0].shape
+    half = rights.shape[0]
+    tile_rows = size // half
+    side = OWNERS * tile_rows
+    me = lax.axis_index("row")
+    owner, part, col = me % OWNERS, me // OWNERS, lax.axis_index("col")
+    for d in range(OWNERS):
+        for away, ref in ((0, near[d]), (1, far[d])):
+            at = pl.multiple_of((part ^ away) * side + (owner ^ d) * tile_rows, tile_rows)
+            start = size if away == 0 else 0
+            for m in range(half):
+                rights[m, pl.ds(at, tile_rows), :] = ref[
+                    start + m * tile_rows : start + (m + 1) * tile_rows
+                ]
+    low = lanes_of((side, width)) < width // 2
+    for m in range(half):
+        left = jnp.concatenate([near[d][m * tile_rows : (m + 1) * tile_rows] for d in range(OWNERS)], 0)
+        pieces = []
+        for dx in (0, 1):
+            block = rights[m, pl.ds(pl.multiple_of((col ^ dx) * side, side), side), :].astype(jnp.float32)
+            pieces += [jnp.where(low, block, 0.0), jnp.where(low, 0.0, block)]
+        right = jnp.concatenate(pieces, 0).astype(jnp.bfloat16)
+        product = nt_dot(left, right).astype(jnp.bfloat16)
+        for d in range(OWNERS):
+            for dx in (0, 1):
+                outs[2 * d + dx][m * tile_rows : (m + 1) * tile_rows] = product[
+                    d * tile_rows : (d + 1) * tile_rows, dx * width : (dx + 1) * width
+                ]
+
+
+def finish_kernel(lens_ref, x_ref, gate_ref, bins_ref, ow_ref, dw_ref, *refs):
+    parts, out_ref, loss_ref, (held, wide) = refs[:8], refs[8], refs[9], refs[10:]
+    tile_rows, tile_cols, channels = x_ref.shape
+    size, width = parts[0].shape
+    half = size // tile_rows
+    packed = OWNERS * half
+    owner = lax.axis_index("row") % OWNERS
+    total = jnp.zeros((tile_rows, width), jnp.float32)
+    for d in range(OWNERS):
+        block = parts[2 * d][...].astype(jnp.float32) + parts[2 * d + 1][...].astype(jnp.float32)
+        held[pl.ds(pl.multiple_of((owner ^ d) * size, size), size), :] = block
+        total = total + jnp.sum(block.reshape(half, tile_rows, width), 0)
+    average = (total + pltpu.roll(total, tile_cols, 1)) * (1.0 / channels)
+    total = jnp.zeros((tile_rows, width), jnp.float32)
+    for om in range(packed):
+        centred = held[om * tile_rows : (om + 1) * tile_rows] - average
+        total = total + centred * centred
+    spread = (total + pltpu.roll(total, tile_cols, 1)) * (1.0 / channels)
+    scale = lax.rsqrt(spread + 1e-05)
+    for om in range(packed):
+        at = slice(om * tile_rows, (om + 1) * tile_rows)
+        held[at] = (held[at] - average) * scale
+    share = channels // OWNERS
+    for o in range(OWNERS):
+        for g in (0, 1):
+            wide[o * half : (o + 1) * half, g * channels : (g + 1) * channels] = ow_ref[
+                o * share + g * half : o * share + (g + 1) * half
+            ]
+    dist = dw_ref[...].astype(jnp.float32).T.astype(jnp.bfloat16)
+    bin_ids = lax.broadcasted_iota(jnp.int32, (dist.shape[0], width), 0)
+    loss = jnp.zeros((1, width), jnp.float32)
+    for first in range(0, tile_rows, 2):
+        updates = []
+        for ii in (first, first + 1):
+            turned = held[pl.ds(ii, packed, stride=tile_rows), :].astype(jnp.bfloat16)
+            both = tn_dot(turned, wide[...])
+            updates.append(both[:tile_cols, :channels] + both[tile_cols:, channels:])
+        update = jnp.concatenate(updates, 0)
+        gate = gate_ref[first * tile_cols : (first + 2) * tile_cols]
+        x = x_ref[first : first + 2].astype(jnp.float32).reshape(2 * tile_cols, channels)
+        pair_out = (x + gate * update).astype(jnp.bfloat16)
+        out_ref[first : first + 2] = pair_out.reshape(2, tile_cols, channels)
+        logits = nt_dot(dist, pair_out)
+        log_total = jnp.log(jnp.sum(jnp.exp(logits), axis=0, keepdims=True))
+        bins = bins_ref[first // 2 : first // 2 + 1]
+        picked = jnp.sum(jnp.where(bin_ids == bins, logits, 0.0), axis=0, keepdims=True)
+        loss = loss + pair_mask(lens_ref, tile_rows, tile_cols, first) * (log_total - picked)
+    loss_ref[...] = jnp.broadcast_to(jnp.sum(loss, axis=1, keepdims=True), loss_ref.shape)
+
+
+def loss_kernel(residues, lens_ref, *refs):
+    total = refs[0][...]
+    for ref in refs[1:-1]:
+        total = total + ref[...]
+    live = residues - lens_ref[lens_ref.shape[0] - 1]
+    count = jnp.full(total.shape, live * live, jnp.int32).astype(jnp.float32)
+    refs[-1][0] = (total / count)[0, 0]
+
+
+def exchange(value, places, mask):
+    return lax.ppermute(value, AXES, [(at, at ^ mask) for at in range(places)])
+
+
+def call(kernel, outs, scratch=(), specs=None, out_specs=None, args=(), flops=0):
+    return pl.pallas_call(
+        kernel,
+        out_shape=outs,
+        in_specs=specs if specs is not None else [VMEM] * len(args),
+        out_specs=out_specs if out_specs is not None else jax.tree.map(lambda _: VMEM, outs),
+        scratch_shapes=list(scratch),
+        compiler_params=PARAMS,
+        cost_estimate=pl.CostEstimate(flops=flops, bytes_accessed=1 << 20, transcendentals=1 << 18),
+    )(*args)
+
+
+def by_kernels(
+    pair_repr,
+    distance_bins,
+    chain_lengths,
+    left_weight,
+    left_gate_weight,
+    right_weight,
+    right_gate_weight,
+    out_weight,
+    out_gate_weight,
+    dist_weight,
+):
+    tile_rows, tile_cols, channels = pair_repr.shape
+    rows, cols = lax.axis_size("row"), lax.axis_size("col")
+    places = rows * cols
+    width = 2 * tile_cols
+    spots = tile_rows * tile_cols
+    size = channels // OWNERS // 2 * tile_rows
+    bf16, f32 = jnp.bfloat16, jnp.float32
+    struct = jax.ShapeDtypeStruct
+    sent = call(
+        project_kernel,
+        [struct((spots, channels), bf16)]
+        + [struct((2 * size, width), bf16)] * OWNERS
+        + [struct((size, width), bf16)] * OWNERS,
+        [
+            pltpu.VMEM((4 * channels, channels), bf16),
+            pltpu.VMEM((OWNERS * size, width), f32),
+            pltpu.VMEM((OWNERS * size, width), f32),
+        ],
+        [SMEM] + [VMEM] * 5,
+        args=(
+            chain_lengths,
+            pair_repr,
+            left_weight,
+            left_gate_weight,
+            right_weight,
+            right_gate_weight,
+        ),
+        flops=8 * spots * channels * channels,
+    )
+    normed, near, far = sent[0], sent[1 : 1 + OWNERS], sent[1 + OWNERS :]
+    far = [exchange(value, places, (OWNERS + d) * cols) for d, value in enumerate(far)]
+    near = [near[0]] + [exchange(near[d], places, d * cols) for d in range(1, OWNERS)]
+    gate = call(
+        gate_kernel,
+        struct((spots, channels), f32),
+        args=(normed, out_gate_weight),
+        flops=2 * spots * channels * channels,
+    )
+    parts = call(
+        tri_kernel,
+        [struct((size, width), bf16)] * (2 * OWNERS),
+        [pltpu.VMEM((size // tile_rows, rows * tile_rows, width), bf16)],
+        args=(*near, *far),
+        flops=2 * OWNERS * size * 2 * OWNERS * tile_rows * width,
+    )
+    parts = [parts[0]] + [exchange(parts[at], places, at) for at in range(1, 2 * OWNERS)]
+    pair_out, loss = call(
+        finish_kernel,
+        [struct(pair_repr.shape, bf16), struct((8, 128), f32)],
+        [
+            pltpu.VMEM((OWNERS * size, width), f32),
+            pltpu.VMEM((channels // 2, 2 * channels), bf16),
+        ],
+        [SMEM] + [VMEM] * 13,
+        args=(
+            chain_lengths,
+            pair_repr,
+            gate,
+            distance_bins.reshape(tile_rows // 2, width),
+            out_weight,
+            dist_weight,
+            *parts,
+        ),
+        flops=6 * spots * channels * channels,
+    )
+    loss = loss + exchange(loss, places, cols)
+    losses = [loss] + [
+        exchange(loss, places, z * 2 * cols + x)
+        for z in range(rows // 2)
+        for x in range(cols)
+        if z or x
+    ]
+    loss_value = call(
+        lambda *refs: loss_kernel(rows * tile_rows, *refs),
+        struct((1,), f32),
+        (),
+        [SMEM] + [VMEM] * len(losses),
+        SMEM,
+        args=(chain_lengths, *losses),
+    )
+    return (pair_out, loss_value)
+
+
+def by_all_to_all(
     pair_repr,
     distance_bins,
     chain_lengths,
@@ -64,9 +341,7 @@
     tri = tri.reshape(channels, spots).astype(jnp.float32)
     tri_normed = layer_norm(tri, 0).astype(jnp.bfloat16)
     out_gate = jax.nn.sigmoid(jnp.dot(normed, out_gate_weight, preferred_element_type=jnp.float32))
-    update = out_gate * lax.dot_general(
-        tri_normed, out_weight, (((0,), (0,)), ((), ())), preferred_element_type=jnp.float32
-    )
+    update = out_gate * tn_dot(tri_normed, out_weight)
     pair_out = (pair_repr.astype(jnp.float32).reshape(spots, channels) + update).astype(
         jnp.bfloat16
     )
@@ -85,6 +360,20 @@
     return (pair_out.reshape(pair_repr.shape), loss_value)
 
 
+def on_device(pair_repr, *others):
+    tile_rows, tile_cols, channels = pair_repr.shape
+    rows, cols = lax.axis_size("row"), lax.axis_size("col")
+    fits = (
+        rows == 2 * OWNERS
+        and cols == 2
+        and tile_rows * rows == tile_cols * cols
+        and 2 * tile_cols == 128
+        and tile_rows % 16 == 0
+        and channels % (32 * OWNERS) == 0
+    )
+    return (by_kernels if fits else by_all_to_all)(pair_repr, *others)
+
+
 def solution(mesh):
     in_specs = (
         P(("groups", "row"), "col", None),

time: 67.1 us -> 59.3 us (0.88)
  starting transfers between devices: 7.72 us -> 30 us
  blocking collectives: 21.7 us -> 0 us
  local copies, waits for them, and re-layouts: 11.9 us -> 4.84 us
  Pallas kernels: 0 us -> 6.83 us
  other arithmetic: 3.64 us -> 0.01 us
  between operations: 3.37 us -> 0.76 us
  matrix products: 2.1 us -> 0 us
    ppermute x0 -> x22, starting transfers between devices: none -> 30 us  [exchange(): return lax.ppermute(value, AXES, [(at, at ^ mask) for at in range(places)])]
    all_to_all x1 -> x0, blocking collectives: 21.7 us -> none  [on_device(): owned = lax.all_to_all(both, AXES, split_axis=0, concat_axis=0, tiled=True)]
    ppermute x0 -> x22, waiting for transfers between devices: none -> 16.4 us  [exchange(): return lax.ppermute(value, AXES, [(at, at ^ mask) for at in range(places)])]
    all_to_all x2 -> x0, waiting for transfers between devices: 15.9 us -> none  [the longest x1 9.59 us: on_device(): tri = lax.all_to_all(tri, AXES, split_axis=0, concat_axis=0, tiled=True)]
    all_to_all x2 -> x0, starting transfers between devices: 7.72 us -> none  [the longest x1 4.23 us: on_device(): tri = lax.all_to_all(tri, AXES, split_axis=0, concat_axis=0, tiled=True)]
    pallas_call x0 -> x5, Pallas kernels: none -> 6.83 us  [call(): pl.pallas_call(kernel, out_shape=outs, in_specs=specs if specs is not Non...]
    slice x4 -> x0, local copies, waits for them, and re-layouts: 4.44 us -> none  [the longest x2 2.35 us: on_device(): owned[1]]
    reduce_sum x6 -> x0, other arithmetic: 2.9 us -> none  [the longest x2 1.21 us: layer_norm(): average = jnp.mean(values, axis=axis, keepdims=True)]
  transfers between devices with their start and end apart: 2 -> 22, of which waited for: 2 -> 10; matrix products, arithmetic and copies ran while one was open for 1% -> 0% of each run, Pallas kernels for 0% -> 0%
where the time goes in v3:
time: 59.3 us; the launch traced here: 58.9 us
  starting transfers between devices  30 us (51%)
  waiting for transfers between devices  16.4 us (28%)
  Pallas kernels  6.83 us (12%)
  local copies, waits for them, and re-layouts  4.84 us (8%)
  between operations  0.76 us (1%)
    ppermute x22, starting transfers between devices, exchange(): return lax.ppermute(value, AXES, [(at, at ^ mask) for at in range(places)])  30 us
    ppermute x22, waiting for transfers between devices, exchange(): return lax.ppermute(value, AXES, [(at, at ^ mask) for at in range(places)])  16.4 us
    pallas_call x5, Pallas kernels, call(): pl.pallas_call(kernel, out_shape=outs, in_specs=specs if specs is not Non...  6.83 us
    unnamed x25, local copies, waits for them, and re-layouts  4.77 us
  transfers between devices with their start and end apart: 22, of which 10 were waited for; matrix products, arithmetic and copies ran while one was open for 0% of the time, Pallas kernels for 0%

profile of v3, /device:TPU:0, one launch (start us, length us, event | category | flops | bytes accessed | tf_op | source)
XLA Modules:
  0.0 58.9 jit_solution(1869212724920229773)
XLA Ops:
  0.6 0.0 copy-start
  0.6 0.9 %copy-done = bf16[16,64,128]{2,1,0:T(8,128)(2,1)S(1)} copy-done((bf16[16,64,128]{2,1,0:T(8,128)(2,1)S(1)}, bf16[16,64,128]{2,1,0:T(8,128)(2,1)}, u32[]{:S(2)}) %copy-start) | copy-done | bytes 262168
  1.6 0.7 %copy-done.4 = s32[5]{0:T(128)S(1)} copy-done((s32[5]{0:T(128)S(1)}, s32[5]{0:T(128)}, u32[]{:S(2)}) %copy-start.4) | copy-done | bytes 44
  2.2 0.8 %copy-done.6 = bf16[128,128]{1,0:T(8,128)(2,1)S(1)} copy-done((bf16[128,128]{1,0:T(8,128)(2,1)S(1)}, bf16[128,128]{1,0:T(8,128)(2,1)}, u32[]{:S(2)}) %copy-start.6) | copy-done | bytes 32792
  3.0 0.8 %copy-done.7 = bf16[128,128]{1,0:T(8,128)(2,1)S(1)} copy-done((bf16[128,128]{1,0:T(8,128)(2,1)S(1)}, bf16[128,128]{1,0:T(8,128)(2,1)}, u32[]{:S(2)}) %copy-start.7) | copy-done | bytes 32792
  3.8 0.8 %copy-done.8 = bf16[128,128]{1,0:T(8,128)(2,1)S(1)} copy-done((bf16[128,128]{1,0:T(8,128)(2,1)S(1)}, bf16[128,128]{1,0:T(8,128)(2,1)}, u32[]{:S(2)}) %copy-start.8) | copy-done | bytes 32792
  4.5 0.8 %copy-done.9 = bf16[128,128]{1,0:T(8,128)(2,1)S(1)} copy-done((bf16[128,128]{1,0:T(8,128)(2,1)S(1)}, bf16[128,128]{1,0:T(8,128)(2,1)}, u32[]{:S(2)}) %copy-start.9) | copy-done | bytes 32792
  5.3 1.9 %shard_map.113 = (bf16[1024,128]{1,0:T(8,128)(2,1)S(1)}, bf16[512,128]{1,0:T(8,128)(2,1)S(1)}, bf16[512,128]{1,0:T(8,128)(2,1)S(1)}, bf16[512,128]{1,0:T(8,128)(...) custom-call(s32[5]{0:T(128)S(1)} %copy-done.4, ...), custom_call_target="tpu_custom_call" | custom-call | flops 134217728 | bytes 1048576 | tf_op jit(solution)/shard_map/pallas_call | solution.py:187
  7.2 4.1 %collective-permute-start.3 = (bf16[256,128]{1,0:T(8,128)(2,1)S(1)}, bf16[256,128]{1,0:T(8,128)(2,1)S(1)}, u32[]{:S(2)}, u32[]{:S(2)}) collective-permute-start(bf16[256,128]{1,0:T(8,128)(2,1)S(1)} %get-tuple-element.26), channel_id=1, source_target_pairs={{0,8},{1,9},{2,10},{3,11},{4,12},{5,13},{6,14},{7,15},{8,0},{9,1},... | collective-permute-start | bytes 196616 | tf_op jit(solution)/shard_map/ppermute | solution.py:183
  11.3 0.0 collective-permute-start.4
  11.3 0.2 collective-permute-start
  11.5 1.8 %collective-permute-start.1 = (bf16[512,128]{1,0:T(8,128)(2,1)S(1)}, bf16[512,128]{1,0:T(8,128)(2,1)S(1)}, u32[]{:S(2)}, u32[]{:S(2)}) collective-permute-start(bf16[512,128]{1,0:T(8,128)(2,1)S(1)} %get-tuple-element.24), channel_id=1, source_target_pairs={{0,4},{1,5},{2,6},{3,7},{4,0},{5,1},{6,2},{7,3},{8,12},{9,13},{10,... | collective-permute-start | bytes 393224 | tf_op jit(solution)/shard_map/ppermute | solution.py:183
  13.4 0.0 collective-permute-start.2
  13.4 1.7 %collective-permute-done.3.refs_4_ = bf16[256,128]{1,0:T(8,128)(2,1)S(1)} collective-permute-done((bf16[256,128]{1,0:T(8,128)(2,1)S(1)}, bf16[256,128]{1,0:T(8,128)(2,1)S(1)}, u32[]{:S(2)}, u32[]{:S(2)}) %collective-permute-start.3) | collective-permute-done | bytes 65568 | tf_op jit(solution)/shard_map/ppermute | solution.py:183
  15.1 4.9 %collective-permute-start.5 = (bf16[256,128]{1,0:T(8,128)(2,1)S(1)}, bf16[256,128]{1,0:T(8,128)(2,1)S(1)}, u32[]{:S(2)}, u32[]{:S(2)}) collective-permute-start(bf16[256,128]{1,0:T(8,128)(2,1)S(1)} %get-tuple-element.28), channel_id=1, source_target_pairs={{0,12},{1,13},{2,14},{3,15},{4,8},{5,9},{6,10},{7,11},{8,4},{9,5},... | collective-permute-start | bytes 196616 | tf_op jit(solution)/shard_map/ppermute | solution.py:183
  20.0 0.0 collective-permute-done.4.refs_5_
  20.0 0.9 %collective-permute-start.6 = (bf16[256,128]{1,0:T(8,128)(2,1)S(1)}, bf16[256,128]{1,0:T(8,128)(2,1)S(1)}, u32[]{:S(2)}, u32[]{:S(2)}) collective-permute-start(bf16[256,128]{1,0:T(8,128)(2,1)S(1)} %get-tuple-element.29), channel_id=1, source_target_pairs={{0,14},{1,15},{2,12},{3,13},{4,10},{5,11},{6,8},{7,9},{8,6},{9,7},... | collective-permute-start | bytes 196616 | tf_op jit(solution)/shard_map/ppermute | solution.py:183
  20.8 3.6 %collective-permute-done.5.refs_6_ = bf16[256,128]{1,0:T(8,128)(2,1)S(1)} collective-permute-done((bf16[256,128]{1,0:T(8,128)(2,1)S(1)}, bf16[256,128]{1,0:T(8,128)(2,1)S(1)}, u32[]{:S(2)}, u32[]{:S(2)}) %collective-permute-start.5) | collective-permute-done | bytes 65568 | tf_op jit(solution)/shard_map/ppermute | solution.py:183
  24.4 1.5 %collective-permute-done.6.refs_7_ = bf16[256,128]{1,0:T(8,128)(2,1)S(1)} collective-permute-done((bf16[256,128]{1,0:T(8,128)(2,1)S(1)}, bf16[256,128]{1,0:T(8,128)(2,1)S(1)}, u32[]{:S(2)}, u32[]{:S(2)}) %collective-permute-start.6) | collective-permute-done | bytes 65568 | tf_op jit(solution)/shard_map/ppermute | solution.py:183
  25.9 0.0 collective-permute-done.refs_1_
  25.9 0.0 collective-permute-done.1.refs_2_
  25.9 0.0 collective-permute-done.2.refs_3_
  25.9 0.0 copy-start.10
  25.9 0.6 shard_map.115
  26.5 0.1 collective-permute-start.10
  26.6 2.9 %collective-permute-start.11 = (bf16[256,128]{1,0:T(8,128)(2,1)S(1)}, bf16[256,128]{1,0:T(8,128)(2,1)S(1)}, u32[]{:S(2)}, u32[]{:S(2)}) collective-permute-start(bf16[256,128]{1,0:T(8,128)(2,1)S(1)} %get-tuple-element.35), channel_id=1, source_target_pairs={{0,5},{1,4},{2,7},{3,6},{4,1},{5,0},{6,3},{7,2},{8,13},{9,12},{10,... | collective-permute-start | bytes 196616 | tf_op jit(solution)/shard_map/ppermute | solution.py:183
  29.5 0.0 collective-permute-start.12
  29.5 1.8 %collective-permute-start.13 = (bf16[256,128]{1,0:T(8,128)(2,1)S(1)}, bf16[256,128]{1,0:T(8,128)(2,1)S(1)}, u32[]{:S(2)}, u32[]{:S(2)}) collective-permute-start(bf16[256,128]{1,0:T(8,128)(2,1)S(1)} %get-tuple-element.37), channel_id=1, source_target_pairs={{0,7},{1,6},{2,5},{3,4},{4,3},{5,2},{6,1},{7,0},{8,15},{9,14},{10,... | collective-permute-start | bytes 196616 | tf_op jit(solution)/shard_map/ppermute | solution.py:183
  31.2 1.5 %collective-permute-start.7 = (bf16[256,128]{1,0:T(8,128)(2,1)S(1)}, bf16[256,128]{1,0:T(8,128)(2,1)S(1)}, u32[]{:S(2)}, u32[]{:S(2)}) collective-permute-start(bf16[256,128]{1,0:T(8,128)(2,1)S(1)} %get-tuple-element.31), channel_id=1, source_target_pairs={{0,1},{1,0},{2,3},{3,2},{4,5},{5,4},{6,7},{7,6},{8,9},{9,8},{10,11... | collective-permute-start | bytes 196616 | tf_op jit(solution)/shard_map/ppermute | solution.py:183
  32.7 0.0 collective-permute-done.10.refs_4_
  32.7 0.0 collective-permute-start.8
  32.7 0.0 collective-permute-done.11.refs_5_
  32.7 0.0 copy-start.11
  32.7 0.7 %collective-permute-start.9 = (bf16[256,128]{1,0:T(8,128)(2,1)S(1)}, bf16[256,128]{1,0:T(8,128)(2,1)S(1)}, u32[]{:S(2)}, u32[]{:S(2)}) collective-permute-start(bf16[256,128]{1,0:T(8,128)(2,1)S(1)} %get-tuple-element.33), channel_id=1, source_target_pairs={{0,3},{1,2},{2,1},{3,0},{4,7},{5,6},{6,5},{7,4},{8,11},{9,10},{10,... | collective-permute-start | bytes 196616 | tf_op jit(solution)/shard_map/ppermute | solution.py:183
  33.4 0.0 copy-done.10
  33.4 0.1 copy.12.dw_ref
  33.5 0.0 copy-done.11
  33.5 0.1 reshape.7.bins_ref
  33.6 0.0 copy-done.2
  33.6 0.2 shard_map.114.gate_ref
  33.8 0.0 copy-start.5
  33.8 0.0 collective-permute-done.12.refs_6_
  33.8 1.5 %collective-permute-done.13.refs_7_ = bf16[256,128]{1,0:T(8,128)(2,1)S(1)} collective-permute-done((bf16[256,128]{1,0:T(8,128)(2,1)S(1)}, bf16[256,128]{1,0:T(8,128)(2,1)S(1)}, u32[]{:S(2)}, u32[]{:S(2)}) %collective-permute-start.13) | collective-permute-done | bytes 65568 | tf_op jit(solution)/shard_map/ppermute | solution.py:183
  35.3 0.9 %collective-permute-done.7.refs_1_ = bf16[256,128]{1,0:T(8,128)(2,1)S(1)} collective-permute-done((bf16[256,128]{1,0:T(8,128)(2,1)S(1)}, bf16[256,128]{1,0:T(8,128)(2,1)S(1)}, u32[]{:S(2)}, u32[]{:S(2)}) %collective-permute-start.7) | collective-permute-done | bytes 65568 | tf_op jit(solution)/shard_map/ppermute | solution.py:183
  36.2 0.0 collective-permute-done.8.refs_2_
  36.2 0.8 %collective-permute-done.9.refs_3_ = bf16[256,128]{1,0:T(8,128)(2,1)S(1)} collective-permute-done((bf16[256,128]{1,0:T(8,128)(2,1)S(1)}, bf16[256,128]{1,0:T(8,128)(2,1)S(1)}, u32[]{:S(2)}, u32[]{:S(2)}) %collective-permute-start.9) | collective-permute-done | bytes 65568 | tf_op jit(solution)/shard_map/ppermute | solution.py:183
  37.1 3.0 %shard_map.116 = (bf16[16,64,128]{2,1,0:T(8,128)(2,1)}, f32[8,128]{1,0:T(8,128)S(1)}) custom-call(s32[5]{0:T(128)S(1)} %copy-done.5, bf16[16,64,128]{2,1,0:T(8,128)(2,1)S(1)} %copy-done.1, f32[1024,128]{1,0:T(8,128)S(1)} %shard_map.114.gate_ref, s32[8,128]{1,0:T(8,128)S(1)} %reshape.7.bins_ref, bf16[128,128]{1,0:T(8,128)(2,1)S(1)} %copy-done.3, ...), custom_call_target="tpu_custom_call" | custom-call | flops 100663296 | bytes 1048576 | tf_op jit(solution)/shard_map/pallas_call | solution.py:187
  40.0 0.2 collective-permute-start.14
  40.2 1.0 %collective-permute-done.14 = f32[8,128]{1,0:T(8,128)S(1)} collective-permute-done((f32[8,128]{1,0:T(8,128)S(1)}, f32[8,128]{1,0:T(8,128)S(1)}, u32[]{:S(2)}, u32[]{:S(2)}) %collective-permute-start.14) | collective-permute-done | bytes 4128 | tf_op jit(solution)/shard_map/ppermute | solution.py:183
  41.2 1.0 %collective-permute-start.15 = (f32[8,128]{1,0:T(8,128)S(1)}, f32[8,128]{1,0:T(8,128)S(1)}, u32[]{:S(2)}, u32[]{:S(2)}) collective-permute-start(f32[8,128]{1,0:T(8,128)S(1)} %add.3.refs_1_), channel_id=1, source_target_pairs={{0,1},{1,0},{2,3},{3,2},{4,5},{5,4},{6,7},{7,6},{8,9},{9,8},{10,11... | collective-permute-start | bytes 12296 | tf_op jit(solution)/shard_map/ppermute | solution.py:183
  42.2 1.6 %collective-permute-start.16 = (f32[8,128]{1,0:T(8,128)S(1)}, f32[8,128]{1,0:T(8,128)S(1)}, u32[]{:S(2)}, u32[]{:S(2)}) collective-permute-start(f32[8,128]{1,0:T(8,128)S(1)} %add.3.refs_1_), channel_id=1, source_target_pairs={{0,4},{1,5},{2,6},{3,7},{4,0},{5,1},{6,2},{7,3},{8,12},{9,13},{10,... | collective-permute-start | bytes 12296 | tf_op jit(solution)/shard_map/ppermute | solution.py:183
  43.8 0.9 %collective-permute-start.17 = (f32[8,128]{1,0:T(8,128)S(1)}, f32[8,128]{1,0:T(8,128)S(1)}, u32[]{:S(2)}, u32[]{:S(2)}) collective-permute-start(f32[8,128]{1,0:T(8,128)S(1)} %add.3.refs_1_), channel_id=1, source_target_pairs={{0,5},{1,4},{2,7},{3,6},{4,1},{5,0},{6,3},{7,2},{8,13},{9,12},{10,... | collective-permute-start | bytes 12296 | tf_op jit(solution)/shard_map/ppermute | solution.py:183
  44.7 2.6 %collective-permute-start.18 = (f32[8,128]{1,0:T(8,128)S(1)}, f32[8,128]{1,0:T(8,128)S(1)}, u32[]{:S(2)}, u32[]{:S(2)}) collective-permute-start(f32[8,128]{1,0:T(8,128)S(1)} %add.3.refs_1_), channel_id=1, source_target_pairs={{0,8},{1,9},{2,10},{3,11},{4,12},{5,13},{6,14},{7,15},{8,0},{9,1},... | collective-permute-start | bytes 12296 | tf_op jit(solution)/shard_map/ppermute | solution.py:183
  47.3 0.7 %collective-permute-start.19 = (f32[8,128]{1,0:T(8,128)S(1)}, f32[8,128]{1,0:T(8,128)S(1)}, u32[]{:S(2)}, u32[]{:S(2)}) collective-permute-start(f32[8,128]{1,0:T(8,128)S(1)} %add.3.refs_1_), channel_id=1, source_target_pairs={{0,9},{1,8},{2,11},{3,10},{4,13},{5,12},{6,15},{7,14},{8,1},{9,0},... | collective-permute-start | bytes 12296 | tf_op jit(solution)/shard_map/ppermute | solution.py:183
  48.1 0.0 collective-permute-done.15.refs_2_
  48.1 3.4 %collective-permute-start.20 = (f32[8,128]{1,0:T(8,128)S(1)}, f32[8,128]{1,0:T(8,128)S(1)}, u32[]{:S(2)}, u32[]{:S(2)}) collective-permute-start(f32[8,128]{1,0:T(8,128)S(1)} %add.3.refs_1_), channel_id=1, source_target_pairs={{0,12},{1,13},{2,14},{3,15},{4,8},{5,9},{6,10},{7,11},{8,4},{9,5},... | collective-permute-start | bytes 12296 | tf_op jit(solution)/shard_map/ppermute | solution.py:183
  51.5 0.0 collective-permute-done.16.refs_3_
  51.5 0.9 %collective-permute-start.21 = (f32[8,128]{1,0:T(8,128)S(1)}, f32[8,128]{1,0:T(8,128)S(1)}, u32[]{:S(2)}, u32[]{:S(2)}) collective-permute-start(f32[8,128]{1,0:T(8,128)S(1)} %add.3.refs_1_), channel_id=1, source_target_pairs={{0,13},{1,12},{2,15},{3,14},{4,9},{5,8},{6,11},{7,10},{8,5},{9,4},... | collective-permute-start | bytes 12296 | tf_op jit(solution)/shard_map/ppermute | solution.py:183
  52.4 0.0 collective-permute-done.17.refs_4_
  52.4 0.0 collective-permute-done.18.refs_5_
  52.4 0.4 collective-permute-done.19.refs_6_
  52.7 0.8 %collective-permute-done.20.refs_7_ = f32[8,128]{1,0:T(8,128)S(1)} collective-permute-done((f32[8,128]{1,0:T(8,128)S(1)}, f32[8,128]{1,0:T(8,128)S(1)}, u32[]{:S(2)}, u32[]{:S(2)}) %collective-permute-start.20) | collective-permute-done | bytes 4128 | tf_op jit(solution)/shard_map/ppermute | solution.py:183
  53.5 4.3 %collective-permute-done.21.refs_8_ = f32[8,128]{1,0:T(8,128)S(1)} collective-permute-done((f32[8,128]{1,0:T(8,128)S(1)}, f32[8,128]{1,0:T(8,128)S(1)}, u32[]{:S(2)}, u32[]{:S(2)}) %collective-permute-start.21) | collective-permute-done | bytes 4128 | tf_op jit(solution)/shard_map/ppermute | solution.py:183
  57.8 1.1 %shard_map.117 = f32[1]{0:T(128)} custom-call(s32[5]{0:T(128)S(1)} %copy-done.5, f32[8,128]{1,0:T(8,128)S(1)} %add.3.refs_1_, f32[8,128]{1,0:T(8,128)S(1)} %collective-permute-done.15.refs_2_, f32[8,128]{1,0:T(8,128)S(1)} %collective-permute-done.16.refs_3_, f32[8,128]{1,0:T(8,128)S(1)} %collective-permute-done.17.refs_4_, ...), custom_call_target="tpu_custom_call" | custom-call | bytes 1048576 | tf_op jit(solution)/shard_map/pallas_call | solution.py:187
  (12 shorter events, 0.0 us)
Async XLA Ops:
  0.6 1.0 %copy-start = (bf16[16,64,128]{2,1,0:T(8,128)(2,1)S(1)}, bf16[16,64,128]{2,1,0:T(8,128)(2,1)}, u32[]{:S(2)}) copy-start(bf16[16,64,128]{2,1,0:T(8,128)(2,1)} %x_ref.3) | copy-start | bytes 786436
  1.6 0.7 %copy-start.4 = (s32[5]{0:T(128)S(1)}, s32[5]{0:T(128)}, u32[]{:S(2)}) copy-start(s32[5]{0:T(128)} %refs_0_.1) | copy-start | bytes 64
  2.2 0.8 %copy-start.6 = (bf16[128,128]{1,0:T(8,128)(2,1)S(1)}, bf16[128,128]{1,0:T(8,128)(2,1)}, u32[]{:S(2)}) copy-start(bf16[128,128]{1,0:T(8,128)(2,1)} %lw_ref.1) | copy-start | bytes 98308
  3.0 0.8 %copy-start.7 = (bf16[128,128]{1,0:T(8,128)(2,1)S(1)}, bf16[128,128]{1,0:T(8,128)(2,1)}, u32[]{:S(2)}) copy-start(bf16[128,128]{1,0:T(8,128)(2,1)} %lg_ref.1) | copy-start | bytes 98308
  3.8 0.8 %copy-start.8 = (bf16[128,128]{1,0:T(8,128)(2,1)S(1)}, bf16[128,128]{1,0:T(8,128)(2,1)}, u32[]{:S(2)}) copy-start(bf16[128,128]{1,0:T(8,128)(2,1)} %rw_ref.1) | copy-start | bytes 98308
  4.5 0.8 %copy-start.9 = (bf16[128,128]{1,0:T(8,128)(2,1)S(1)}, bf16[128,128]{1,0:T(8,128)(2,1)}, u32[]{:S(2)}) copy-start(bf16[128,128]{1,0:T(8,128)(2,1)} %rg_ref.1) | copy-start | bytes 98308
  7.2 7.9 %collective-permute-start.3 = (bf16[256,128]{1,0:T(8,128)(2,1)S(1)}, bf16[256,128]{1,0:T(8,128)(2,1)S(1)}, u32[]{:S(2)}, u32[]{:S(2)}) collective-permute-start(bf16[256,128]{1,0:T(8,128)(2,1)S(1)} %get-tuple-element.26), channel_id=1, source_target_pairs={{0,8},{1,9},{2,10},{3,11},{4,12},{5,13},{6,14},{7,15},{8,0},{9,1},... | collective-permute-start | bytes 196616 | tf_op jit(solution)/shard_map/ppermute | solution.py:183
  11.3 8.6 %collective-permute-start.4 = (bf16[256,128]{1,0:T(8,128)(2,1)S(1)}, bf16[256,128]{1,0:T(8,128)(2,1)S(1)}, u32[]{:S(2)}, u32[]{:S(2)}) collective-permute-start(bf16[256,128]{1,0:T(8,128)(2,1)S(1)} %get-tuple-element.27), channel_id=1, source_target_pairs={{0,10},{1,11},{2,8},{3,9},{4,14},{5,15},{6,12},{7,13},{8,2},{9,3},... | collective-permute-start | bytes 196616 | tf_op jit(solution)/shard_map/ppermute | solution.py:183
  11.3 14.5 %collective-permute-start = (bf16[512,128]{1,0:T(8,128)(2,1)S(1)}, bf16[512,128]{1,0:T(8,128)(2,1)S(1)}, u32[]{:S(2)}, u32[]{:S(2)}) collective-permute-start(bf16[512,128]{1,0:T(8,128)(2,1)S(1)} %get-tuple-element.23), channel_id=1, source_target_pairs={{0,2},{1,3},{2,0},{3,1},{4,6},{5,7},{6,4},{7,5},{8,10},{9,11},{10,... | collective-permute-start | bytes 393224 | tf_op jit(solution)/shard_map/ppermute | solution.py:183
  11.5 14.4 %collective-permute-start.1 = (bf16[512,128]{1,0:T(8,128)(2,1)S(1)}, bf16[512,128]{1,0:T(8,128)(2,1)S(1)}, u32[]{:S(2)}, u32[]{:S(2)}) collective-permute-start(bf16[512,128]{1,0:T(8,128)(2,1)S(1)} %get-tuple-element.24), channel_id=1, source_target_pairs={{0,4},{1,5},{2,6},{3,7},{4,0},{5,1},{6,2},{7,3},{8,12},{9,13},{10,... | collective-permute-start | bytes 393224 | tf_op jit(solution)/shard_map/ppermute | solution.py:183
  13.4 12.5 %collective-permute-start.2 = (bf16[512,128]{1,0:T(8,128)(2,1)S(1)}, bf16[512,128]{1,0:T(8,128)(2,1)S(1)}, u32[]{:S(2)}, u32[]{:S(2)}) collective-permute-start(bf16[512,128]{1,0:T(8,128)(2,1)S(1)} %get-tuple-element.25), channel_id=1, source_target_pairs={{0,6},{1,7},{2,4},{3,5},{4,2},{5,3},{6,0},{7,1},{8,14},{9,15},{10,... | collective-permute-start | bytes 393224 | tf_op jit(solution)/shard_map/ppermute | solution.py:183
  15.1 9.3 %collective-permute-start.5 = (bf16[256,128]{1,0:T(8,128)(2,1)S(1)}, bf16[256,128]{1,0:T(8,128)(2,1)S(1)}, u32[]{:S(2)}, u32[]{:S(2)}) collective-permute-start(bf16[256,128]{1,0:T(8,128)(2,1)S(1)} %get-tuple-element.28), channel_id=1, source_target_pairs={{0,12},{1,13},{2,14},{3,15},{4,8},{5,9},{6,10},{7,11},{8,4},{9,5},... | collective-permute-start | bytes 196616 | tf_op jit(solution)/shard_map/ppermute | solution.py:183
  20.0 5.9 %collective-permute-start.6 = (bf16[256,128]{1,0:T(8,128)(2,1)S(1)}, bf16[256,128]{1,0:T(8,128)(2,1)S(1)}, u32[]{:S(2)}, u32[]{:S(2)}) collective-permute-start(bf16[256,128]{1,0:T(8,128)(2,1)S(1)} %get-tuple-element.29), channel_id=1, source_target_pairs={{0,14},{1,15},{2,12},{3,13},{4,10},{5,11},{6,8},{7,9},{8,6},{9,7},... | collective-permute-start | bytes 196616 | tf_op jit(solution)/shard_map/ppermute | solution.py:183
  25.9 7.5 %copy-start.10 = (bf16[128,64]{0,1:T(8,128)(2,1)S(1)}, bf16[128,64]{0,1:T(8,128)(2,1)}, u32[]{:S(2)}) copy-start(bf16[128,64]{0,1:T(8,128)(2,1)} %param.19) | copy-start | bytes 49156
  26.5 6.2 %collective-permute-start.10 = (bf16[256,128]{1,0:T(8,128)(2,1)S(1)}, bf16[256,128]{1,0:T(8,128)(2,1)S(1)}, u32[]{:S(2)}, u32[]{:S(2)}) collective-permute-start(bf16[256,128]{1,0:T(8,128)(2,1)S(1)} %get-tuple-element.34), channel_id=1, source_target_pairs={{0,4},{1,5},{2,6},{3,7},{4,0},{5,1},{6,2},{7,3},{8,12},{9,13},{10,... | collective-permute-start | bytes 196616 | tf_op jit(solution)/shard_map/ppermute | solution.py:183
  26.6 6.1 %collective-permute-start.11 = (bf16[256,128]{1,0:T(8,128)(2,1)S(1)}, bf16[256,128]{1,0:T(8,128)(2,1)S(1)}, u32[]{:S(2)}, u32[]{:S(2)}) collective-permute-start(bf16[256,128]{1,0:T(8,128)(2,1)S(1)} %get-tuple-element.35), channel_id=1, source_target_pairs={{0,5},{1,4},{2,7},{3,6},{4,1},{5,0},{6,3},{7,2},{8,13},{9,12},{10,... | collective-permute-start | bytes 196616 | tf_op jit(solution)/shard_map/ppermute | solution.py:183
  29.5 4.4 %collective-permute-start.12 = (bf16[256,128]{1,0:T(8,128)(2,1)S(1)}, bf16[256,128]{1,0:T(8,128)(2,1)S(1)}, u32[]{:S(2)}, u32[]{:S(2)}) collective-permute-start(bf16[256,128]{1,0:T(8,128)(2,1)S(1)} %get-tuple-element.36), channel_id=1, source_target_pairs={{0,6},{1,7},{2,4},{3,5},{4,2},{5,3},{6,0},{7,1},{8,14},{9,15},{10,... | collective-permute-start | bytes 196616 | tf_op jit(solution)/shard_map/ppermute | solution.py:183
  29.5 5.9 %collective-permute-start.13 = (bf16[256,128]{1,0:T(8,128)(2,1)S(1)}, bf16[256,128]{1,0:T(8,128)(2,1)S(1)}, u32[]{:S(2)}, u32[]{:S(2)}) collective-permute-start(bf16[256,128]{1,0:T(8,128)(2,1)S(1)} %get-tuple-element.37), channel_id=1, source_target_pairs={{0,7},{1,6},{2,5},{3,4},{4,3},{5,2},{6,1},{7,0},{8,15},{9,14},{10,... | collective-permute-start | bytes 196616 | tf_op jit(solution)/shard_map/ppermute | solution.py:183
  31.2 5.0 %collective-permute-start.7 = (bf16[256,128]{1,0:T(8,128)(2,1)S(1)}, bf16[256,128]{1,0:T(8,128)(2,1)S(1)}, u32[]{:S(2)}, u32[]{:S(2)}) collective-permute-start(bf16[256,128]{1,0:T(8,128)(2,1)S(1)} %get-tuple-element.31), channel_id=1, source_target_pairs={{0,1},{1,0},{2,3},{3,2},{4,5},{5,4},{6,7},{7,6},{8,9},{9,8},{10,11... | collective-permute-start | bytes 196616 | tf_op jit(solution)/shard_map/ppermute | solution.py:183
  32.7 0.9 %copy-start.2 = (bf16[128,128]{1,0:T(8,128)(2,1)S(1)}, bf16[128,128]{1,0:T(8,128)(2,1)}, u32[]{:S(2)}) copy-start(bf16[128,128]{1,0:T(8,128)(2,1)} %w_ref.1) | copy-start | bytes 98308
  32.7 3.5 %collective-permute-start.8 = (bf16[256,128]{1,0:T(8,128)(2,1)S(1)}, bf16[256,128]{1,0:T(8,128)(2,1)S(1)}, u32[]{:S(2)}, u32[]{:S(2)}) collective-permute-start(bf16[256,128]{1,0:T(8,128)(2,1)S(1)} %get-tuple-element.32), channel_id=1, source_target_pairs={{0,2},{1,3},{2,0},{3,1},{4,6},{5,7},{6,4},{7,5},{8,10},{9,11},{10,... | collective-permute-start | bytes 196616 | tf_op jit(solution)/shard_map/ppermute | solution.py:183
  32.7 0.8 %copy-start.11 = (s32[16,64]{1,0:T(8,128)S(1)}, s32[16,64]{1,0:T(8,128)}, u32[]{:S(2)}) copy-start(s32[16,64]{1,0:T(8,128)} %param.11) | copy-start | bytes 12292
  32.7 4.3 %collective-permute-start.9 = (bf16[256,128]{1,0:T(8,128)(2,1)S(1)}, bf16[256,128]{1,0:T(8,128)(2,1)S(1)}, u32[]{:S(2)}, u32[]{:S(2)}) collective-permute-start(bf16[256,128]{1,0:T(8,128)(2,1)S(1)} %get-tuple-element.33), channel_id=1, source_target_pairs={{0,3},{1,2},{2,1},{3,0},{4,7},{5,6},{6,5},{7,4},{8,11},{9,10},{10,... | collective-permute-start | bytes 196616 | tf_op jit(solution)/shard_map/ppermute | solution.py:183
  33.6 3.5 %copy-start.1 = (bf16[16,64,128]{2,1,0:T(8,128)(2,1)S(1)}, bf16[16,64,128]{2,1,0:T(8,128)(2,1)}, u32[]{:S(2)}) copy-start(bf16[16,64,128]{2,1,0:T(8,128)(2,1)} %x_ref.3) | copy-start | bytes 786436
  33.6 3.5 %copy-start.3 = (bf16[128,128]{1,0:T(8,128)(2,1)S(1)}, bf16[128,128]{1,0:T(8,128)(2,1)}, u32[]{:S(2)}) copy-start(bf16[128,128]{1,0:T(8,128)(2,1)} %ow_ref.1) | copy-start | bytes 98308
  33.8 3.2 %copy-start.5 = (s32[5]{0:T(128)S(1)}, s32[5]{0:T(128)}, u32[]{:S(2)}) copy-start(s32[5]{0:T(128)} %refs_0_.1) | copy-start | bytes 64
  40.0 1.2 %collective-permute-start.14 = (f32[8,128]{1,0:T(8,128)S(1)}, f32[8,128]{1,0:T(8,128)S(1)}, u32[]{:S(2)}, u32[]{:S(2)}) collective-permute-start(f32[8,128]{1,0:T(8,128)S(1)} %get-tuple-element.39), channel_id=1, source_target_pairs={{0,2},{1,3},{2,0},{3,1},{4,6},{5,7},{6,4},{7,5},{8,10},{9,11},{10,... | collective-permute-start | bytes 12296 | tf_op jit(solution)/shard_map/ppermute | solution.py:183
  41.2 6.9 %collective-permute-start.15 = (f32[8,128]{1,0:T(8,128)S(1)}, f32[8,128]{1,0:T(8,128)S(1)}, u32[]{:S(2)}, u32[]{:S(2)}) collective-permute-start(f32[8,128]{1,0:T(8,128)S(1)} %add.3.refs_1_), channel_id=1, source_target_pairs={{0,1},{1,0},{2,3},{3,2},{4,5},{5,4},{6,7},{7,6},{8,9},{9,8},{10,11... | collective-permute-start | bytes 12296 | tf_op jit(solution)/shard_map/ppermute | solution.py:183
  42.2 9.3 %collective-permute-start.16 = (f32[8,128]{1,0:T(8,128)S(1)}, f32[8,128]{1,0:T(8,128)S(1)}, u32[]{:S(2)}, u32[]{:S(2)}) collective-permute-start(f32[8,128]{1,0:T(8,128)S(1)} %add.3.refs_1_), channel_id=1, source_target_pairs={{0,4},{1,5},{2,6},{3,7},{4,0},{5,1},{6,2},{7,3},{8,12},{9,13},{10,... | collective-permute-start | bytes 12296 | tf_op jit(solution)/shard_map/ppermute | solution.py:183
  43.8 8.6 %collective-permute-start.17 = (f32[8,128]{1,0:T(8,128)S(1)}, f32[8,128]{1,0:T(8,128)S(1)}, u32[]{:S(2)}, u32[]{:S(2)}) collective-permute-start(f32[8,128]{1,0:T(8,128)S(1)} %add.3.refs_1_), channel_id=1, source_target_pairs={{0,5},{1,4},{2,7},{3,6},{4,1},{5,0},{6,3},{7,2},{8,13},{9,12},{10,... | collective-permute-start | bytes 12296 | tf_op jit(solution)/shard_map/ppermute | solution.py:183
  44.7 7.7 %collective-permute-start.18 = (f32[8,128]{1,0:T(8,128)S(1)}, f32[8,128]{1,0:T(8,128)S(1)}, u32[]{:S(2)}, u32[]{:S(2)}) collective-permute-start(f32[8,128]{1,0:T(8,128)S(1)} %add.3.refs_1_), channel_id=1, source_target_pairs={{0,8},{1,9},{2,10},{3,11},{4,12},{5,13},{6,14},{7,15},{8,0},{9,1},... | collective-permute-start | bytes 12296 | tf_op jit(solution)/shard_map/ppermute | solution.py:183
  47.3 5.4 %collective-permute-start.19 = (f32[8,128]{1,0:T(8,128)S(1)}, f32[8,128]{1,0:T(8,128)S(1)}, u32[]{:S(2)}, u32[]{:S(2)}) collective-permute-start(f32[8,128]{1,0:T(8,128)S(1)} %add.3.refs_1_), channel_id=1, source_target_pairs={{0,9},{1,8},{2,11},{3,10},{4,13},{5,12},{6,15},{7,14},{8,1},{9,0},... | collective-permute-start | bytes 12296 | tf_op jit(solution)/shard_map/ppermute | solution.py:183
  48.1 5.4 %collective-permute-start.20 = (f32[8,128]{1,0:T(8,128)S(1)}, f32[8,128]{1,0:T(8,128)S(1)}, u32[]{:S(2)}, u32[]{:S(2)}) collective-permute-start(f32[8,128]{1,0:T(8,128)S(1)} %add.3.refs_1_), channel_id=1, source_target_pairs={{0,12},{1,13},{2,14},{3,15},{4,8},{5,9},{6,10},{7,11},{8,4},{9,5},... | collective-permute-start | bytes 12296 | tf_op jit(solution)/shard_map/ppermute | solution.py:183
  51.5 6.3 %collective-permute-start.21 = (f32[8,128]{1,0:T(8,128)S(1)}, f32[8,128]{1,0:T(8,128)S(1)}, u32[]{:S(2)}, u32[]{:S(2)}) collective-permute-start(f32[8,128]{1,0:T(8,128)S(1)} %add.3.refs_1_), channel_id=1, source_target_pairs={{0,13},{1,12},{2,15},{3,14},{4,9},{5,8},{6,11},{7,10},{8,5},{9,4},... | collective-permute-start | bytes 12296 | tf_op jit(solution)/shard_map/ppermute | solution.py:183

commit v4 on v3

--- a/solution.py
+++ b/solution.py
@@ -43,44 +43,69 @@
     return ((row < live) & (col < live)).astype(jnp.float32)
 
 
-def project_kernel(lens_ref, x_ref, lw_ref, lg_ref, rw_ref, rg_ref, *refs):
-    normed_ref, outs, (turned, held_left, held_right) = refs[0], refs[1:-3], refs[-3:]
-    tile_rows, tile_cols, channels = x_ref.shape
+def turn(w_refs, turned):
+    channels = w_refs[0].shape[0]
     share = channels // OWNERS
     half = share // 2
-    packed = OWNERS * half
-    for at, w_ref in enumerate((lw_ref, lg_ref, rw_ref, rg_ref)):
+    for at, w_ref in enumerate(w_refs):
         w = w_ref[...].astype(jnp.float32).T
         blocks = [
             w[o * share + g * half : o * share + (g + 1) * half] for g in (0, 1) for o in range(OWNERS)
         ]
         turned[at * channels : (at + 1) * channels] = jnp.concatenate(blocks, 0).astype(jnp.bfloat16)
+
+
+def project(normed, turned, mask, held, first, tile_rows, tile_cols):
+    channels = normed.shape[1]
+    packed = channels // 2
+    flat = nt_dot(turned[...], normed)
+    value = sigmoid(flat[channels:]) * flat[:channels] * mask
+    a, b = value[:packed], value[packed:]
     low = lanes_of((packed, 2 * tile_cols)) < tile_cols
+    held[pl.ds(first, packed, stride=tile_rows), :] = jnp.where(low, a, pltpu.roll(b, tile_cols, 1))
+    held[pl.ds(first + 1, packed, stride=tile_rows), :] = jnp.where(
+        low, pltpu.roll(a, tile_cols, 1), b
+    )
+
+
+def owner_place():
+    return lax.axis_index("row") // 2 % 2 * 2 + lax.axis_index("col")
+
+
+def owner_block(held, d, size):
+    at = pl.multiple_of((owner_place() ^ d) * size, size)
+    return held[pl.ds(at, size)].astype(jnp.bfloat16)
+
+
+def norm_kernel(x_ref, normed_ref):
+    x = x_ref[...].astype(jnp.float32).reshape(normed_ref.shape)
+    normed_ref[...] = layer_norm(x, -1).astype(jnp.bfloat16)
+
+
+def project_all(lens_ref, normed_ref, w_ref, g_ref, turned, held):
+    tile_rows = held.shape[0] // turned.shape[1] * 2
+    tile_cols = held.shape[1] // 2
+    turn((w_ref, g_ref), turned)
     for first in range(0, tile_rows, 2):
-        x = x_ref[first : first + 2].astype(jnp.float32).reshape(2 * tile_cols, channels)
-        normed = layer_norm(x, -1).astype(jnp.bfloat16)
-        normed_ref[first * tile_cols : (first + 2) * tile_cols] = normed
-        flat = nt_dot(turned[...], normed)
+        normed = normed_ref[first * tile_cols : (first + 2) * tile_cols]
         mask = pair_mask(lens_ref, tile_rows, tile_cols, first)
-        for at, held in ((0, held_left), (2, held_right)):
-            value = flat[at * channels : (at + 1) * channels]
-            gate = flat[(at + 1) * channels : (at + 2) * channels]
-            value = sigmoid(gate) * value * mask
-            a, b = value[:packed], value[packed:]
-            held[pl.ds(first, packed, stride=tile_rows), :] = jnp.where(
-                low, a, pltpu.roll(b, tile_cols, 1)
-            )
-            held[pl.ds(first + 1, packed, stride=tile_rows), :] = jnp.where(
-                low, pltpu.roll(a, tile_cols, 1), b
-            )
-    me = lax.axis_index("row") % OWNERS
-    size = half * tile_rows
+        project(normed, turned, mask, held, first, tile_rows, tile_cols)
+
+
+def right_kernel(lens_ref, normed_ref, w_ref, g_ref, *refs):
+    outs, (turned, held) = refs[:OWNERS], refs[OWNERS:]
+    project_all(lens_ref, normed_ref, w_ref, g_ref, turned, held)
     for d in range(OWNERS):
-        at = pl.multiple_of((me ^ d) * size, size)
-        right = held_right[pl.ds(at, size)].astype(jnp.bfloat16)
-        outs[d][:size] = held_left[pl.ds(at, size)].astype(jnp.bfloat16)
-        outs[d][size:] = right
-        outs[OWNERS + d][...] = right
+        outs[d][...] = owner_block(held, d, outs[d].shape[0])
+
+
+def left_kernel(lens_ref, normed_ref, w_ref, g_ref, *refs):
+    rights, outs, (turned, held) = refs[:OWNERS], refs[OWNERS : 2 * OWNERS], refs[2 * OWNERS :]
+    project_all(lens_ref, normed_ref, w_ref, g_ref, turned, held)
+    size = rights[0].shape[0]
+    for d in range(OWNERS):
+        outs[d][:size] = owner_block(held, d, size)
+        outs[d][size:] = rights[d][...]
 
 
 def gate_kernel(normed_ref, w_ref, gate_ref):
@@ -88,48 +113,58 @@
 
 
 def tri_kernel(*refs):
-    near, far, outs = refs[:OWNERS], refs[OWNERS : 2 * OWNERS], refs[2 * OWNERS : -1]
-    rights = refs[-1]
+    near, far = refs[:OWNERS], refs[OWNERS : 2 * OWNERS]
+    near_over, far_over = refs[2 * OWNERS : 3 * OWNERS], refs[3 * OWNERS : 4 * OWNERS]
+    outs, rights = refs[4 * OWNERS : -1], refs[-1]
     size, width = far[0].shape
-    half = rights.shape[0]
+    half = rights.shape[1]
     tile_rows = size // half
-    side = OWNERS * tile_rows
-    me = lax.axis_index("row")
-    owner, part, col = me % OWNERS, me // OWNERS, lax.axis_index("col")
+    side = width // 2
+    me, col = lax.axis_index("row"), lax.axis_index("col")
     for d in range(OWNERS):
-        for away, ref in ((0, near[d]), (1, far[d])):
-            at = pl.multiple_of((part ^ away) * side + (owner ^ d) * tile_rows, tile_rows)
-            start = size if away == 0 else 0
+        for away, ref in (
+            (d // 2 * 2, near[d]),
+            (d // 2 * 2 + 1, near_over[d]),
+            (d // 2 * 2 + 4, far[d]),
+            (d // 2 * 2 + 5, far_over[d]),
+        ):
+            at = pl.multiple_of((me ^ away) * tile_rows, tile_rows)
+            start = ref.shape[0] - size
             for m in range(half):
-                rights[m, pl.ds(at, tile_rows), :] = ref[
+                rights[d % 2, m, pl.ds(at, tile_rows), :] = ref[
                     start + m * tile_rows : start + (m + 1) * tile_rows
                 ]
-    low = lanes_of((side, width)) < width // 2
+    low = lanes_of((side, width)) < side
     for m in range(half):
-        left = jnp.concatenate([near[d][m * tile_rows : (m + 1) * tile_rows] for d in range(OWNERS)], 0)
-        pieces = []
-        for dx in (0, 1):
-            block = rights[m, pl.ds(pl.multiple_of((col ^ dx) * side, side), side), :].astype(jnp.float32)
-            pieces += [jnp.where(low, block, 0.0), jnp.where(low, 0.0, block)]
-        right = jnp.concatenate(pieces, 0).astype(jnp.bfloat16)
-        product = nt_dot(left, right).astype(jnp.bfloat16)
-        for d in range(OWNERS):
+        at = slice(m * tile_rows, (m + 1) * tile_rows)
+        product = 0.0
+        for dk in (0, 1):
+            left = jnp.concatenate([near[dk][at], near[2 + dk][at]], 0)
+            pieces = []
             for dx in (0, 1):
-                outs[2 * d + dx][m * tile_rows : (m + 1) * tile_rows] = product[
-                    d * tile_rows : (d + 1) * tile_rows, dx * width : (dx + 1) * width
+                block = rights[dk, m, pl.ds(pl.multiple_of((col ^ dx) * side, side), side), :]
+                block = block.astype(jnp.float32)
+                pieces += [jnp.where(low, block, 0.0), jnp.where(low, 0.0, block)]
+            right = jnp.concatenate(pieces, 0).astype(jnp.bfloat16)
+            product = product + nt_dot(left, right)
+        product = product.astype(jnp.bfloat16)
+        for dz in (0, 1):
+            for dx in (0, 1):
+                outs[2 * dz + dx][at] = product[
+                    dz * tile_rows : (dz + 1) * tile_rows, dx * width : (dx + 1) * width
                 ]
 
 
 def finish_kernel(lens_ref, x_ref, gate_ref, bins_ref, ow_ref, dw_ref, *refs):
-    parts, out_ref, loss_ref, (held, wide) = refs[:8], refs[8], refs[9], refs[10:]
+    parts, (out_ref, loss_ref, held, wide) = refs[:OWNERS], refs[OWNERS:]
     tile_rows, tile_cols, channels = x_ref.shape
     size, width = parts[0].shape
     half = size // tile_rows
     packed = OWNERS * half
-    owner = lax.axis_index("row") % OWNERS
+    owner = owner_place()
     total = jnp.zeros((tile_rows, width), jnp.float32)
     for d in range(OWNERS):
-        block = parts[2 * d][...].astype(jnp.float32) + parts[2 * d + 1][...].astype(jnp.float32)
+        block = parts[d][...].astype(jnp.float32)
         held[pl.ds(pl.multiple_of((owner ^ d) * size, size), size), :] = block
         total = total + jnp.sum(block.reshape(half, tile_rows, width), 0)
     average = (total + pltpu.roll(total, tile_cols, 1)) * (1.0 / channels)
@@ -167,16 +202,10 @@
         bins = bins_ref[first // 2 : first // 2 + 1]
         picked = jnp.sum(jnp.where(bin_ids == bins, logits, 0.0), axis=0, keepdims=True)
         loss = loss + pair_mask(lens_ref, tile_rows, tile_cols, first) * (log_total - picked)
-    loss_ref[...] = jnp.broadcast_to(jnp.sum(loss, axis=1, keepdims=True), loss_ref.shape)
-
-
-def loss_kernel(residues, lens_ref, *refs):
-    total = refs[0][...]
-    for ref in refs[1:-1]:
-        total = total + ref[...]
-    live = residues - lens_ref[lens_ref.shape[0] - 1]
-    count = jnp.full(total.shape, live * live, jnp.int32).astype(jnp.float32)
-    refs[-1][0] = (total / count)[0, 0]
+    live = tile_rows * lax.axis_size("row") - lens_ref[lens_ref.shape[0] - 1]
+    count = jnp.full((1, 1), live * live, jnp.int32).astype(jnp.float32)
+    loss = jnp.sum(loss, axis=1, keepdims=True) / count
+    loss_ref[...] = jnp.broadcast_to(loss, loss_ref.shape)
 
 
 def exchange(value, places, mask):
@@ -215,30 +244,33 @@
     size = channels // OWNERS // 2 * tile_rows
     bf16, f32 = jnp.bfloat16, jnp.float32
     struct = jax.ShapeDtypeStruct
-    sent = call(
-        project_kernel,
-        [struct((spots, channels), bf16)]
-        + [struct((2 * size, width), bf16)] * OWNERS
-        + [struct((size, width), bf16)] * OWNERS,
-        [
-            pltpu.VMEM((4 * channels, channels), bf16),
-            pltpu.VMEM((OWNERS * size, width), f32),
-            pltpu.VMEM((OWNERS * size, width), f32),
-        ],
-        [SMEM] + [VMEM] * 5,
-        args=(
-            chain_lengths,
-            pair_repr,
-            left_weight,
-            left_gate_weight,
-            right_weight,
-            right_gate_weight,
-        ),
-        flops=8 * spots * channels * channels,
-    )
-    normed, near, far = sent[0], sent[1 : 1 + OWNERS], sent[1 + OWNERS :]
-    far = [exchange(value, places, (OWNERS + d) * cols) for d, value in enumerate(far)]
-    near = [near[0]] + [exchange(near[d], places, d * cols) for d in range(1, OWNERS)]
+    turned = pltpu.VMEM((2 * channels, channels), bf16)
+    held = pltpu.VMEM((OWNERS * size, width), f32)
+    over_core, over_half = cols, 4 * cols
+    over = [0, 1, 2 * cols, 2 * cols + 1]
+    normed = call(
+        norm_kernel, struct((spots, channels), bf16), args=(pair_repr,), flops=1 << 30
+    )
+    rights = call(
+        right_kernel,
+        [struct((size, width), bf16)] * OWNERS,
+        [turned, held],
+        [SMEM] + [VMEM] * 3,
+        args=(chain_lengths, normed, right_weight, right_gate_weight),
+        flops=4 * spots * channels * channels,
+    )
+    far = [exchange(rights[d], places, over_half + over[d]) for d in range(OWNERS)]
+    near = call(
+        left_kernel,
+        [struct((2 * size, width), bf16)] * OWNERS,
+        [turned, held],
+        [SMEM] + [VMEM] * (3 + OWNERS),
+        args=(chain_lengths, normed, left_weight, left_gate_weight, *rights),
+        flops=4 * spots * channels * channels,
+    )
+    near = [near[0]] + [exchange(near[d], places, over[d]) for d in range(1, OWNERS)]
+    near_over = [exchange(value, places, over_core) for value in [rights[0]] + near[1:]]
+    far_over = [exchange(value, places, over_core) for value in far]
     gate = call(
         gate_kernel,
         struct((spots, channels), f32),
@@ -247,20 +279,17 @@
     )
     parts = call(
         tri_kernel,
-        [struct((size, width), bf16)] * (2 * OWNERS),
-        [pltpu.VMEM((size // tile_rows, rows * tile_rows, width), bf16)],
-        args=(*near, *far),
-        flops=2 * OWNERS * size * 2 * OWNERS * tile_rows * width,
-    )
-    parts = [parts[0]] + [exchange(parts[at], places, at) for at in range(1, 2 * OWNERS)]
+        [struct((size, width), bf16)] * OWNERS,
+        [pltpu.VMEM((cols, size // tile_rows, rows * tile_rows, width), bf16)],
+        args=(*near, *far, *near_over, *far_over),
+        flops=8 * size * 2 * tile_rows * 2 * width,
+    )
+    parts = [parts[0]] + [exchange(parts[d], places, over[d]) for d in range(1, OWNERS)]
     pair_out, loss = call(
         finish_kernel,
-        [struct(pair_repr.shape, bf16), struct((8, 128), f32)],
-        [
-            pltpu.VMEM((OWNERS * size, width), f32),
-            pltpu.VMEM((channels // 2, 2 * channels), bf16),
-        ],
-        [SMEM] + [VMEM] * 13,
+        [struct(pair_repr.shape, bf16), struct((1, 128), f32)],
+        [held, pltpu.VMEM((channels // 2, 2 * channels), bf16)],
+        [SMEM] + [VMEM] * 9,
         args=(
             chain_lengths,
             pair_repr,
@@ -272,22 +301,9 @@
         ),
         flops=6 * spots * channels * channels,
     )
-    loss = loss + exchange(loss, places, cols)
-    losses = [loss] + [
-        exchange(loss, places, z * 2 * cols + x)
-        for z in range(rows // 2)
-        for x in range(cols)
-        if z or x
-    ]
-    loss_value = call(
-        lambda *refs: loss_kernel(rows * tile_rows, *refs),
-        struct((1,), f32),
-        (),
-        [SMEM] + [VMEM] * len(losses),
-        SMEM,
-        args=(chain_lengths, *losses),
-    )
-    return (pair_out, loss_value)
+    for mask in (over_core, over[1], over[2], over_half):
+        loss = loss + exchange(loss, places, mask)
+    return (pair_out, loss[0, :1])
 
 
 def by_all_to_all(

time: 59.3 us -> 51.1 us (0.86)
  starting transfers between devices: 30 us -> 24.9 us
  local copies, waits for them, and re-layouts: 4.84 us -> 1.6 us
    ppermute x22, starting transfers between devices: 30 us -> 24.9 us  [exchange(): return lax.ppermute(value, AXES, [(at, at ^ mask) for at in range(places)])]
    unnamed x25 -> x23, local copies, waits for them, and re-layouts: 4.77 us -> 1.53 us
    pallas_call x5 -> x6, Pallas kernels: 6.83 us -> 6.65 us  [call(): pl.pallas_call(kernel, out_shape=outs, in_specs=specs if specs is not Non...]
  transfers between devices with their start and end apart: 22 -> 22, of which waited for: 10 -> 11; matrix products, arithmetic and copies ran while one was open for 0% -> 0% of each run, Pallas kernels for 0% -> 3%
where the time goes in v4:
time: 51.1 us; the launch traced here: 50.9 us
  starting transfers between devices  24.9 us (49%)
  waiting for transfers between devices  16.4 us (32%)
  Pallas kernels  6.65 us (13%)
  local copies, waits for them, and re-layouts  1.6 us (3%)
  between operations  0.74 us (1%)
  other arithmetic  0.52 us (1%)
    ppermute x22, starting transfers between devices, exchange(): return lax.ppermute(value, AXES, [(at, at ^ mask) for at in range(places)])  24.9 us
    ppermute x22, waiting for transfers between devices, exchange(): return lax.ppermute(value, AXES, [(at, at ^ mask) for at in range(places)])  16.4 us
    pallas_call x6, Pallas kernels, call(): pl.pallas_call(kernel, out_shape=outs, in_specs=specs if specs is not Non...  6.65 us
    unnamed x23, local copies, waits for them, and re-layouts  1.53 us
  transfers between devices with their start and end apart: 22, of which 11 were waited for; matrix products, arithmetic and copies ran while one was open for 0% of the time, Pallas kernels for 3%

profile of v4, /device:TPU:0, one launch (start us, length us, event | category | flops | bytes accessed | tf_op | source)
XLA Modules:
  0.0 50.9 jit_solution(13077088525626308492)
XLA Ops:
  0.6 0.0 copy-start
  0.6 0.9 %copy-done = bf16[16,64,128]{2,1,0:T(8,128)(2,1)S(1)} copy-done((bf16[16,64,128]{2,1,0:T(8,128)(2,1)S(1)}, bf16[16,64,128]{2,1,0:T(8,128)(2,1)}, u32[]{:S(2)}) %copy-start) | copy-done | bytes 262168
  1.6 0.4 shard_map.113.normed_ref
  1.9 0.3 copy-done.6
  2.2 0.1 copy-done.7
  2.4 0.0 copy-done.8
  2.4 1.1 %shard_map.115 = (bf16[256,128]{1,0:T(8,128)(2,1)S(1)}, bf16[256,128]{1,0:T(8,128)(2,1)S(1)}, bf16[256,128]{1,0:T(8,128)(2,1)S(1)}, bf16[256,128]{1,0:T(8,128)(2,1)S(1)}) custom-call(s32[5]{0:T(128)S(1)} %copy-done.6, bf16[1024,128]{1,0:T(8,128)(2,1)S(1)} %shard_map.113.normed_ref, bf16[128,128]{1,0:T(8,128)(2,1)S(1)} %copy-done.7, ...), custom_call_target="tpu_custom_call" | custom-call | flops 67108864 | bytes 1048576 | tf_op jit(solution)/shard_map/pallas_call | solution.py:216
  3.5 4.1 %collective-permute-start.3 = (bf16[256,128]{1,0:T(8,128)(2,1)S(1)}, bf16[256,128]{1,0:T(8,128)(2,1)S(1)}, u32[]{:S(2)}, u32[]{:S(2)}) collective-permute-start(bf16[256,128]{1,0:T(8,128)(2,1)S(1)} %get-tuple-element.16.refs_0_), channel_id=1, source_target_pairs={{0,8},{1,9},{2,10},{3,11},{4,12},{5,13},{6,14},{7,15},{8,0},{9,1},... | collective-permute-start | bytes 196616 | tf_op jit(solution)/shard_map/ppermute | solution.py:212
  7.6 1.3 %collective-permute-start.4 = (bf16[256,128]{1,0:T(8,128)(2,1)S(1)}, bf16[256,128]{1,0:T(8,128)(2,1)S(1)}, u32[]{:S(2)}, u32[]{:S(2)}) collective-permute-start(bf16[256,128]{1,0:T(8,128)(2,1)S(1)} %get-tuple-element.17.refs_1_), channel_id=1, source_target_pairs={{0,9},{1,8},{2,11},{3,10},{4,13},{5,12},{6,15},{7,14},{8,1},{9,0},... | collective-permute-start | bytes 196616 | tf_op jit(solution)/shard_map/ppermute | solution.py:212
  8.8 3.6 %collective-permute-start.5 = (bf16[256,128]{1,0:T(8,128)(2,1)S(1)}, bf16[256,128]{1,0:T(8,128)(2,1)S(1)}, u32[]{:S(2)}, u32[]{:S(2)}) collective-permute-start(bf16[256,128]{1,0:T(8,128)(2,1)S(1)} %get-tuple-element.18.refs_2_), channel_id=1, source_target_pairs={{0,12},{1,13},{2,14},{3,15},{4,8},{5,9},{6,10},{7,11},{8,4},{9,5},... | collective-permute-start | bytes 196616 | tf_op jit(solution)/shard_map/ppermute | solution.py:212
  12.5 0.0 copy-done.4
  12.5 0.0 copy-done.5
  12.5 1.1 %shard_map.116 = (bf16[512,128]{1,0:T(8,128)(2,1)S(1)}, bf16[512,128]{1,0:T(8,128)(2,1)S(1)}, bf16[512,128]{1,0:T(8,128)(2,1)S(1)}, bf16[512,128]{1,0:T(8,128)(2,1)S(1)}) custom-call(s32[5]{0:T(128)S(1)} %copy-done.6, bf16[1024,128]{1,0:T(8,128)(2,1)S(1)} %shard_map.113.normed_ref, bf16[128,128]{1,0:T(8,128)(2,1)S(1)} %copy-done.4, ...), custom_call_target="tpu_custom_call" | custom-call | flops 67108864 | bytes 1048576 | tf_op jit(solution)/shard_map/pallas_call | solution.py:216
  13.6 0.1 collective-permute-start.2
  13.7 1.0 %collective-permute-start = (bf16[512,128]{1,0:T(8,128)(2,1)S(1)}, bf16[512,128]{1,0:T(8,128)(2,1)S(1)}, u32[]{:S(2)}, u32[]{:S(2)}) collective-permute-start(bf16[512,128]{1,0:T(8,128)(2,1)S(1)} %get-tuple-element.21), channel_id=1, source_target_pairs={{0,1},{1,0},{2,3},{3,2},{4,5},{5,4},{6,7},{7,6},{8,9},{9,8},{10,11... | collective-permute-start | bytes 393224 | tf_op jit(solution)/shard_map/ppermute | solution.py:212
  14.7 0.0 collective-permute-done.3.refs_4_
  14.7 2.5 %collective-permute-start.1 = (bf16[512,128]{1,0:T(8,128)(2,1)S(1)}, bf16[512,128]{1,0:T(8,128)(2,1)S(1)}, u32[]{:S(2)}, u32[]{:S(2)}) collective-permute-start(bf16[512,128]{1,0:T(8,128)(2,1)S(1)} %get-tuple-element.22), channel_id=1, source_target_pairs={{0,4},{1,5},{2,6},{3,7},{4,0},{5,1},{6,2},{7,3},{8,12},{9,13},{10,... | collective-permute-start | bytes 393224 | tf_op jit(solution)/shard_map/ppermute | solution.py:212
  17.1 0.0 collective-permute-done.4.refs_5_
  17.2 2.9 %collective-permute-start.6 = (bf16[256,128]{1,0:T(8,128)(2,1)S(1)}, bf16[256,128]{1,0:T(8,128)(2,1)S(1)}, u32[]{:S(2)}, u32[]{:S(2)}) collective-permute-start(bf16[256,128]{1,0:T(8,128)(2,1)S(1)} %get-tuple-element.19.refs_3_), channel_id=1, source_target_pairs={{0,13},{1,12},{2,15},{3,14},{4,9},{5,8},{6,11},{7,10},{8,5},{9,4},... | collective-permute-start | bytes 196616 | tf_op jit(solution)/shard_map/ppermute | solution.py:212
  20.1 0.0 collective-permute-done.5.refs_6_
  20.1 0.0 collective-permute-start.7
  20.1 4.0 %collective-permute-done.6.refs_7_ = bf16[256,128]{1,0:T(8,128)(2,1)S(1)} collective-permute-done((bf16[256,128]{1,0:T(8,128)(2,1)S(1)}, bf16[256,128]{1,0:T(8,128)(2,1)S(1)}, u32[]{:S(2)}, u32[]{:S(2)}) %collective-permute-start.6) | collective-permute-done | bytes 65568 | tf_op jit(solution)/shard_map/ppermute | solution.py:212
  24.1 0.0 collective-permute-start.11
  24.1 0.0 collective-permute-done.7.refs_8_
  24.1 0.5 collective-permute-start.12
  24.6 0.0 collective-permute-done.2.refs_3_
  24.6 0.1 collective-permute-start.10
  24.7 0.0 collective-permute-done.refs_1_
  24.7 0.4 collective-permute-start.8
  25.1 0.0 collective-permute-done.1.refs_2_
  25.2 0.1 collective-permute-start.9
  25.2 0.1 collective-permute-done.11.refs_12_
  25.4 0.3 collective-permute-start.13
  25.7 0.0 collective-permute-done.12.refs_13_
  25.7 0.2 collective-permute-start.14
  25.9 0.7 %collective-permute-done.13.refs_14_ = bf16[256,128]{1,0:T(8,128)(2,1)S(1)} collective-permute-done((bf16[256,128]{1,0:T(8,128)(2,1)S(1)}, bf16[256,128]{1,0:T(8,128)(2,1)S(1)}, u32[]{:S(2)}, u32[]{:S(2)}) %collective-permute-start.13) | collective-permute-done | bytes 65568 | tf_op jit(solution)/shard_map/ppermute | solution.py:212
  26.6 0.3 collective-permute-done.14.refs_15_
  26.9 0.0 collective-permute-done.10.refs_11_
  26.9 0.0 collective-permute-done.8.refs_9_
  26.9 0.0 collective-permute-done.9.refs_10_
  26.9 0.0 copy-start.9
  27.0 0.9 %shard_map.117 = (bf16[256,128]{1,0:T(8,128)(2,1)S(1)}, bf16[256,128]{1,0:T(8,128)(2,1)S(1)}, bf16[256,128]{1,0:T(8,128)(2,1)S(1)}, bf16[256,128]{1,0:T(8,128)(2,1)S(1)}) custom-call(bf16[512,128]{1,0:T(8,128)(2,1)S(1)} %get-tuple-element.20.refs_0_, bf16[512,128]{1,0:T(8,128)(2,1)S(1)} %collective-permute-done.refs_1_, ...), custom_call_target="tpu_custom_call" | custom-call | flops 16777216 | bytes 1048576 | tf_op jit(solution)/shard_map/pallas_call | solution.py:216
  27.9 0.0 copy-start.2
  27.9 0.8 %collective-permute-start.15 = (bf16[256,128]{1,0:T(8,128)(2,1)S(1)}, bf16[256,128]{1,0:T(8,128)(2,1)S(1)}, u32[]{:S(2)}, u32[]{:S(2)}) collective-permute-start(bf16[256,128]{1,0:T(8,128)(2,1)S(1)} %get-tuple-element.25), channel_id=1, source_target_pairs={{0,1},{1,0},{2,3},{3,2},{4,5},{5,4},{6,7},{7,6},{8,9},{9,8},{10,11... | collective-permute-start | bytes 196616 | tf_op jit(solution)/shard_map/ppermute | solution.py:212
  28.7 0.0 collective-permute-start.16
  28.7 2.8 %collective-permute-start.17 = (bf16[256,128]{1,0:T(8,128)(2,1)S(1)}, bf16[256,128]{1,0:T(8,128)(2,1)S(1)}, u32[]{:S(2)}, u32[]{:S(2)}) collective-permute-start(bf16[256,128]{1,0:T(8,128)(2,1)S(1)} %get-tuple-element.27), channel_id=1, source_target_pairs={{0,5},{1,4},{2,7},{3,6},{4,1},{5,0},{6,3},{7,2},{8,13},{9,12},{10,... | collective-permute-start | bytes 196616 | tf_op jit(solution)/shard_map/ppermute | solution.py:212
  31.4 0.0 copy-done.9
  31.4 0.1 copy.12.dw_ref
  31.6 0.0 copy-done.10
  31.6 0.1 reshape.7.bins_ref
  31.6 0.2 shard_map.114.gate_ref
  31.9 0.3 collective-permute-done.15.refs_1_
  32.2 1.1 %collective-permute-done.16.refs_2_ = bf16[256,128]{1,0:T(8,128)(2,1)S(1)} collective-permute-done((bf16[256,128]{1,0:T(8,128)(2,1)S(1)}, bf16[256,128]{1,0:T(8,128)(2,1)S(1)}, u32[]{:S(2)}, u32[]{:S(2)}) %collective-permute-start.16) | collective-permute-done | bytes 65568 | tf_op jit(solution)/shard_map/ppermute | solution.py:212
  33.3 1.4 %collective-permute-done.17.refs_3_ = bf16[256,128]{1,0:T(8,128)(2,1)S(1)} collective-permute-done((bf16[256,128]{1,0:T(8,128)(2,1)S(1)}, bf16[256,128]{1,0:T(8,128)(2,1)S(1)}, u32[]{:S(2)}, u32[]{:S(2)}) %collective-permute-start.17) | collective-permute-done | bytes 65568 | tf_op jit(solution)/shard_map/ppermute | solution.py:212
  34.8 3.0 %shard_map.118 = (bf16[16,64,128]{2,1,0:T(8,128)(2,1)}, f32[1,128]{1,0:T(1,128)S(1)}) custom-call(s32[5]{0:T(128)S(1)} %copy-done.6, bf16[16,64,128]{2,1,0:T(8,128)(2,1)S(1)} %copy-done.1, f32[1024,128]{1,0:T(8,128)S(1)} %shard_map.114.gate_ref, s32[8,128]{1,0:T(8,128)S(1)} %reshape.7.bins_ref, bf16[128,128]{1,0:T(8,128)(2,1)S(1)} %copy-done.3, ...), custom_call_target="tpu_custom_call" | custom-call | flops 100663296 | bytes 1048576 | tf_op jit(solution)/shard_map/pallas_call | solution.py:216
  37.7 0.0 collective-permute-start.18
  37.7 1.1 %collective-permute-done.18 = f32[1,128]{1,0:T(1,128)S(1)} collective-permute-done((f32[1,128]{1,0:T(1,128)S(1)}, f32[1,128]{1,0:T(1,128)S(1)}, u32[]{:S(2)}, u32[]{:S(2)}) %collective-permute-start.18) | collective-permute-done | bytes 544 | tf_op jit(solution)/shard_map/ppermute | solution.py:212
  38.8 0.8 %collective-permute-start.19 = (f32[1,128]{1,0:T(1,128)S(1)}, f32[1,128]{1,0:T(1,128)S(1)}, u32[]{:S(2)}, u32[]{:S(2)}) collective-permute-start(f32[1,128]{1,0:T(1,128)S(1)} %add.12), channel_id=1, source_target_pairs={{0,1},{1,0},{2,3},{3,2},{4,5},{5,4},{6,7},{7,6},{8,9},{9,8},{10,11... | collective-permute-start | bytes 1544 | tf_op jit(solution)/shard_map/ppermute | solution.py:212
  39.6 2.8 %collective-permute-done.19 = f32[1,128]{1,0:T(1,128)S(1)} collective-permute-done((f32[1,128]{1,0:T(1,128)S(1)}, f32[1,128]{1,0:T(1,128)S(1)}, u32[]{:S(2)}, u32[]{:S(2)}) %collective-permute-start.19) | collective-permute-done | bytes 544 | tf_op jit(solution)/shard_map/ppermute | solution.py:212
  42.4 1.1 %collective-permute-start.20 = (f32[1,128]{1,0:T(1,128)S(1)}, f32[1,128]{1,0:T(1,128)S(1)}, u32[]{:S(2)}, u32[]{:S(2)}) collective-permute-start(f32[1,128]{1,0:T(1,128)S(1)} %add.13), channel_id=1, source_target_pairs={{0,4},{1,5},{2,6},{3,7},{4,0},{5,1},{6,2},{7,3},{8,12},{9,13},{10,... | collective-permute-start | bytes 1544 | tf_op jit(solution)/shard_map/ppermute | solution.py:212
  43.5 2.4 %collective-permute-done.20 = f32[1,128]{1,0:T(1,128)S(1)} collective-permute-done((f32[1,128]{1,0:T(1,128)S(1)}, f32[1,128]{1,0:T(1,128)S(1)}, u32[]{:S(2)}, u32[]{:S(2)}) %collective-permute-start.20) | collective-permute-done | bytes 544 | tf_op jit(solution)/shard_map/ppermute | solution.py:212
  45.9 2.4 %collective-permute-start.21 = (f32[1,128]{1,0:T(1,128)S(1)}, f32[1,128]{1,0:T(1,128)S(1)}, u32[]{:S(2)}, u32[]{:S(2)}) collective-permute-start(f32[1,128]{1,0:T(1,128)S(1)} %add.14), channel_id=1, source_target_pairs={{0,8},{1,9},{2,10},{3,11},{4,12},{5,13},{6,14},{7,15},{8,0},{9,1},... | collective-permute-start | bytes 1544 | tf_op jit(solution)/shard_map/ppermute | solution.py:212
  48.3 2.0 %collective-permute-done.21 = f32[1,128]{1,0:T(1,128)S(1)} collective-permute-done((f32[1,128]{1,0:T(1,128)S(1)}, f32[1,128]{1,0:T(1,128)S(1)}, u32[]{:S(2)}, u32[]{:S(2)}) %collective-permute-start.21) | collective-permute-done | bytes 544 | tf_op jit(solution)/shard_map/ppermute | solution.py:212
  50.4 0.5 %add.15 = f32[1,128]{1,0:T(1,128)} add(f32[1,128]{1,0:T(1,128)S(1)} %add.14, f32[1,128]{1,0:T(1,128)S(1)} %collective-permute-done.21) | non-fusion elementwise | flops 128 | bytes 1536 | tf_op jit(solution)/shard_map/add | solution.py:305
  (14 shorter events, 0.0 us)
Async XLA Ops:
  0.6 1.0 %copy-start = (bf16[16,64,128]{2,1,0:T(8,128)(2,1)S(1)}, bf16[16,64,128]{2,1,0:T(8,128)(2,1)}, u32[]{:S(2)}) copy-start(bf16[16,64,128]{2,1,0:T(8,128)(2,1)} %x_ref.3) | copy-start | bytes 786436
  1.6 0.7 %copy-start.6 = (s32[5]{0:T(128)S(1)}, s32[5]{0:T(128)}, u32[]{:S(2)}) copy-start(s32[5]{0:T(128)} %lens_ref.5) | copy-start | bytes 64
  1.6 0.8 %copy-start.7 = (bf16[128,128]{1,0:T(8,128)(2,1)S(1)}, bf16[128,128]{1,0:T(8,128)(2,1)}, u32[]{:S(2)}) copy-start(bf16[128,128]{1,0:T(8,128)(2,1)} %w_ref.4) | copy-start | bytes 98308
  1.6 0.8 %copy-start.8 = (bf16[128,128]{1,0:T(8,128)(2,1)S(1)}, bf16[128,128]{1,0:T(8,128)(2,1)}, u32[]{:S(2)}) copy-start(bf16[128,128]{1,0:T(8,128)(2,1)} %g_ref.2) | copy-start | bytes 98308
  2.4 10.1 %copy-start.4 = (bf16[128,128]{1,0:T(8,128)(2,1)S(1)}, bf16[128,128]{1,0:T(8,128)(2,1)}, u32[]{:S(2)}) copy-start(bf16[128,128]{1,0:T(8,128)(2,1)} %w_ref.5) | copy-start | bytes 98308
  2.4 10.1 %copy-start.5 = (bf16[128,128]{1,0:T(8,128)(2,1)S(1)}, bf16[128,128]{1,0:T(8,128)(2,1)}, u32[]{:S(2)}) copy-start(bf16[128,128]{1,0:T(8,128)(2,1)} %g_ref.3) | copy-start | bytes 98308
  3.5 11.2 %collective-permute-start.3 = (bf16[256,128]{1,0:T(8,128)(2,1)S(1)}, bf16[256,128]{1,0:T(8,128)(2,1)S(1)}, u32[]{:S(2)}, u32[]{:S(2)}) collective-permute-start(bf16[256,128]{1,0:T(8,128)(2,1)S(1)} %get-tuple-element.16.refs_0_), channel_id=1, source_target_pairs={{0,8},{1,9},{2,10},{3,11},{4,12},{5,13},{6,14},{7,15},{8,0},{9,1},... | collective-permute-start | bytes 196616 | tf_op jit(solution)/shard_map/ppermute | solution.py:212
  7.6 9.6 %collective-permute-start.4 = (bf16[256,128]{1,0:T(8,128)(2,1)S(1)}, bf16[256,128]{1,0:T(8,128)(2,1)S(1)}, u32[]{:S(2)}, u32[]{:S(2)}) collective-permute-start(bf16[256,128]{1,0:T(8,128)(2,1)S(1)} %get-tuple-element.17.refs_1_), channel_id=1, source_target_pairs={{0,9},{1,8},{2,11},{3,10},{4,13},{5,12},{6,15},{7,14},{8,1},{9,0},... | collective-permute-start | bytes 196616 | tf_op jit(solution)/shard_map/ppermute | solution.py:212
  8.8 11.2 %collective-permute-start.5 = (bf16[256,128]{1,0:T(8,128)(2,1)S(1)}, bf16[256,128]{1,0:T(8,128)(2,1)S(1)}, u32[]{:S(2)}, u32[]{:S(2)}) collective-permute-start(bf16[256,128]{1,0:T(8,128)(2,1)S(1)} %get-tuple-element.18.refs_2_), channel_id=1, source_target_pairs={{0,12},{1,13},{2,14},{3,15},{4,8},{5,9},{6,10},{7,11},{8,4},{9,5},... | collective-permute-start | bytes 196616 | tf_op jit(solution)/shard_map/ppermute | solution.py:212
  13.6 11.0 %collective-permute-start.2 = (bf16[512,128]{1,0:T(8,128)(2,1)S(1)}, bf16[512,128]{1,0:T(8,128)(2,1)S(1)}, u32[]{:S(2)}, u32[]{:S(2)}) collective-permute-start(bf16[512,128]{1,0:T(8,128)(2,1)S(1)} %get-tuple-element.23), channel_id=1, source_target_pairs={{0,5},{1,4},{2,7},{3,6},{4,1},{5,0},{6,3},{7,2},{8,13},{9,12},{10,... | collective-permute-start | bytes 393224 | tf_op jit(solution)/shard_map/ppermute | solution.py:212
  13.7 11.0 %collective-permute-start = (bf16[512,128]{1,0:T(8,128)(2,1)S(1)}, bf16[512,128]{1,0:T(8,128)(2,1)S(1)}, u32[]{:S(2)}, u32[]{:S(2)}) collective-permute-start(bf16[512,128]{1,0:T(8,128)(2,1)S(1)} %get-tuple-element.21), channel_id=1, source_target_pairs={{0,1},{1,0},{2,3},{3,2},{4,5},{5,4},{6,7},{7,6},{8,9},{9,8},{10,11... | collective-permute-start | bytes 393224 | tf_op jit(solution)/shard_map/ppermute | solution.py:212
  14.7 10.5 %collective-permute-start.1 = (bf16[512,128]{1,0:T(8,128)(2,1)S(1)}, bf16[512,128]{1,0:T(8,128)(2,1)S(1)}, u32[]{:S(2)}, u32[]{:S(2)}) collective-permute-start(bf16[512,128]{1,0:T(8,128)(2,1)S(1)} %get-tuple-element.22), channel_id=1, source_target_pairs={{0,4},{1,5},{2,6},{3,7},{4,0},{5,1},{6,2},{7,3},{8,12},{9,13},{10,... | collective-permute-start | bytes 393224 | tf_op jit(solution)/shard_map/ppermute | solution.py:212
  17.2 7.0 %collective-permute-start.6 = (bf16[256,128]{1,0:T(8,128)(2,1)S(1)}, bf16[256,128]{1,0:T(8,128)(2,1)S(1)}, u32[]{:S(2)}, u32[]{:S(2)}) collective-permute-start(bf16[256,128]{1,0:T(8,128)(2,1)S(1)} %get-tuple-element.19.refs_3_), channel_id=1, source_target_pairs={{0,13},{1,12},{2,15},{3,14},{4,9},{5,8},{6,11},{7,10},{8,5},{9,4},... | collective-permute-start | bytes 196616 | tf_op jit(solution)/shard_map/ppermute | solution.py:212
  20.1 4.0 %collective-permute-start.7 = (bf16[256,128]{1,0:T(8,128)(2,1)S(1)}, bf16[256,128]{1,0:T(8,128)(2,1)S(1)}, u32[]{:S(2)}, u32[]{:S(2)}) collective-permute-start(bf16[256,128]{1,0:T(8,128)(2,1)S(1)} %get-tuple-element.16.refs_0_), channel_id=1, source_target_pairs={{0,2},{1,3},{2,0},{3,1},{4,6},{5,7},{6,4},{7,5},{8,10},{9,11},{10,... | collective-permute-start | bytes 196616 | tf_op jit(solution)/shard_map/ppermute | solution.py:212
  24.1 1.3 %collective-permute-start.11 = (bf16[256,128]{1,0:T(8,128)(2,1)S(1)}, bf16[256,128]{1,0:T(8,128)(2,1)S(1)}, u32[]{:S(2)}, u32[]{:S(2)}) collective-permute-start(bf16[256,128]{1,0:T(8,128)(2,1)S(1)} %collective-permute-done.3.refs_4_), channel_id=1, source_target_pairs={{0,2},{1,3},{2,0},{3,1},{4,6},{5,7},{6,4},{7,5},{8,10},{9,11},{10,... | collective-permute-start | bytes 196616 | tf_op jit(solution)/shard_map/ppermute | solution.py:212
  24.1 1.5 %collective-permute-start.12 = (bf16[256,128]{1,0:T(8,128)(2,1)S(1)}, bf16[256,128]{1,0:T(8,128)(2,1)S(1)}, u32[]{:S(2)}, u32[]{:S(2)}) collective-permute-start(bf16[256,128]{1,0:T(8,128)(2,1)S(1)} %collective-permute-done.4.refs_5_), channel_id=1, source_target_pairs={{0,2},{1,3},{2,0},{3,1},{4,6},{5,7},{6,4},{7,5},{8,10},{9,11},{10,... | collective-permute-start | bytes 196616 | tf_op jit(solution)/shard_map/ppermute | solution.py:212
  24.6 2.3 %collective-permute-start.10 = (bf16[512,128]{1,0:T(8,128)(2,1)S(1)}, bf16[512,128]{1,0:T(8,128)(2,1)S(1)}, u32[]{:S(2)}, u32[]{:S(2)}) collective-permute-start(bf16[512,128]{1,0:T(8,128)(2,1)S(1)} %collective-permute-done.2.refs_3_), channel_id=1, source_target_pairs={{0,2},{1,3},{2,0},{3,1},{4,6},{5,7},{6,4},{7,5},{8,10},{9,11},{10,... | collective-permute-start | bytes 393224 | tf_op jit(solution)/shard_map/ppermute | solution.py:212
  24.7 2.2 %collective-permute-start.8 = (bf16[512,128]{1,0:T(8,128)(2,1)S(1)}, bf16[512,128]{1,0:T(8,128)(2,1)S(1)}, u32[]{:S(2)}, u32[]{:S(2)}) collective-permute-start(bf16[512,128]{1,0:T(8,128)(2,1)S(1)} %collective-permute-done.refs_1_), channel_id=1, source_target_pairs={{0,2},{1,3},{2,0},{3,1},{4,6},{5,7},{6,4},{7,5},{8,10},{9,11},{10,... | collective-permute-start | bytes 393224 | tf_op jit(solution)/shard_map/ppermute | solution.py:212
  25.2 1.8 %collective-permute-start.9 = (bf16[512,128]{1,0:T(8,128)(2,1)S(1)}, bf16[512,128]{1,0:T(8,128)(2,1)S(1)}, u32[]{:S(2)}, u32[]{:S(2)}) collective-permute-start(bf16[512,128]{1,0:T(8,128)(2,1)S(1)} %collective-permute-done.1.refs_2_), channel_id=1, source_target_pairs={{0,2},{1,3},{2,0},{3,1},{4,6},{5,7},{6,4},{7,5},{8,10},{9,11},{10,... | collective-permute-start | bytes 393224 | tf_op jit(solution)/shard_map/ppermute | solution.py:212
  25.4 1.3 %collective-permute-start.13 = (bf16[256,128]{1,0:T(8,128)(2,1)S(1)}, bf16[256,128]{1,0:T(8,128)(2,1)S(1)}, u32[]{:S(2)}, u32[]{:S(2)}) collective-permute-start(bf16[256,128]{1,0:T(8,128)(2,1)S(1)} %collective-permute-done.5.refs_6_), channel_id=1, source_target_pairs={{0,2},{1,3},{2,0},{3,1},{4,6},{5,7},{6,4},{7,5},{8,10},{9,11},{10,... | collective-permute-start | bytes 196616 | tf_op jit(solution)/shard_map/ppermute | solution.py:212
  25.7 1.3 %collective-permute-start.14 = (bf16[256,128]{1,0:T(8,128)(2,1)S(1)}, bf16[256,128]{1,0:T(8,128)(2,1)S(1)}, u32[]{:S(2)}, u32[]{:S(2)}) collective-permute-start(bf16[256,128]{1,0:T(8,128)(2,1)S(1)} %collective-permute-done.6.refs_7_), channel_id=1, source_target_pairs={{0,2},{1,3},{2,0},{3,1},{4,6},{5,7},{6,4},{7,5},{8,10},{9,11},{10,... | collective-permute-start | bytes 196616 | tf_op jit(solution)/shard_map/ppermute | solution.py:212
  26.9 4.5 %copy-start.9 = (bf16[128,64]{0,1:T(8,128)(2,1)S(1)}, bf16[128,64]{0,1:T(8,128)(2,1)}, u32[]{:S(2)}) copy-start(bf16[128,64]{0,1:T(8,128)(2,1)} %param.19) | copy-start | bytes 49156
  27.9 3.8 %copy-start.2 = (bf16[128,128]{1,0:T(8,128)(2,1)S(1)}, bf16[128,128]{1,0:T(8,128)(2,1)}, u32[]{:S(2)}) copy-start(bf16[128,128]{1,0:T(8,128)(2,1)} %w_ref.3) | copy-start | bytes 98308
  27.9 4.3 %collective-permute-start.15 = (bf16[256,128]{1,0:T(8,128)(2,1)S(1)}, bf16[256,128]{1,0:T(8,128)(2,1)S(1)}, u32[]{:S(2)}, u32[]{:S(2)}) collective-permute-start(bf16[256,128]{1,0:T(8,128)(2,1)S(1)} %get-tuple-element.25), channel_id=1, source_target_pairs={{0,1},{1,0},{2,3},{3,2},{4,5},{5,4},{6,7},{7,6},{8,9},{9,8},{10,11... | collective-permute-start | bytes 196616 | tf_op jit(solution)/shard_map/ppermute | solution.py:212
  28.7 4.7 %collective-permute-start.16 = (bf16[256,128]{1,0:T(8,128)(2,1)S(1)}, bf16[256,128]{1,0:T(8,128)(2,1)S(1)}, u32[]{:S(2)}, u32[]{:S(2)}) collective-permute-start(bf16[256,128]{1,0:T(8,128)(2,1)S(1)} %get-tuple-element.26), channel_id=1, source_target_pairs={{0,4},{1,5},{2,6},{3,7},{4,0},{5,1},{6,2},{7,3},{8,12},{9,13},{10,... | collective-permute-start | bytes 196616 | tf_op jit(solution)/shard_map/ppermute | solution.py:212
  28.7 2.9 %copy-start.10 = (s32[16,64]{1,0:T(8,128)S(1)}, s32[16,64]{1,0:T(8,128)}, u32[]{:S(2)}) copy-start(s32[16,64]{1,0:T(8,128)} %param.11) | copy-start | bytes 12292
  28.7 6.1 %collective-permute-start.17 = (bf16[256,128]{1,0:T(8,128)(2,1)S(1)}, bf16[256,128]{1,0:T(8,128)(2,1)S(1)}, u32[]{:S(2)}, u32[]{:S(2)}) collective-permute-start(bf16[256,128]{1,0:T(8,128)(2,1)S(1)} %get-tuple-element.27), channel_id=1, source_target_pairs={{0,5},{1,4},{2,7},{3,6},{4,1},{5,0},{6,3},{7,2},{8,13},{9,12},{10,... | collective-permute-start | bytes 196616 | tf_op jit(solution)/shard_map/ppermute | solution.py:212
  31.6 3.1 %copy-start.1 = (bf16[16,64,128]{2,1,0:T(8,128)(2,1)S(1)}, bf16[16,64,128]{2,1,0:T(8,128)(2,1)}, u32[]{:S(2)}) copy-start(bf16[16,64,128]{2,1,0:T(8,128)(2,1)} %x_ref.3) | copy-start | bytes 786436
  31.6 3.1 %copy-start.3 = (bf16[128,128]{1,0:T(8,128)(2,1)S(1)}, bf16[128,128]{1,0:T(8,128)(2,1)}, u32[]{:S(2)}) copy-start(bf16[128,128]{1,0:T(8,128)(2,1)} %ow_ref.1) | copy-start | bytes 98308
  37.7 1.1 %collective-permute-start.18 = (f32[1,128]{1,0:T(1,128)S(1)}, f32[1,128]{1,0:T(1,128)S(1)}, u32[]{:S(2)}, u32[]{:S(2)}) collective-permute-start(f32[1,128]{1,0:T(1,128)S(1)} %get-tuple-element.29), channel_id=1, source_target_pairs={{0,2},{1,3},{2,0},{3,1},{4,6},{5,7},{6,4},{7,5},{8,10},{9,11},{10,... | collective-permute-start | bytes 1544 | tf_op jit(solution)/shard_map/ppermute | solution.py:212
  38.8 3.5 %collective-permute-start.19 = (f32[1,128]{1,0:T(1,128)S(1)}, f32[1,128]{1,0:T(1,128)S(1)}, u32[]{:S(2)}, u32[]{:S(2)}) collective-permute-start(f32[1,128]{1,0:T(1,128)S(1)} %add.12), channel_id=1, source_target_pairs={{0,1},{1,0},{2,3},{3,2},{4,5},{5,4},{6,7},{7,6},{8,9},{9,8},{10,11... | collective-permute-start | bytes 1544 | tf_op jit(solution)/shard_map/ppermute | solution.py:212
  42.4 3.5 %collective-permute-start.20 = (f32[1,128]{1,0:T(1,128)S(1)}, f32[1,128]{1,0:T(1,128)S(1)}, u32[]{:S(2)}, u32[]{:S(2)}) collective-permute-start(f32[1,128]{1,0:T(1,128)S(1)} %add.13), channel_id=1, source_target_pairs={{0,4},{1,5},{2,6},{3,7},{4,0},{5,1},{6,2},{7,3},{8,12},{9,13},{10,... | collective-permute-start | bytes 1544 | tf_op jit(solution)/shard_map/ppermute | solution.py:212
  45.9 4.4 %collective-permute-start.21 = (f32[1,128]{1,0:T(1,128)S(1)}, f32[1,128]{1,0:T(1,128)S(1)}, u32[]{:S(2)}, u32[]{:S(2)}) collective-permute-start(f32[1,128]{1,0:T(1,128)S(1)} %add.14), channel_id=1, source_target_pairs={{0,8},{1,9},{2,10},{3,11},{4,12},{5,13},{6,14},{7,15},{8,0},{9,1},... | collective-permute-start | bytes 1544 | tf_op jit(solution)/shard_map/ppermute | solution.py:212

commit v5 on v4

--- a/solution.py
+++ b/solution.py
@@ -55,11 +55,13 @@
         turned[at * channels : (at + 1) * channels] = jnp.concatenate(blocks, 0).astype(jnp.bfloat16)
 
 
-def project(normed, turned, mask, held, first, tile_rows, tile_cols):
+def project(normed, turned, held, first, tile_rows, tile_cols, mask=None):
     channels = normed.shape[1]
     packed = channels // 2
     flat = nt_dot(turned[...], normed)
-    value = sigmoid(flat[channels:]) * flat[:channels] * mask
+    value = sigmoid(flat[channels:]) * flat[:channels]
+    if mask is not None:
+        value = value * mask
     a, b = value[:packed], value[packed:]
     low = lanes_of((packed, 2 * tile_cols)) < tile_cols
     held[pl.ds(first, packed, stride=tile_rows), :] = jnp.where(low, a, pltpu.roll(b, tile_cols, 1))
@@ -88,13 +90,13 @@
     turn((w_ref, g_ref), turned)
     for first in range(0, tile_rows, 2):
         normed = normed_ref[first * tile_cols : (first + 2) * tile_cols]
-        mask = pair_mask(lens_ref, tile_rows, tile_cols, first)
-        project(normed, turned, mask, held, first, tile_rows, tile_cols)
-
-
-def right_kernel(lens_ref, normed_ref, w_ref, g_ref, *refs):
+        mask = None if lens_ref is None else pair_mask(lens_ref, tile_rows, tile_cols, first)
+        project(normed, turned, held, first, tile_rows, tile_cols, mask)
+
+
+def right_kernel(normed_ref, w_ref, g_ref, *refs):
     outs, (turned, held) = refs[:OWNERS], refs[OWNERS:]
-    project_all(lens_ref, normed_ref, w_ref, g_ref, turned, held)
+    project_all(None, normed_ref, w_ref, g_ref, turned, held)
     for d in range(OWNERS):
         outs[d][...] = owner_block(held, d, outs[d].shape[0])
 
@@ -108,11 +110,26 @@
         outs[d][size:] = rights[d][...]
 
 
-def gate_kernel(normed_ref, w_ref, gate_ref):
-    gate_ref[...] = sigmoid(jnp.dot(normed_ref[...], w_ref[...], preferred_element_type=jnp.float32))
-
-
-def tri_kernel(*refs):
+def gate_kernel(x_ref, normed_ref, gw_ref, ow_ref, dw_ref, gate_ref, x_turned_ref, ow_turned, dw_turned):
+    tile_rows, tile_cols, channels = x_ref.shape
+    share = channels // OWNERS
+    half = share // 2
+    blocks = [
+        ow_ref[o * share + g * half : o * share + (g + 1) * half].astype(jnp.float32)
+        for g in (0, 1)
+        for o in range(OWNERS)
+    ]
+    ow_turned[...] = jnp.concatenate(blocks, 0).T.astype(jnp.bfloat16)
+    dw_turned[...] = dw_ref[...].astype(jnp.float32).T.astype(jnp.bfloat16)
+    gate_turned = gw_ref[...].astype(jnp.float32).T.astype(jnp.bfloat16)
+    for first in range(0, tile_rows, 2):
+        at = slice(first * tile_cols, (first + 2) * tile_cols)
+        gate_ref[:, at] = sigmoid(nt_dot(gate_turned, normed_ref[at]))
+        x = x_ref[first : first + 2].astype(jnp.float32).reshape(2 * tile_cols, channels)
+        x_turned_ref[:, at] = x.T
+
+
+def tri_kernel(lens_ref, *refs):
     near, far = refs[:OWNERS], refs[OWNERS : 2 * OWNERS]
     near_over, far_over = refs[2 * OWNERS : 3 * OWNERS], refs[3 * OWNERS : 4 * OWNERS]
     outs, rights = refs[4 * OWNERS : -1], refs[-1]
@@ -121,20 +138,24 @@
     tile_rows = size // half
     side = width // 2
     me, col = lax.axis_index("row"), lax.axis_index("col")
+    pieces = []
     for d in range(OWNERS):
-        for away, ref in (
-            (d // 2 * 2, near[d]),
-            (d // 2 * 2 + 1, near_over[d]),
-            (d // 2 * 2 + 4, far[d]),
-            (d // 2 * 2 + 5, far_over[d]),
-        ):
-            at = pl.multiple_of((me ^ away) * tile_rows, tile_rows)
-            start = ref.shape[0] - size
-            for m in range(half):
-                rights[d % 2, m, pl.ds(at, tile_rows), :] = ref[
-                    start + m * tile_rows : start + (m + 1) * tile_rows
-                ]
-    low = lanes_of((side, width)) < side
+        away = d // 2 * 2
+        pieces += [(d % 2, away, near[d]), (d % 2, away + 4, far[d])]
+        pieces += [(d % 2, away + 1, near_over[d]), (d % 2, away + 5, far_over[d])]
+    for dk, away, ref in pieces:
+        start = ref.shape[0] - size
+        at = pl.multiple_of((me ^ away) * tile_rows, tile_rows)
+        for m in range(half):
+            rights[dk, m, pl.ds(at, tile_rows), :] = ref[
+                start + m * tile_rows : start + (m + 1) * tile_rows
+            ]
+    live = lens_ref.shape[0] - 1
+    live = tile_rows * lax.axis_size("row") - lens_ref[live]
+    lane = lanes_of((side, width))
+    place = lax.broadcasted_iota(jnp.int32, (side, width), 0)
+    keep = [place + (col ^ dx) * side < live for dx in (0, 1)]
+    picks = [((lane < side) & keep[dx], (lane >= side) & keep[dx]) for dx in (0, 1)]
     for m in range(half):
         at = slice(m * tile_rows, (m + 1) * tile_rows)
         product = 0.0
@@ -144,7 +165,7 @@
             for dx in (0, 1):
                 block = rights[dk, m, pl.ds(pl.multiple_of((col ^ dx) * side, side), side), :]
                 block = block.astype(jnp.float32)
-                pieces += [jnp.where(low, block, 0.0), jnp.where(low, 0.0, block)]
+                pieces += [jnp.where(pick, block, 0.0) for pick in picks[dx]]
             right = jnp.concatenate(pieces, 0).astype(jnp.bfloat16)
             product = product + nt_dot(left, right)
         product = product.astype(jnp.bfloat16)
@@ -156,10 +177,11 @@
 
 
 def finish_kernel(lens_ref, x_ref, gate_ref, bins_ref, ow_ref, dw_ref, *refs):
-    parts, (out_ref, loss_ref, held, wide) = refs[:OWNERS], refs[OWNERS:]
-    tile_rows, tile_cols, channels = x_ref.shape
+    parts, (out_ref, loss_ref, held) = refs[:OWNERS], refs[OWNERS:]
+    channels = x_ref.shape[0]
     size, width = parts[0].shape
-    half = size // tile_rows
+    half = channels // 2 // OWNERS
+    tile_rows, tile_cols = size // half, width // 2
     packed = OWNERS * half
     owner = owner_place()
     total = jnp.zeros((tile_rows, width), jnp.float32)
@@ -174,30 +196,26 @@
         total = total + centred * centred
     spread = (total + pltpu.roll(total, tile_cols, 1)) * (1.0 / channels)
     scale = lax.rsqrt(spread + 1e-05)
-    for om in range(packed):
-        at = slice(om * tile_rows, (om + 1) * tile_rows)
-        held[at] = (held[at] - average) * scale
-    share = channels // OWNERS
-    for o in range(OWNERS):
-        for g in (0, 1):
-            wide[o * half : (o + 1) * half, g * channels : (g + 1) * channels] = ow_ref[
-                o * share + g * half : o * share + (g + 1) * half
-            ]
-    dist = dw_ref[...].astype(jnp.float32).T.astype(jnp.bfloat16)
-    bin_ids = lax.broadcasted_iota(jnp.int32, (dist.shape[0], width), 0)
+    low = lanes_of((packed, width)) < tile_cols
+    bin_ids = lax.broadcasted_iota(jnp.int32, (dw_ref.shape[0], width), 0)
     loss = jnp.zeros((1, width), jnp.float32)
     for first in range(0, tile_rows, 2):
-        updates = []
-        for ii in (first, first + 1):
-            turned = held[pl.ds(ii, packed, stride=tile_rows), :].astype(jnp.bfloat16)
-            both = tn_dot(turned, wide[...])
-            updates.append(both[:tile_cols, :channels] + both[tile_cols:, channels:])
-        update = jnp.concatenate(updates, 0)
-        gate = gate_ref[first * tile_cols : (first + 2) * tile_cols]
-        x = x_ref[first : first + 2].astype(jnp.float32).reshape(2 * tile_cols, channels)
-        pair_out = (x + gate * update).astype(jnp.bfloat16)
-        out_ref[first : first + 2] = pair_out.reshape(2, tile_cols, channels)
-        logits = nt_dot(dist, pair_out)
+        a, b = [
+            (held[pl.ds(ii, packed, stride=tile_rows), :] - average[ii : ii + 1]) * scale[ii : ii + 1]
+            for ii in (first, first + 1)
+        ]
+        normed = jnp.concatenate(
+            [
+                jnp.where(low, a, pltpu.roll(b, tile_cols, 1)),
+                jnp.where(low, pltpu.roll(a, tile_cols, 1), b),
+            ],
+            0,
+        ).astype(jnp.bfloat16)
+        update = jnp.dot(ow_ref[...], normed, preferred_element_type=jnp.float32)
+        at = slice(first * tile_cols, (first + 2) * tile_cols)
+        pair_out = (x_ref[:, at] + gate_ref[:, at] * update).astype(jnp.bfloat16)
+        out_ref[:, at] = pair_out
+        logits = jnp.dot(dw_ref[...], pair_out, preferred_element_type=jnp.float32)
         log_total = jnp.log(jnp.sum(jnp.exp(logits), axis=0, keepdims=True))
         bins = bins_ref[first // 2 : first // 2 + 1]
         picked = jnp.sum(jnp.where(bin_ids == bins, logits, 0.0), axis=0, keepdims=True)
@@ -205,7 +223,14 @@
     live = tile_rows * lax.axis_size("row") - lens_ref[lens_ref.shape[0] - 1]
     count = jnp.full((1, 1), live * live, jnp.int32).astype(jnp.float32)
     loss = jnp.sum(loss, axis=1, keepdims=True) / count
-    loss_ref[...] = jnp.broadcast_to(loss, loss_ref.shape)
+    loss_ref[...] = jnp.broadcast_to(loss[None], loss_ref.shape)
+
+
+def turn_back_kernel(turned_ref, out_ref):
+    tile_rows, tile_cols, channels = out_ref.shape
+    for first in range(0, tile_rows, 2):
+        block = turned_ref[:, first * tile_cols : (first + 2) * tile_cols].astype(jnp.float32).T
+        out_ref[first : first + 2] = block.astype(jnp.bfloat16).reshape(2, tile_cols, channels)
 
 
 def exchange(value, places, mask):
@@ -255,8 +280,7 @@
         right_kernel,
         [struct((size, width), bf16)] * OWNERS,
         [turned, held],
-        [SMEM] + [VMEM] * 3,
-        args=(chain_lengths, normed, right_weight, right_gate_weight),
+        args=(normed, right_weight, right_gate_weight),
         flops=4 * spots * channels * channels,
     )
     far = [exchange(rights[d], places, over_half + over[d]) for d in range(OWNERS)]
@@ -271,39 +295,50 @@
     near = [near[0]] + [exchange(near[d], places, over[d]) for d in range(1, OWNERS)]
     near_over = [exchange(value, places, over_core) for value in [rights[0]] + near[1:]]
     far_over = [exchange(value, places, over_core) for value in far]
-    gate = call(
-        gate_kernel,
-        struct((spots, channels), f32),
-        args=(normed, out_gate_weight),
-        flops=2 * spots * channels * channels,
-    )
     parts = call(
         tri_kernel,
         [struct((size, width), bf16)] * OWNERS,
         [pltpu.VMEM((cols, size // tile_rows, rows * tile_rows, width), bf16)],
-        args=(*near, *far, *near_over, *far_over),
+        [SMEM] + [VMEM] * (4 * OWNERS),
+        args=(chain_lengths, *near, *far, *near_over, *far_over),
         flops=8 * size * 2 * tile_rows * 2 * width,
     )
     parts = [parts[0]] + [exchange(parts[d], places, over[d]) for d in range(1, OWNERS)]
+    gate, x_turned, out_turned, dist_turned = call(
+        gate_kernel,
+        [
+            struct((channels, spots), f32),
+            struct((channels, spots), f32),
+            struct((channels, channels), bf16),
+            struct(dist_weight.shape[::-1], bf16),
+        ],
+        args=(pair_repr, normed, out_gate_weight, out_weight, dist_weight),
+        flops=2 * spots * channels * channels,
+    )
     pair_out, loss = call(
         finish_kernel,
-        [struct(pair_repr.shape, bf16), struct((1, 128), f32)],
-        [held, pltpu.VMEM((channels // 2, 2 * channels), bf16)],
+        [struct((channels, spots), bf16), struct((places // 2, 8, 128), f32)],
+        [held],
         [SMEM] + [VMEM] * 9,
         args=(
             chain_lengths,
-            pair_repr,
+            x_turned,
             gate,
             distance_bins.reshape(tile_rows // 2, width),
-            out_weight,
-            dist_weight,
+            out_turned,
+            dist_turned,
             *parts,
         ),
         flops=6 * spots * channels * channels,
     )
-    for mask in (over_core, over[1], over[2], over_half):
-        loss = loss + exchange(loss, places, mask)
-    return (pair_out, loss[0, :1])
+    pair_out = call(turn_back_kernel, struct(pair_repr.shape, bf16), args=(pair_out,), flops=1 << 26)
+    loss = loss + exchange(loss, places, over_core)
+    chips = [
+        [(place * 2 + core) * cols + col for place in range(rows // 2) for col in range(cols)]
+        for core in (0, 1)
+    ]
+    loss = lax.all_to_all(loss, AXES, 0, 0, axis_index_groups=chips, tiled=True)
+    return (pair_out, jnp.sum(loss, axis=0)[0, :1])
 
 
 def by_all_to_all(

time: 51.1 us -> 50 us (0.978)
  waiting for transfers between devices: 16.4 us -> 15.1 us
  Pallas kernels: 6.65 us -> 6.13 us
    ppermute x22 -> x19, waiting for transfers between devices: 16.4 us -> 9.22 us  [exchange(): return lax.ppermute(value, AXES, [(at, at ^ mask) for at in range(places)])]
    all_to_all x0 -> x1, waiting for transfers between devices: none -> 5.84 us  [by_kernels(): loss = lax.all_to_all(loss, AXES, 0, 0, axis_index_groups=chips, tiled=True)]
    all_to_all x0 -> x1, starting transfers between devices: none -> 4.46 us  [by_kernels(): loss = lax.all_to_all(loss, AXES, 0, 0, axis_index_groups=chips, tiled=True)]
    ppermute x22 -> x19, starting transfers between devices: 24.9 us -> 20.6 us  [exchange(): return lax.ppermute(value, AXES, [(at, at ^ mask) for at in range(places)])]
    pallas_call x6 -> x7, Pallas kernels: 6.65 us -> 6.13 us  [call(): pl.pallas_call(kernel, out_shape=outs, in_specs=specs if specs is not Non...]
    slice x0 -> x1, local copies, waits for them, and re-layouts: none -> 0.51 us  [by_kernels(): return (pair_out, jnp.sum(loss, axis=0)[0, :1])]
  transfers between devices with their start and end apart: 22 -> 20, of which waited for: 11 -> 9; matrix products, arithmetic and copies ran while one was open for 0% -> 0% of each run, Pallas kernels for 3% -> 5%
where the time goes in v5:
time: 50 us; the launch traced here: 49.7 us
  starting transfers between devices  25 us (50%)
  waiting for transfers between devices  15.1 us (30%)
  Pallas kernels  6.13 us (12%)
  local copies, waits for them, and re-layouts  2.11 us (4%)
  between operations  0.76 us (2%)
  other arithmetic  0.63 us (1%)
    ppermute x19, starting transfers between devices, exchange(): return lax.ppermute(value, AXES, [(at, at ^ mask) for at in range(places)])  20.6 us
    ppermute x19, waiting for transfers between devices, exchange(): return lax.ppermute(value, AXES, [(at, at ^ mask) for at in range(places)])  9.22 us
    pallas_call x7, Pallas kernels, call(): pl.pallas_call(kernel, out_shape=outs, in_specs=specs if specs is not Non...  6.13 us
    all_to_all x1, waiting for transfers between devices, by_kernels(): loss = lax.all_to_all(loss, AXES, 0, 0, axis_index_groups=chips, tiled=True)  5.84 us
    all_to_all x1, starting transfers between devices, by_kernels(): loss = lax.all_to_all(loss, AXES, 0, 0, axis_index_groups=chips, tiled=True)  4.46 us
    unnamed x23, local copies, waits for them, and re-layouts  1.53 us
  transfers between devices with their start and end apart: 20, of which 9 were waited for; matrix products, arithmetic and copies ran while one was open for 0% of the time, Pallas kernels for 5%

profile of v5, /device:TPU:0, one launch (start us, length us, event | category | flops | bytes accessed | tf_op | source)
XLA Modules:
  0.0 49.7 jit_solution(4506044278035702484)
XLA Ops:
  0.6 0.0 copy-start
  0.6 0.9 %copy-done = bf16[16,64,128]{2,1,0:T(8,128)(2,1)S(1)} copy-done((bf16[16,64,128]{2,1,0:T(8,128)(2,1)S(1)}, bf16[16,64,128]{2,1,0:T(8,128)(2,1)}, u32[]{:S(2)}) %copy-start) | copy-done | bytes 262168
  1.6 0.4 shard_map.113.normed_ref
  1.9 0.4 copy-done.7
  2.3 0.0 copy-done.8
  2.4 0.6 %shard_map.115 = (bf16[256,128]{1,0:T(8,128)(2,1)S(1)}, bf16[256,128]{1,0:T(8,128)(2,1)S(1)}, bf16[256,128]{1,0:T(8,128)(2,1)S(1)}, bf16[256,128]{1,0:T(8,128)(2,1)S(1)}) custom-call(bf16[1024,128]{1,0:T(8,128)(2,1)S(1)} %shard_map.113.normed_ref, bf16[128,128]{1,0:T(8,128)(2,1)S(1)} %copy-done.7, bf16[128,128]{1,0:T(8,128)(2,1)S(1)} %copy-done.8), custom_call_target="tpu_custom_call" | custom-call | flops 67108864 | bytes 1048576 | tf_op jit(solution)/shard_map/pallas_call | solution.py:241
  2.9 4.1 %collective-permute-start.3 = (bf16[256,128]{1,0:T(8,128)(2,1)S(1)}, bf16[256,128]{1,0:T(8,128)(2,1)S(1)}, u32[]{:S(2)}, u32[]{:S(2)}) collective-permute-start(bf16[256,128]{1,0:T(8,128)(2,1)S(1)} %get-tuple-element.24.refs_0_), channel_id=1, source_target_pairs={{0,8},{1,9},{2,10},{3,11},{4,12},{5,13},{6,14},{7,15},{8,0},{9,1},... | collective-permute-start | bytes 196616 | tf_op jit(solution)/shard_map/ppermute | solution.py:237
  7.0 1.3 %collective-permute-start.4 = (bf16[256,128]{1,0:T(8,128)(2,1)S(1)}, bf16[256,128]{1,0:T(8,128)(2,1)S(1)}, u32[]{:S(2)}, u32[]{:S(2)}) collective-permute-start(bf16[256,128]{1,0:T(8,128)(2,1)S(1)} %get-tuple-element.25.refs_1_), channel_id=1, source_target_pairs={{0,9},{1,8},{2,11},{3,10},{4,13},{5,12},{6,15},{7,14},{8,1},{9,0},... | collective-permute-start | bytes 196616 | tf_op jit(solution)/shard_map/ppermute | solution.py:237
  8.3 3.6 %collective-permute-start.5 = (bf16[256,128]{1,0:T(8,128)(2,1)S(1)}, bf16[256,128]{1,0:T(8,128)(2,1)S(1)}, u32[]{:S(2)}, u32[]{:S(2)}) collective-permute-start(bf16[256,128]{1,0:T(8,128)(2,1)S(1)} %get-tuple-element.26.refs_2_), channel_id=1, source_target_pairs={{0,12},{1,13},{2,14},{3,15},{4,8},{5,9},{6,10},{7,11},{8,4},{9,5},... | collective-permute-start | bytes 196616 | tf_op jit(solution)/shard_map/ppermute | solution.py:237
  11.9 0.0 copy-done.4
  11.9 0.0 copy-done.5
  11.9 0.0 copy-done.6
  11.9 1.1 %shard_map.116 = (bf16[512,128]{1,0:T(8,128)(2,1)S(1)}, bf16[512,128]{1,0:T(8,128)(2,1)S(1)}, bf16[512,128]{1,0:T(8,128)(2,1)S(1)}, bf16[512,128]{1,0:T(8,128)(2,1)S(1)}) custom-call(s32[5]{0:T(128)S(1)} %copy-done.6, bf16[1024,128]{1,0:T(8,128)(2,1)S(1)} %shard_map.113.normed_ref, bf16[128,128]{1,0:T(8,128)(2,1)S(1)} %copy-done.4, ...), custom_call_target="tpu_custom_call" | custom-call | flops 67108864 | bytes 1048576 | tf_op jit(solution)/shard_map/pallas_call | solution.py:241
  13.0 0.1 collective-permute-start.2
  13.1 1.0 %collective-permute-start = (bf16[512,128]{1,0:T(8,128)(2,1)S(1)}, bf16[512,128]{1,0:T(8,128)(2,1)S(1)}, u32[]{:S(2)}, u32[]{:S(2)}) collective-permute-start(bf16[512,128]{1,0:T(8,128)(2,1)S(1)} %get-tuple-element.29), channel_id=1, source_target_pairs={{0,1},{1,0},{2,3},{3,2},{4,5},{5,4},{6,7},{7,6},{8,9},{9,8},{10,11... | collective-permute-start | bytes 393224 | tf_op jit(solution)/shard_map/ppermute | solution.py:237
  14.1 0.0 collective-permute-done.3.refs_4_
  14.1 2.5 %collective-permute-start.1 = (bf16[512,128]{1,0:T(8,128)(2,1)S(1)}, bf16[512,128]{1,0:T(8,128)(2,1)S(1)}, u32[]{:S(2)}, u32[]{:S(2)}) collective-permute-start(bf16[512,128]{1,0:T(8,128)(2,1)S(1)} %get-tuple-element.30), channel_id=1, source_target_pairs={{0,4},{1,5},{2,6},{3,7},{4,0},{5,1},{6,2},{7,3},{8,12},{9,13},{10,... | collective-permute-start | bytes 393224 | tf_op jit(solution)/shard_map/ppermute | solution.py:237
  16.6 0.0 collective-permute-done.4.refs_5_
  16.6 2.9 %collective-permute-start.6 = (bf16[256,128]{1,0:T(8,128)(2,1)S(1)}, bf16[256,128]{1,0:T(8,128)(2,1)S(1)}, u32[]{:S(2)}, u32[]{:S(2)}) collective-permute-start(bf16[256,128]{1,0:T(8,128)(2,1)S(1)} %get-tuple-element.27.refs_3_), channel_id=1, source_target_pairs={{0,13},{1,12},{2,15},{3,14},{4,9},{5,8},{6,11},{7,10},{8,5},{9,4},... | collective-permute-start | bytes 196616 | tf_op jit(solution)/shard_map/ppermute | solution.py:237
  19.5 0.0 collective-permute-done.5.refs_6_
  19.5 0.0 collective-permute-start.7
  19.5 4.1 %collective-permute-done.6.refs_7_ = bf16[256,128]{1,0:T(8,128)(2,1)S(1)} collective-permute-done((bf16[256,128]{1,0:T(8,128)(2,1)S(1)}, bf16[256,128]{1,0:T(8,128)(2,1)S(1)}, u32[]{:S(2)}, u32[]{:S(2)}) %collective-permute-start.6) | collective-permute-done | bytes 65568 | tf_op jit(solution)/shard_map/ppermute | solution.py:237
  23.6 0.0 collective-permute-start.11
  23.6 0.0 collective-permute-done.7.refs_8_
  23.6 0.5 %collective-permute-start.12 = (bf16[256,128]{1,0:T(8,128)(2,1)S(1)}, bf16[256,128]{1,0:T(8,128)(2,1)S(1)}, u32[]{:S(2)}, u32[]{:S(2)}) collective-permute-start(bf16[256,128]{1,0:T(8,128)(2,1)S(1)} %collective-permute-done.4.refs_5_), channel_id=1, source_target_pairs={{0,2},{1,3},{2,0},{3,1},{4,6},{5,7},{6,4},{7,5},{8,10},{9,11},{10,... | collective-permute-start | bytes 196616 | tf_op jit(solution)/shard_map/ppermute | solution.py:237
  24.1 0.0 collective-permute-done.2.refs_3_
  24.1 0.1 collective-permute-start.10
  24.2 0.0 collective-permute-done.refs_1_
  24.2 0.4 collective-permute-start.8
  24.6 0.0 collective-permute-done.1.refs_2_
  24.6 0.1 collective-permute-start.9
  24.7 0.1 collective-permute-done.11.refs_12_
  24.8 0.3 collective-permute-start.13
  25.1 0.0 collective-permute-done.12.refs_13_
  25.1 0.2 collective-permute-start.14
  25.3 0.7 %collective-permute-done.13.refs_14_ = bf16[256,128]{1,0:T(8,128)(2,1)S(1)} collective-permute-done((bf16[256,128]{1,0:T(8,128)(2,1)S(1)}, bf16[256,128]{1,0:T(8,128)(2,1)S(1)}, u32[]{:S(2)}, u32[]{:S(2)}) %collective-permute-start.13) | collective-permute-done | bytes 65568 | tf_op jit(solution)/shard_map/ppermute | solution.py:237
  26.1 0.3 collective-permute-done.14.refs_15_
  26.4 0.0 collective-permute-done.10.refs_11_
  26.4 0.0 collective-permute-done.8.refs_9_
  26.4 0.0 collective-permute-done.9.refs_10_
  26.4 0.0 copy-start.9
  26.4 0.0 copy-start.10
  26.4 0.0 copy-start.1
  26.4 1.5 %shard_map.117 = (bf16[256,128]{1,0:T(8,128)(2,1)S(1)}, bf16[256,128]{1,0:T(8,128)(2,1)S(1)}, bf16[256,128]{1,0:T(8,128)(2,1)S(1)}, bf16[256,128]{1,0:T(8,128)(2,1)S(1)}) custom-call(s32[5]{0:T(128)S(1)} %copy-done.6, bf16[512,128]{1,0:T(8,128)(2,1)S(1)} %get-tuple-element.28.refs_0_, bf16[512,128]{1,0:T(8,128)(2,1)S(1)} %collective-permute-done.refs_1_, ...), custom_call_target="tpu_custom_call" | custom-call | flops 16777216 | bytes 1048576 | tf_op jit(solution)/shard_map/pallas_call | solution.py:241
  27.9 0.0 copy-start.3
  27.9 0.0 copy-start.2
  27.9 0.9 %collective-permute-start.15 = (bf16[256,128]{1,0:T(8,128)(2,1)S(1)}, bf16[256,128]{1,0:T(8,128)(2,1)S(1)}, u32[]{:S(2)}, u32[]{:S(2)}) collective-permute-start(bf16[256,128]{1,0:T(8,128)(2,1)S(1)} %get-tuple-element.33), channel_id=1, source_target_pairs={{0,1},{1,0},{2,3},{3,2},{4,5},{5,4},{6,7},{7,6},{8,9},{9,8},{10,11... | collective-permute-start | bytes 196616 | tf_op jit(solution)/shard_map/ppermute | solution.py:237
  28.8 0.0 collective-permute-start.16
  28.8 2.7 %collective-permute-start.17 = (bf16[256,128]{1,0:T(8,128)(2,1)S(1)}, bf16[256,128]{1,0:T(8,128)(2,1)S(1)}, u32[]{:S(2)}, u32[]{:S(2)}) collective-permute-start(bf16[256,128]{1,0:T(8,128)(2,1)S(1)} %get-tuple-element.35), channel_id=1, source_target_pairs={{0,5},{1,4},{2,7},{3,6},{4,1},{5,0},{6,3},{7,2},{8,13},{9,12},{10,... | collective-permute-start | bytes 196616 | tf_op jit(solution)/shard_map/ppermute | solution.py:237
  31.5 0.1 copy.12.dw_ref
  31.6 0.1 reshape.7.bins_ref
  31.7 0.0 copy-done.1
  31.7 0.4 shard_map.114
  32.1 0.2 collective-permute-done.15.refs_1_
  32.3 1.2 %collective-permute-done.16.refs_2_ = bf16[256,128]{1,0:T(8,128)(2,1)S(1)} collective-permute-done((bf16[256,128]{1,0:T(8,128)(2,1)S(1)}, bf16[256,128]{1,0:T(8,128)(2,1)S(1)}, u32[]{:S(2)}, u32[]{:S(2)}) %collective-permute-start.16) | collective-permute-done | bytes 65568 | tf_op jit(solution)/shard_map/ppermute | solution.py:237
  33.4 1.4 %collective-permute-done.17.refs_3_ = bf16[256,128]{1,0:T(8,128)(2,1)S(1)} collective-permute-done((bf16[256,128]{1,0:T(8,128)(2,1)S(1)}, bf16[256,128]{1,0:T(8,128)(2,1)S(1)}, u32[]{:S(2)}, u32[]{:S(2)}) %collective-permute-start.17) | collective-permute-done | bytes 65568 | tf_op jit(solution)/shard_map/ppermute | solution.py:237
  34.8 1.4 %shard_map.118 = (bf16[128,1024]{1,0:T(8,128)(2,1)S(1)}, f32[8,8,128]{2,1,0:T(8,128)S(1)}) custom-call(s32[5]{0:T(128)S(1)} %copy-done.6, f32[128,1024]{1,0:T(8,128)S(1)} %get-tuple-element.20.x_ref, f32[128,1024]{1,0:T(8,128)S(1)} %get-tuple-element.21.gate_ref, s32[8,128]{1,0:T(8,128)S(1)} %reshape.7.bins_ref, ...), custom_call_target="tpu_custom_call" | custom-call | flops 100663296 | bytes 1048576 | tf_op jit(solution)/shard_map/pallas_call | solution.py:241
  36.2 0.0 collective-permute-start.18
  36.2 1.2 %collective-permute-done.18 = f32[8,8,128]{2,1,0:T(8,128)S(1)} collective-permute-done((f32[8,8,128]{2,1,0:T(8,128)S(1)}, f32[8,8,128]{2,1,0:T(8,128)S(1)}, u32[]{:S(2)}, u32[]{:S(2)}) %collective-permute-start.18) | collective-permute-done | bytes 32800 | tf_op jit(solution)/shard_map/ppermute | solution.py:237
  37.5 0.6 %add.3 = f32[8,8,128]{2,1,0:T(8,128)} add(f32[8,8,128]{2,1,0:T(8,128)S(1)} %get-tuple-element.37, f32[8,8,128]{2,1,0:T(8,128)S(1)} %collective-permute-done.18) | non-fusion elementwise | flops 8192 | bytes 98304 | tf_op jit(solution)/shard_map/add | solution.py:335
  38.1 4.5 %all-to-all-start = ((f32[8,8,128]{2,1,0:T(8,128)}), f32[8,8,128]{2,1,0:T(8,128)S(1)}, u32[]{:S(2)}, u32[]{:S(2)}) async-start(f32[8,8,128]{2,1,0:T(8,128)} %add.3), calls=%async_computation | async-start | bytes 65536 | tf_op jit(solution)/shard_map/all_to_all | solution.py:340
  42.5 0.8 %shard_map.119 = bf16[16,64,128]{2,1,0:T(8,128)(2,1)} custom-call(bf16[128,1024]{1,0:T(8,128)(2,1)S(1)} %get-tuple-element.36.turned_ref), custom_call_target="tpu_custom_call" | custom-call | flops 67108864 | bytes 1048576 | tf_op jit(solution)/shard_map/pallas_call | solution.py:241
  43.4 5.8 %all-to-all-done = f32[8,8,128]{2,1,0:T(8,128)S(1)} async-done(((f32[8,8,128]{2,1,0:T(8,128)}), f32[8,8,128]{2,1,0:T(8,128)S(1)}, u32[]{:S(2)}, u32[]{:S(2)}) %all-to-all-start) | async-done | bytes 32800 | tf_op jit(solution)/shard_map/all_to_all | solution.py:340
  49.2 0.5 %slice.3 = f32[1,1]{1,0:T(1,128)} slice(f32[8,128]{1,0:T(8,128)S(1)} %reduce_sum.9), slice={[0:1], [0:1]} | slice | bytes 8 | tf_op jit(solution)/shard_map/slice | solution.py:341
  (10 shorter events, 0.0 us)
Async XLA Ops:
  0.6 1.0 %copy-start = (bf16[16,64,128]{2,1,0:T(8,128)(2,1)S(1)}, bf16[16,64,128]{2,1,0:T(8,128)(2,1)}, u32[]{:S(2)}) copy-start(bf16[16,64,128]{2,1,0:T(8,128)(2,1)} %x_ref.3) | copy-start | bytes 786436
  1.6 0.8 %copy-start.7 = (bf16[128,128]{1,0:T(8,128)(2,1)S(1)}, bf16[128,128]{1,0:T(8,128)(2,1)}, u32[]{:S(2)}) copy-start(bf16[128,128]{1,0:T(8,128)(2,1)} %w_ref.2) | copy-start | bytes 98308
  1.6 0.8 %copy-start.8 = (bf16[128,128]{1,0:T(8,128)(2,1)S(1)}, bf16[128,128]{1,0:T(8,128)(2,1)}, u32[]{:S(2)}) copy-start(bf16[128,128]{1,0:T(8,128)(2,1)} %g_ref.2) | copy-start | bytes 98308
  2.4 9.5 %copy-start.4 = (bf16[128,128]{1,0:T(8,128)(2,1)S(1)}, bf16[128,128]{1,0:T(8,128)(2,1)}, u32[]{:S(2)}) copy-start(bf16[128,128]{1,0:T(8,128)(2,1)} %w_ref.3) | copy-start | bytes 98308
  2.4 9.5 %copy-start.5 = (bf16[128,128]{1,0:T(8,128)(2,1)S(1)}, bf16[128,128]{1,0:T(8,128)(2,1)}, u32[]{:S(2)}) copy-start(bf16[128,128]{1,0:T(8,128)(2,1)} %g_ref.3) | copy-start | bytes 98308
  2.9 11.2 %collective-permute-start.3 = (bf16[256,128]{1,0:T(8,128)(2,1)S(1)}, bf16[256,128]{1,0:T(8,128)(2,1)S(1)}, u32[]{:S(2)}, u32[]{:S(2)}) collective-permute-start(bf16[256,128]{1,0:T(8,128)(2,1)S(1)} %get-tuple-element.24.refs_0_), channel_id=1, source_target_pairs={{0,8},{1,9},{2,10},{3,11},{4,12},{5,13},{6,14},{7,15},{8,0},{9,1},... | collective-permute-start | bytes 196616 | tf_op jit(solution)/shard_map/ppermute | solution.py:237
  7.0 9.6 %collective-permute-start.4 = (bf16[256,128]{1,0:T(8,128)(2,1)S(1)}, bf16[256,128]{1,0:T(8,128)(2,1)S(1)}, u32[]{:S(2)}, u32[]{:S(2)}) collective-permute-start(bf16[256,128]{1,0:T(8,128)(2,1)S(1)} %get-tuple-element.25.refs_1_), channel_id=1, source_target_pairs={{0,9},{1,8},{2,11},{3,10},{4,13},{5,12},{6,15},{7,14},{8,1},{9,0},... | collective-permute-start | bytes 196616 | tf_op jit(solution)/shard_map/ppermute | solution.py:237
  8.3 3.6 %copy-start.6 = (s32[5]{0:T(128)S(1)}, s32[5]{0:T(128)}, u32[]{:S(2)}) copy-start(s32[5]{0:T(128)} %lens_ref.5) | copy-start | bytes 64
  8.3 11.2 %collective-permute-start.5 = (bf16[256,128]{1,0:T(8,128)(2,1)S(1)}, bf16[256,128]{1,0:T(8,128)(2,1)S(1)}, u32[]{:S(2)}, u32[]{:S(2)}) collective-permute-start(bf16[256,128]{1,0:T(8,128)(2,1)S(1)} %get-tuple-element.26.refs_2_), channel_id=1, source_target_pairs={{0,12},{1,13},{2,14},{3,15},{4,8},{5,9},{6,10},{7,11},{8,4},{9,5},... | collective-permute-start | bytes 196616 | tf_op jit(solution)/shard_map/ppermute | solution.py:237
  13.0 11.0 %collective-permute-start.2 = (bf16[512,128]{1,0:T(8,128)(2,1)S(1)}, bf16[512,128]{1,0:T(8,128)(2,1)S(1)}, u32[]{:S(2)}, u32[]{:S(2)}) collective-permute-start(bf16[512,128]{1,0:T(8,128)(2,1)S(1)} %get-tuple-element.31), channel_id=1, source_target_pairs={{0,5},{1,4},{2,7},{3,6},{4,1},{5,0},{6,3},{7,2},{8,13},{9,12},{10,... | collective-permute-start | bytes 393224 | tf_op jit(solution)/shard_map/ppermute | solution.py:237
  13.1 11.0 %collective-permute-start = (bf16[512,128]{1,0:T(8,128)(2,1)S(1)}, bf16[512,128]{1,0:T(8,128)(2,1)S(1)}, u32[]{:S(2)}, u32[]{:S(2)}) collective-permute-start(bf16[512,128]{1,0:T(8,128)(2,1)S(1)} %get-tuple-element.29), channel_id=1, source_target_pairs={{0,1},{1,0},{2,3},{3,2},{4,5},{5,4},{6,7},{7,6},{8,9},{9,8},{10,11... | collective-permute-start | bytes 393224 | tf_op jit(solution)/shard_map/ppermute | solution.py:237
  14.1 10.5 %collective-permute-start.1 = (bf16[512,128]{1,0:T(8,128)(2,1)S(1)}, bf16[512,128]{1,0:T(8,128)(2,1)S(1)}, u32[]{:S(2)}, u32[]{:S(2)}) collective-permute-start(bf16[512,128]{1,0:T(8,128)(2,1)S(1)} %get-tuple-element.30), channel_id=1, source_target_pairs={{0,4},{1,5},{2,6},{3,7},{4,0},{5,1},{6,2},{7,3},{8,12},{9,13},{10,... | collective-permute-start | bytes 393224 | tf_op jit(solution)/shard_map/ppermute | solution.py:237
  16.6 7.0 %collective-permute-start.6 = (bf16[256,128]{1,0:T(8,128)(2,1)S(1)}, bf16[256,128]{1,0:T(8,128)(2,1)S(1)}, u32[]{:S(2)}, u32[]{:S(2)}) collective-permute-start(bf16[256,128]{1,0:T(8,128)(2,1)S(1)} %get-tuple-element.27.refs_3_), channel_id=1, source_target_pairs={{0,13},{1,12},{2,15},{3,14},{4,9},{5,8},{6,11},{7,10},{8,5},{9,4},... | collective-permute-start | bytes 196616 | tf_op jit(solution)/shard_map/ppermute | solution.py:237
  19.5 4.1 %collective-permute-start.7 = (bf16[256,128]{1,0:T(8,128)(2,1)S(1)}, bf16[256,128]{1,0:T(8,128)(2,1)S(1)}, u32[]{:S(2)}, u32[]{:S(2)}) collective-permute-start(bf16[256,128]{1,0:T(8,128)(2,1)S(1)} %get-tuple-element.24.refs_0_), channel_id=1, source_target_pairs={{0,2},{1,3},{2,0},{3,1},{4,6},{5,7},{6,4},{7,5},{8,10},{9,11},{10,... | collective-permute-start | bytes 196616 | tf_op jit(solution)/shard_map/ppermute | solution.py:237
  23.6 1.3 %collective-permute-start.11 = (bf16[256,128]{1,0:T(8,128)(2,1)S(1)}, bf16[256,128]{1,0:T(8,128)(2,1)S(1)}, u32[]{:S(2)}, u32[]{:S(2)}) collective-permute-start(bf16[256,128]{1,0:T(8,128)(2,1)S(1)} %collective-permute-done.3.refs_4_), channel_id=1, source_target_pairs={{0,2},{1,3},{2,0},{3,1},{4,6},{5,7},{6,4},{7,5},{8,10},{9,11},{10,... | collective-permute-start | bytes 196616 | tf_op jit(solution)/shard_map/ppermute | solution.py:237
  23.6 1.5 %collective-permute-start.12 = (bf16[256,128]{1,0:T(8,128)(2,1)S(1)}, bf16[256,128]{1,0:T(8,128)(2,1)S(1)}, u32[]{:S(2)}, u32[]{:S(2)}) collective-permute-start(bf16[256,128]{1,0:T(8,128)(2,1)S(1)} %collective-permute-done.4.refs_5_), channel_id=1, source_target_pairs={{0,2},{1,3},{2,0},{3,1},{4,6},{5,7},{6,4},{7,5},{8,10},{9,11},{10,... | collective-permute-start | bytes 196616 | tf_op jit(solution)/shard_map/ppermute | solution.py:237
  24.1 2.3 %collective-permute-start.10 = (bf16[512,128]{1,0:T(8,128)(2,1)S(1)}, bf16[512,128]{1,0:T(8,128)(2,1)S(1)}, u32[]{:S(2)}, u32[]{:S(2)}) collective-permute-start(bf16[512,128]{1,0:T(8,128)(2,1)S(1)} %collective-permute-done.2.refs_3_), channel_id=1, source_target_pairs={{0,2},{1,3},{2,0},{3,1},{4,6},{5,7},{6,4},{7,5},{8,10},{9,11},{10,... | collective-permute-start | bytes 393224 | tf_op jit(solution)/shard_map/ppermute | solution.py:237
  24.2 2.2 %collective-permute-start.8 = (bf16[512,128]{1,0:T(8,128)(2,1)S(1)}, bf16[512,128]{1,0:T(8,128)(2,1)S(1)}, u32[]{:S(2)}, u32[]{:S(2)}) collective-permute-start(bf16[512,128]{1,0:T(8,128)(2,1)S(1)} %collective-permute-done.refs_1_), channel_id=1, source_target_pairs={{0,2},{1,3},{2,0},{3,1},{4,6},{5,7},{6,4},{7,5},{8,10},{9,11},{10,... | collective-permute-start | bytes 393224 | tf_op jit(solution)/shard_map/ppermute | solution.py:237
  24.6 1.8 %collective-permute-start.9 = (bf16[512,128]{1,0:T(8,128)(2,1)S(1)}, bf16[512,128]{1,0:T(8,128)(2,1)S(1)}, u32[]{:S(2)}, u32[]{:S(2)}) collective-permute-start(bf16[512,128]{1,0:T(8,128)(2,1)S(1)} %collective-permute-done.1.refs_2_), channel_id=1, source_target_pairs={{0,2},{1,3},{2,0},{3,1},{4,6},{5,7},{6,4},{7,5},{8,10},{9,11},{10,... | collective-permute-start | bytes 393224 | tf_op jit(solution)/shard_map/ppermute | solution.py:237
  24.8 1.3 %collective-permute-start.13 = (bf16[256,128]{1,0:T(8,128)(2,1)S(1)}, bf16[256,128]{1,0:T(8,128)(2,1)S(1)}, u32[]{:S(2)}, u32[]{:S(2)}) collective-permute-start(bf16[256,128]{1,0:T(8,128)(2,1)S(1)} %collective-permute-done.5.refs_6_), channel_id=1, source_target_pairs={{0,2},{1,3},{2,0},{3,1},{4,6},{5,7},{6,4},{7,5},{8,10},{9,11},{10,... | collective-permute-start | bytes 196616 | tf_op jit(solution)/shard_map/ppermute | solution.py:237
  25.1 1.3 %collective-permute-start.14 = (bf16[256,128]{1,0:T(8,128)(2,1)S(1)}, bf16[256,128]{1,0:T(8,128)(2,1)S(1)}, u32[]{:S(2)}, u32[]{:S(2)}) collective-permute-start(bf16[256,128]{1,0:T(8,128)(2,1)S(1)} %collective-permute-done.6.refs_7_), channel_id=1, source_target_pairs={{0,2},{1,3},{2,0},{3,1},{4,6},{5,7},{6,4},{7,5},{8,10},{9,11},{10,... | collective-permute-start | bytes 196616 | tf_op jit(solution)/shard_map/ppermute | solution.py:237
  26.4 5.1 %copy-start.9 = (bf16[128,64]{0,1:T(8,128)(2,1)S(1)}, bf16[128,64]{0,1:T(8,128)(2,1)}, u32[]{:S(2)}) copy-start(bf16[128,64]{0,1:T(8,128)(2,1)} %param.19) | copy-start | bytes 49156
  26.4 5.2 %copy-start.10 = (s32[16,64]{1,0:T(8,128)S(1)}, s32[16,64]{1,0:T(8,128)}, u32[]{:S(2)}) copy-start(s32[16,64]{1,0:T(8,128)} %param.11) | copy-start | bytes 12292
  26.4 5.3 %copy-start.1 = (bf16[16,64,128]{2,1,0:T(8,128)(2,1)S(1)}, bf16[16,64,128]{2,1,0:T(8,128)(2,1)}, u32[]{:S(2)}) copy-start(bf16[16,64,128]{2,1,0:T(8,128)(2,1)} %x_ref.3) | copy-start | bytes 786436
  27.9 3.8 %copy-start.3 = (bf16[128,128]{1,0:T(8,128)(2,1)S(1)}, bf16[128,128]{1,0:T(8,128)(2,1)}, u32[]{:S(2)}) copy-start(bf16[128,128]{1,0:T(8,128)(2,1)} %ow_ref.1) | copy-start | bytes 98308
  27.9 3.8 %copy-start.2 = (bf16[128,128]{1,0:T(8,128)(2,1)S(1)}, bf16[128,128]{1,0:T(8,128)(2,1)}, u32[]{:S(2)}) copy-start(bf16[128,128]{1,0:T(8,128)(2,1)} %gw_ref.1) | copy-start | bytes 98308
  27.9 4.3 %collective-permute-start.15 = (bf16[256,128]{1,0:T(8,128)(2,1)S(1)}, bf16[256,128]{1,0:T(8,128)(2,1)S(1)}, u32[]{:S(2)}, u32[]{:S(2)}) collective-permute-start(bf16[256,128]{1,0:T(8,128)(2,1)S(1)} %get-tuple-element.33), channel_id=1, source_target_pairs={{0,1},{1,0},{2,3},{3,2},{4,5},{5,4},{6,7},{7,6},{8,9},{9,8},{10,11... | collective-permute-start | bytes 196616 | tf_op jit(solution)/shard_map/ppermute | solution.py:237
  28.8 4.6 %collective-permute-start.16 = (bf16[256,128]{1,0:T(8,128)(2,1)S(1)}, bf16[256,128]{1,0:T(8,128)(2,1)S(1)}, u32[]{:S(2)}, u32[]{:S(2)}) collective-permute-start(bf16[256,128]{1,0:T(8,128)(2,1)S(1)} %get-tuple-element.34), channel_id=1, source_target_pairs={{0,4},{1,5},{2,6},{3,7},{4,0},{5,1},{6,2},{7,3},{8,12},{9,13},{10,... | collective-permute-start | bytes 196616 | tf_op jit(solution)/shard_map/ppermute | solution.py:237
  28.8 6.0 %collective-permute-start.17 = (bf16[256,128]{1,0:T(8,128)(2,1)S(1)}, bf16[256,128]{1,0:T(8,128)(2,1)S(1)}, u32[]{:S(2)}, u32[]{:S(2)}) collective-permute-start(bf16[256,128]{1,0:T(8,128)(2,1)S(1)} %get-tuple-element.35), channel_id=1, source_target_pairs={{0,5},{1,4},{2,7},{3,6},{4,1},{5,0},{6,3},{7,2},{8,13},{9,12},{10,... | collective-permute-start | bytes 196616 | tf_op jit(solution)/shard_map/ppermute | solution.py:237
  36.2 1.2 %collective-permute-start.18 = (f32[8,8,128]{2,1,0:T(8,128)S(1)}, f32[8,8,128]{2,1,0:T(8,128)S(1)}, u32[]{:S(2)}, u32[]{:S(2)}) collective-permute-start(f32[8,8,128]{2,1,0:T(8,128)S(1)} %get-tuple-element.37), channel_id=1, source_target_pairs={{0,2},{1,3},{2,0},{3,1},{4,6},{5,7},{6,4},{7,5},{8,10},{9,11},{10,... | collective-permute-start | bytes 98312 | tf_op jit(solution)/shard_map/ppermute | solution.py:237
  38.1 11.2 %all-to-all-start = ((f32[8,8,128]{2,1,0:T(8,128)}), f32[8,8,128]{2,1,0:T(8,128)S(1)}, u32[]{:S(2)}, u32[]{:S(2)}) async-start(f32[8,8,128]{2,1,0:T(8,128)} %add.3), calls=%async_computation | async-start | bytes 65536 | tf_op jit(solution)/shard_map/all_to_all | solution.py:340

commit v6 on v5

--- a/solution.py
+++ b/solution.py
@@ -35,12 +35,19 @@
     return lax.broadcasted_iota(jnp.int32, shape, 1)
 
 
-def pair_mask(lens_ref, tile_rows, tile_cols, first):
+def make_masks(lens_ref, tile_rows, tile_cols):
     live = tile_rows * lax.axis_size("row") - lens_ref[lens_ref.shape[0] - 1]
     lane = lanes_of((1, 2 * tile_cols))
-    row = lax.axis_index("row") * tile_rows + first + (lane >= tile_cols).astype(jnp.int32)
-    col = lax.axis_index("col") * tile_cols + lane % tile_cols
-    return ((row < live) & (col < live)).astype(jnp.float32)
+    upper = (lane >= tile_cols).astype(jnp.int32)
+    place = lane - tile_cols * upper
+    row, col = lax.axis_index("row") * tile_rows, lax.axis_index("col")
+    keeps = [(place + (col ^ dx) * tile_cols < live).astype(jnp.float32) for dx in (0, 1)]
+    pairs = [
+        (row + first + upper < live).astype(jnp.float32) * keeps[0]
+        for first in range(0, tile_rows, 2)
+    ]
+    count = jnp.full(lane.shape, live * live, jnp.int32).astype(jnp.float32)
+    return pairs, keeps, 1.0 / count
 
 
 def turn(w_refs, turned):
@@ -55,23 +62,28 @@
         turned[at * channels : (at + 1) * channels] = jnp.concatenate(blocks, 0).astype(jnp.bfloat16)
 
 
-def project(normed, turned, held, first, tile_rows, tile_cols, mask=None):
-    channels = normed.shape[1]
+def project(normed_ref, w_ref, g_ref, turned, held, masks=None):
+    channels = normed_ref.shape[1]
     packed = channels // 2
-    flat = nt_dot(turned[...], normed)
-    value = sigmoid(flat[channels:]) * flat[:channels]
-    if mask is not None:
-        value = value * mask
-    a, b = value[:packed], value[packed:]
+    tile_rows, tile_cols = held.shape[0] // packed, held.shape[1] // 2
+    turn((w_ref, g_ref), turned)
     low = lanes_of((packed, 2 * tile_cols)) < tile_cols
-    held[pl.ds(first, packed, stride=tile_rows), :] = jnp.where(low, a, pltpu.roll(b, tile_cols, 1))
-    held[pl.ds(first + 1, packed, stride=tile_rows), :] = jnp.where(
-        low, pltpu.roll(a, tile_cols, 1), b
-    )
+    for first in range(0, tile_rows, 2):
+        flat = nt_dot(turned[...], normed_ref[first * tile_cols : (first + 2) * tile_cols])
+        value = sigmoid(flat[channels:]) * flat[:channels]
+        if masks is not None:
+            value = value * masks[first // 2]
+        a, b = value[:packed], value[packed:]
+        held[pl.ds(first, packed, stride=tile_rows), :] = jnp.where(
+            low, a, pltpu.roll(b, tile_cols, 1)
+        )
+        held[pl.ds(first + 1, packed, stride=tile_rows), :] = jnp.where(
+            low, pltpu.roll(a, tile_cols, 1), b
+        )
 
 
 def owner_place():
-    return lax.axis_index("row") // 2 % 2 * 2 + lax.axis_index("col")
+    return lax.axis_index("row") % OWNERS
 
 
 def owner_block(held, d, size):
@@ -84,30 +96,26 @@
     normed_ref[...] = layer_norm(x, -1).astype(jnp.bfloat16)
 
 
-def project_all(lens_ref, normed_ref, w_ref, g_ref, turned, held):
-    tile_rows = held.shape[0] // turned.shape[1] * 2
-    tile_cols = held.shape[1] // 2
-    turn((w_ref, g_ref), turned)
-    for first in range(0, tile_rows, 2):
-        normed = normed_ref[first * tile_cols : (first + 2) * tile_cols]
-        mask = None if lens_ref is None else pair_mask(lens_ref, tile_rows, tile_cols, first)
-        project(normed, turned, held, first, tile_rows, tile_cols, mask)
-
-
-def right_kernel(normed_ref, w_ref, g_ref, *refs):
-    outs, (turned, held) = refs[:OWNERS], refs[OWNERS:]
-    project_all(None, normed_ref, w_ref, g_ref, turned, held)
-    for d in range(OWNERS):
-        outs[d][...] = owner_block(held, d, outs[d].shape[0])
+def right_kernel(normed_ref, w_ref, g_ref, stay_ref, move_ref, turned, held):
+    project(normed_ref, w_ref, g_ref, turned, held)
+    size = stay_ref.shape[0] // 2
+    for d, ref in enumerate((stay_ref, stay_ref, move_ref, move_ref)):
+        ref[d % 2 * size : (d % 2 + 1) * size] = owner_block(held, d, size)
 
 
 def left_kernel(lens_ref, normed_ref, w_ref, g_ref, *refs):
-    rights, outs, (turned, held) = refs[:OWNERS], refs[OWNERS : 2 * OWNERS], refs[2 * OWNERS :]
-    project_all(lens_ref, normed_ref, w_ref, g_ref, turned, held)
-    size = rights[0].shape[0]
-    for d in range(OWNERS):
-        outs[d][:size] = owner_block(held, d, size)
-        outs[d][size:] = rights[d][...]
+    (stay_ref, move_ref), outs, (masks_ref, turned, held) = refs[:2], refs[2:-3], refs[-3:]
+    tile_rows = held.shape[0] // normed_ref.shape[1] * 2
+    pairs, keeps, share = make_masks(lens_ref, tile_rows, held.shape[1] // 2)
+    project(normed_ref, w_ref, g_ref, turned, held, pairs)
+    masks_ref[...] = jnp.concatenate(
+        pairs + keeps + [share] * (masks_ref.shape[0] - len(pairs) - len(keeps)), 0
+    )
+    size = stay_ref.shape[0] // 2
+    for d, ref in enumerate(outs):
+        right_ref = (stay_ref, move_ref)[d // 2]
+        ref[:size] = owner_block(held, d, size)
+        ref[size:] = right_ref[d % 2 * size : (d % 2 + 1) * size]
 
 
 def gate_kernel(x_ref, normed_ref, gw_ref, ow_ref, dw_ref, gate_ref, x_turned_ref, ow_turned, dw_turned):
@@ -129,64 +137,66 @@
         x_turned_ref[:, at] = x.T
 
 
-def tri_kernel(lens_ref, *refs):
-    near, far = refs[:OWNERS], refs[OWNERS : 2 * OWNERS]
-    near_over, far_over = refs[2 * OWNERS : 3 * OWNERS], refs[3 * OWNERS : 4 * OWNERS]
-    outs, rights = refs[4 * OWNERS : -1], refs[-1]
-    size, width = far[0].shape
-    half = rights.shape[1]
+def tri_kernel(masks_ref, own, core, near, near_over, far, far_over, cross, cross_over, *refs):
+    outs, rights = refs[:-1], refs[-1]
+    half, _, width = rights.shape
+    size = own.shape[0] // 2
     tile_rows = size // half
-    side = width // 2
+    side = OWNERS * tile_rows
     me, col = lax.axis_index("row"), lax.axis_index("col")
-    pieces = []
-    for d in range(OWNERS):
-        away = d // 2 * 2
-        pieces += [(d % 2, away, near[d]), (d % 2, away + 4, far[d])]
-        pieces += [(d % 2, away + 1, near_over[d]), (d % 2, away + 5, far_over[d])]
-    for dk, away, ref in pieces:
-        start = ref.shape[0] - size
+    lefts = (own, core, near, near_over)
+    pieces = (
+        (0, own, size),
+        (1, core, size),
+        (2, near, size),
+        (3, near_over, size),
+        (4, far, 0),
+        (5, far_over, size),
+        (6, cross, 0),
+        (7, cross_over, size),
+    )
+    for away, ref, start in pieces:
         at = pl.multiple_of((me ^ away) * tile_rows, tile_rows)
         for m in range(half):
-            rights[dk, m, pl.ds(at, tile_rows), :] = ref[
+            rights[m, pl.ds(at, tile_rows), :] = ref[
                 start + m * tile_rows : start + (m + 1) * tile_rows
             ]
-    live = lens_ref.shape[0] - 1
-    live = tile_rows * lax.axis_size("row") - lens_ref[live]
-    lane = lanes_of((side, width))
-    place = lax.broadcasted_iota(jnp.int32, (side, width), 0)
-    keep = [place + (col ^ dx) * side < live for dx in (0, 1)]
-    picks = [((lane < side) & keep[dx], (lane >= side) & keep[dx]) for dx in (0, 1)]
+    low = lanes_of((side, width)) < width // 2
+    first = masks_ref.shape[0] // 2
+    keep = jnp.concatenate([masks_ref[first : first + 1], masks_ref[first + 1 : first + 2]], 1)
     for m in range(half):
-        at = slice(m * tile_rows, (m + 1) * tile_rows)
-        product = 0.0
-        for dk in (0, 1):
-            left = jnp.concatenate([near[dk][at], near[2 + dk][at]], 0)
-            pieces = []
+        left = jnp.concatenate(
+            [ref[m * tile_rows : (m + 1) * tile_rows] for ref in lefts], 0
+        )
+        pieces = []
+        for dx in (0, 1):
+            block = rights[m, pl.ds(pl.multiple_of((col ^ dx) * side, side), side), :]
+            block = block.astype(jnp.float32)
+            pieces += [jnp.where(low, block, 0.0), jnp.where(low, 0.0, block)]
+        right = jnp.concatenate(pieces, 0).astype(jnp.bfloat16)
+        product = (nt_dot(left, right) * keep).astype(jnp.bfloat16)
+        for d in range(OWNERS):
             for dx in (0, 1):
-                block = rights[dk, m, pl.ds(pl.multiple_of((col ^ dx) * side, side), side), :]
-                block = block.astype(jnp.float32)
-                pieces += [jnp.where(pick, block, 0.0) for pick in picks[dx]]
-            right = jnp.concatenate(pieces, 0).astype(jnp.bfloat16)
-            product = product + nt_dot(left, right)
-        product = product.astype(jnp.bfloat16)
-        for dz in (0, 1):
-            for dx in (0, 1):
-                outs[2 * dz + dx][at] = product[
-                    dz * tile_rows : (dz + 1) * tile_rows, dx * width : (dx + 1) * width
+                at = d % 2 * size + m * tile_rows
+                outs[d // 2 * 2 + dx][at : at + tile_rows] = product[
+                    d * tile_rows : (d + 1) * tile_rows, dx * width : (dx + 1) * width
                 ]
 
 
-def finish_kernel(lens_ref, x_ref, gate_ref, bins_ref, ow_ref, dw_ref, *refs):
-    parts, (out_ref, loss_ref, held) = refs[:OWNERS], refs[OWNERS:]
+def finish_kernel(masks_ref, x_ref, gate_ref, bins_ref, ow_ref, dw_ref, *refs):
+    parts, overs = refs[:OWNERS], refs[OWNERS : 2 * OWNERS]
+    out_ref, loss_ref, held = refs[2 * OWNERS :]
     channels = x_ref.shape[0]
-    size, width = parts[0].shape
+    size, width = parts[0].shape[0] // 2, parts[0].shape[1]
     half = channels // 2 // OWNERS
     tile_rows, tile_cols = size // half, width // 2
     packed = OWNERS * half
     owner = owner_place()
     total = jnp.zeros((tile_rows, width), jnp.float32)
     for d in range(OWNERS):
-        block = parts[d][...].astype(jnp.float32)
+        refs, at = ((parts, 0), (overs, size))[d % 2]
+        a, b = [refs[d // 2 * 2 + dx][at : at + size].astype(jnp.float32) for dx in (0, 1)]
+        block = a + b
         held[pl.ds(pl.multiple_of((owner ^ d) * size, size), size), :] = block
         total = total + jnp.sum(block.reshape(half, tile_rows, width), 0)
     average = (total + pltpu.roll(total, tile_cols, 1)) * (1.0 / channels)
@@ -219,10 +229,9 @@
         log_total = jnp.log(jnp.sum(jnp.exp(logits), axis=0, keepdims=True))
         bins = bins_ref[first // 2 : first // 2 + 1]
         picked = jnp.sum(jnp.where(bin_ids == bins, logits, 0.0), axis=0, keepdims=True)
-        loss = loss + pair_mask(lens_ref, tile_rows, tile_cols, first) * (log_total - picked)
-    live = tile_rows * lax.axis_size("row") - lens_ref[lens_ref.shape[0] - 1]
-    count = jnp.full((1, 1), live * live, jnp.int32).astype(jnp.float32)
-    loss = jnp.sum(loss, axis=1, keepdims=True) / count
+        loss = loss + masks_ref[first // 2 : first // 2 + 1] * (log_total - picked)
+    last = masks_ref.shape[0] - 1
+    loss = jnp.sum(loss * masks_ref[last : last + 1], axis=1, keepdims=True)
     loss_ref[...] = jnp.broadcast_to(loss[None], loss_ref.shape)
 
 
@@ -271,39 +280,43 @@
     struct = jax.ShapeDtypeStruct
     turned = pltpu.VMEM((2 * channels, channels), bf16)
     held = pltpu.VMEM((OWNERS * size, width), f32)
-    over_core, over_half = cols, 4 * cols
-    over = [0, 1, 2 * cols, 2 * cols + 1]
+    over_x, over_core, over_z, over_half = 1, cols, 2 * cols, OWNERS * cols
     normed = call(
         norm_kernel, struct((spots, channels), bf16), args=(pair_repr,), flops=1 << 30
     )
-    rights = call(
+    stay, move = call(
         right_kernel,
-        [struct((size, width), bf16)] * OWNERS,
+        [struct((2 * size, width), bf16)] * 2,
         [turned, held],
         args=(normed, right_weight, right_gate_weight),
         flops=4 * spots * channels * channels,
     )
-    far = [exchange(rights[d], places, over_half + over[d]) for d in range(OWNERS)]
-    near = call(
+    cross = exchange(move, places, over_half + over_z)
+    far = exchange(stay, places, over_half)
+    own, core, near, near_over, masks = call(
         left_kernel,
-        [struct((2 * size, width), bf16)] * OWNERS,
+        [struct((2 * size, width), bf16)] * OWNERS + [struct((tile_rows, width), f32)],
         [turned, held],
-        [SMEM] + [VMEM] * (3 + OWNERS),
-        args=(chain_lengths, normed, left_weight, left_gate_weight, *rights),
+        [SMEM] + [VMEM] * 5,
+        args=(chain_lengths, normed, left_weight, left_gate_weight, stay, move),
         flops=4 * spots * channels * channels,
     )
-    near = [near[0]] + [exchange(near[d], places, over[d]) for d in range(1, OWNERS)]
-    near_over = [exchange(value, places, over_core) for value in [rights[0]] + near[1:]]
-    far_over = [exchange(value, places, over_core) for value in far]
+    near_over = exchange(near_over, places, over_z + over_core)
+    near = exchange(near, places, over_z)
+    core, far_over, cross_over = [
+        exchange(value, places, over_core) for value in (core, far, cross)
+    ]
     parts = call(
         tri_kernel,
-        [struct((size, width), bf16)] * OWNERS,
-        [pltpu.VMEM((cols, size // tile_rows, rows * tile_rows, width), bf16)],
-        [SMEM] + [VMEM] * (4 * OWNERS),
-        args=(chain_lengths, *near, *far, *near_over, *far_over),
+        [struct((2 * size, width), bf16)] * OWNERS,
+        [pltpu.VMEM((size // tile_rows, rows * tile_rows, width), bf16)],
+        args=(masks, own, core, near, near_over, far, far_over, cross, cross_over),
         flops=8 * size * 2 * tile_rows * 2 * width,
     )
-    parts = [parts[0]] + [exchange(parts[d], places, over[d]) for d in range(1, OWNERS)]
+    parts = [parts[0]] + [
+        exchange(parts[d], places, d // 2 * over_z + d % 2 * over_x) for d in range(1, OWNERS)
+    ]
+    parts += [exchange(value, places, over_core) for value in parts]
     gate, x_turned, out_turned, dist_turned = call(
         gate_kernel,
         [
@@ -317,11 +330,10 @@
     )
     pair_out, loss = call(
         finish_kernel,
-        [struct((channels, spots), bf16), struct((places // 2, 8, 128), f32)],
+        [struct((channels, spots), bf16), struct((places, 8, 128), f32)],
         [held],
-        [SMEM] + [VMEM] * 9,
         args=(
-            chain_lengths,
+            masks,
             x_turned,
             gate,
             distance_bins.reshape(tile_rows // 2, width),
@@ -332,12 +344,7 @@
         flops=6 * spots * channels * channels,
     )
     pair_out = call(turn_back_kernel, struct(pair_repr.shape, bf16), args=(pair_out,), flops=1 << 26)
-    loss = loss + exchange(loss, places, over_core)
-    chips = [
-        [(place * 2 + core) * cols + col for place in range(rows // 2) for col in range(cols)]
-        for core in (0, 1)
-    ]
-    loss = lax.all_to_all(loss, AXES, 0, 0, axis_index_groups=chips, tiled=True)
+    loss = lax.all_to_all(loss, AXES, 0, 0, tiled=True)
     return (pair_out, jnp.sum(loss, axis=0)[0, :1])
 
 
@@ -419,7 +426,7 @@
         and cols == 2
         and tile_rows * rows == tile_cols * cols
         and 2 * tile_cols == 128
-        and tile_rows % 16 == 0
+        and tile_rows == 16
         and channels % (32 * OWNERS) == 0
     )
     return (by_kernels if fits else by_all_to_all)(pair_repr, *others)

time: 50 us -> 48 us (0.960)
  starting transfers between devices: 25 us -> 17.1 us
  waiting for transfers between devices: 15.1 us -> 22.3 us
  Pallas kernels: 6.13 us -> 5.32 us
  other arithmetic: 0.63 us -> 0.02 us
    ppermute x19 -> x14, starting transfers between devices: 20.6 us -> 11.5 us  [exchange(): return lax.ppermute(value, AXES, [(at, at ^ mask) for at in range(places)])]
    ppermute x19 -> x14, waiting for transfers between devices: 9.22 us -> 16.5 us  [exchange(): return lax.ppermute(value, AXES, [(at, at ^ mask) for at in range(places)])]
    all_to_all x1, starting transfers between devices: 4.46 us -> 5.67 us  [by_kernels(): loss = lax.all_to_all(loss, AXES, 0, 0, tiled=True)]
    pallas_call x7, Pallas kernels: 6.13 us -> 5.32 us  [call(): pl.pallas_call(kernel, out_shape=outs, in_specs=specs if specs is not Non...]
    add x1 -> x0, other arithmetic: 0.62 us -> none  [by_kernels(): loss = loss + exchange(loss, places, over_core)]
  transfers between devices with their start and end apart: 20 -> 15, of which waited for: 9 -> 8; matrix products, arithmetic and copies ran while one was open for 0% -> 0% of each run, Pallas kernels for 5% -> 5%
where the time goes in v6:
time: 48 us; the launch traced here: 47.7 us
  waiting for transfers between devices  22.3 us (46%)
  starting transfers between devices  17.1 us (36%)
  Pallas kernels  5.32 us (11%)
  local copies, waits for them, and re-layouts  2.09 us (4%)
  between operations  0.79 us (2%)
    ppermute x14, waiting for transfers between devices, exchange(): return lax.ppermute(value, AXES, [(at, at ^ mask) for at in range(places)])  16.5 us
    ppermute x14, starting transfers between devices, exchange(): return lax.ppermute(value, AXES, [(at, at ^ mask) for at in range(places)])  11.5 us
    all_to_all x1, waiting for transfers between devices, by_kernels(): loss = lax.all_to_all(loss, AXES, 0, 0, tiled=True)  5.83 us
    all_to_all x1, starting transfers between devices, by_kernels(): loss = lax.all_to_all(loss, AXES, 0, 0, tiled=True)  5.67 us
    pallas_call x7, Pallas kernels, call(): pl.pallas_call(kernel, out_shape=outs, in_specs=specs if specs is not Non...  5.32 us
    unnamed x23, local copies, waits for them, and re-layouts  1.51 us
  transfers between devices with their start and end apart: 15, of which 8 were waited for; matrix products, arithmetic and copies ran while one was open for 0% of the time, Pallas kernels for 5%

profile of v6, /device:TPU:0, one launch (start us, length us, event | category | flops | bytes accessed | tf_op | source)
XLA Modules:
  0.0 47.7 jit_solution(4988836290320955119)
XLA Ops:
  0.6 0.0 copy-start
  0.6 0.9 %copy-done = bf16[16,64,128]{2,1,0:T(8,128)(2,1)S(1)} copy-done((bf16[16,64,128]{2,1,0:T(8,128)(2,1)S(1)}, bf16[16,64,128]{2,1,0:T(8,128)(2,1)}, u32[]{:S(2)}) %copy-start) | copy-done | bytes 262168
  1.6 0.0 copy-start.7
  1.6 0.0 copy-start.8
  1.6 0.4 shard_map.113.normed_ref
  1.9 0.4 copy-done.7
  2.3 0.0 copy-done.8
  2.4 0.0 copy-start.4
  2.4 0.0 copy-start.5
  2.4 0.6 %shard_map.114 = (bf16[512,128]{1,0:T(8,128)(2,1)S(1)}, bf16[512,128]{1,0:T(8,128)(2,1)S(1)}) custom-call(bf16[1024,128]{1,0:T(8,128)(2,1)S(1)} %shard_map.113.normed_ref, bf16[128,128]{1,0:T(8,128)(2,1)S(1)} %copy-done.7, bf16[128,128]{1,0:T(8,128)(2,1)S(1)} %copy-done.8), custom_call_target="tpu_custom_call" | custom-call | flops 67108864 | bytes 1048576 | tf_op jit(solution)/shard_map/pallas_call | solution.py:250
  2.9 0.0 copy-start.6
  2.9 4.1 %collective-permute-start.3 = (bf16[512,128]{1,0:T(8,128)(2,1)S(1)}, bf16[512,128]{1,0:T(8,128)(2,1)S(1)}, u32[]{:S(2)}, u32[]{:S(2)}) collective-permute-start(bf16[512,128]{1,0:T(8,128)(2,1)S(1)} %get-tuple-element.19.refs_0_), channel_id=1, source_target_pairs={{0,8},{1,9},{2,10},{3,11},{4,12},{5,13},{6,14},{7,15},{8,0},{9,1},... | collective-permute-start | bytes 393224 | tf_op jit(solution)/shard_map/ppermute | solution.py:246
  7.0 1.3 %collective-permute-start.5 = (bf16[512,128]{1,0:T(8,128)(2,1)S(1)}, bf16[512,128]{1,0:T(8,128)(2,1)S(1)}, u32[]{:S(2)}, u32[]{:S(2)}) collective-permute-start(bf16[512,128]{1,0:T(8,128)(2,1)S(1)} %get-tuple-element.20.refs_1_), channel_id=1, source_target_pairs={{0,12},{1,13},{2,14},{3,15},{4,8},{5,9},{6,10},{7,11},{8,4},{9,5},... | collective-permute-start | bytes 393224 | tf_op jit(solution)/shard_map/ppermute | solution.py:246
  8.4 0.0 copy-done.4
  8.4 0.0 copy-done.5
  8.4 0.0 copy-done.6
  8.4 1.1 %shard_map.115 = (bf16[512,128]{1,0:T(8,128)(2,1)S(1)}, bf16[512,128]{1,0:T(8,128)(2,1)S(1)}, bf16[512,128]{1,0:T(8,128)(2,1)S(1)}, bf16[512,128]{1,0:T(8,128)(2,1)S(1)}, f32[16,128]{1,0:T(8,128)S(1)}) custom-call(s32[5]{0:T(128)S(1)} %copy-done.6, bf16[1024,128]{1,0:T(8,128)(2,1)S(1)} %shard_map.113.normed_ref, bf16[128,128]{1,0:T(8,128)(2,1)S(1)} %copy-done.4, ...), custom_call_target="tpu_custom_call" | custom-call | flops 67108864 | bytes 1048576 | tf_op jit(solution)/shard_map/pallas_call | solution.py:250
  9.5 0.1 collective-permute-start
  9.6 0.3 collective-permute-start.1
  9.9 1.6 %collective-permute-start.2 = (bf16[512,128]{1,0:T(8,128)(2,1)S(1)}, bf16[512,128]{1,0:T(8,128)(2,1)S(1)}, u32[]{:S(2)}, u32[]{:S(2)}) collective-permute-start(bf16[512,128]{1,0:T(8,128)(2,1)S(1)} %get-tuple-element.29), channel_id=1, source_target_pairs={{0,6},{1,7},{2,4},{3,5},{4,2},{5,3},{6,0},{7,1},{8,14},{9,15},{10,... | collective-permute-start | bytes 393224 | tf_op jit(solution)/shard_map/ppermute | solution.py:246
  11.5 5.6 %collective-permute-done.3.far = bf16[512,128]{1,0:T(8,128)(2,1)S(1)} collective-permute-done((bf16[512,128]{1,0:T(8,128)(2,1)S(1)}, bf16[512,128]{1,0:T(8,128)(2,1)S(1)}, u32[]{:S(2)}, u32[]{:S(2)}) %collective-permute-start.3) | collective-permute-done | bytes 131104 | tf_op jit(solution)/shard_map/ppermute | solution.py:246
  17.0 0.0 collective-permute-start.4
  17.0 0.0 collective-permute-done.5.cross
  17.0 0.5 %collective-permute-start.6 = (bf16[512,128]{1,0:T(8,128)(2,1)S(1)}, bf16[512,128]{1,0:T(8,128)(2,1)S(1)}, u32[]{:S(2)}, u32[]{:S(2)}) collective-permute-start(bf16[512,128]{1,0:T(8,128)(2,1)S(1)} %collective-permute-done.5.cross), channel_id=1, source_target_pairs={{0,2},{1,3},{2,0},{3,1},{4,6},{5,7},{6,4},{7,5},{8,10},{9,11},{10,... | collective-permute-start | bytes 393224 | tf_op jit(solution)/shard_map/ppermute | solution.py:246
  17.6 0.0 collective-permute-done.core
  17.6 1.5 %collective-permute-done.1.near = bf16[512,128]{1,0:T(8,128)(2,1)S(1)} collective-permute-done((bf16[512,128]{1,0:T(8,128)(2,1)S(1)}, bf16[512,128]{1,0:T(8,128)(2,1)S(1)}, u32[]{:S(2)}, u32[]{:S(2)}) %collective-permute-start.1) | collective-permute-done | bytes 131104 | tf_op jit(solution)/shard_map/ppermute | solution.py:246
  19.0 2.7 %collective-permute-done.2.near_over = bf16[512,128]{1,0:T(8,128)(2,1)S(1)} collective-permute-done((bf16[512,128]{1,0:T(8,128)(2,1)S(1)}, bf16[512,128]{1,0:T(8,128)(2,1)S(1)}, u32[]{:S(2)}, u32[]{:S(2)}) %collective-permute-start.2) | collective-permute-done | bytes 131104 | tf_op jit(solution)/shard_map/ppermute | solution.py:246
  21.7 0.0 collective-permute-done.4.far_over
  21.7 0.0 collective-permute-done.6.cross_over
  21.7 0.0 copy-start.10
  21.7 0.0 copy-start.9
  21.7 0.0 copy-start.1
  21.8 0.5 %shard_map.117 = (bf16[512,128]{1,0:T(8,128)(2,1)S(1)}, bf16[512,128]{1,0:T(8,128)(2,1)S(1)}, bf16[512,128]{1,0:T(8,128)(2,1)S(1)}, bf16[512,128]{1,0:T(8,128)(2,1)S(1)}) custom-call(f32[16,128]{1,0:T(8,128)S(1)} %get-tuple-element.21.masks_ref, bf16[512,128]{1,0:T(8,128)(2,1)S(1)} %get-tuple-element.26.own, bf16[512,128]{1,0:T(8,128)(2,1)S(1)} %collective-permute-done.core, ...), custom_call_target="tpu_custom_call" | custom-call | flops 16777216 | bytes 1048576 | tf_op jit(solution)/shard_map/pallas_call | solution.py:250
  22.3 1.6 %collective-permute-start.7 = (bf16[512,128]{1,0:T(8,128)(2,1)S(1)}, bf16[512,128]{1,0:T(8,128)(2,1)S(1)}, u32[]{:S(2)}, u32[]{:S(2)}) collective-permute-start(bf16[512,128]{1,0:T(8,128)(2,1)S(1)} %get-tuple-element.31), channel_id=1, source_target_pairs={{0,1},{1,0},{2,3},{3,2},{4,5},{5,4},{6,7},{7,6},{8,9},{9,8},{10,11... | collective-permute-start | bytes 393224 | tf_op jit(solution)/shard_map/ppermute | solution.py:246
  23.9 0.0 copy-start.3
  23.9 0.0 copy-start.2
  23.9 0.0 collective-permute-start.8
  23.9 1.9 %collective-permute-start.9 = (bf16[512,128]{1,0:T(8,128)(2,1)S(1)}, bf16[512,128]{1,0:T(8,128)(2,1)S(1)}, u32[]{:S(2)}, u32[]{:S(2)}) collective-permute-start(bf16[512,128]{1,0:T(8,128)(2,1)S(1)} %get-tuple-element.33), channel_id=1, source_target_pairs={{0,5},{1,4},{2,7},{3,6},{4,1},{5,0},{6,3},{7,2},{8,13},{9,12},{10,... | collective-permute-start | bytes 393224 | tf_op jit(solution)/shard_map/ppermute | solution.py:246
  25.9 0.0 collective-permute-start.10
  25.9 2.0 %collective-permute-done.7.refs_1_ = bf16[512,128]{1,0:T(8,128)(2,1)S(1)} collective-permute-done((bf16[512,128]{1,0:T(8,128)(2,1)S(1)}, bf16[512,128]{1,0:T(8,128)(2,1)S(1)}, u32[]{:S(2)}, u32[]{:S(2)}) %collective-permute-start.7) | collective-permute-done | bytes 131104 | tf_op jit(solution)/shard_map/ppermute | solution.py:246
  27.9 0.0 collective-permute-start.11
  27.9 2.4 %collective-permute-done.8.refs_2_ = bf16[512,128]{1,0:T(8,128)(2,1)S(1)} collective-permute-done((bf16[512,128]{1,0:T(8,128)(2,1)S(1)}, bf16[512,128]{1,0:T(8,128)(2,1)S(1)}, u32[]{:S(2)}, u32[]{:S(2)}) %collective-permute-start.8) | collective-permute-done | bytes 131104 | tf_op jit(solution)/shard_map/ppermute | solution.py:246
  30.3 0.0 collective-permute-start.12
  30.3 1.6 %collective-permute-done.9.refs_3_ = bf16[512,128]{1,0:T(8,128)(2,1)S(1)} collective-permute-done((bf16[512,128]{1,0:T(8,128)(2,1)S(1)}, bf16[512,128]{1,0:T(8,128)(2,1)S(1)}, u32[]{:S(2)}, u32[]{:S(2)}) %collective-permute-start.9) | collective-permute-done | bytes 131104 | tf_op jit(solution)/shard_map/ppermute | solution.py:246
  31.9 0.0 collective-permute-start.13
  31.9 0.0 copy-done.10
  31.9 0.1 reshape.7.bins_ref
  32.0 0.0 copy-done.9
  32.0 0.1 copy.12.dw_ref
  32.1 0.0 copy-done.1
  32.1 0.0 copy-done.3
  32.1 0.0 copy-done.2
  32.1 0.4 shard_map.116
  32.5 0.0 collective-permute-done.10.refs_4_
  32.5 0.0 collective-permute-done.11.refs_5_
  32.5 0.0 collective-permute-done.12.refs_6_
  32.5 0.7 %collective-permute-done.13.refs_7_ = bf16[512,128]{1,0:T(8,128)(2,1)S(1)} collective-permute-done((bf16[512,128]{1,0:T(8,128)(2,1)S(1)}, bf16[512,128]{1,0:T(8,128)(2,1)S(1)}, u32[]{:S(2)}, u32[]{:S(2)}) %collective-permute-start.13) | collective-permute-done | bytes 131104 | tf_op jit(solution)/shard_map/ppermute | solution.py:246
  33.2 1.5 %shard_map.118 = (bf16[128,1024]{1,0:T(8,128)(2,1)S(1)}, f32[16,8,128]{2,1,0:T(8,128)}) custom-call(f32[16,128]{1,0:T(8,128)S(1)} %get-tuple-element.21.masks_ref, f32[128,1024]{1,0:T(8,128)S(1)} %get-tuple-element.22.x_ref, f32[128,1024]{1,0:T(8,128)S(1)} %get-tuple-element.23.gate_ref, s32[8,128]{1,0:T(8,128)S(1)} %reshape.7.bins_ref, ...), custom_call_target="tpu_custom_call" | custom-call | flops 100663296 | bytes 1048576 | tf_op jit(solution)/shard_map/pallas_call | solution.py:250
  34.8 5.7 %all-to-all-start = ((f32[16,8,128]{2,1,0:T(8,128)}), f32[16,8,128]{2,1,0:T(8,128)S(1)}, u32[]{:S(2)}, u32[]{:S(2)}) async-start(f32[16,8,128]{2,1,0:T(8,128)} %get-tuple-element.35), calls=%async_computation | async-start | bytes 131072 | tf_op jit(solution)/shard_map/all_to_all | solution.py:347
  40.5 0.8 %shard_map.119 = bf16[16,64,128]{2,1,0:T(8,128)(2,1)} custom-call(bf16[128,1024]{1,0:T(8,128)(2,1)S(1)} %get-tuple-element.34.turned_ref), custom_call_target="tpu_custom_call" | custom-call | flops 67108864 | bytes 1048576 | tf_op jit(solution)/shard_map/pallas_call | solution.py:250
  41.3 5.8 %all-to-all-done = f32[16,8,128]{2,1,0:T(8,128)S(1)} async-done(((f32[16,8,128]{2,1,0:T(8,128)}), f32[16,8,128]{2,1,0:T(8,128)S(1)}, u32[]{:S(2)}, u32[]{:S(2)}) %all-to-all-start) | async-done | bytes 65568 | tf_op jit(solution)/shard_map/all_to_all | solution.py:347
  47.2 0.5 %slice.3 = f32[1,1]{1,0:T(1,128)} slice(f32[8,128]{1,0:T(8,128)S(1)} %reduce_sum.9), slice={[0:1], [0:1]} | slice | bytes 8 | tf_op jit(solution)/shard_map/slice | solution.py:348
  (1 shorter events, 0.0 us)
Async XLA Ops:
  0.6 1.0 %copy-start = (bf16[16,64,128]{2,1,0:T(8,128)(2,1)S(1)}, bf16[16,64,128]{2,1,0:T(8,128)(2,1)}, u32[]{:S(2)}) copy-start(bf16[16,64,128]{2,1,0:T(8,128)(2,1)} %x_ref.3) | copy-start | bytes 786436
  1.6 0.8 %copy-start.7 = (bf16[128,128]{1,0:T(8,128)(2,1)S(1)}, bf16[128,128]{1,0:T(8,128)(2,1)}, u32[]{:S(2)}) copy-start(bf16[128,128]{1,0:T(8,128)(2,1)} %w_ref.2) | copy-start | bytes 98308
  1.6 0.8 %copy-start.8 = (bf16[128,128]{1,0:T(8,128)(2,1)S(1)}, bf16[128,128]{1,0:T(8,128)(2,1)}, u32[]{:S(2)}) copy-start(bf16[128,128]{1,0:T(8,128)(2,1)} %g_ref.2) | copy-start | bytes 98308
  2.4 6.0 %copy-start.4 = (bf16[128,128]{1,0:T(8,128)(2,1)S(1)}, bf16[128,128]{1,0:T(8,128)(2,1)}, u32[]{:S(2)}) copy-start(bf16[128,128]{1,0:T(8,128)(2,1)} %w_ref.3) | copy-start | bytes 98308
  2.4 6.0 %copy-start.5 = (bf16[128,128]{1,0:T(8,128)(2,1)S(1)}, bf16[128,128]{1,0:T(8,128)(2,1)}, u32[]{:S(2)}) copy-start(bf16[128,128]{1,0:T(8,128)(2,1)} %g_ref.3) | copy-start | bytes 98308
  2.9 5.5 %copy-start.6 = (s32[5]{0:T(128)S(1)}, s32[5]{0:T(128)}, u32[]{:S(2)}) copy-start(s32[5]{0:T(128)} %lens_ref.1) | copy-start | bytes 64
  2.9 14.1 %collective-permute-start.3 = (bf16[512,128]{1,0:T(8,128)(2,1)S(1)}, bf16[512,128]{1,0:T(8,128)(2,1)S(1)}, u32[]{:S(2)}, u32[]{:S(2)}) collective-permute-start(bf16[512,128]{1,0:T(8,128)(2,1)S(1)} %get-tuple-element.19.refs_0_), channel_id=1, source_target_pairs={{0,8},{1,9},{2,10},{3,11},{4,12},{5,13},{6,14},{7,15},{8,0},{9,1},... | collective-permute-start | bytes 393224 | tf_op jit(solution)/shard_map/ppermute | solution.py:246
  7.0 10.0 %collective-permute-start.5 = (bf16[512,128]{1,0:T(8,128)(2,1)S(1)}, bf16[512,128]{1,0:T(8,128)(2,1)S(1)}, u32[]{:S(2)}, u32[]{:S(2)}) collective-permute-start(bf16[512,128]{1,0:T(8,128)(2,1)S(1)} %get-tuple-element.20.refs_1_), channel_id=1, source_target_pairs={{0,12},{1,13},{2,14},{3,15},{4,8},{5,9},{6,10},{7,11},{8,4},{9,5},... | collective-permute-start | bytes 393224 | tf_op jit(solution)/shard_map/ppermute | solution.py:246
  9.5 8.0 %collective-permute-start = (bf16[512,128]{1,0:T(8,128)(2,1)S(1)}, bf16[512,128]{1,0:T(8,128)(2,1)S(1)}, u32[]{:S(2)}, u32[]{:S(2)}) collective-permute-start(bf16[512,128]{1,0:T(8,128)(2,1)S(1)} %get-tuple-element.27), channel_id=1, source_target_pairs={{0,2},{1,3},{2,0},{3,1},{4,6},{5,7},{6,4},{7,5},{8,10},{9,11},{10,... | collective-permute-start | bytes 393224 | tf_op jit(solution)/shard_map/ppermute | solution.py:246
  9.6 9.4 %collective-permute-start.1 = (bf16[512,128]{1,0:T(8,128)(2,1)S(1)}, bf16[512,128]{1,0:T(8,128)(2,1)S(1)}, u32[]{:S(2)}, u32[]{:S(2)}) collective-permute-start(bf16[512,128]{1,0:T(8,128)(2,1)S(1)} %get-tuple-element.28), channel_id=1, source_target_pairs={{0,4},{1,5},{2,6},{3,7},{4,0},{5,1},{6,2},{7,3},{8,12},{9,13},{10,... | collective-permute-start | bytes 393224 | tf_op jit(solution)/shard_map/ppermute | solution.py:246
  9.9 11.8 %collective-permute-start.2 = (bf16[512,128]{1,0:T(8,128)(2,1)S(1)}, bf16[512,128]{1,0:T(8,128)(2,1)S(1)}, u32[]{:S(2)}, u32[]{:S(2)}) collective-permute-start(bf16[512,128]{1,0:T(8,128)(2,1)S(1)} %get-tuple-element.29), channel_id=1, source_target_pairs={{0,6},{1,7},{2,4},{3,5},{4,2},{5,3},{6,0},{7,1},{8,14},{9,15},{10,... | collective-permute-start | bytes 393224 | tf_op jit(solution)/shard_map/ppermute | solution.py:246
  17.0 4.7 %collective-permute-start.4 = (bf16[512,128]{1,0:T(8,128)(2,1)S(1)}, bf16[512,128]{1,0:T(8,128)(2,1)S(1)}, u32[]{:S(2)}, u32[]{:S(2)}) collective-permute-start(bf16[512,128]{1,0:T(8,128)(2,1)S(1)} %collective-permute-done.3.far), channel_id=1, source_target_pairs={{0,2},{1,3},{2,0},{3,1},{4,6},{5,7},{6,4},{7,5},{8,10},{9,11},{10,... | collective-permute-start | bytes 393224 | tf_op jit(solution)/shard_map/ppermute | solution.py:246
  17.0 4.7 %collective-permute-start.6 = (bf16[512,128]{1,0:T(8,128)(2,1)S(1)}, bf16[512,128]{1,0:T(8,128)(2,1)S(1)}, u32[]{:S(2)}, u32[]{:S(2)}) collective-permute-start(bf16[512,128]{1,0:T(8,128)(2,1)S(1)} %collective-permute-done.5.cross), channel_id=1, source_target_pairs={{0,2},{1,3},{2,0},{3,1},{4,6},{5,7},{6,4},{7,5},{8,10},{9,11},{10,... | collective-permute-start | bytes 393224 | tf_op jit(solution)/shard_map/ppermute | solution.py:246
  21.7 10.2 %copy-start.10 = (s32[16,64]{1,0:T(8,128)S(1)}, s32[16,64]{1,0:T(8,128)}, u32[]{:S(2)}) copy-start(s32[16,64]{1,0:T(8,128)} %param.11) | copy-start | bytes 12292
  21.7 10.2 %copy-start.9 = (bf16[128,64]{0,1:T(8,128)(2,1)S(1)}, bf16[128,64]{0,1:T(8,128)(2,1)}, u32[]{:S(2)}) copy-start(bf16[128,64]{0,1:T(8,128)(2,1)} %param.19) | copy-start | bytes 49156
  21.7 10.3 %copy-start.1 = (bf16[16,64,128]{2,1,0:T(8,128)(2,1)S(1)}, bf16[16,64,128]{2,1,0:T(8,128)(2,1)}, u32[]{:S(2)}) copy-start(bf16[16,64,128]{2,1,0:T(8,128)(2,1)} %x_ref.3) | copy-start | bytes 786436
  22.3 5.6 %collective-permute-start.7 = (bf16[512,128]{1,0:T(8,128)(2,1)S(1)}, bf16[512,128]{1,0:T(8,128)(2,1)S(1)}, u32[]{:S(2)}, u32[]{:S(2)}) collective-permute-start(bf16[512,128]{1,0:T(8,128)(2,1)S(1)} %get-tuple-element.31), channel_id=1, source_target_pairs={{0,1},{1,0},{2,3},{3,2},{4,5},{5,4},{6,7},{7,6},{8,9},{9,8},{10,11... | collective-permute-start | bytes 393224 | tf_op jit(solution)/shard_map/ppermute | solution.py:246
  23.9 8.2 %copy-start.3 = (bf16[128,128]{1,0:T(8,128)(2,1)S(1)}, bf16[128,128]{1,0:T(8,128)(2,1)}, u32[]{:S(2)}) copy-start(bf16[128,128]{1,0:T(8,128)(2,1)} %ow_ref.1) | copy-start | bytes 98308
  23.9 8.2 %copy-start.2 = (bf16[128,128]{1,0:T(8,128)(2,1)S(1)}, bf16[128,128]{1,0:T(8,128)(2,1)}, u32[]{:S(2)}) copy-start(bf16[128,128]{1,0:T(8,128)(2,1)} %gw_ref.1) | copy-start | bytes 98308
  23.9 6.4 %collective-permute-start.8 = (bf16[512,128]{1,0:T(8,128)(2,1)S(1)}, bf16[512,128]{1,0:T(8,128)(2,1)S(1)}, u32[]{:S(2)}, u32[]{:S(2)}) collective-permute-start(bf16[512,128]{1,0:T(8,128)(2,1)S(1)} %get-tuple-element.32), channel_id=1, source_target_pairs={{0,4},{1,5},{2,6},{3,7},{4,0},{5,1},{6,2},{7,3},{8,12},{9,13},{10,... | collective-permute-start | bytes 393224 | tf_op jit(solution)/shard_map/ppermute | solution.py:246
  23.9 8.0 %collective-permute-start.9 = (bf16[512,128]{1,0:T(8,128)(2,1)S(1)}, bf16[512,128]{1,0:T(8,128)(2,1)S(1)}, u32[]{:S(2)}, u32[]{:S(2)}) collective-permute-start(bf16[512,128]{1,0:T(8,128)(2,1)S(1)} %get-tuple-element.33), channel_id=1, source_target_pairs={{0,5},{1,4},{2,7},{3,6},{4,1},{5,0},{6,3},{7,2},{8,13},{9,12},{10,... | collective-permute-start | bytes 393224 | tf_op jit(solution)/shard_map/ppermute | solution.py:246
  25.9 6.6 %collective-permute-start.10 = (bf16[512,128]{1,0:T(8,128)(2,1)S(1)}, bf16[512,128]{1,0:T(8,128)(2,1)S(1)}, u32[]{:S(2)}, u32[]{:S(2)}) collective-permute-start(bf16[512,128]{1,0:T(8,128)(2,1)S(1)} %get-tuple-element.30.refs_0_), channel_id=1, source_target_pairs={{0,2},{1,3},{2,0},{3,1},{4,6},{5,7},{6,4},{7,5},{8,10},{9,11},{10,... | collective-permute-start | bytes 393224 | tf_op jit(solution)/shard_map/ppermute | solution.py:246
  27.9 4.6 %collective-permute-start.11 = (bf16[512,128]{1,0:T(8,128)(2,1)S(1)}, bf16[512,128]{1,0:T(8,128)(2,1)S(1)}, u32[]{:S(2)}, u32[]{:S(2)}) collective-permute-start(bf16[512,128]{1,0:T(8,128)(2,1)S(1)} %collective-permute-done.7.refs_1_), channel_id=1, source_target_pairs={{0,2},{1,3},{2,0},{3,1},{4,6},{5,7},{6,4},{7,5},{8,10},{9,11},{10,... | collective-permute-start | bytes 393224 | tf_op jit(solution)/shard_map/ppermute | solution.py:246
  30.3 2.2 %collective-permute-start.12 = (bf16[512,128]{1,0:T(8,128)(2,1)S(1)}, bf16[512,128]{1,0:T(8,128)(2,1)S(1)}, u32[]{:S(2)}, u32[]{:S(2)}) collective-permute-start(bf16[512,128]{1,0:T(8,128)(2,1)S(1)} %collective-permute-done.8.refs_2_), channel_id=1, source_target_pairs={{0,2},{1,3},{2,0},{3,1},{4,6},{5,7},{6,4},{7,5},{8,10},{9,11},{10,... | collective-permute-start | bytes 393224 | tf_op jit(solution)/shard_map/ppermute | solution.py:246
  31.9 1.3 %collective-permute-start.13 = (bf16[512,128]{1,0:T(8,128)(2,1)S(1)}, bf16[512,128]{1,0:T(8,128)(2,1)S(1)}, u32[]{:S(2)}, u32[]{:S(2)}) collective-permute-start(bf16[512,128]{1,0:T(8,128)(2,1)S(1)} %collective-permute-done.9.refs_3_), channel_id=1, source_target_pairs={{0,2},{1,3},{2,0},{3,1},{4,6},{5,7},{6,4},{7,5},{8,10},{9,11},{10,... | collective-permute-start | bytes 393224 | tf_op jit(solution)/shard_map/ppermute | solution.py:246
  34.8 12.4 %all-to-all-start = ((f32[16,8,128]{2,1,0:T(8,128)}), f32[16,8,128]{2,1,0:T(8,128)S(1)}, u32[]{:S(2)}, u32[]{:S(2)}) async-start(f32[16,8,128]{2,1,0:T(8,128)} %get-tuple-element.35), calls=%async_computation | async-start | bytes 131072 | tf_op jit(solution)/shard_map/all_to_all | solution.py:347

commit v7 on v6

--- a/solution.py
+++ b/solution.py
@@ -83,7 +83,7 @@
 
 
 def owner_place():
-    return lax.axis_index("row") % OWNERS
+    return lax.axis_index("row") // 2 % 2 * 2 + lax.axis_index("col")
 
 
 def owner_block(held, d, size):
@@ -96,26 +96,25 @@
     normed_ref[...] = layer_norm(x, -1).astype(jnp.bfloat16)
 
 
-def right_kernel(normed_ref, w_ref, g_ref, stay_ref, move_ref, turned, held):
+def right_kernel(normed_ref, w_ref, g_ref, all_ref, *refs):
+    outs, (turned, held) = refs[:OWNERS], refs[OWNERS:]
     project(normed_ref, w_ref, g_ref, turned, held)
-    size = stay_ref.shape[0] // 2
-    for d, ref in enumerate((stay_ref, stay_ref, move_ref, move_ref)):
-        ref[d % 2 * size : (d % 2 + 1) * size] = owner_block(held, d, size)
-
-
-def left_kernel(lens_ref, normed_ref, w_ref, g_ref, *refs):
-    (stay_ref, move_ref), outs, (masks_ref, turned, held) = refs[:2], refs[2:-3], refs[-3:]
+    for d, ref in enumerate(outs):
+        ref[...] = owner_block(held, d, ref.shape[0])
+    all_ref[...] = held[...].astype(jnp.bfloat16)
+
+
+def left_kernel(lens_ref, normed_ref, w_ref, g_ref, all_ref, near_ref, masks_ref, turned, held):
     tile_rows = held.shape[0] // normed_ref.shape[1] * 2
     pairs, keeps, share = make_masks(lens_ref, tile_rows, held.shape[1] // 2)
     project(normed_ref, w_ref, g_ref, turned, held, pairs)
     masks_ref[...] = jnp.concatenate(
         pairs + keeps + [share] * (masks_ref.shape[0] - len(pairs) - len(keeps)), 0
     )
-    size = stay_ref.shape[0] // 2
-    for d, ref in enumerate(outs):
-        right_ref = (stay_ref, move_ref)[d // 2]
-        ref[:size] = owner_block(held, d, size)
-        ref[size:] = right_ref[d % 2 * size : (d % 2 + 1) * size]
+    size = near_ref.shape[1] // 2
+    for o in range(OWNERS):
+        near_ref[o, :size] = held[o * size : (o + 1) * size].astype(jnp.bfloat16)
+        near_ref[o, size:] = all_ref[o * size : (o + 1) * size]
 
 
 def gate_kernel(x_ref, normed_ref, gw_ref, ow_ref, dw_ref, gate_ref, x_turned_ref, ow_turned, dw_turned):
@@ -137,66 +136,59 @@
         x_turned_ref[:, at] = x.T
 
 
-def tri_kernel(masks_ref, own, core, near, near_over, far, far_over, cross, cross_over, *refs):
-    outs, rights = refs[:-1], refs[-1]
-    half, _, width = rights.shape
-    size = own.shape[0] // 2
+def tri_kernel(masks_ref, near_ref, near_over_ref, *refs):
+    far, far_over = refs[:OWNERS], refs[OWNERS : 2 * OWNERS]
+    outs, rights = refs[2 * OWNERS : -1], refs[-1]
+    size, width = far[0].shape
+    half = rights.shape[1]
     tile_rows = size // half
-    side = OWNERS * tile_rows
-    me, col = lax.axis_index("row"), lax.axis_index("col")
-    lefts = (own, core, near, near_over)
-    pieces = (
-        (0, own, size),
-        (1, core, size),
-        (2, near, size),
-        (3, near_over, size),
-        (4, far, 0),
-        (5, far_over, size),
-        (6, cross, 0),
-        (7, cross_over, size),
-    )
-    for away, ref, start in pieces:
-        at = pl.multiple_of((me ^ away) * tile_rows, tile_rows)
-        for m in range(half):
-            rights[m, pl.ds(at, tile_rows), :] = ref[
-                start + m * tile_rows : start + (m + 1) * tile_rows
-            ]
-    low = lanes_of((side, width)) < width // 2
+    side = width // 2
+    me, col, owner = lax.axis_index("row"), lax.axis_index("col"), owner_place()
+    for d in range(OWNERS):
+        away = d // 2 * 2
+        for step, load in (
+            (0, lambda at: near_ref[owner ^ d, size + at : size + at + tile_rows]),
+            (1, lambda at: near_over_ref[owner ^ d, size + at : size + at + tile_rows]),
+            (4, lambda at: far[d][at : at + tile_rows]),
+            (5, lambda at: far_over[d][at : at + tile_rows]),
+        ):
+            place = pl.multiple_of((me ^ (away + step)) * tile_rows, tile_rows)
+            for m in range(half):
+                rights[d % 2, m, pl.ds(place, tile_rows), :] = load(m * tile_rows)
+    low = lanes_of((side, width)) < side
     first = masks_ref.shape[0] // 2
     keep = jnp.concatenate([masks_ref[first : first + 1], masks_ref[first + 1 : first + 2]], 1)
     for m in range(half):
-        left = jnp.concatenate(
-            [ref[m * tile_rows : (m + 1) * tile_rows] for ref in lefts], 0
-        )
-        pieces = []
-        for dx in (0, 1):
-            block = rights[m, pl.ds(pl.multiple_of((col ^ dx) * side, side), side), :]
-            block = block.astype(jnp.float32)
-            pieces += [jnp.where(low, block, 0.0), jnp.where(low, 0.0, block)]
-        right = jnp.concatenate(pieces, 0).astype(jnp.bfloat16)
-        product = (nt_dot(left, right) * keep).astype(jnp.bfloat16)
-        for d in range(OWNERS):
+        at = slice(m * tile_rows, (m + 1) * tile_rows)
+        product = 0.0
+        for dk in (0, 1):
+            left = jnp.concatenate([near_ref[owner ^ dk, at], near_ref[owner ^ (2 + dk), at]], 0)
+            pieces = []
             for dx in (0, 1):
-                at = d % 2 * size + m * tile_rows
-                outs[d // 2 * 2 + dx][at : at + tile_rows] = product[
-                    d * tile_rows : (d + 1) * tile_rows, dx * width : (dx + 1) * width
+                block = rights[dk, m, pl.ds(pl.multiple_of((col ^ dx) * side, side), side), :]
+                block = block.astype(jnp.float32)
+                pieces += [jnp.where(low, block, 0.0), jnp.where(low, 0.0, block)]
+            right = jnp.concatenate(pieces, 0).astype(jnp.bfloat16)
+            product = product + nt_dot(left, right)
+        product = (product * keep).astype(jnp.bfloat16)
+        for dz in (0, 1):
+            for dx in (0, 1):
+                outs[2 * dz + dx][at] = product[
+                    dz * tile_rows : (dz + 1) * tile_rows, dx * width : (dx + 1) * width
                 ]
 
 
 def finish_kernel(masks_ref, x_ref, gate_ref, bins_ref, ow_ref, dw_ref, *refs):
-    parts, overs = refs[:OWNERS], refs[OWNERS : 2 * OWNERS]
-    out_ref, loss_ref, held = refs[2 * OWNERS :]
+    parts, (out_ref, loss_ref, held) = refs[:OWNERS], refs[OWNERS:]
     channels = x_ref.shape[0]
-    size, width = parts[0].shape[0] // 2, parts[0].shape[1]
+    size, width = parts[0].shape
     half = channels // 2 // OWNERS
     tile_rows, tile_cols = size // half, width // 2
     packed = OWNERS * half
     owner = owner_place()
     total = jnp.zeros((tile_rows, width), jnp.float32)
     for d in range(OWNERS):
-        refs, at = ((parts, 0), (overs, size))[d % 2]
-        a, b = [refs[d // 2 * 2 + dx][at : at + size].astype(jnp.float32) for dx in (0, 1)]
-        block = a + b
+        block = parts[d][...].astype(jnp.float32)
         held[pl.ds(pl.multiple_of((owner ^ d) * size, size), size), :] = block
         total = total + jnp.sum(block.reshape(half, tile_rows, width), 0)
     average = (total + pltpu.roll(total, tile_cols, 1)) * (1.0 / channels)
@@ -284,39 +276,39 @@
     normed = call(
         norm_kernel, struct((spots, channels), bf16), args=(pair_repr,), flops=1 << 30
     )
-    stay, move = call(
+    whole, *rights = call(
         right_kernel,
-        [struct((2 * size, width), bf16)] * 2,
+        [struct((OWNERS * size, width), bf16)] + [struct((size, width), bf16)] * OWNERS,
         [turned, held],
         args=(normed, right_weight, right_gate_weight),
         flops=4 * spots * channels * channels,
     )
-    cross = exchange(move, places, over_half + over_z)
-    far = exchange(stay, places, over_half)
-    own, core, near, near_over, masks = call(
+    over = [d // 2 * over_z + d % 2 * over_x for d in range(OWNERS)]
+    far = [exchange(rights[d], places, over_half + over[d]) for d in range(OWNERS)]
+    near, masks = call(
         left_kernel,
-        [struct((2 * size, width), bf16)] * OWNERS + [struct((tile_rows, width), f32)],
+        [struct((OWNERS, 2 * size, width), bf16), struct((tile_rows, width), f32)],
         [turned, held],
-        [SMEM] + [VMEM] * 5,
-        args=(chain_lengths, normed, left_weight, left_gate_weight, stay, move),
+        [SMEM] + [VMEM] * 4,
+        args=(chain_lengths, normed, left_weight, left_gate_weight, whole),
         flops=4 * spots * channels * channels,
     )
-    near_over = exchange(near_over, places, over_z + over_core)
-    near = exchange(near, places, over_z)
-    core, far_over, cross_over = [
-        exchange(value, places, over_core) for value in (core, far, cross)
+    sides = [
+        [part * over_half + z * over_z + core * over_core + x for z in (0, 1) for x in (0, 1)]
+        for part in (0, 1)
+        for core in (0, 1)
     ]
+    near = lax.all_to_all(near, AXES, 0, 0, axis_index_groups=sides, tiled=True)
+    near_over = exchange(near, places, over_core)
+    far_over = [exchange(value, places, over_core) for value in far]
     parts = call(
         tri_kernel,
-        [struct((2 * size, width), bf16)] * OWNERS,
-        [pltpu.VMEM((size // tile_rows, rows * tile_rows, width), bf16)],
-        args=(masks, own, core, near, near_over, far, far_over, cross, cross_over),
+        [struct((size, width), bf16)] * OWNERS,
+        [pltpu.VMEM((cols, size // tile_rows, rows * tile_rows, width), bf16)],
+        args=(masks, near, near_over, *far, *far_over),
         flops=8 * size * 2 * tile_rows * 2 * width,
     )
-    parts = [parts[0]] + [
-        exchange(parts[d], places, d // 2 * over_z + d % 2 * over_x) for d in range(1, OWNERS)
-    ]
-    parts += [exchange(value, places, over_core) for value in parts]
+    parts = [parts[0]] + [exchange(parts[d], places, over[d]) for d in range(1, OWNERS)]
     gate, x_turned, out_turned, dist_turned = call(
         gate_kernel,
         [

time: 48 us -> 56.2 us (1.17)
  blocking collectives: 0 us -> 13.5 us
  waiting for transfers between devices: 22.3 us -> 16.3 us
  local copies, waits for them, and re-layouts: 2.09 us -> 2.74 us
    all_to_all x0 -> x1, blocking collectives: none -> 13.5 us  [by_kernels(): near = lax.all_to_all(near, AXES, 0, 0, axis_index_groups=sides, tiled=True)]
    ppermute x14 -> x12, waiting for transfers between devices: 16.5 us -> 10.5 us  [exchange(): return lax.ppermute(value, AXES, [(at, at ^ mask) for at in range(places)])]
    all_to_all x1, starting transfers between devices: 5.67 us -> 4.44 us  [by_kernels(): loss = lax.all_to_all(loss, AXES, 0, 0, tiled=True)]
    ppermute x14 -> x12, starting transfers between devices: 11.5 us -> 12.3 us  [exchange(): return lax.ppermute(value, AXES, [(at, at ^ mask) for at in range(places)])]
    unnamed x23, local copies, waits for them, and re-layouts: 1.51 us -> 2.16 us
  transfers between devices with their start and end apart: 15 -> 13, of which waited for: 8 -> 9; matrix products, arithmetic and copies ran while one was open for 0% -> 0% of each run, Pallas kernels for 5% -> 2%
where the time goes in v7:
time: 56.2 us; the launch traced here: 55.8 us
  starting transfers between devices  16.7 us (30%)
  waiting for transfers between devices  16.3 us (29%)
  blocking collectives  13.5 us (24%)
  Pallas kernels  5.68 us (10%)
  local copies, waits for them, and re-layouts  2.74 us (5%)
  between operations  0.75 us (1%)
    all_to_all x1, blocking collectives, by_kernels(): near = lax.all_to_all(near, AXES, 0, 0, axis_index_groups=sides, tiled=True)  13.5 us
    ppermute x12, starting transfers between devices, exchange(): return lax.ppermute(value, AXES, [(at, at ^ mask) for at in range(places)])  12.3 us
    ppermute x12, waiting for transfers between devices, exchange(): return lax.ppermute(value, AXES, [(at, at ^ mask) for at in range(places)])  10.5 us
    all_to_all x1, waiting for transfers between devices, by_kernels(): loss = lax.all_to_all(loss, AXES, 0, 0, tiled=True)  5.83 us
    pallas_call x7, Pallas kernels, call(): pl.pallas_call(kernel, out_shape=outs, in_specs=specs if specs is not Non...  5.68 us
    all_to_all x1, starting transfers between devices, by_kernels(): loss = lax.all_to_all(loss, AXES, 0, 0, tiled=True)  4.44 us
    unnamed x23, local copies, waits for them, and re-layouts  2.16 us
  transfers between devices with their start and end apart: 13, of which 9 were waited for; matrix products, arithmetic and copies ran while one was open for 0% of the time, Pallas kernels for 2%

profile of v7, /device:TPU:0, one launch (start us, length us, event | category | flops | bytes accessed | tf_op | source)
XLA Modules:
  0.0 55.8 jit_solution(11126523306249024173)
XLA Ops:
  0.6 0.0 copy-start
  0.6 0.9 %copy-done = bf16[16,64,128]{2,1,0:T(8,128)(2,1)S(1)} copy-done((bf16[16,64,128]{2,1,0:T(8,128)(2,1)S(1)}, bf16[16,64,128]{2,1,0:T(8,128)(2,1)}, u32[]{:S(2)}) %copy-start) | copy-done | bytes 262168
  1.6 0.0 copy-start.7
  1.6 0.0 copy-start.8
  1.6 0.4 shard_map.113.normed_ref
  1.9 0.4 copy-done.7
  2.3 0.0 copy-done.8
  2.4 0.0 copy-start.4
  2.4 0.0 copy-start.5
  2.4 0.6 %shard_map.114 = (bf16[1024,128]{1,0:T(8,128)(2,1)S(1)}, bf16[256,128]{1,0:T(8,128)(2,1)S(1)}, bf16[256,128]{1,0:T(8,128)(2,1)S(1)}, bf16[256,128]{1,0:T(8,128)(2,1)S(1)}, bf16[256,128]{1,0:T(8,128)(2,1)S(1)}) custom-call(bf16[1024,128]{1,0:T(8,128)(2,1)S(1)} %shard_map.113.normed_ref, bf16[128,128]{1,0:T(8,128)(2,1)S(1)} %copy-done.7, ...), custom_call_target="tpu_custom_call" | custom-call | flops 67108864 | bytes 1048576 | tf_op jit(solution)/shard_map/pallas_call | solution.py:242
  3.0 0.0 copy-start.6
  3.0 0.2 copy-done.4
  3.1 0.0 copy-done.5
  3.1 0.5 copy-done.6
  3.6 1.1 %shard_map.115 = (bf16[4,512,128]{2,1,0:T(8,128)(2,1)S(1)}, f32[16,128]{1,0:T(8,128)S(1)}) custom-call(s32[5]{0:T(128)S(1)} %copy-done.6, bf16[1024,128]{1,0:T(8,128)(2,1)S(1)} %shard_map.113.normed_ref, bf16[128,128]{1,0:T(8,128)(2,1)S(1)} %copy-done.4, bf16[128,128]{1,0:T(8,128)(2,1)S(1)} %copy-done.5, bf16[1024,128]{1,0:T(8,128)(2,1)S(1)} %get-tuple-element.19.all_ref), custom_call_target="tpu_custom_call" | custom-call | flops 67108864 | bytes 1048576 | tf_op jit(solution)/shard_map/pallas_call | solution.py:242
  4.7 13.5 %all_to_all.10.near_ref = bf16[4,512,128]{2,1,0:T(8,128)(2,1)S(1)} all-to-all(bf16[4,512,128]{2,1,0:T(8,128)(2,1)S(1)} %get-tuple-element.25), channel_id=1, replica_groups={{0,1,4,5},{2,3,6,7},{8,9,12,13},{10,11,14,15},{16,17,20,21},{18,19,22,2..., dimensions={0} | all-to-all | bytes 1048576 | tf_op jit(solution)/shard_map/all_to_all | solution.py:301
  18.3 0.0 collective-permute-start
  18.3 2.6 %collective-permute-start.1 = (bf16[256,128]{1,0:T(8,128)(2,1)S(1)}, bf16[256,128]{1,0:T(8,128)(2,1)S(1)}, u32[]{:S(2)}, u32[]{:S(2)}) collective-permute-start(bf16[256,128]{1,0:T(8,128)(2,1)S(1)} %get-tuple-element.26), channel_id=1, source_target_pairs={{0,8},{1,9},{2,10},{3,11},{4,12},{5,13},{6,14},{7,15},{8,0},{9,1},... | collective-permute-start | bytes 196616 | tf_op jit(solution)/shard_map/ppermute | solution.py:238
  20.9 0.7 %collective-permute-start.2 = (bf16[256,128]{1,0:T(8,128)(2,1)S(1)}, bf16[256,128]{1,0:T(8,128)(2,1)S(1)}, u32[]{:S(2)}, u32[]{:S(2)}) collective-permute-start(bf16[256,128]{1,0:T(8,128)(2,1)S(1)} %get-tuple-element.27), channel_id=1, source_target_pairs={{0,9},{1,8},{2,11},{3,10},{4,13},{5,12},{6,15},{7,14},{8,1},{9,0},... | collective-permute-start | bytes 196616 | tf_op jit(solution)/shard_map/ppermute | solution.py:238
  21.6 2.6 %collective-permute-start.3 = (bf16[256,128]{1,0:T(8,128)(2,1)S(1)}, bf16[256,128]{1,0:T(8,128)(2,1)S(1)}, u32[]{:S(2)}, u32[]{:S(2)}) collective-permute-start(bf16[256,128]{1,0:T(8,128)(2,1)S(1)} %get-tuple-element.28), channel_id=1, source_target_pairs={{0,12},{1,13},{2,14},{3,15},{4,8},{5,9},{6,10},{7,11},{8,4},{9,5},... | collective-permute-start | bytes 196616 | tf_op jit(solution)/shard_map/ppermute | solution.py:238
  24.2 1.8 %collective-permute-start.4 = (bf16[256,128]{1,0:T(8,128)(2,1)S(1)}, bf16[256,128]{1,0:T(8,128)(2,1)S(1)}, u32[]{:S(2)}, u32[]{:S(2)}) collective-permute-start(bf16[256,128]{1,0:T(8,128)(2,1)S(1)} %get-tuple-element.29), channel_id=1, source_target_pairs={{0,13},{1,12},{2,15},{3,14},{4,9},{5,8},{6,11},{7,10},{8,5},{9,4},... | collective-permute-start | bytes 196616 | tf_op jit(solution)/shard_map/ppermute | solution.py:238
  25.9 2.0 %collective-permute-done.1.refs_0_ = bf16[256,128]{1,0:T(8,128)(2,1)S(1)} collective-permute-done((bf16[256,128]{1,0:T(8,128)(2,1)S(1)}, bf16[256,128]{1,0:T(8,128)(2,1)S(1)}, u32[]{:S(2)}, u32[]{:S(2)}) %collective-permute-start.1) | collective-permute-done | bytes 65568 | tf_op jit(solution)/shard_map/ppermute | solution.py:238
  28.0 0.0 collective-permute-start.5
  28.0 3.5 %collective-permute-done.2.refs_1_ = bf16[256,128]{1,0:T(8,128)(2,1)S(1)} collective-permute-done((bf16[256,128]{1,0:T(8,128)(2,1)S(1)}, bf16[256,128]{1,0:T(8,128)(2,1)S(1)}, u32[]{:S(2)}, u32[]{:S(2)}) %collective-permute-start.2) | collective-permute-done | bytes 65568 | tf_op jit(solution)/shard_map/ppermute | solution.py:238
  31.5 0.0 collective-permute-start.6
  31.5 0.0 collective-permute-done.3.refs_2_
  31.5 0.5 collective-permute-start.7
  32.0 0.0 collective-permute-done.4.refs_3_
  32.0 0.1 collective-permute-start.8
  32.1 0.0 collective-permute-done.5.refs_4_
  32.1 0.7 %collective-permute-done.6.refs_5_ = bf16[256,128]{1,0:T(8,128)(2,1)S(1)} collective-permute-done((bf16[256,128]{1,0:T(8,128)(2,1)S(1)}, bf16[256,128]{1,0:T(8,128)(2,1)S(1)}, u32[]{:S(2)}, u32[]{:S(2)}) %collective-permute-start.6) | collective-permute-done | bytes 65568 | tf_op jit(solution)/shard_map/ppermute | solution.py:238
  32.8 0.2 collective-permute-done.7.refs_6_
  32.9 0.4 collective-permute-done.8.refs_7_
  33.3 0.0 collective-permute-done.near_over_ref
  33.3 0.0 copy-start.9
  33.3 0.0 copy-start.10
  33.3 0.0 copy-start.1
  33.3 0.9 %shard_map.117 = (bf16[256,128]{1,0:T(8,128)(2,1)S(1)}, bf16[256,128]{1,0:T(8,128)(2,1)S(1)}, bf16[256,128]{1,0:T(8,128)(2,1)S(1)}, bf16[256,128]{1,0:T(8,128)(2,1)S(1)}) custom-call(f32[16,128]{1,0:T(8,128)S(1)} %get-tuple-element.20.masks_ref, bf16[4,512,128]{2,1,0:T(8,128)(2,1)S(1)} %all_to_all.10.near_ref, ...), custom_call_target="tpu_custom_call" | custom-call | flops 16777216 | bytes 1048576 | tf_op jit(solution)/shard_map/pallas_call | solution.py:242
  34.2 0.0 copy-start.3
  34.3 0.0 copy-start.2
  34.3 2.5 %collective-permute-start.10 = (bf16[256,128]{1,0:T(8,128)(2,1)S(1)}, bf16[256,128]{1,0:T(8,128)(2,1)S(1)}, u32[]{:S(2)}, u32[]{:S(2)}) collective-permute-start(bf16[256,128]{1,0:T(8,128)(2,1)S(1)} %get-tuple-element.32), channel_id=1, source_target_pairs={{0,4},{1,5},{2,6},{3,7},{4,0},{5,1},{6,2},{7,3},{8,12},{9,13},{10,... | collective-permute-start | bytes 196616 | tf_op jit(solution)/shard_map/ppermute | solution.py:238
  36.8 0.6 %collective-permute-start.11 = (bf16[256,128]{1,0:T(8,128)(2,1)S(1)}, bf16[256,128]{1,0:T(8,128)(2,1)S(1)}, u32[]{:S(2)}, u32[]{:S(2)}) collective-permute-start(bf16[256,128]{1,0:T(8,128)(2,1)S(1)} %get-tuple-element.33), channel_id=1, source_target_pairs={{0,5},{1,4},{2,7},{3,6},{4,1},{5,0},{6,3},{7,2},{8,13},{9,12},{10,... | collective-permute-start | bytes 196616 | tf_op jit(solution)/shard_map/ppermute | solution.py:238
  37.4 1.0 %collective-permute-start.9 = (bf16[256,128]{1,0:T(8,128)(2,1)S(1)}, bf16[256,128]{1,0:T(8,128)(2,1)S(1)}, u32[]{:S(2)}, u32[]{:S(2)}) collective-permute-start(bf16[256,128]{1,0:T(8,128)(2,1)S(1)} %get-tuple-element.31), channel_id=1, source_target_pairs={{0,1},{1,0},{2,3},{3,2},{4,5},{5,4},{6,7},{7,6},{8,9},{9,8},{10,11... | collective-permute-start | bytes 196616 | tf_op jit(solution)/shard_map/ppermute | solution.py:238
  38.3 0.0 copy-done.9
  38.3 0.1 copy.12.dw_ref
  38.4 0.0 copy-done.10
  38.5 0.1 reshape.7.bins_ref
  38.5 0.0 copy-done.1
  38.5 0.0 copy-done.3
  38.5 0.0 copy-done.2
  38.5 0.4 shard_map.116
  38.9 0.3 collective-permute-done.10.refs_2_
  39.2 2.8 %collective-permute-done.11.refs_3_ = bf16[256,128]{1,0:T(8,128)(2,1)S(1)} collective-permute-done((bf16[256,128]{1,0:T(8,128)(2,1)S(1)}, bf16[256,128]{1,0:T(8,128)(2,1)S(1)}, u32[]{:S(2)}, u32[]{:S(2)}) %collective-permute-start.11) | collective-permute-done | bytes 65568 | tf_op jit(solution)/shard_map/ppermute | solution.py:238
  42.0 0.6 %collective-permute-done.9.refs_1_ = bf16[256,128]{1,0:T(8,128)(2,1)S(1)} collective-permute-done((bf16[256,128]{1,0:T(8,128)(2,1)S(1)}, bf16[256,128]{1,0:T(8,128)(2,1)S(1)}, u32[]{:S(2)}, u32[]{:S(2)}) %collective-permute-start.9) | collective-permute-done | bytes 65568 | tf_op jit(solution)/shard_map/ppermute | solution.py:238
  42.6 1.5 %shard_map.118 = (bf16[128,1024]{1,0:T(8,128)(2,1)S(1)}, f32[16,8,128]{2,1,0:T(8,128)}) custom-call(f32[16,128]{1,0:T(8,128)S(1)} %get-tuple-element.20.masks_ref, f32[128,1024]{1,0:T(8,128)S(1)} %get-tuple-element.21.x_ref, f32[128,1024]{1,0:T(8,128)S(1)} %get-tuple-element.22.gate_ref, s32[8,128]{1,0:T(8,128)S(1)} %reshape.7.bins_ref, ...), custom_call_target="tpu_custom_call" | custom-call | flops 100663296 | bytes 1048576 | tf_op jit(solution)/shard_map/pallas_call | solution.py:242
  44.2 4.4 %all-to-all-start.1 = ((f32[16,8,128]{2,1,0:T(8,128)}), f32[16,8,128]{2,1,0:T(8,128)S(1)}, u32[]{:S(2)}, u32[]{:S(2)}) async-start(f32[16,8,128]{2,1,0:T(8,128)} %get-tuple-element.35), calls=%async_computation.1 | async-start | bytes 131072 | tf_op jit(solution)/shard_map/all_to_all | solution.py:339
  48.6 0.8 %shard_map.119 = bf16[16,64,128]{2,1,0:T(8,128)(2,1)} custom-call(bf16[128,1024]{1,0:T(8,128)(2,1)S(1)} %get-tuple-element.34.turned_ref), custom_call_target="tpu_custom_call" | custom-call | flops 67108864 | bytes 1048576 | tf_op jit(solution)/shard_map/pallas_call | solution.py:242
  49.4 5.8 %all-to-all-done.1 = f32[16,8,128]{2,1,0:T(8,128)S(1)} async-done(((f32[16,8,128]{2,1,0:T(8,128)}), f32[16,8,128]{2,1,0:T(8,128)S(1)}, u32[]{:S(2)}, u32[]{:S(2)}) %all-to-all-start.1) | async-done | bytes 65568 | tf_op jit(solution)/shard_map/all_to_all | solution.py:339
  55.3 0.5 slice.3
  (1 shorter events, 0.0 us)
Async XLA Ops:
  0.6 1.0 %copy-start = (bf16[16,64,128]{2,1,0:T(8,128)(2,1)S(1)}, bf16[16,64,128]{2,1,0:T(8,128)(2,1)}, u32[]{:S(2)}) copy-start(bf16[16,64,128]{2,1,0:T(8,128)(2,1)} %x_ref.3) | copy-start | bytes 786436
  1.6 0.8 %copy-start.7 = (bf16[128,128]{1,0:T(8,128)(2,1)S(1)}, bf16[128,128]{1,0:T(8,128)(2,1)}, u32[]{:S(2)}) copy-start(bf16[128,128]{1,0:T(8,128)(2,1)} %w_ref.2) | copy-start | bytes 98308
  1.6 0.8 %copy-start.8 = (bf16[128,128]{1,0:T(8,128)(2,1)S(1)}, bf16[128,128]{1,0:T(8,128)(2,1)}, u32[]{:S(2)}) copy-start(bf16[128,128]{1,0:T(8,128)(2,1)} %g_ref.2) | copy-start | bytes 98308
  2.4 0.8 %copy-start.4 = (bf16[128,128]{1,0:T(8,128)(2,1)S(1)}, bf16[128,128]{1,0:T(8,128)(2,1)}, u32[]{:S(2)}) copy-start(bf16[128,128]{1,0:T(8,128)(2,1)} %w_ref.3) | copy-start | bytes 98308
  2.4 0.8 %copy-start.5 = (bf16[128,128]{1,0:T(8,128)(2,1)S(1)}, bf16[128,128]{1,0:T(8,128)(2,1)}, u32[]{:S(2)}) copy-start(bf16[128,128]{1,0:T(8,128)(2,1)} %g_ref.3) | copy-start | bytes 98308
  3.0 0.7 %copy-start.6 = (s32[5]{0:T(128)S(1)}, s32[5]{0:T(128)}, u32[]{:S(2)}) copy-start(s32[5]{0:T(128)} %lens_ref.1) | copy-start | bytes 64
  18.3 15.0 %collective-permute-start = (bf16[4,512,128]{2,1,0:T(8,128)(2,1)S(1)}, bf16[4,512,128]{2,1,0:T(8,128)(2,1)S(1)}, u32[]{:S(2)}, u32[]{:S(2)}) collective-permute-start(bf16[4,512,128]{2,1,0:T(8,128)(2,1)S(1)} %all_to_all.10.near_ref), channel_id=1, source_target_pairs={{0,2},{1,3},{2,0},{3,1},{4,6},{5,7},{6,4},{7,5},{8,10},{9,11},{10,... | collective-permute-start | bytes 1572872 | tf_op jit(solution)/shard_map/ppermute | solution.py:238
  18.3 9.7 %collective-permute-start.1 = (bf16[256,128]{1,0:T(8,128)(2,1)S(1)}, bf16[256,128]{1,0:T(8,128)(2,1)S(1)}, u32[]{:S(2)}, u32[]{:S(2)}) collective-permute-start(bf16[256,128]{1,0:T(8,128)(2,1)S(1)} %get-tuple-element.26), channel_id=1, source_target_pairs={{0,8},{1,9},{2,10},{3,11},{4,12},{5,13},{6,14},{7,15},{8,0},{9,1},... | collective-permute-start | bytes 196616 | tf_op jit(solution)/shard_map/ppermute | solution.py:238
  20.9 10.6 %collective-permute-start.2 = (bf16[256,128]{1,0:T(8,128)(2,1)S(1)}, bf16[256,128]{1,0:T(8,128)(2,1)S(1)}, u32[]{:S(2)}, u32[]{:S(2)}) collective-permute-start(bf16[256,128]{1,0:T(8,128)(2,1)S(1)} %get-tuple-element.27), channel_id=1, source_target_pairs={{0,9},{1,8},{2,11},{3,10},{4,13},{5,12},{6,15},{7,14},{8,1},{9,0},... | collective-permute-start | bytes 196616 | tf_op jit(solution)/shard_map/ppermute | solution.py:238
  21.6 10.0 %collective-permute-start.3 = (bf16[256,128]{1,0:T(8,128)(2,1)S(1)}, bf16[256,128]{1,0:T(8,128)(2,1)S(1)}, u32[]{:S(2)}, u32[]{:S(2)}) collective-permute-start(bf16[256,128]{1,0:T(8,128)(2,1)S(1)} %get-tuple-element.28), channel_id=1, source_target_pairs={{0,12},{1,13},{2,14},{3,15},{4,8},{5,9},{6,10},{7,11},{8,4},{9,5},... | collective-permute-start | bytes 196616 | tf_op jit(solution)/shard_map/ppermute | solution.py:238
  24.2 7.9 %collective-permute-start.4 = (bf16[256,128]{1,0:T(8,128)(2,1)S(1)}, bf16[256,128]{1,0:T(8,128)(2,1)S(1)}, u32[]{:S(2)}, u32[]{:S(2)}) collective-permute-start(bf16[256,128]{1,0:T(8,128)(2,1)S(1)} %get-tuple-element.29), channel_id=1, source_target_pairs={{0,13},{1,12},{2,15},{3,14},{4,9},{5,8},{6,11},{7,10},{8,5},{9,4},... | collective-permute-start | bytes 196616 | tf_op jit(solution)/shard_map/ppermute | solution.py:238
  28.0 4.1 %collective-permute-start.5 = (bf16[256,128]{1,0:T(8,128)(2,1)S(1)}, bf16[256,128]{1,0:T(8,128)(2,1)S(1)}, u32[]{:S(2)}, u32[]{:S(2)}) collective-permute-start(bf16[256,128]{1,0:T(8,128)(2,1)S(1)} %collective-permute-done.1.refs_0_), channel_id=1, source_target_pairs={{0,2},{1,3},{2,0},{3,1},{4,6},{5,7},{6,4},{7,5},{8,10},{9,11},{10,... | collective-permute-start | bytes 196616 | tf_op jit(solution)/shard_map/ppermute | solution.py:238
  31.5 1.3 %collective-permute-start.6 = (bf16[256,128]{1,0:T(8,128)(2,1)S(1)}, bf16[256,128]{1,0:T(8,128)(2,1)S(1)}, u32[]{:S(2)}, u32[]{:S(2)}) collective-permute-start(bf16[256,128]{1,0:T(8,128)(2,1)S(1)} %collective-permute-done.2.refs_1_), channel_id=1, source_target_pairs={{0,2},{1,3},{2,0},{3,1},{4,6},{5,7},{6,4},{7,5},{8,10},{9,11},{10,... | collective-permute-start | bytes 196616 | tf_op jit(solution)/shard_map/ppermute | solution.py:238
  31.5 1.4 %collective-permute-start.7 = (bf16[256,128]{1,0:T(8,128)(2,1)S(1)}, bf16[256,128]{1,0:T(8,128)(2,1)S(1)}, u32[]{:S(2)}, u32[]{:S(2)}) collective-permute-start(bf16[256,128]{1,0:T(8,128)(2,1)S(1)} %collective-permute-done.3.refs_2_), channel_id=1, source_target_pairs={{0,2},{1,3},{2,0},{3,1},{4,6},{5,7},{6,4},{7,5},{8,10},{9,11},{10,... | collective-permute-start | bytes 196616 | tf_op jit(solution)/shard_map/ppermute | solution.py:238
  32.0 1.3 %collective-permute-start.8 = (bf16[256,128]{1,0:T(8,128)(2,1)S(1)}, bf16[256,128]{1,0:T(8,128)(2,1)S(1)}, u32[]{:S(2)}, u32[]{:S(2)}) collective-permute-start(bf16[256,128]{1,0:T(8,128)(2,1)S(1)} %collective-permute-done.4.refs_3_), channel_id=1, source_target_pairs={{0,2},{1,3},{2,0},{3,1},{4,6},{5,7},{6,4},{7,5},{8,10},{9,11},{10,... | collective-permute-start | bytes 196616 | tf_op jit(solution)/shard_map/ppermute | solution.py:238
  33.3 5.0 %copy-start.9 = (bf16[128,64]{0,1:T(8,128)(2,1)S(1)}, bf16[128,64]{0,1:T(8,128)(2,1)}, u32[]{:S(2)}) copy-start(bf16[128,64]{0,1:T(8,128)(2,1)} %param.19) | copy-start | bytes 49156
  33.3 5.1 %copy-start.10 = (s32[16,64]{1,0:T(8,128)S(1)}, s32[16,64]{1,0:T(8,128)}, u32[]{:S(2)}) copy-start(s32[16,64]{1,0:T(8,128)} %param.11) | copy-start | bytes 12292
  33.3 5.2 %copy-start.1 = (bf16[16,64,128]{2,1,0:T(8,128)(2,1)S(1)}, bf16[16,64,128]{2,1,0:T(8,128)(2,1)}, u32[]{:S(2)}) copy-start(bf16[16,64,128]{2,1,0:T(8,128)(2,1)} %x_ref.3) | copy-start | bytes 786436
  34.2 4.3 %copy-start.3 = (bf16[128,128]{1,0:T(8,128)(2,1)S(1)}, bf16[128,128]{1,0:T(8,128)(2,1)}, u32[]{:S(2)}) copy-start(bf16[128,128]{1,0:T(8,128)(2,1)} %ow_ref.1) | copy-start | bytes 98308
  34.3 4.3 %copy-start.2 = (bf16[128,128]{1,0:T(8,128)(2,1)S(1)}, bf16[128,128]{1,0:T(8,128)(2,1)}, u32[]{:S(2)}) copy-start(bf16[128,128]{1,0:T(8,128)(2,1)} %gw_ref.1) | copy-start | bytes 98308
  34.3 4.9 %collective-permute-start.10 = (bf16[256,128]{1,0:T(8,128)(2,1)S(1)}, bf16[256,128]{1,0:T(8,128)(2,1)S(1)}, u32[]{:S(2)}, u32[]{:S(2)}) collective-permute-start(bf16[256,128]{1,0:T(8,128)(2,1)S(1)} %get-tuple-element.32), channel_id=1, source_target_pairs={{0,4},{1,5},{2,6},{3,7},{4,0},{5,1},{6,2},{7,3},{8,12},{9,13},{10,... | collective-permute-start | bytes 196616 | tf_op jit(solution)/shard_map/ppermute | solution.py:238
  36.8 5.2 %collective-permute-start.11 = (bf16[256,128]{1,0:T(8,128)(2,1)S(1)}, bf16[256,128]{1,0:T(8,128)(2,1)S(1)}, u32[]{:S(2)}, u32[]{:S(2)}) collective-permute-start(bf16[256,128]{1,0:T(8,128)(2,1)S(1)} %get-tuple-element.33), channel_id=1, source_target_pairs={{0,5},{1,4},{2,7},{3,6},{4,1},{5,0},{6,3},{7,2},{8,13},{9,12},{10,... | collective-permute-start | bytes 196616 | tf_op jit(solution)/shard_map/ppermute | solution.py:238
  37.4 5.3 %collective-permute-start.9 = (bf16[256,128]{1,0:T(8,128)(2,1)S(1)}, bf16[256,128]{1,0:T(8,128)(2,1)S(1)}, u32[]{:S(2)}, u32[]{:S(2)}) collective-permute-start(bf16[256,128]{1,0:T(8,128)(2,1)S(1)} %get-tuple-element.31), channel_id=1, source_target_pairs={{0,1},{1,0},{2,3},{3,2},{4,5},{5,4},{6,7},{7,6},{8,9},{9,8},{10,11... | collective-permute-start | bytes 196616 | tf_op jit(solution)/shard_map/ppermute | solution.py:238
  44.2 11.1 %all-to-all-start.1 = ((f32[16,8,128]{2,1,0:T(8,128)}), f32[16,8,128]{2,1,0:T(8,128)S(1)}, u32[]{:S(2)}, u32[]{:S(2)}) async-start(f32[16,8,128]{2,1,0:T(8,128)} %get-tuple-element.35), calls=%async_computation.1 | async-start | bytes 131072 | tf_op jit(solution)/shard_map/all_to_all | solution.py:339

commit v8 on v7

--- a/solution.py
+++ b/solution.py
@@ -96,25 +96,32 @@
     normed_ref[...] = layer_norm(x, -1).astype(jnp.bfloat16)
 
 
-def right_kernel(normed_ref, w_ref, g_ref, all_ref, *refs):
+def right_kernel(normed_ref, w_ref, g_ref, *refs):
     outs, (turned, held) = refs[:OWNERS], refs[OWNERS:]
     project(normed_ref, w_ref, g_ref, turned, held)
     for d, ref in enumerate(outs):
         ref[...] = owner_block(held, d, ref.shape[0])
-    all_ref[...] = held[...].astype(jnp.bfloat16)
-
-
-def left_kernel(lens_ref, normed_ref, w_ref, g_ref, all_ref, near_ref, masks_ref, turned, held):
+
+
+def left_kernel(lens_ref, normed_ref, w_ref, g_ref, *refs):
+    rights, outs = refs[:OWNERS], refs[OWNERS : 2 * OWNERS]
+    masks_ref, turned, held = refs[2 * OWNERS :]
     tile_rows = held.shape[0] // normed_ref.shape[1] * 2
     pairs, keeps, share = make_masks(lens_ref, tile_rows, held.shape[1] // 2)
     project(normed_ref, w_ref, g_ref, turned, held, pairs)
     masks_ref[...] = jnp.concatenate(
         pairs + keeps + [share] * (masks_ref.shape[0] - len(pairs) - len(keeps)), 0
     )
-    size = near_ref.shape[1] // 2
-    for o in range(OWNERS):
-        near_ref[o, :size] = held[o * size : (o + 1) * size].astype(jnp.bfloat16)
-        near_ref[o, size:] = all_ref[o * size : (o + 1) * size]
+    size = rights[0].shape[0]
+    for d, ref in enumerate(outs):
+        ref[:size] = owner_block(held, d, size)
+        ref[size:] = rights[d][...]
+
+
+def pack_kernel(*refs):
+    size = refs[0].shape[0]
+    for at, ref in enumerate(refs[:-1]):
+        refs[-1][at * size : (at + 1) * size] = ref[...]
 
 
 def gate_kernel(x_ref, normed_ref, gw_ref, ow_ref, dw_ref, gate_ref, x_turned_ref, ow_turned, dw_turned):
@@ -136,25 +143,25 @@
         x_turned_ref[:, at] = x.T
 
 
-def tri_kernel(masks_ref, near_ref, near_over_ref, *refs):
-    far, far_over = refs[:OWNERS], refs[OWNERS : 2 * OWNERS]
-    outs, rights = refs[2 * OWNERS : -1], refs[-1]
+def tri_kernel(masks_ref, far_over, *refs):
+    near, far, near_over = [refs[at * OWNERS : (at + 1) * OWNERS] for at in range(3)]
+    outs, rights = refs[3 * OWNERS : -1], refs[-1]
     size, width = far[0].shape
     half = rights.shape[1]
     tile_rows = size // half
     side = width // 2
-    me, col, owner = lax.axis_index("row"), lax.axis_index("col"), owner_place()
+    me, col = lax.axis_index("row"), lax.axis_index("col")
     for d in range(OWNERS):
-        away = d // 2 * 2
-        for step, load in (
-            (0, lambda at: near_ref[owner ^ d, size + at : size + at + tile_rows]),
-            (1, lambda at: near_over_ref[owner ^ d, size + at : size + at + tile_rows]),
-            (4, lambda at: far[d][at : at + tile_rows]),
-            (5, lambda at: far_over[d][at : at + tile_rows]),
+        for step, ref, start in (
+            (0, near[d], size),
+            (1, near_over[d], near_over[d].shape[0] - size),
+            (4, far[d], 0),
+            (5, far_over, d * size),
         ):
-            place = pl.multiple_of((me ^ (away + step)) * tile_rows, tile_rows)
+            place = pl.multiple_of((me ^ (d // 2 * 2 + step)) * tile_rows, tile_rows)
             for m in range(half):
-                rights[d % 2, m, pl.ds(place, tile_rows), :] = load(m * tile_rows)
+                at = start + m * tile_rows
+                rights[d % 2, m, pl.ds(place, tile_rows), :] = ref[at : at + tile_rows]
     low = lanes_of((side, width)) < side
     first = masks_ref.shape[0] // 2
     keep = jnp.concatenate([masks_ref[first : first + 1], masks_ref[first + 1 : first + 2]], 1)
@@ -162,7 +169,7 @@
         at = slice(m * tile_rows, (m + 1) * tile_rows)
         product = 0.0
         for dk in (0, 1):
-            left = jnp.concatenate([near_ref[owner ^ dk, at], near_ref[owner ^ (2 + dk), at]], 0)
+            left = jnp.concatenate([near[dk][at], near[2 + dk][at]], 0)
             pieces = []
             for dx in (0, 1):
                 block = rights[dk, m, pl.ds(pl.multiple_of((col ^ dx) * side, side), side), :]
@@ -276,36 +283,32 @@
     normed = call(
         norm_kernel, struct((spots, channels), bf16), args=(pair_repr,), flops=1 << 30
     )
-    whole, *rights = call(
+    rights = call(
         right_kernel,
-        [struct((OWNERS * size, width), bf16)] + [struct((size, width), bf16)] * OWNERS,
+        [struct((size, width), bf16)] * OWNERS,
         [turned, held],
         args=(normed, right_weight, right_gate_weight),
         flops=4 * spots * channels * channels,
     )
     over = [d // 2 * over_z + d % 2 * over_x for d in range(OWNERS)]
     far = [exchange(rights[d], places, over_half + over[d]) for d in range(OWNERS)]
-    near, masks = call(
+    *near, masks = call(
         left_kernel,
-        [struct((OWNERS, 2 * size, width), bf16), struct((tile_rows, width), f32)],
+        [struct((2 * size, width), bf16)] * OWNERS + [struct((tile_rows, width), f32)],
         [turned, held],
-        [SMEM] + [VMEM] * 4,
-        args=(chain_lengths, normed, left_weight, left_gate_weight, whole),
+        [SMEM] + [VMEM] * (3 + OWNERS),
+        args=(chain_lengths, normed, left_weight, left_gate_weight, *rights),
         flops=4 * spots * channels * channels,
     )
-    sides = [
-        [part * over_half + z * over_z + core * over_core + x for z in (0, 1) for x in (0, 1)]
-        for part in (0, 1)
-        for core in (0, 1)
-    ]
-    near = lax.all_to_all(near, AXES, 0, 0, axis_index_groups=sides, tiled=True)
-    near_over = exchange(near, places, over_core)
-    far_over = [exchange(value, places, over_core) for value in far]
+    near = [near[0]] + [exchange(near[d], places, over[d]) for d in range(1, OWNERS)]
+    near_over = [exchange(value, places, over_core) for value in (rights[0], *near[1:])]
+    far_over = call(pack_kernel, struct((OWNERS * size, width), bf16), args=far)
+    far_over = exchange(far_over, places, over_core)
     parts = call(
         tri_kernel,
         [struct((size, width), bf16)] * OWNERS,
         [pltpu.VMEM((cols, size // tile_rows, rows * tile_rows, width), bf16)],
-        args=(masks, near, near_over, *far, *far_over),
+        args=(masks, far_over, *near, *far, *near_over),
         flops=8 * size * 2 * tile_rows * 2 * width,
     )
     parts = [parts[0]] + [exchange(parts[d], places, over[d]) for d in range(1, OWNERS)]

time: 56.2 us -> 48.6 us (0.86)
  blocking collectives: 13.5 us -> 0 us
  starting transfers between devices: 16.7 us -> 23.1 us
  local copies, waits for them, and re-layouts: 2.74 us -> 2.1 us
    all_to_all x1 -> x0, blocking collectives: 13.5 us -> none  [by_kernels(): near = lax.all_to_all(near, AXES, 0, 0, axis_index_groups=sides, tiled=True)]
    ppermute x12 -> x15, starting transfers between devices: 12.3 us -> 17.8 us  [exchange(): return lax.ppermute(value, AXES, [(at, at ^ mask) for at in range(places)])]
    all_to_all x1, starting transfers between devices: 4.44 us -> 5.34 us  [by_kernels(): loss = lax.all_to_all(loss, AXES, 0, 0, tiled=True)]
    unnamed x23, local copies, waits for them, and re-layouts: 2.16 us -> 1.51 us
    ppermute x12 -> x15, waiting for transfers between devices: 10.5 us -> 10.8 us  [exchange(): return lax.ppermute(value, AXES, [(at, at ^ mask) for at in range(places)])]
    pallas_call x7 -> x8, Pallas kernels: 5.68 us -> 5.69 us  [call(): pl.pallas_call(kernel, out_shape=outs, in_specs=specs if specs is not Non...]
  transfers between devices with their start and end apart: 13 -> 16, of which waited for: 9 -> 10; matrix products, arithmetic and copies ran while one was open for 0% -> 0% of each run, Pallas kernels for 2% -> 5%
where the time goes in v8:
time: 48.6 us; the launch traced here: 48.3 us
  starting transfers between devices  23.1 us (48%)
  waiting for transfers between devices  16.6 us (34%)
  Pallas kernels  5.69 us (12%)
  local copies, waits for them, and re-layouts  2.1 us (4%)
  between operations  0.81 us (2%)
    ppermute x15, starting transfers between devices, exchange(): return lax.ppermute(value, AXES, [(at, at ^ mask) for at in range(places)])  17.8 us
    ppermute x15, waiting for transfers between devices, exchange(): return lax.ppermute(value, AXES, [(at, at ^ mask) for at in range(places)])  10.8 us
    all_to_all x1, waiting for transfers between devices, by_kernels(): loss = lax.all_to_all(loss, AXES, 0, 0, tiled=True)  5.83 us
    pallas_call x8, Pallas kernels, call(): pl.pallas_call(kernel, out_shape=outs, in_specs=specs if specs is not Non...  5.69 us
    all_to_all x1, starting transfers between devices, by_kernels(): loss = lax.all_to_all(loss, AXES, 0, 0, tiled=True)  5.34 us
    unnamed x23, local copies, waits for them, and re-layouts  1.51 us
  transfers between devices with their start and end apart: 16, of which 10 were waited for; matrix products, arithmetic and copies ran while one was open for 0% of the time, Pallas kernels for 5%

profile of v8, /device:TPU:0, one launch (start us, length us, event | category | flops | bytes accessed | tf_op | source)
XLA Modules:
  0.0 48.3 jit_solution(6725915969697916426)
XLA Ops:
  0.6 0.0 copy-start
  0.6 0.9 %copy-done = bf16[16,64,128]{2,1,0:T(8,128)(2,1)S(1)} copy-done((bf16[16,64,128]{2,1,0:T(8,128)(2,1)S(1)}, bf16[16,64,128]{2,1,0:T(8,128)(2,1)}, u32[]{:S(2)}) %copy-start) | copy-done | bytes 262168
  1.6 0.0 copy-start.7
  1.6 0.0 copy-start.8
  1.6 0.4 shard_map.113.normed_ref
  1.9 0.4 copy-done.7
  2.3 0.0 copy-done.8
  2.4 0.0 copy-start.4
  2.4 0.0 copy-start.5
  2.4 0.6 %shard_map.114 = (bf16[256,128]{1,0:T(8,128)(2,1)S(1)}, bf16[256,128]{1,0:T(8,128)(2,1)S(1)}, bf16[256,128]{1,0:T(8,128)(2,1)S(1)}, bf16[256,128]{1,0:T(8,128)(2,1)S(1)}) custom-call(bf16[1024,128]{1,0:T(8,128)(2,1)S(1)} %shard_map.113.normed_ref, bf16[128,128]{1,0:T(8,128)(2,1)S(1)} %copy-done.7, bf16[128,128]{1,0:T(8,128)(2,1)S(1)} %copy-done.8), custom_call_target="tpu_custom_call" | custom-call | flops 67108864 | bytes 1048576 | tf_op jit(solution)/shard_map/pallas_call | solution.py:249
  2.9 4.1 %collective-permute-start = (bf16[256,128]{1,0:T(8,128)(2,1)S(1)}, bf16[256,128]{1,0:T(8,128)(2,1)S(1)}, u32[]{:S(2)}, u32[]{:S(2)}) collective-permute-start(bf16[256,128]{1,0:T(8,128)(2,1)S(1)} %get-tuple-element.21.refs_0_), channel_id=1, source_target_pairs={{0,8},{1,9},{2,10},{3,11},{4,12},{5,13},{6,14},{7,15},{8,0},{9,1},... | collective-permute-start | bytes 196616 | tf_op jit(solution)/shard_map/ppermute | solution.py:245
  7.0 1.3 %collective-permute-start.1 = (bf16[256,128]{1,0:T(8,128)(2,1)S(1)}, bf16[256,128]{1,0:T(8,128)(2,1)S(1)}, u32[]{:S(2)}, u32[]{:S(2)}) collective-permute-start(bf16[256,128]{1,0:T(8,128)(2,1)S(1)} %get-tuple-element.22.refs_1_), channel_id=1, source_target_pairs={{0,9},{1,8},{2,11},{3,10},{4,13},{5,12},{6,15},{7,14},{8,1},{9,0},... | collective-permute-start | bytes 196616 | tf_op jit(solution)/shard_map/ppermute | solution.py:245
  8.3 0.0 copy-start.6
  8.3 3.6 %collective-permute-start.2 = (bf16[256,128]{1,0:T(8,128)(2,1)S(1)}, bf16[256,128]{1,0:T(8,128)(2,1)S(1)}, u32[]{:S(2)}, u32[]{:S(2)}) collective-permute-start(bf16[256,128]{1,0:T(8,128)(2,1)S(1)} %get-tuple-element.23.refs_2_), channel_id=1, source_target_pairs={{0,12},{1,13},{2,14},{3,15},{4,8},{5,9},{6,10},{7,11},{8,4},{9,5},... | collective-permute-start | bytes 196616 | tf_op jit(solution)/shard_map/ppermute | solution.py:245
  11.9 0.0 collective-permute-start.3
  11.9 0.0 copy-done.4
  11.9 0.0 copy-done.5
  11.9 0.0 copy-done.6
  11.9 1.1 %shard_map.115 = (bf16[512,128]{1,0:T(8,128)(2,1)S(1)}, bf16[512,128]{1,0:T(8,128)(2,1)S(1)}, bf16[512,128]{1,0:T(8,128)(2,1)S(1)}, bf16[512,128]{1,0:T(8,128)(2,1)S(1)}, f32[16,128]{1,0:T(8,128)S(1)}) custom-call(s32[5]{0:T(128)S(1)} %copy-done.6, bf16[1024,128]{1,0:T(8,128)(2,1)S(1)} %shard_map.113.normed_ref, bf16[128,128]{1,0:T(8,128)(2,1)S(1)} %copy-done.4, ...), custom_call_target="tpu_custom_call" | custom-call | flops 67108864 | bytes 1048576 | tf_op jit(solution)/shard_map/pallas_call | solution.py:249
  13.1 0.1 collective-permute-start.6
  13.1 0.0 collective-permute-done.refs_0_.refs_4_
  13.1 3.1 %collective-permute-start.7 = (bf16[512,128]{1,0:T(8,128)(2,1)S(1)}, bf16[512,128]{1,0:T(8,128)(2,1)S(1)}, u32[]{:S(2)}, u32[]{:S(2)}) collective-permute-start(bf16[512,128]{1,0:T(8,128)(2,1)S(1)} %get-tuple-element.33), channel_id=1, source_target_pairs={{0,5},{1,4},{2,7},{3,6},{4,1},{5,0},{6,3},{7,2},{8,13},{9,12},{10,... | collective-permute-start | bytes 393224 | tf_op jit(solution)/shard_map/ppermute | solution.py:245
  16.3 0.8 %collective-permute-done.1.refs_1_.refs_5_ = bf16[256,128]{1,0:T(8,128)(2,1)S(1)} collective-permute-done((bf16[256,128]{1,0:T(8,128)(2,1)S(1)}, bf16[256,128]{1,0:T(8,128)(2,1)S(1)}, u32[]{:S(2)}, u32[]{:S(2)}) %collective-permute-start.1) | collective-permute-done | bytes 65568 | tf_op jit(solution)/shard_map/ppermute | solution.py:245
  17.1 1.5 %collective-permute-start.5 = (bf16[512,128]{1,0:T(8,128)(2,1)S(1)}, bf16[512,128]{1,0:T(8,128)(2,1)S(1)}, u32[]{:S(2)}, u32[]{:S(2)}) collective-permute-start(bf16[512,128]{1,0:T(8,128)(2,1)S(1)} %get-tuple-element.31), channel_id=1, source_target_pairs={{0,1},{1,0},{2,3},{3,2},{4,5},{5,4},{6,7},{7,6},{8,9},{9,8},{10,11... | collective-permute-start | bytes 393224 | tf_op jit(solution)/shard_map/ppermute | solution.py:245
  18.6 0.0 collective-permute-done.2.refs_2_.refs_6_
  18.6 1.0 %collective-permute-done.3.refs_3_.refs_7_ = bf16[256,128]{1,0:T(8,128)(2,1)S(1)} collective-permute-done((bf16[256,128]{1,0:T(8,128)(2,1)S(1)}, bf16[256,128]{1,0:T(8,128)(2,1)S(1)}, u32[]{:S(2)}, u32[]{:S(2)}) %collective-permute-start.3) | collective-permute-done | bytes 65568 | tf_op jit(solution)/shard_map/ppermute | solution.py:245
  19.5 0.1 collective-permute-start.4
  19.6 0.8 %collective-permute-done.6.refs_2_ = bf16[512,128]{1,0:T(8,128)(2,1)S(1)} collective-permute-done((bf16[512,128]{1,0:T(8,128)(2,1)S(1)}, bf16[512,128]{1,0:T(8,128)(2,1)S(1)}, u32[]{:S(2)}, u32[]{:S(2)}) %collective-permute-start.6) | collective-permute-done | bytes 131104 | tf_op jit(solution)/shard_map/ppermute | solution.py:245
  20.5 0.0 collective-permute-start.10
  20.5 2.6 %collective-permute-done.7.refs_3_ = bf16[512,128]{1,0:T(8,128)(2,1)S(1)} collective-permute-done((bf16[512,128]{1,0:T(8,128)(2,1)S(1)}, bf16[512,128]{1,0:T(8,128)(2,1)S(1)}, u32[]{:S(2)}, u32[]{:S(2)}) %collective-permute-start.7) | collective-permute-done | bytes 131104 | tf_op jit(solution)/shard_map/ppermute | solution.py:245
  23.1 0.0 collective-permute-start.11
  23.1 1.5 %collective-permute-done.5.refs_1_ = bf16[512,128]{1,0:T(8,128)(2,1)S(1)} collective-permute-done((bf16[512,128]{1,0:T(8,128)(2,1)S(1)}, bf16[512,128]{1,0:T(8,128)(2,1)S(1)}, u32[]{:S(2)}, u32[]{:S(2)}) %collective-permute-start.5) | collective-permute-done | bytes 131104 | tf_op jit(solution)/shard_map/ppermute | solution.py:245
  24.6 0.0 collective-permute-start.9
  24.6 0.5 %collective-permute-start.8 = (bf16[256,128]{1,0:T(8,128)(2,1)S(1)}, bf16[256,128]{1,0:T(8,128)(2,1)S(1)}, u32[]{:S(2)}, u32[]{:S(2)}) collective-permute-start(bf16[256,128]{1,0:T(8,128)(2,1)S(1)} %get-tuple-element.21.refs_0_), channel_id=1, source_target_pairs={{0,2},{1,3},{2,0},{3,1},{4,6},{5,7},{6,4},{7,5},{8,10},{9,11},{10,... | collective-permute-start | bytes 196616 | tf_op jit(solution)/shard_map/ppermute | solution.py:245
  25.1 0.9 %collective-permute-done.8.refs_8_ = bf16[256,128]{1,0:T(8,128)(2,1)S(1)} collective-permute-done((bf16[256,128]{1,0:T(8,128)(2,1)S(1)}, bf16[256,128]{1,0:T(8,128)(2,1)S(1)}, u32[]{:S(2)}, u32[]{:S(2)}) %collective-permute-start.8) | collective-permute-done | bytes 65568 | tf_op jit(solution)/shard_map/ppermute | solution.py:245
  26.1 0.0 collective-permute-done.10.refs_10_
  26.1 0.0 collective-permute-done.11.refs_11_
  26.1 0.0 collective-permute-done.9.refs_9_
  26.1 0.0 collective-permute-done.4.far_over
  26.1 0.0 copy-start.9
  26.1 0.0 copy-start.10
  26.1 0.0 copy-start.1
  26.1 0.9 %shard_map.118 = (bf16[256,128]{1,0:T(8,128)(2,1)S(1)}, bf16[256,128]{1,0:T(8,128)(2,1)S(1)}, bf16[256,128]{1,0:T(8,128)(2,1)S(1)}, bf16[256,128]{1,0:T(8,128)(2,1)S(1)}) custom-call(f32[16,128]{1,0:T(8,128)S(1)} %get-tuple-element.25.masks_ref, bf16[1024,128]{1,0:T(8,128)(2,1)S(1)} %collective-permute-done.4.far_over, ...), custom_call_target="tpu_custom_call" | custom-call | flops 16777216 | bytes 1048576 | tf_op jit(solution)/shard_map/pallas_call | solution.py:249
  27.0 0.0 copy-start.3
  27.0 0.0 copy-start.2
  27.1 1.0 %collective-permute-start.12 = (bf16[256,128]{1,0:T(8,128)(2,1)S(1)}, bf16[256,128]{1,0:T(8,128)(2,1)S(1)}, u32[]{:S(2)}, u32[]{:S(2)}) collective-permute-start(bf16[256,128]{1,0:T(8,128)(2,1)S(1)} %get-tuple-element.35), channel_id=1, source_target_pairs={{0,1},{1,0},{2,3},{3,2},{4,5},{5,4},{6,7},{7,6},{8,9},{9,8},{10,11... | collective-permute-start | bytes 196616 | tf_op jit(solution)/shard_map/ppermute | solution.py:245
  28.0 0.9 %collective-permute-start.13 = (bf16[256,128]{1,0:T(8,128)(2,1)S(1)}, bf16[256,128]{1,0:T(8,128)(2,1)S(1)}, u32[]{:S(2)}, u32[]{:S(2)}) collective-permute-start(bf16[256,128]{1,0:T(8,128)(2,1)S(1)} %get-tuple-element.36), channel_id=1, source_target_pairs={{0,4},{1,5},{2,6},{3,7},{4,0},{5,1},{6,2},{7,3},{8,12},{9,13},{10,... | collective-permute-start | bytes 196616 | tf_op jit(solution)/shard_map/ppermute | solution.py:245
  29.0 1.7 %collective-permute-start.14 = (bf16[256,128]{1,0:T(8,128)(2,1)S(1)}, bf16[256,128]{1,0:T(8,128)(2,1)S(1)}, u32[]{:S(2)}, u32[]{:S(2)}) collective-permute-start(bf16[256,128]{1,0:T(8,128)(2,1)S(1)} %get-tuple-element.37), channel_id=1, source_target_pairs={{0,5},{1,4},{2,7},{3,6},{4,1},{5,0},{6,3},{7,2},{8,13},{9,12},{10,... | collective-permute-start | bytes 196616 | tf_op jit(solution)/shard_map/ppermute | solution.py:245
  30.6 0.0 copy-done.9
  30.6 0.1 copy.12.dw_ref
  30.7 0.0 copy-done.10
  30.7 0.1 reshape.7.bins_ref
  30.8 0.0 copy-done.1
  30.8 0.0 copy-done.3
  30.8 0.0 copy-done.2
  30.8 0.4 shard_map.116
  31.2 0.3 collective-permute-done.12.refs_1_
  31.4 1.2 %collective-permute-done.13.refs_2_ = bf16[256,128]{1,0:T(8,128)(2,1)S(1)} collective-permute-done((bf16[256,128]{1,0:T(8,128)(2,1)S(1)}, bf16[256,128]{1,0:T(8,128)(2,1)S(1)}, u32[]{:S(2)}, u32[]{:S(2)}) %collective-permute-start.13) | collective-permute-done | bytes 65568 | tf_op jit(solution)/shard_map/ppermute | solution.py:245
  32.7 1.6 %collective-permute-done.14.refs_3_ = bf16[256,128]{1,0:T(8,128)(2,1)S(1)} collective-permute-done((bf16[256,128]{1,0:T(8,128)(2,1)S(1)}, bf16[256,128]{1,0:T(8,128)(2,1)S(1)}, u32[]{:S(2)}, u32[]{:S(2)}) %collective-permute-start.14) | collective-permute-done | bytes 65568 | tf_op jit(solution)/shard_map/ppermute | solution.py:245
  34.3 1.5 %shard_map.119 = (bf16[128,1024]{1,0:T(8,128)(2,1)S(1)}, f32[16,8,128]{2,1,0:T(8,128)}) custom-call(f32[16,128]{1,0:T(8,128)S(1)} %get-tuple-element.25.masks_ref, f32[128,1024]{1,0:T(8,128)S(1)} %get-tuple-element.26.x_ref, f32[128,1024]{1,0:T(8,128)S(1)} %get-tuple-element.27.gate_ref, s32[8,128]{1,0:T(8,128)S(1)} %reshape.7.bins_ref, ...), custom_call_target="tpu_custom_call" | custom-call | flops 100663296 | bytes 1048576 | tf_op jit(solution)/shard_map/pallas_call | solution.py:249
  35.8 5.3 %all-to-all-start = ((f32[16,8,128]{2,1,0:T(8,128)}), f32[16,8,128]{2,1,0:T(8,128)S(1)}, u32[]{:S(2)}, u32[]{:S(2)}) async-start(f32[16,8,128]{2,1,0:T(8,128)} %get-tuple-element.39), calls=%async_computation | async-start | bytes 131072 | tf_op jit(solution)/shard_map/all_to_all | solution.py:342
  41.1 0.8 %shard_map.120 = bf16[16,64,128]{2,1,0:T(8,128)(2,1)} custom-call(bf16[128,1024]{1,0:T(8,128)(2,1)S(1)} %get-tuple-element.38.turned_ref), custom_call_target="tpu_custom_call" | custom-call | flops 67108864 | bytes 1048576 | tf_op jit(solution)/shard_map/pallas_call | solution.py:249
  42.0 5.8 %all-to-all-done = f32[16,8,128]{2,1,0:T(8,128)S(1)} async-done(((f32[16,8,128]{2,1,0:T(8,128)}), f32[16,8,128]{2,1,0:T(8,128)S(1)}, u32[]{:S(2)}, u32[]{:S(2)}) %all-to-all-start) | async-done | bytes 65568 | tf_op jit(solution)/shard_map/all_to_all | solution.py:342
  47.8 0.5 %slice.3 = f32[1,1]{1,0:T(1,128)} slice(f32[8,128]{1,0:T(8,128)S(1)} %reduce_sum.9), slice={[0:1], [0:1]} | slice | bytes 8 | tf_op jit(solution)/shard_map/slice | solution.py:343
  (2 shorter events, 0.0 us)
Async XLA Ops:
  0.6 1.0 %copy-start = (bf16[16,64,128]{2,1,0:T(8,128)(2,1)S(1)}, bf16[16,64,128]{2,1,0:T(8,128)(2,1)}, u32[]{:S(2)}) copy-start(bf16[16,64,128]{2,1,0:T(8,128)(2,1)} %x_ref.3) | copy-start | bytes 786436
  1.6 0.8 %copy-start.7 = (bf16[128,128]{1,0:T(8,128)(2,1)S(1)}, bf16[128,128]{1,0:T(8,128)(2,1)}, u32[]{:S(2)}) copy-start(bf16[128,128]{1,0:T(8,128)(2,1)} %w_ref.2) | copy-start | bytes 98308
  1.6 0.8 %copy-start.8 = (bf16[128,128]{1,0:T(8,128)(2,1)S(1)}, bf16[128,128]{1,0:T(8,128)(2,1)}, u32[]{:S(2)}) copy-start(bf16[128,128]{1,0:T(8,128)(2,1)} %g_ref.2) | copy-start | bytes 98308
  2.4 9.5 %copy-start.4 = (bf16[128,128]{1,0:T(8,128)(2,1)S(1)}, bf16[128,128]{1,0:T(8,128)(2,1)}, u32[]{:S(2)}) copy-start(bf16[128,128]{1,0:T(8,128)(2,1)} %w_ref.3) | copy-start | bytes 98308
  2.4 9.5 %copy-start.5 = (bf16[128,128]{1,0:T(8,128)(2,1)S(1)}, bf16[128,128]{1,0:T(8,128)(2,1)}, u32[]{:S(2)}) copy-start(bf16[128,128]{1,0:T(8,128)(2,1)} %g_ref.3) | copy-start | bytes 98308
  2.9 10.2 %collective-permute-start = (bf16[256,128]{1,0:T(8,128)(2,1)S(1)}, bf16[256,128]{1,0:T(8,128)(2,1)S(1)}, u32[]{:S(2)}, u32[]{:S(2)}) collective-permute-start(bf16[256,128]{1,0:T(8,128)(2,1)S(1)} %get-tuple-element.21.refs_0_), channel_id=1, source_target_pairs={{0,8},{1,9},{2,10},{3,11},{4,12},{5,13},{6,14},{7,15},{8,0},{9,1},... | collective-permute-start | bytes 196616 | tf_op jit(solution)/shard_map/ppermute | solution.py:245
  7.0 10.0 %collective-permute-start.1 = (bf16[256,128]{1,0:T(8,128)(2,1)S(1)}, bf16[256,128]{1,0:T(8,128)(2,1)S(1)}, u32[]{:S(2)}, u32[]{:S(2)}) collective-permute-start(bf16[256,128]{1,0:T(8,128)(2,1)S(1)} %get-tuple-element.22.refs_1_), channel_id=1, source_target_pairs={{0,9},{1,8},{2,11},{3,10},{4,13},{5,12},{6,15},{7,14},{8,1},{9,0},... | collective-permute-start | bytes 196616 | tf_op jit(solution)/shard_map/ppermute | solution.py:245
  8.3 3.6 %copy-start.6 = (s32[5]{0:T(128)S(1)}, s32[5]{0:T(128)}, u32[]{:S(2)}) copy-start(s32[5]{0:T(128)} %lens_ref.1) | copy-start | bytes 64
  8.3 10.3 %collective-permute-start.2 = (bf16[256,128]{1,0:T(8,128)(2,1)S(1)}, bf16[256,128]{1,0:T(8,128)(2,1)S(1)}, u32[]{:S(2)}, u32[]{:S(2)}) collective-permute-start(bf16[256,128]{1,0:T(8,128)(2,1)S(1)} %get-tuple-element.23.refs_2_), channel_id=1, source_target_pairs={{0,12},{1,13},{2,14},{3,15},{4,8},{5,9},{6,10},{7,11},{8,4},{9,5},... | collective-permute-start | bytes 196616 | tf_op jit(solution)/shard_map/ppermute | solution.py:245
  11.9 7.6 %collective-permute-start.3 = (bf16[256,128]{1,0:T(8,128)(2,1)S(1)}, bf16[256,128]{1,0:T(8,128)(2,1)S(1)}, u32[]{:S(2)}, u32[]{:S(2)}) collective-permute-start(bf16[256,128]{1,0:T(8,128)(2,1)S(1)} %get-tuple-element.24.refs_3_), channel_id=1, source_target_pairs={{0,13},{1,12},{2,15},{3,14},{4,9},{5,8},{6,11},{7,10},{8,5},{9,4},... | collective-permute-start | bytes 196616 | tf_op jit(solution)/shard_map/ppermute | solution.py:245
  13.1 7.4 %collective-permute-start.6 = (bf16[512,128]{1,0:T(8,128)(2,1)S(1)}, bf16[512,128]{1,0:T(8,128)(2,1)S(1)}, u32[]{:S(2)}, u32[]{:S(2)}) collective-permute-start(bf16[512,128]{1,0:T(8,128)(2,1)S(1)} %get-tuple-element.32), channel_id=1, source_target_pairs={{0,4},{1,5},{2,6},{3,7},{4,0},{5,1},{6,2},{7,3},{8,12},{9,13},{10,... | collective-permute-start | bytes 393224 | tf_op jit(solution)/shard_map/ppermute | solution.py:245
  13.1 10.0 %collective-permute-start.7 = (bf16[512,128]{1,0:T(8,128)(2,1)S(1)}, bf16[512,128]{1,0:T(8,128)(2,1)S(1)}, u32[]{:S(2)}, u32[]{:S(2)}) collective-permute-start(bf16[512,128]{1,0:T(8,128)(2,1)S(1)} %get-tuple-element.33), channel_id=1, source_target_pairs={{0,5},{1,4},{2,7},{3,6},{4,1},{5,0},{6,3},{7,2},{8,13},{9,12},{10,... | collective-permute-start | bytes 393224 | tf_op jit(solution)/shard_map/ppermute | solution.py:245
  17.1 7.5 %collective-permute-start.5 = (bf16[512,128]{1,0:T(8,128)(2,1)S(1)}, bf16[512,128]{1,0:T(8,128)(2,1)S(1)}, u32[]{:S(2)}, u32[]{:S(2)}) collective-permute-start(bf16[512,128]{1,0:T(8,128)(2,1)S(1)} %get-tuple-element.31), channel_id=1, source_target_pairs={{0,1},{1,0},{2,3},{3,2},{4,5},{5,4},{6,7},{7,6},{8,9},{9,8},{10,11... | collective-permute-start | bytes 393224 | tf_op jit(solution)/shard_map/ppermute | solution.py:245
  19.5 6.5 %collective-permute-start.4 = (bf16[1024,128]{1,0:T(8,128)(2,1)S(1)}, bf16[1024,128]{1,0:T(8,128)(2,1)S(1)}, u32[]{:S(2)}, u32[]{:S(2)}) collective-permute-start(bf16[1024,128]{1,0:T(8,128)(2,1)S(1)} %shard_map.117), channel_id=1, source_target_pairs={{0,2},{1,3},{2,0},{3,1},{4,6},{5,7},{6,4},{7,5},{8,10},{9,11},{10,... | collective-permute-start | bytes 786440 | tf_op jit(solution)/shard_map/ppermute | solution.py:245
  20.5 5.6 %collective-permute-start.10 = (bf16[512,128]{1,0:T(8,128)(2,1)S(1)}, bf16[512,128]{1,0:T(8,128)(2,1)S(1)}, u32[]{:S(2)}, u32[]{:S(2)}) collective-permute-start(bf16[512,128]{1,0:T(8,128)(2,1)S(1)} %collective-permute-done.6.refs_2_), channel_id=1, source_target_pairs={{0,2},{1,3},{2,0},{3,1},{4,6},{5,7},{6,4},{7,5},{8,10},{9,11},{10,... | collective-permute-start | bytes 393224 | tf_op jit(solution)/shard_map/ppermute | solution.py:245
  23.1 2.9 %collective-permute-start.11 = (bf16[512,128]{1,0:T(8,128)(2,1)S(1)}, bf16[512,128]{1,0:T(8,128)(2,1)S(1)}, u32[]{:S(2)}, u32[]{:S(2)}) collective-permute-start(bf16[512,128]{1,0:T(8,128)(2,1)S(1)} %collective-permute-done.7.refs_3_), channel_id=1, source_target_pairs={{0,2},{1,3},{2,0},{3,1},{4,6},{5,7},{6,4},{7,5},{8,10},{9,11},{10,... | collective-permute-start | bytes 393224 | tf_op jit(solution)/shard_map/ppermute | solution.py:245
  24.6 1.5 %collective-permute-start.9 = (bf16[512,128]{1,0:T(8,128)(2,1)S(1)}, bf16[512,128]{1,0:T(8,128)(2,1)S(1)}, u32[]{:S(2)}, u32[]{:S(2)}) collective-permute-start(bf16[512,128]{1,0:T(8,128)(2,1)S(1)} %collective-permute-done.5.refs_1_), channel_id=1, source_target_pairs={{0,2},{1,3},{2,0},{3,1},{4,6},{5,7},{6,4},{7,5},{8,10},{9,11},{10,... | collective-permute-start | bytes 393224 | tf_op jit(solution)/shard_map/ppermute | solution.py:245
  24.6 1.4 %collective-permute-start.8 = (bf16[256,128]{1,0:T(8,128)(2,1)S(1)}, bf16[256,128]{1,0:T(8,128)(2,1)S(1)}, u32[]{:S(2)}, u32[]{:S(2)}) collective-permute-start(bf16[256,128]{1,0:T(8,128)(2,1)S(1)} %get-tuple-element.21.refs_0_), channel_id=1, source_target_pairs={{0,2},{1,3},{2,0},{3,1},{4,6},{5,7},{6,4},{7,5},{8,10},{9,11},{10,... | collective-permute-start | bytes 196616 | tf_op jit(solution)/shard_map/ppermute | solution.py:245
  26.1 4.5 %copy-start.9 = (bf16[128,64]{0,1:T(8,128)(2,1)S(1)}, bf16[128,64]{0,1:T(8,128)(2,1)}, u32[]{:S(2)}) copy-start(bf16[128,64]{0,1:T(8,128)(2,1)} %param.19) | copy-start | bytes 49156
  26.1 4.6 %copy-start.10 = (s32[16,64]{1,0:T(8,128)S(1)}, s32[16,64]{1,0:T(8,128)}, u32[]{:S(2)}) copy-start(s32[16,64]{1,0:T(8,128)} %param.11) | copy-start | bytes 12292
  26.1 4.7 %copy-start.1 = (bf16[16,64,128]{2,1,0:T(8,128)(2,1)S(1)}, bf16[16,64,128]{2,1,0:T(8,128)(2,1)}, u32[]{:S(2)}) copy-start(bf16[16,64,128]{2,1,0:T(8,128)(2,1)} %x_ref.3) | copy-start | bytes 786436
  27.0 3.8 %copy-start.3 = (bf16[128,128]{1,0:T(8,128)(2,1)S(1)}, bf16[128,128]{1,0:T(8,128)(2,1)}, u32[]{:S(2)}) copy-start(bf16[128,128]{1,0:T(8,128)(2,1)} %ow_ref.1) | copy-start | bytes 98308
  27.0 3.8 %copy-start.2 = (bf16[128,128]{1,0:T(8,128)(2,1)S(1)}, bf16[128,128]{1,0:T(8,128)(2,1)}, u32[]{:S(2)}) copy-start(bf16[128,128]{1,0:T(8,128)(2,1)} %gw_ref.1) | copy-start | bytes 98308
  27.1 4.4 %collective-permute-start.12 = (bf16[256,128]{1,0:T(8,128)(2,1)S(1)}, bf16[256,128]{1,0:T(8,128)(2,1)S(1)}, u32[]{:S(2)}, u32[]{:S(2)}) collective-permute-start(bf16[256,128]{1,0:T(8,128)(2,1)S(1)} %get-tuple-element.35), channel_id=1, source_target_pairs={{0,1},{1,0},{2,3},{3,2},{4,5},{5,4},{6,7},{7,6},{8,9},{9,8},{10,11... | collective-permute-start | bytes 196616 | tf_op jit(solution)/shard_map/ppermute | solution.py:245
  28.0 4.6 %collective-permute-start.13 = (bf16[256,128]{1,0:T(8,128)(2,1)S(1)}, bf16[256,128]{1,0:T(8,128)(2,1)S(1)}, u32[]{:S(2)}, u32[]{:S(2)}) collective-permute-start(bf16[256,128]{1,0:T(8,128)(2,1)S(1)} %get-tuple-element.36), channel_id=1, source_target_pairs={{0,4},{1,5},{2,6},{3,7},{4,0},{5,1},{6,2},{7,3},{8,12},{9,13},{10,... | collective-permute-start | bytes 196616 | tf_op jit(solution)/shard_map/ppermute | solution.py:245
  29.0 5.3 %collective-permute-start.14 = (bf16[256,128]{1,0:T(8,128)(2,1)S(1)}, bf16[256,128]{1,0:T(8,128)(2,1)S(1)}, u32[]{:S(2)}, u32[]{:S(2)}) collective-permute-start(bf16[256,128]{1,0:T(8,128)(2,1)S(1)} %get-tuple-element.37), channel_id=1, source_target_pairs={{0,5},{1,4},{2,7},{3,6},{4,1},{5,0},{6,3},{7,2},{8,13},{9,12},{10,... | collective-permute-start | bytes 196616 | tf_op jit(solution)/shard_map/ppermute | solution.py:245
  35.8 12.0 %all-to-all-start = ((f32[16,8,128]{2,1,0:T(8,128)}), f32[16,8,128]{2,1,0:T(8,128)S(1)}, u32[]{:S(2)}, u32[]{:S(2)}) async-start(f32[16,8,128]{2,1,0:T(8,128)} %get-tuple-element.39), calls=%async_computation | async-start | bytes 131072 | tf_op jit(solution)/shard_map/all_to_all | solution.py:342

commit v9 on v6

--- a/solution.py
+++ b/solution.py
@@ -1,3 +1,5 @@
+import functools
+
 import jax
 import jax.numpy as jnp
 from jax import lax
@@ -35,19 +37,25 @@
     return lax.broadcasted_iota(jnp.int32, shape, 1)
 
 
-def make_masks(lens_ref, tile_rows, tile_cols):
+def mask_kernel(lens_ref, masks_ref):
+    width = masks_ref.shape[1]
+    tile_cols = width // 2
+    tile_rows = tile_cols * lax.axis_size("col") // lax.axis_size("row")
     live = tile_rows * lax.axis_size("row") - lens_ref[lens_ref.shape[0] - 1]
-    lane = lanes_of((1, 2 * tile_cols))
+    lane = lanes_of((1, width))
     upper = (lane >= tile_cols).astype(jnp.int32)
     place = lane - tile_cols * upper
-    row, col = lax.axis_index("row") * tile_rows, lax.axis_index("col")
+    row, col = lax.axis_index("row"), lax.axis_index("col")
     keeps = [(place + (col ^ dx) * tile_cols < live).astype(jnp.float32) for dx in (0, 1)]
-    pairs = [
-        (row + first + upper < live).astype(jnp.float32) * keeps[0]
+    lines = [
+        ((row ^ d) * tile_rows + first + upper < live).astype(jnp.float32) * keeps[0]
+        for d in range(OWNERS)
         for first in range(0, tile_rows, 2)
     ]
+    lines += keeps
     count = jnp.full(lane.shape, live * live, jnp.int32).astype(jnp.float32)
-    return pairs, keeps, 1.0 / count
+    lines += [1.0 / count] * (masks_ref.shape[0] - len(lines))
+    masks_ref[...] = jnp.concatenate(lines, 0)
 
 
 def turn(w_refs, turned):
@@ -62,24 +70,12 @@
         turned[at * channels : (at + 1) * channels] = jnp.concatenate(blocks, 0).astype(jnp.bfloat16)
 
 
-def project(normed_ref, w_ref, g_ref, turned, held, masks=None):
-    channels = normed_ref.shape[1]
-    packed = channels // 2
-    tile_rows, tile_cols = held.shape[0] // packed, held.shape[1] // 2
-    turn((w_ref, g_ref), turned)
-    low = lanes_of((packed, 2 * tile_cols)) < tile_cols
-    for first in range(0, tile_rows, 2):
-        flat = nt_dot(turned[...], normed_ref[first * tile_cols : (first + 2) * tile_cols])
-        value = sigmoid(flat[channels:]) * flat[:channels]
-        if masks is not None:
-            value = value * masks[first // 2]
-        a, b = value[:packed], value[packed:]
-        held[pl.ds(first, packed, stride=tile_rows), :] = jnp.where(
-            low, a, pltpu.roll(b, tile_cols, 1)
-        )
-        held[pl.ds(first + 1, packed, stride=tile_rows), :] = jnp.where(
-            low, pltpu.roll(a, tile_cols, 1), b
-        )
+def store_rows(held, first, stride, value, tile_cols):
+    packed = value.shape[0] // 2
+    a, b = value[:packed], value[packed:]
+    low = lanes_of(a.shape) < tile_cols
+    held[pl.ds(first, packed, stride=stride), :] = jnp.where(low, a, pltpu.roll(b, tile_cols, 1))
+    held[pl.ds(first + 1, packed, stride=stride), :] = jnp.where(low, pltpu.roll(a, tile_cols, 1), b)
 
 
 def owner_place():
@@ -97,25 +93,51 @@
 
 
 def right_kernel(normed_ref, w_ref, g_ref, stay_ref, move_ref, turned, held):
-    project(normed_ref, w_ref, g_ref, turned, held)
+    channels = normed_ref.shape[1]
+    width = held.shape[1]
+    turn((w_ref, g_ref), turned)
+    for at in range(normed_ref.shape[0] // width):
+        flat = nt_dot(turned[...], normed_ref[at * width : (at + 1) * width])
+        value = sigmoid(flat[channels:]) * flat[:channels]
+        store_rows(held, 2 * at, 2 * held.shape[0] // channels, value, width // 2)
     size = stay_ref.shape[0] // 2
     for d, ref in enumerate((stay_ref, stay_ref, move_ref, move_ref)):
         ref[d % 2 * size : (d % 2 + 1) * size] = owner_block(held, d, size)
 
 
-def left_kernel(lens_ref, normed_ref, w_ref, g_ref, *refs):
-    (stay_ref, move_ref), outs, (masks_ref, turned, held) = refs[:2], refs[2:-3], refs[-3:]
-    tile_rows = held.shape[0] // normed_ref.shape[1] * 2
-    pairs, keeps, share = make_masks(lens_ref, tile_rows, held.shape[1] // 2)
-    project(normed_ref, w_ref, g_ref, turned, held, pairs)
-    masks_ref[...] = jnp.concatenate(
-        pairs + keeps + [share] * (masks_ref.shape[0] - len(pairs) - len(keeps)), 0
-    )
-    size = stay_ref.shape[0] // 2
-    for d, ref in enumerate(outs):
-        right_ref = (stay_ref, move_ref)[d // 2]
-        ref[:size] = owner_block(held, d, size)
-        ref[size:] = right_ref[d % 2 * size : (d % 2 + 1) * size]
+def side_kernel(base, masks_ref, a_ref, b_ref, *refs):
+    weights, (left_ref, right_ref, turned, mine, held_left, held_right) = refs[:4], refs[4:]
+    tile_rows, tile_cols, channels = a_ref.shape
+    size = held_left.shape[0]
+    half = size // tile_rows
+    turn(weights, turned)
+    owner = owner_place()
+    for at in range(8):
+        start = pl.multiple_of(at * (channels // 2) + owner * half, half)
+        mine[at * half : (at + 1) * half] = turned[pl.ds(start, half), :]
+    for tile, x_ref in enumerate((a_ref, b_ref)):
+        for first in range(0, tile_rows, 2):
+            x = x_ref[first : first + 2].astype(jnp.float32).reshape(2 * tile_cols, channels)
+            flat = nt_dot(mine[...], layer_norm(x, -1).astype(jnp.bfloat16))
+            lv, lg, rv, rg = [flat[at * 2 * half : (at + 1) * 2 * half] for at in range(4)]
+            line = ((base + tile) * tile_rows + first) // 2
+            left = sigmoid(lg) * lv * masks_ref[line : line + 1]
+            store_rows(held_left, first, tile_rows, left, tile_cols)
+            store_rows(held_right, first, tile_rows, sigmoid(rg) * rv, tile_cols)
+        left_ref[tile * size : (tile + 1) * size] = held_left[...].astype(jnp.bfloat16)
+        right_ref[tile * size : (tile + 1) * size] = held_right[...].astype(jnp.bfloat16)
+
+
+def pass_kernel(value_ref, ready_ref, out_ref):
+    del ready_ref
+    out_ref[...] = value_ref[...]
+
+
+def pack_kernel(far_ref, cross_ref, ready_ref, out_ref):
+    del ready_ref
+    size = out_ref.shape[0] // 2
+    out_ref[:size] = far_ref[size:]
+    out_ref[size:] = cross_ref[size:]
 
 
 def gate_kernel(x_ref, normed_ref, gw_ref, ow_ref, dw_ref, gate_ref, x_turned_ref, ow_turned, dw_turned):
@@ -137,23 +159,25 @@
         x_turned_ref[:, at] = x.T
 
 
-def tri_kernel(masks_ref, own, core, near, near_over, far, far_over, cross, cross_over, *refs):
+def tri_kernel(
+    masks_ref, left, right, left_near, right_near, far, cross, both_over, *refs
+):
     outs, rights = refs[:-1], refs[-1]
     half, _, width = rights.shape
-    size = own.shape[0] // 2
+    size = far.shape[0] // 2
     tile_rows = size // half
     side = OWNERS * tile_rows
     me, col = lax.axis_index("row"), lax.axis_index("col")
-    lefts = (own, core, near, near_over)
+    lefts = ((left, 0), (left, size), (left_near, 0), (left_near, size))
     pieces = (
-        (0, own, size),
-        (1, core, size),
-        (2, near, size),
-        (3, near_over, size),
+        (0, right, 0),
+        (1, right, size),
+        (2, right_near, 0),
+        (3, right_near, size),
         (4, far, 0),
-        (5, far_over, size),
+        (5, both_over, 0),
         (6, cross, 0),
-        (7, cross_over, size),
+        (7, both_over, size),
     )
     for away, ref, start in pieces:
         at = pl.multiple_of((me ^ away) * tile_rows, tile_rows)
@@ -162,19 +186,19 @@
                 start + m * tile_rows : start + (m + 1) * tile_rows
             ]
     low = lanes_of((side, width)) < width // 2
-    first = masks_ref.shape[0] // 2
+    first = OWNERS * tile_rows // 2
     keep = jnp.concatenate([masks_ref[first : first + 1], masks_ref[first + 1 : first + 2]], 1)
     for m in range(half):
-        left = jnp.concatenate(
-            [ref[m * tile_rows : (m + 1) * tile_rows] for ref in lefts], 0
+        rows = jnp.concatenate(
+            [ref[at + m * tile_rows : at + (m + 1) * tile_rows] for ref, at in lefts], 0
         )
         pieces = []
         for dx in (0, 1):
             block = rights[m, pl.ds(pl.multiple_of((col ^ dx) * side, side), side), :]
             block = block.astype(jnp.float32)
             pieces += [jnp.where(low, block, 0.0), jnp.where(low, 0.0, block)]
-        right = jnp.concatenate(pieces, 0).astype(jnp.bfloat16)
-        product = (nt_dot(left, right) * keep).astype(jnp.bfloat16)
+        columns = jnp.concatenate(pieces, 0).astype(jnp.bfloat16)
+        product = (nt_dot(rows, columns) * keep).astype(jnp.bfloat16)
         for d in range(OWNERS):
             for dx in (0, 1):
                 at = d % 2 * size + m * tile_rows
@@ -281,6 +305,8 @@
     turned = pltpu.VMEM((2 * channels, channels), bf16)
     held = pltpu.VMEM((OWNERS * size, width), f32)
     over_x, over_core, over_z, over_half = 1, cols, 2 * cols, OWNERS * cols
+    near = exchange(pair_repr, places, over_z)
+    core = exchange(pair_repr, places, over_core)
     normed = call(
         norm_kernel, struct((spots, channels), bf16), args=(pair_repr,), flops=1 << 30
     )
@@ -293,24 +319,53 @@
     )
     cross = exchange(move, places, over_half + over_z)
     far = exchange(stay, places, over_half)
-    own, core, near, near_over, masks = call(
-        left_kernel,
-        [struct((2 * size, width), bf16)] * OWNERS + [struct((tile_rows, width), f32)],
-        [turned, held],
-        [SMEM] + [VMEM] * 5,
-        args=(chain_lengths, normed, left_weight, left_gate_weight, stay, move),
-        flops=4 * spots * channels * channels,
-    )
-    near_over = exchange(near_over, places, over_z + over_core)
-    near = exchange(near, places, over_z)
-    core, far_over, cross_over = [
-        exchange(value, places, over_core) for value in (core, far, cross)
+    near_over = call(
+        pass_kernel,
+        struct(pair_repr.shape, bf16),
+        specs=[VMEM, pl.BlockSpec(memory_space=pl.ANY)],
+        args=(near, stay),
+    )
+    near_over = exchange(near_over, places, over_core)
+    masks = call(
+        mask_kernel,
+        struct((OWNERS * tile_rows // 2 + 8, width), f32),
+        specs=[SMEM],
+        args=(chain_lengths,),
+    )
+    sides = [
+        call(
+            functools.partial(side_kernel, base),
+            [struct((2 * size, width), bf16)] * 2,
+            [
+                pltpu.VMEM((4 * channels, channels), bf16),
+                pltpu.VMEM((channels, channels), bf16),
+                pltpu.VMEM((size, width), f32),
+                pltpu.VMEM((size, width), f32),
+            ],
+            args=(
+                masks,
+                *tiles,
+                left_weight,
+                left_gate_weight,
+                right_weight,
+                right_gate_weight,
+            ),
+            flops=4 * spots * channels * channels,
+        )
+        for base, tiles in ((0, (pair_repr, core)), (2, (near, near_over)))
     ]
+    both_over = call(
+        pack_kernel,
+        struct((2 * size, width), bf16),
+        specs=[VMEM, VMEM, pl.BlockSpec(memory_space=pl.ANY)],
+        args=(far, cross, sides[1][1]),
+    )
+    both_over = exchange(both_over, places, over_core)
     parts = call(
         tri_kernel,
         [struct((2 * size, width), bf16)] * OWNERS,
         [pltpu.VMEM((size // tile_rows, rows * tile_rows, width), bf16)],
-        args=(masks, own, core, near, near_over, far, far_over, cross, cross_over),
+        args=(masks, *sides[0], *sides[1], far, cross, both_over),
         flops=8 * size * 2 * tile_rows * 2 * width,
     )
     parts = [parts[0]] + [
@@ -427,7 +482,7 @@
         and tile_rows * rows == tile_cols * cols
         and 2 * tile_cols == 128
         and tile_rows == 16
-        and channels % (32 * OWNERS) == 0
+        and channels == 32 * OWNERS
     )
     return (by_kernels if fits else by_all_to_all)(pair_repr, *others)
 

time: 48 us -> 55.3 us (1.15)
  Pallas kernels: 5.32 us -> 10.4 us
  waiting for transfers between devices: 22.3 us -> 25.5 us
  starting transfers between devices: 17.1 us -> 15.3 us
  local copies, waits for them, and re-layouts: 2.09 us -> 2.96 us
    pallas_call x7 -> x11, Pallas kernels: 5.32 us -> 10.4 us  [call(): pl.pallas_call(kernel, out_shape=outs, in_specs=specs if specs is not Non...]
    ppermute x14 -> x13, waiting for transfers between devices: 16.5 us -> 19.7 us  [exchange(): return lax.ppermute(value, AXES, [(at, at ^ mask) for at in range(places)])]
    ppermute x14 -> x13, starting transfers between devices: 11.5 us -> 10.6 us  [exchange(): return lax.ppermute(value, AXES, [(at, at ^ mask) for at in range(places)])]
    all_to_all x1, starting transfers between devices: 5.67 us -> 4.78 us  [by_kernels(): loss = lax.all_to_all(loss, AXES, 0, 0, tiled=True)]
    unnamed x23, local copies, waits for them, and re-layouts: 1.51 us -> 2.38 us
  transfers between devices with their start and end apart: 15 -> 14, of which waited for: 8 -> 8; matrix products, arithmetic and copies ran while one was open for 0% -> 0% of each run, Pallas kernels for 5% -> 15%
where the time goes in v9:
time: 55.3 us; the launch traced here: 55 us
  waiting for transfers between devices  25.5 us (46%)
  starting transfers between devices  15.3 us (28%)
  Pallas kernels  10.4 us (19%)
  local copies, waits for them, and re-layouts  2.96 us (5%)
  between operations  0.83 us (2%)
    ppermute x13, waiting for transfers between devices, exchange(): return lax.ppermute(value, AXES, [(at, at ^ mask) for at in range(places)])  19.7 us
    ppermute x13, starting transfers between devices, exchange(): return lax.ppermute(value, AXES, [(at, at ^ mask) for at in range(places)])  10.6 us
    pallas_call x11, Pallas kernels, call(): pl.pallas_call(kernel, out_shape=outs, in_specs=specs if specs is not Non...  10.4 us
    all_to_all x1, waiting for transfers between devices, by_kernels(): loss = lax.all_to_all(loss, AXES, 0, 0, tiled=True)  5.83 us
    all_to_all x1, starting transfers between devices, by_kernels(): loss = lax.all_to_all(loss, AXES, 0, 0, tiled=True)  4.78 us
    unnamed x23, local copies, waits for them, and re-layouts  2.38 us
  transfers between devices with their start and end apart: 14, of which 8 were waited for; matrix products, arithmetic and copies ran while one was open for 0% of the time, Pallas kernels for 15%

profile of v9, /device:TPU:0, one launch (start us, length us, event | category | flops | bytes accessed | tf_op | source)
XLA Modules:
  0.0 55.0 jit_solution(6562105599237546853)
XLA Ops:
  0.6 3.1 %collective-permute-start.1 = (bf16[16,64,128]{2,1,0:T(8,128)(2,1)}, bf16[16,64,128]{2,1,0:T(8,128)(2,1)S(1)}, u32[]{:S(2)}, u32[]{:S(2)}) collective-permute-start(bf16[16,64,128]{2,1,0:T(8,128)(2,1)} %a_ref.1), channel_id=1, source_target_pairs={{0,4},{1,5},{2,6},{3,7},{4,0},{5,1},{6,2},{7,3},{8,12},{9,13},{10,... | collective-permute-start | bytes 786440 | tf_op jit(solution)/shard_map/ppermute | solution.py:270
  3.7 0.0 copy-start
  3.7 1.0 %copy-done = bf16[16,64,128]{2,1,0:T(8,128)(2,1)S(1)} copy-done((bf16[16,64,128]{2,1,0:T(8,128)(2,1)S(1)}, bf16[16,64,128]{2,1,0:T(8,128)(2,1)}, u32[]{:S(2)}) %copy-start) | copy-done | bytes 262168
  4.7 0.0 copy-start.4
  4.7 0.0 copy-start.5
  4.7 0.4 shard_map.114.normed_ref
  5.1 0.4 copy-done.4
  5.5 0.0 copy-done.5
  5.5 0.6 %shard_map.117 = (bf16[512,128]{1,0:T(8,128)(2,1)S(1)}, bf16[512,128]{1,0:T(8,128)(2,1)S(1)}) custom-call(bf16[1024,128]{1,0:T(8,128)(2,1)S(1)} %shard_map.114.normed_ref, bf16[128,128]{1,0:T(8,128)(2,1)S(1)} %copy-done.4, bf16[128,128]{1,0:T(8,128)(2,1)S(1)} %copy-done.5), custom_call_target="tpu_custom_call" | custom-call | flops 67108864 | bytes 1048576 | tf_op jit(solution)/shard_map/pallas_call | solution.py:274
  6.0 4.2 %collective-permute-done.1.value_ref.a_ref = bf16[16,64,128]{2,1,0:T(8,128)(2,1)S(1)} collective-permute-done((bf16[16,64,128]{2,1,0:T(8,128)(2,1)}, bf16[16,64,128]{2,1,0:T(8,128)(2,1)S(1)}, u32[]{:S(2)}, u32[]{:S(2)}) %collective-permute-start.1) | collective-permute-done | bytes 262176 | tf_op jit(solution)/shard_map/ppermute | solution.py:270
  10.2 0.0 copy-start.1
  10.3 0.0 copy-start.8
  10.3 0.1 collective-permute-start.2
  10.4 0.8 %copy-done.1 = bf16[16,64,128]{2,1,0:T(8,128)(2,1)S(1)} copy-done((bf16[16,64,128]{2,1,0:T(8,128)(2,1)S(1)}, bf16[16,64,128]{2,1,0:T(8,128)(2,1)}, u32[]{:S(2)}) %copy-start.1) | copy-done | bytes 262168
  11.2 0.0 collective-permute-start
  11.2 0.0 copy-start.2
  11.2 0.0 copy-start.3
  11.2 3.8 %collective-permute-start.4 = (bf16[512,128]{1,0:T(8,128)(2,1)S(1)}, bf16[512,128]{1,0:T(8,128)(2,1)S(1)}, u32[]{:S(2)}, u32[]{:S(2)}) collective-permute-start(bf16[512,128]{1,0:T(8,128)(2,1)S(1)} %get-tuple-element.27), channel_id=1, source_target_pairs={{0,12},{1,13},{2,14},{3,15},{4,8},{5,9},{6,10},{7,11},{8,4},{9,5},... | collective-permute-start | bytes 393224 | tf_op jit(solution)/shard_map/ppermute | solution.py:270
  15.0 0.0 collective-permute-start.3
  15.0 0.0 copy-done.8
  15.0 0.6 %shard_map.113.masks_ref = f32[40,128]{1,0:T(8,128)S(1)} custom-call(s32[5]{0:T(128)S(1)} %copy-done.8), custom_call_target="tpu_custom_call" | custom-call | bytes 1048576 | tf_op jit(solution)/shard_map/pallas_call | solution.py:274
  15.6 0.0 collective-permute-done.2.b_ref
  15.6 0.0 copy-done.2
  15.6 0.0 copy-done.3
  15.6 2.8 %shard_map.119 = (bf16[512,128]{1,0:T(8,128)(2,1)S(1)}, bf16[512,128]{1,0:T(8,128)(2,1)S(1)}) custom-call(f32[40,128]{1,0:T(8,128)S(1)} %shard_map.113.masks_ref, bf16[16,64,128]{2,1,0:T(8,128)(2,1)S(1)} %collective-permute-done.1.value_ref.a_ref, bf16[16,64,128]{2,1,0:T(8,128)(2,1)S(1)} %collective-permute-done.2.b_ref, bf16[128,128]{1,0:T(8,128)(2,1)S(1)} %copy-done.2, ...), custom_call_target="tpu_custom_call" | custom-call | flops 67108864 | bytes 1048576 | tf_op jit(solution)/shard_map/pallas_call | solution.py:274
  18.4 1.1 %collective-permute-done.4.cross_ref.cross = bf16[512,128]{1,0:T(8,128)(2,1)S(1)} collective-permute-done((bf16[512,128]{1,0:T(8,128)(2,1)S(1)}, bf16[512,128]{1,0:T(8,128)(2,1)S(1)}, u32[]{:S(2)}, u32[]{:S(2)}) %collective-permute-start.4) | collective-permute-done | bytes 131104 | tf_op jit(solution)/shard_map/ppermute | solution.py:270
  19.5 7.2 %collective-permute-done.3.far_ref.far = bf16[512,128]{1,0:T(8,128)(2,1)S(1)} collective-permute-done((bf16[512,128]{1,0:T(8,128)(2,1)S(1)}, bf16[512,128]{1,0:T(8,128)(2,1)S(1)}, u32[]{:S(2)}, u32[]{:S(2)}) %collective-permute-start.3) | collective-permute-done | bytes 131104 | tf_op jit(solution)/shard_map/ppermute | solution.py:270
  26.7 0.1 collective-permute-start.5
  26.8 0.0 collective-permute-done.b_ref
  26.8 2.8 %shard_map.116 = (bf16[512,128]{1,0:T(8,128)(2,1)S(1)}, bf16[512,128]{1,0:T(8,128)(2,1)S(1)}) custom-call(f32[40,128]{1,0:T(8,128)S(1)} %shard_map.113.masks_ref, bf16[16,64,128]{2,1,0:T(8,128)(2,1)S(1)} %copy-done.1, bf16[16,64,128]{2,1,0:T(8,128)(2,1)S(1)} %collective-permute-done.b_ref, bf16[128,128]{1,0:T(8,128)(2,1)S(1)} %copy-done.2, ...), custom_call_target="tpu_custom_call" | custom-call | flops 67108864 | bytes 1048576 | tf_op jit(solution)/shard_map/pallas_call | solution.py:274
  29.6 0.0 collective-permute-done.5.both_over
  29.6 0.0 copy-start.10
  29.6 0.0 copy-start.9
  29.6 0.6 %shard_map.121 = (bf16[512,128]{1,0:T(8,128)(2,1)S(1)}, bf16[512,128]{1,0:T(8,128)(2,1)S(1)}, bf16[512,128]{1,0:T(8,128)(2,1)S(1)}, bf16[512,128]{1,0:T(8,128)(2,1)S(1)}) custom-call(f32[40,128]{1,0:T(8,128)S(1)} %shard_map.113.masks_ref, bf16[512,128]{1,0:T(8,128)(2,1)S(1)} %get-tuple-element.22.left, bf16[512,128]{1,0:T(8,128)(2,1)S(1)} %get-tuple-element.23.right, ...), custom_call_target="tpu_custom_call" | custom-call | flops 16777216 | bytes 1048576 | tf_op jit(solution)/shard_map/pallas_call | solution.py:274
  30.2 1.6 %collective-permute-start.6 = (bf16[512,128]{1,0:T(8,128)(2,1)S(1)}, bf16[512,128]{1,0:T(8,128)(2,1)S(1)}, u32[]{:S(2)}, u32[]{:S(2)}) collective-permute-start(bf16[512,128]{1,0:T(8,128)(2,1)S(1)} %get-tuple-element.29), channel_id=1, source_target_pairs={{0,1},{1,0},{2,3},{3,2},{4,5},{5,4},{6,7},{7,6},{8,9},{9,8},{10,11... | collective-permute-start | bytes 393224 | tf_op jit(solution)/shard_map/ppermute | solution.py:270
  31.7 0.0 copy-start.7
  31.7 0.0 copy-start.6
  31.8 0.0 collective-permute-start.7
  31.8 2.0 %collective-permute-start.8 = (bf16[512,128]{1,0:T(8,128)(2,1)S(1)}, bf16[512,128]{1,0:T(8,128)(2,1)S(1)}, u32[]{:S(2)}, u32[]{:S(2)}) collective-permute-start(bf16[512,128]{1,0:T(8,128)(2,1)S(1)} %get-tuple-element.31), channel_id=1, source_target_pairs={{0,5},{1,4},{2,7},{3,6},{4,1},{5,0},{6,3},{7,2},{8,13},{9,12},{10,... | collective-permute-start | bytes 393224 | tf_op jit(solution)/shard_map/ppermute | solution.py:270
  33.8 0.0 collective-permute-start.9
  33.8 2.4 %collective-permute-done.6.refs_1_ = bf16[512,128]{1,0:T(8,128)(2,1)S(1)} collective-permute-done((bf16[512,128]{1,0:T(8,128)(2,1)S(1)}, bf16[512,128]{1,0:T(8,128)(2,1)S(1)}, u32[]{:S(2)}, u32[]{:S(2)}) %collective-permute-start.6) | collective-permute-done | bytes 131104 | tf_op jit(solution)/shard_map/ppermute | solution.py:270
  36.1 0.0 collective-permute-start.10
  36.1 1.9 %collective-permute-done.7.refs_2_ = bf16[512,128]{1,0:T(8,128)(2,1)S(1)} collective-permute-done((bf16[512,128]{1,0:T(8,128)(2,1)S(1)}, bf16[512,128]{1,0:T(8,128)(2,1)S(1)}, u32[]{:S(2)}, u32[]{:S(2)}) %collective-permute-start.7) | collective-permute-done | bytes 131104 | tf_op jit(solution)/shard_map/ppermute | solution.py:270
  38.1 0.0 collective-permute-start.11
  38.1 2.0 %collective-permute-done.8.refs_3_ = bf16[512,128]{1,0:T(8,128)(2,1)S(1)} collective-permute-done((bf16[512,128]{1,0:T(8,128)(2,1)S(1)}, bf16[512,128]{1,0:T(8,128)(2,1)S(1)}, u32[]{:S(2)}, u32[]{:S(2)}) %collective-permute-start.8) | collective-permute-done | bytes 131104 | tf_op jit(solution)/shard_map/ppermute | solution.py:270
  40.1 0.0 collective-permute-start.12
  40.1 0.0 copy-done.10
  40.1 0.1 reshape.7.bins_ref
  40.2 0.0 copy-done.9
  40.2 0.1 copy.12.dw_ref
  40.3 0.0 copy-done.7
  40.3 0.0 copy-done.6
  40.4 0.4 shard_map.115
  40.7 0.0 collective-permute-done.9.refs_4_
  40.7 0.0 collective-permute-done.10.refs_5_
  40.7 0.0 collective-permute-done.11.refs_6_
  40.7 0.7 %collective-permute-done.12.refs_7_ = bf16[512,128]{1,0:T(8,128)(2,1)S(1)} collective-permute-done((bf16[512,128]{1,0:T(8,128)(2,1)S(1)}, bf16[512,128]{1,0:T(8,128)(2,1)S(1)}, u32[]{:S(2)}, u32[]{:S(2)}) %collective-permute-start.12) | collective-permute-done | bytes 131104 | tf_op jit(solution)/shard_map/ppermute | solution.py:270
  41.5 1.5 %shard_map.122 = (bf16[128,1024]{1,0:T(8,128)(2,1)S(1)}, f32[16,8,128]{2,1,0:T(8,128)}) custom-call(f32[40,128]{1,0:T(8,128)S(1)} %shard_map.113.masks_ref, f32[128,1024]{1,0:T(8,128)S(1)} %get-tuple-element.18.x_ref, f32[128,1024]{1,0:T(8,128)S(1)} %get-tuple-element.19.gate_ref, s32[8,128]{1,0:T(8,128)S(1)} %reshape.7.bins_ref, ...), custom_call_target="tpu_custom_call" | custom-call | flops 100663296 | bytes 1048576 | tf_op jit(solution)/shard_map/pallas_call | solution.py:274
  43.0 4.8 %all-to-all-start = ((f32[16,8,128]{2,1,0:T(8,128)}), f32[16,8,128]{2,1,0:T(8,128)S(1)}, u32[]{:S(2)}, u32[]{:S(2)}) async-start(f32[16,8,128]{2,1,0:T(8,128)} %get-tuple-element.33), calls=%async_computation | async-start | bytes 131072 | tf_op jit(solution)/shard_map/all_to_all | solution.py:402
  47.8 0.8 %shard_map.123 = bf16[16,64,128]{2,1,0:T(8,128)(2,1)} custom-call(bf16[128,1024]{1,0:T(8,128)(2,1)S(1)} %get-tuple-element.32.turned_ref), custom_call_target="tpu_custom_call" | custom-call | flops 67108864 | bytes 1048576 | tf_op jit(solution)/shard_map/pallas_call | solution.py:274
  48.7 5.8 %all-to-all-done = f32[16,8,128]{2,1,0:T(8,128)S(1)} async-done(((f32[16,8,128]{2,1,0:T(8,128)}), f32[16,8,128]{2,1,0:T(8,128)S(1)}, u32[]{:S(2)}, u32[]{:S(2)}) %all-to-all-start) | async-done | bytes 65568 | tf_op jit(solution)/shard_map/all_to_all | solution.py:402
  54.5 0.5 slice.3
  (3 shorter events, 0.0 us)
Async XLA Ops:
  0.6 9.6 %collective-permute-start.1 = (bf16[16,64,128]{2,1,0:T(8,128)(2,1)}, bf16[16,64,128]{2,1,0:T(8,128)(2,1)S(1)}, u32[]{:S(2)}, u32[]{:S(2)}) collective-permute-start(bf16[16,64,128]{2,1,0:T(8,128)(2,1)} %a_ref.1), channel_id=1, source_target_pairs={{0,4},{1,5},{2,6},{3,7},{4,0},{5,1},{6,2},{7,3},{8,12},{9,13},{10,... | collective-permute-start | bytes 786440 | tf_op jit(solution)/shard_map/ppermute | solution.py:270
  3.7 1.0 %copy-start = (bf16[16,64,128]{2,1,0:T(8,128)(2,1)S(1)}, bf16[16,64,128]{2,1,0:T(8,128)(2,1)}, u32[]{:S(2)}) copy-start(bf16[16,64,128]{2,1,0:T(8,128)(2,1)} %a_ref.1) | copy-start | bytes 786436
  4.7 0.8 %copy-start.4 = (bf16[128,128]{1,0:T(8,128)(2,1)S(1)}, bf16[128,128]{1,0:T(8,128)(2,1)}, u32[]{:S(2)}) copy-start(bf16[128,128]{1,0:T(8,128)(2,1)} %refs_2_.3) | copy-start | bytes 98308
  4.7 0.8 %copy-start.5 = (bf16[128,128]{1,0:T(8,128)(2,1)S(1)}, bf16[128,128]{1,0:T(8,128)(2,1)}, u32[]{:S(2)}) copy-start(bf16[128,128]{1,0:T(8,128)(2,1)} %refs_3_.3) | copy-start | bytes 98308
  10.2 1.0 %copy-start.1 = (bf16[16,64,128]{2,1,0:T(8,128)(2,1)S(1)}, bf16[16,64,128]{2,1,0:T(8,128)(2,1)}, u32[]{:S(2)}) copy-start(bf16[16,64,128]{2,1,0:T(8,128)(2,1)} %a_ref.1) | copy-start | bytes 786436
  10.3 4.7 %copy-start.8 = (s32[5]{0:T(128)S(1)}, s32[5]{0:T(128)}, u32[]{:S(2)}) copy-start(s32[5]{0:T(128)} %lens_ref.1) | copy-start | bytes 64
  10.3 5.3 %collective-permute-start.2 = (bf16[16,64,128]{2,1,0:T(8,128)(2,1)S(1)}, bf16[16,64,128]{2,1,0:T(8,128)(2,1)S(1)}, u32[]{:S(2)}, u32[]{:S(2)}) collective-permute-start(bf16[16,64,128]{2,1,0:T(8,128)(2,1)S(1)} %shard_map.118), channel_id=1, source_target_pairs={{0,2},{1,3},{2,0},{3,1},{4,6},{5,7},{6,4},{7,5},{8,10},{9,11},{10,... | collective-permute-start | bytes 786440 | tf_op jit(solution)/shard_map/ppermute | solution.py:270
  11.2 15.6 %collective-permute-start = (bf16[16,64,128]{2,1,0:T(8,128)(2,1)S(1)}, bf16[16,64,128]{2,1,0:T(8,128)(2,1)S(1)}, u32[]{:S(2)}, u32[]{:S(2)}) collective-permute-start(bf16[16,64,128]{2,1,0:T(8,128)(2,1)S(1)} %copy-done.1), channel_id=1, source_target_pairs={{0,2},{1,3},{2,0},{3,1},{4,6},{5,7},{6,4},{7,5},{8,10},{9,11},{10,... | collective-permute-start | bytes 786440 | tf_op jit(solution)/shard_map/ppermute | solution.py:270
  11.2 4.4 %copy-start.2 = (bf16[128,128]{1,0:T(8,128)(2,1)S(1)}, bf16[128,128]{1,0:T(8,128)(2,1)}, u32[]{:S(2)}) copy-start(bf16[128,128]{1,0:T(8,128)(2,1)} %refs_0_.3) | copy-start | bytes 98308
  11.2 4.4 %copy-start.3 = (bf16[128,128]{1,0:T(8,128)(2,1)S(1)}, bf16[128,128]{1,0:T(8,128)(2,1)}, u32[]{:S(2)}) copy-start(bf16[128,128]{1,0:T(8,128)(2,1)} %refs_1_.3) | copy-start | bytes 98308
  11.2 8.3 %collective-permute-start.4 = (bf16[512,128]{1,0:T(8,128)(2,1)S(1)}, bf16[512,128]{1,0:T(8,128)(2,1)S(1)}, u32[]{:S(2)}, u32[]{:S(2)}) collective-permute-start(bf16[512,128]{1,0:T(8,128)(2,1)S(1)} %get-tuple-element.27), channel_id=1, source_target_pairs={{0,12},{1,13},{2,14},{3,15},{4,8},{5,9},{6,10},{7,11},{8,4},{9,5},... | collective-permute-start | bytes 393224 | tf_op jit(solution)/shard_map/ppermute | solution.py:270
  15.0 11.7 %collective-permute-start.3 = (bf16[512,128]{1,0:T(8,128)(2,1)S(1)}, bf16[512,128]{1,0:T(8,128)(2,1)S(1)}, u32[]{:S(2)}, u32[]{:S(2)}) collective-permute-start(bf16[512,128]{1,0:T(8,128)(2,1)S(1)} %get-tuple-element.24.ready_ref), channel_id=1, source_target_pairs={{0,8},{1,9},{2,10},{3,11},{4,12},{5,13},{6,14},{7,15},{8,0},{9,1},... | collective-permute-start | bytes 393224 | tf_op jit(solution)/shard_map/ppermute | solution.py:270
  26.7 2.9 %collective-permute-start.5 = (bf16[512,128]{1,0:T(8,128)(2,1)S(1)}, bf16[512,128]{1,0:T(8,128)(2,1)S(1)}, u32[]{:S(2)}, u32[]{:S(2)}) collective-permute-start(bf16[512,128]{1,0:T(8,128)(2,1)S(1)} %shard_map.120), channel_id=1, source_target_pairs={{0,2},{1,3},{2,0},{3,1},{4,6},{5,7},{6,4},{7,5},{8,10},{9,11},{10,... | collective-permute-start | bytes 393224 | tf_op jit(solution)/shard_map/ppermute | solution.py:270
  29.6 10.5 %copy-start.10 = (s32[16,64]{1,0:T(8,128)S(1)}, s32[16,64]{1,0:T(8,128)}, u32[]{:S(2)}) copy-start(s32[16,64]{1,0:T(8,128)} %param.11) | copy-start | bytes 12292
  29.6 10.6 %copy-start.9 = (bf16[128,64]{0,1:T(8,128)(2,1)S(1)}, bf16[128,64]{0,1:T(8,128)(2,1)}, u32[]{:S(2)}) copy-start(bf16[128,64]{0,1:T(8,128)(2,1)} %param.19) | copy-start | bytes 49156
  30.2 5.9 %collective-permute-start.6 = (bf16[512,128]{1,0:T(8,128)(2,1)S(1)}, bf16[512,128]{1,0:T(8,128)(2,1)S(1)}, u32[]{:S(2)}, u32[]{:S(2)}) collective-permute-start(bf16[512,128]{1,0:T(8,128)(2,1)S(1)} %get-tuple-element.29), channel_id=1, source_target_pairs={{0,1},{1,0},{2,3},{3,2},{4,5},{5,4},{6,7},{7,6},{8,9},{9,8},{10,11... | collective-permute-start | bytes 393224 | tf_op jit(solution)/shard_map/ppermute | solution.py:270
  31.7 8.6 %copy-start.7 = (bf16[128,128]{1,0:T(8,128)(2,1)S(1)}, bf16[128,128]{1,0:T(8,128)(2,1)}, u32[]{:S(2)}) copy-start(bf16[128,128]{1,0:T(8,128)(2,1)} %ow_ref.1) | copy-start | bytes 98308
  31.7 8.6 %copy-start.6 = (bf16[128,128]{1,0:T(8,128)(2,1)S(1)}, bf16[128,128]{1,0:T(8,128)(2,1)}, u32[]{:S(2)}) copy-start(bf16[128,128]{1,0:T(8,128)(2,1)} %gw_ref.1) | copy-start | bytes 98308
  31.8 6.3 %collective-permute-start.7 = (bf16[512,128]{1,0:T(8,128)(2,1)S(1)}, bf16[512,128]{1,0:T(8,128)(2,1)S(1)}, u32[]{:S(2)}, u32[]{:S(2)}) collective-permute-start(bf16[512,128]{1,0:T(8,128)(2,1)S(1)} %get-tuple-element.30), channel_id=1, source_target_pairs={{0,4},{1,5},{2,6},{3,7},{4,0},{5,1},{6,2},{7,3},{8,12},{9,13},{10,... | collective-permute-start | bytes 393224 | tf_op jit(solution)/shard_map/ppermute | solution.py:270
  31.8 8.4 %collective-permute-start.8 = (bf16[512,128]{1,0:T(8,128)(2,1)S(1)}, bf16[512,128]{1,0:T(8,128)(2,1)S(1)}, u32[]{:S(2)}, u32[]{:S(2)}) collective-permute-start(bf16[512,128]{1,0:T(8,128)(2,1)S(1)} %get-tuple-element.31), channel_id=1, source_target_pairs={{0,5},{1,4},{2,7},{3,6},{4,1},{5,0},{6,3},{7,2},{8,13},{9,12},{10,... | collective-permute-start | bytes 393224 | tf_op jit(solution)/shard_map/ppermute | solution.py:270
  33.8 7.0 %collective-permute-start.9 = (bf16[512,128]{1,0:T(8,128)(2,1)S(1)}, bf16[512,128]{1,0:T(8,128)(2,1)S(1)}, u32[]{:S(2)}, u32[]{:S(2)}) collective-permute-start(bf16[512,128]{1,0:T(8,128)(2,1)S(1)} %get-tuple-element.28.refs_0_), channel_id=1, source_target_pairs={{0,2},{1,3},{2,0},{3,1},{4,6},{5,7},{6,4},{7,5},{8,10},{9,11},{10,... | collective-permute-start | bytes 393224 | tf_op jit(solution)/shard_map/ppermute | solution.py:270
  36.1 4.6 %collective-permute-start.10 = (bf16[512,128]{1,0:T(8,128)(2,1)S(1)}, bf16[512,128]{1,0:T(8,128)(2,1)S(1)}, u32[]{:S(2)}, u32[]{:S(2)}) collective-permute-start(bf16[512,128]{1,0:T(8,128)(2,1)S(1)} %collective-permute-done.6.refs_1_), channel_id=1, source_target_pairs={{0,2},{1,3},{2,0},{3,1},{4,6},{5,7},{6,4},{7,5},{8,10},{9,11},{10,... | collective-permute-start | bytes 393224 | tf_op jit(solution)/shard_map/ppermute | solution.py:270
  38.1 2.7 %collective-permute-start.11 = (bf16[512,128]{1,0:T(8,128)(2,1)S(1)}, bf16[512,128]{1,0:T(8,128)(2,1)S(1)}, u32[]{:S(2)}, u32[]{:S(2)}) collective-permute-start(bf16[512,128]{1,0:T(8,128)(2,1)S(1)} %collective-permute-done.7.refs_2_), channel_id=1, source_target_pairs={{0,2},{1,3},{2,0},{3,1},{4,6},{5,7},{6,4},{7,5},{8,10},{9,11},{10,... | collective-permute-start | bytes 393224 | tf_op jit(solution)/shard_map/ppermute | solution.py:270
  40.1 1.3 %collective-permute-start.12 = (bf16[512,128]{1,0:T(8,128)(2,1)S(1)}, bf16[512,128]{1,0:T(8,128)(2,1)S(1)}, u32[]{:S(2)}, u32[]{:S(2)}) collective-permute-start(bf16[512,128]{1,0:T(8,128)(2,1)S(1)} %collective-permute-done.8.refs_3_), channel_id=1, source_target_pairs={{0,2},{1,3},{2,0},{3,1},{4,6},{5,7},{6,4},{7,5},{8,10},{9,11},{10,... | collective-permute-start | bytes 393224 | tf_op jit(solution)/shard_map/ppermute | solution.py:270
  43.0 11.5 %all-to-all-start = ((f32[16,8,128]{2,1,0:T(8,128)}), f32[16,8,128]{2,1,0:T(8,128)S(1)}, u32[]{:S(2)}, u32[]{:S(2)}) async-start(f32[16,8,128]{2,1,0:T(8,128)} %get-tuple-element.33), calls=%async_computation | async-start | bytes 131072 | tf_op jit(solution)/shard_map/all_to_all | solution.py:402

commit v10 on v6

--- a/solution.py
+++ b/solution.py
@@ -40,10 +40,11 @@
     lane = lanes_of((1, 2 * tile_cols))
     upper = (lane >= tile_cols).astype(jnp.int32)
     place = lane - tile_cols * upper
-    row, col = lax.axis_index("row") * tile_rows, lax.axis_index("col")
+    row, col = lax.axis_index("row"), lax.axis_index("col")
     keeps = [(place + (col ^ dx) * tile_cols < live).astype(jnp.float32) for dx in (0, 1)]
     pairs = [
-        (row + first + upper < live).astype(jnp.float32) * keeps[0]
+        ((row ^ d) * tile_rows + first + upper < live).astype(jnp.float32) * keeps[0]
+        for d in (0, OWNERS // 2)
         for first in range(0, tile_rows, 2)
     ]
     count = jnp.full(lane.shape, live * live, jnp.int32).astype(jnp.float32)
@@ -62,24 +63,21 @@
         turned[at * channels : (at + 1) * channels] = jnp.concatenate(blocks, 0).astype(jnp.bfloat16)
 
 
-def project(normed_ref, w_ref, g_ref, turned, held, masks=None):
-    channels = normed_ref.shape[1]
-    packed = channels // 2
-    tile_rows, tile_cols = held.shape[0] // packed, held.shape[1] // 2
-    turn((w_ref, g_ref), turned)
-    low = lanes_of((packed, 2 * tile_cols)) < tile_cols
-    for first in range(0, tile_rows, 2):
-        flat = nt_dot(turned[...], normed_ref[first * tile_cols : (first + 2) * tile_cols])
-        value = sigmoid(flat[channels:]) * flat[:channels]
-        if masks is not None:
-            value = value * masks[first // 2]
-        a, b = value[:packed], value[packed:]
-        held[pl.ds(first, packed, stride=tile_rows), :] = jnp.where(
-            low, a, pltpu.roll(b, tile_cols, 1)
-        )
-        held[pl.ds(first + 1, packed, stride=tile_rows), :] = jnp.where(
-            low, pltpu.roll(a, tile_cols, 1), b
-        )
+def store_rows(held, first, value, tile_cols):
+    packed = value.shape[0] // 2
+    stride = held.shape[0] // packed
+    a, b = value[:packed], value[packed:]
+    low = lanes_of(a.shape) < tile_cols
+    held[pl.ds(first, packed, stride=stride), :] = jnp.where(low, a, pltpu.roll(b, tile_cols, 1))
+    held[pl.ds(first + 1, packed, stride=stride), :] = jnp.where(low, pltpu.roll(a, tile_cols, 1), b)
+
+
+def chip_rows(turned, mine):
+    size = mine.shape[0] // (turned.shape[0] // mine.shape[1]) // 2
+    pair = owner_place() // 2
+    for at in range(mine.shape[0] // size):
+        start = pl.multiple_of(at * (mine.shape[1] // 2) + pair * size, size)
+        mine[at * size : (at + 1) * size] = turned[pl.ds(start, size), :]
 
 
 def owner_place():
@@ -91,31 +89,71 @@
     return held[pl.ds(at, size)].astype(jnp.bfloat16)
 
 
+def core_block(held, d, size):
+    at = pl.multiple_of((owner_place() % 2 ^ d) * size, size)
+    return held[pl.ds(at, size)].astype(jnp.bfloat16)
+
+
 def norm_kernel(x_ref, normed_ref):
     x = x_ref[...].astype(jnp.float32).reshape(normed_ref.shape)
     normed_ref[...] = layer_norm(x, -1).astype(jnp.bfloat16)
 
 
 def right_kernel(normed_ref, w_ref, g_ref, stay_ref, move_ref, turned, held):
-    project(normed_ref, w_ref, g_ref, turned, held)
+    channels = normed_ref.shape[1]
+    width = held.shape[1]
+    turn((w_ref, g_ref), turned)
+    for at in range(normed_ref.shape[0] // width):
+        flat = nt_dot(turned[...], normed_ref[at * width : (at + 1) * width])
+        store_rows(held, 2 * at, sigmoid(flat[channels:]) * flat[:channels], width // 2)
     size = stay_ref.shape[0] // 2
     for d, ref in enumerate((stay_ref, stay_ref, move_ref, move_ref)):
         ref[d % 2 * size : (d % 2 + 1) * size] = owner_block(held, d, size)
 
 
-def left_kernel(lens_ref, normed_ref, w_ref, g_ref, *refs):
-    (stay_ref, move_ref), outs, (masks_ref, turned, held) = refs[:2], refs[2:-3], refs[-3:]
-    tile_rows = held.shape[0] // normed_ref.shape[1] * 2
-    pairs, keeps, share = make_masks(lens_ref, tile_rows, held.shape[1] // 2)
-    project(normed_ref, w_ref, g_ref, turned, held, pairs)
+def left_kernel(lens_ref, normed_ref, w_ref, g_ref, stay_ref, own_ref, core_ref, masks_ref, *refs):
+    turned, mine, held = refs
+    width = held.shape[1]
+    half = mine.shape[0] // 2
+    pairs, keeps, share = make_masks(lens_ref, 2 * normed_ref.shape[0] // width, width // 2)
     masks_ref[...] = jnp.concatenate(
         pairs + keeps + [share] * (masks_ref.shape[0] - len(pairs) - len(keeps)), 0
     )
+    turn((w_ref, g_ref), turned)
+    chip_rows(turned, mine)
+    for at in range(normed_ref.shape[0] // width):
+        flat = nt_dot(mine[...], normed_ref[at * width : (at + 1) * width])
+        store_rows(held, 2 * at, sigmoid(flat[half:]) * flat[:half] * pairs[at], width // 2)
     size = stay_ref.shape[0] // 2
-    for d, ref in enumerate(outs):
-        right_ref = (stay_ref, move_ref)[d // 2]
-        ref[:size] = owner_block(held, d, size)
-        ref[size:] = right_ref[d % 2 * size : (d % 2 + 1) * size]
+    for d, ref in enumerate((own_ref, core_ref)):
+        ref[:size] = core_block(held, d, size)
+        ref[size:] = stay_ref[d * size : (d + 1) * size]
+
+
+def near_kernel(masks_ref, x_ref, lw_ref, lg_ref, rw_ref, rg_ref, near_ref, over_ref, *refs):
+    turned, mine, held_left, held_right = refs
+    tile_rows, tile_cols, channels = x_ref.shape
+    share = mine.shape[0] // 4
+    turn((lw_ref, lg_ref, rw_ref, rg_ref), turned)
+    chip_rows(turned, mine)
+    for first in range(0, tile_rows, 2):
+        x = x_ref[first : first + 2].astype(jnp.float32).reshape(2 * tile_cols, channels)
+        flat = nt_dot(mine[...], layer_norm(x, -1).astype(jnp.bfloat16))
+        lv, lg, rv, rg = [flat[at * share : (at + 1) * share] for at in range(4)]
+        line = (tile_rows + first) // 2
+        store_rows(held_left, first, sigmoid(lg) * lv * masks_ref[line : line + 1], tile_cols)
+        store_rows(held_right, first, sigmoid(rg) * rv, tile_cols)
+    size = near_ref.shape[0] // 2
+    for d, ref in enumerate((near_ref, over_ref)):
+        ref[:size] = core_block(held_left, d, size)
+        ref[size:] = core_block(held_right, d, size)
+
+
+def pack_kernel(far_ref, cross_ref, ready_ref, out_ref):
+    del ready_ref
+    size = out_ref.shape[0] // 2
+    out_ref[:size] = far_ref[size:]
+    out_ref[size:] = cross_ref[size:]
 
 
 def gate_kernel(x_ref, normed_ref, gw_ref, ow_ref, dw_ref, gate_ref, x_turned_ref, ow_turned, dw_turned):
@@ -137,7 +175,7 @@
         x_turned_ref[:, at] = x.T
 
 
-def tri_kernel(masks_ref, own, core, near, near_over, far, far_over, cross, cross_over, *refs):
+def tri_kernel(masks_ref, own, core, near, near_over, far, cross, both_over, *refs):
     outs, rights = refs[:-1], refs[-1]
     half, _, width = rights.shape
     size = own.shape[0] // 2
@@ -151,9 +189,9 @@
         (2, near, size),
         (3, near_over, size),
         (4, far, 0),
-        (5, far_over, size),
+        (5, both_over, 0),
         (6, cross, 0),
-        (7, cross_over, size),
+        (7, both_over, size),
     )
     for away, ref, start in pieces:
         at = pl.multiple_of((me ^ away) * tile_rows, tile_rows)
@@ -162,7 +200,7 @@
                 start + m * tile_rows : start + (m + 1) * tile_rows
             ]
     low = lanes_of((side, width)) < width // 2
-    first = masks_ref.shape[0] // 2
+    first = masks_ref.shape[0] - tile_rows // 2
     keep = jnp.concatenate([masks_ref[first : first + 1], masks_ref[first + 1 : first + 2]], 1)
     for m in range(half):
         left = jnp.concatenate(
@@ -281,6 +319,7 @@
     turned = pltpu.VMEM((2 * channels, channels), bf16)
     held = pltpu.VMEM((OWNERS * size, width), f32)
     over_x, over_core, over_z, over_half = 1, cols, 2 * cols, OWNERS * cols
+    near = exchange(pair_repr, places, over_z)
     normed = call(
         norm_kernel, struct((spots, channels), bf16), args=(pair_repr,), flops=1 << 30
     )
@@ -293,24 +332,41 @@
     )
     cross = exchange(move, places, over_half + over_z)
     far = exchange(stay, places, over_half)
-    own, core, near, near_over, masks = call(
+    block = struct((2 * size, width), bf16)
+    own, core, masks = call(
         left_kernel,
-        [struct((2 * size, width), bf16)] * OWNERS + [struct((tile_rows, width), f32)],
-        [turned, held],
-        [SMEM] + [VMEM] * 5,
-        args=(chain_lengths, normed, left_weight, left_gate_weight, stay, move),
+        [block, block, struct((3 * tile_rows // 2, width), f32)],
+        [turned, pltpu.VMEM((channels, channels), bf16), pltpu.VMEM((2 * size, width), f32)],
+        [SMEM] + [VMEM] * 4,
+        args=(chain_lengths, normed, left_weight, left_gate_weight, stay),
+        flops=2 * spots * channels * channels,
+    )
+    near, near_over = call(
+        near_kernel,
+        [block, block],
+        [
+            pltpu.VMEM((4 * channels, channels), bf16),
+            pltpu.VMEM((2 * channels, channels), bf16),
+            pltpu.VMEM((2 * size, width), f32),
+            pltpu.VMEM((2 * size, width), f32),
+        ],
+        args=(masks, near, left_weight, left_gate_weight, right_weight, right_gate_weight),
         flops=4 * spots * channels * channels,
     )
-    near_over = exchange(near_over, places, over_z + over_core)
-    near = exchange(near, places, over_z)
-    core, far_over, cross_over = [
-        exchange(value, places, over_core) for value in (core, far, cross)
-    ]
+    near_over = exchange(near_over, places, over_core)
+    core = exchange(core, places, over_core)
+    both_over = call(
+        pack_kernel,
+        block,
+        specs=[VMEM, VMEM, pl.BlockSpec(memory_space=pl.ANY)],
+        args=(far, cross, near_over),
+    )
+    both_over = exchange(both_over, places, over_core)
     parts = call(
         tri_kernel,
         [struct((2 * size, width), bf16)] * OWNERS,
         [pltpu.VMEM((size // tile_rows, rows * tile_rows, width), bf16)],
-        args=(masks, own, core, near, near_over, far, far_over, cross, cross_over),
+        args=(masks, own, core, near, near_over, far, cross, both_over),
         flops=8 * size * 2 * tile_rows * 2 * width,
     )
     parts = [parts[0]] + [
@@ -427,7 +483,7 @@
         and tile_rows * rows == tile_cols * cols
         and 2 * tile_cols == 128
         and tile_rows == 16
-        and channels % (32 * OWNERS) == 0
+        and channels == 32 * OWNERS
     )
     return (by_kernels if fits else by_all_to_all)(pair_repr, *others)
 

time: 48 us -> 47.3 us (0.985)
  starting transfers between devices: 17.1 us -> 15 us
  Pallas kernels: 5.32 us -> 6.31 us
  waiting for transfers between devices: 22.3 us -> 22.8 us
    ppermute x14 -> x13, starting transfers between devices: 11.5 us -> 10 us  [exchange(): return lax.ppermute(value, AXES, [(at, at ^ mask) for at in range(places)])]
    pallas_call x7 -> x9, Pallas kernels: 5.32 us -> 6.31 us  [call(): pl.pallas_call(kernel, out_shape=outs, in_specs=specs if specs is not Non...]
    all_to_all x1, starting transfers between devices: 5.67 us -> 4.95 us  [by_kernels(): loss = lax.all_to_all(loss, AXES, 0, 0, tiled=True)]
    ppermute x14 -> x13, waiting for transfers between devices: 16.5 us -> 17 us  [exchange(): return lax.ppermute(value, AXES, [(at, at ^ mask) for at in range(places)])]
  transfers between devices with their start and end apart: 15 -> 14, of which waited for: 8 -> 9; matrix products, arithmetic and copies ran while one was open for 0% -> 0% of each run, Pallas kernels for 5% -> 9%
where the time goes in v10:
time: 47.3 us; the launch traced here: 47 us
  waiting for transfers between devices  22.8 us (48%)
  starting transfers between devices  15 us (32%)
  Pallas kernels  6.31 us (13%)
  local copies, waits for them, and re-layouts  2.13 us (5%)
  between operations  0.79 us (2%)
    ppermute x13, waiting for transfers between devices, exchange(): return lax.ppermute(value, AXES, [(at, at ^ mask) for at in range(places)])  17 us
    ppermute x13, starting transfers between devices, exchange(): return lax.ppermute(value, AXES, [(at, at ^ mask) for at in range(places)])  10 us
    pallas_call x9, Pallas kernels, call(): pl.pallas_call(kernel, out_shape=outs, in_specs=specs if specs is not Non...  6.31 us
    all_to_all x1, waiting for transfers between devices, by_kernels(): loss = lax.all_to_all(loss, AXES, 0, 0, tiled=True)  5.83 us
    all_to_all x1, starting transfers between devices, by_kernels(): loss = lax.all_to_all(loss, AXES, 0, 0, tiled=True)  4.95 us
    unnamed x23, local copies, waits for them, and re-layouts  1.54 us
  transfers between devices with their start and end apart: 14, of which 9 were waited for; matrix products, arithmetic and copies ran while one was open for 0% of the time, Pallas kernels for 9%

profile of v10, /device:TPU:0, one launch (start us, length us, event | category | flops | bytes accessed | tf_op | source)
XLA Modules:
  0.0 47.0 jit_solution(2790106370439639208)
XLA Ops:
  0.6 3.1 %collective-permute-start.1 = (bf16[16,64,128]{2,1,0:T(8,128)(2,1)}, bf16[16,64,128]{2,1,0:T(8,128)(2,1)S(1)}, u32[]{:S(2)}, u32[]{:S(2)}) collective-permute-start(bf16[16,64,128]{2,1,0:T(8,128)(2,1)} %x_ref.3), channel_id=1, source_target_pairs={{0,4},{1,5},{2,6},{3,7},{4,0},{5,1},{6,2},{7,3},{8,12},{9,13},{10,... | collective-permute-start | bytes 786440 | tf_op jit(solution)/shard_map/ppermute | solution.py:284
  3.7 0.0 copy-start
  3.7 1.0 %copy-done = bf16[16,64,128]{2,1,0:T(8,128)(2,1)S(1)} copy-done((bf16[16,64,128]{2,1,0:T(8,128)(2,1)S(1)}, bf16[16,64,128]{2,1,0:T(8,128)(2,1)}, u32[]{:S(2)}) %copy-start) | copy-done | bytes 262168
  4.7 0.0 copy-start.6
  4.7 0.0 copy-start.7
  4.7 0.4 shard_map.113.normed_ref
  5.1 0.4 copy-done.6
  5.5 0.0 copy-done.7
  5.5 0.0 copy-start.4
  5.5 0.0 copy-start.5
  5.5 0.6 %shard_map.114 = (bf16[512,128]{1,0:T(8,128)(2,1)S(1)}, bf16[512,128]{1,0:T(8,128)(2,1)S(1)}) custom-call(bf16[1024,128]{1,0:T(8,128)(2,1)S(1)} %shard_map.113.normed_ref, bf16[128,128]{1,0:T(8,128)(2,1)S(1)} %copy-done.6, bf16[128,128]{1,0:T(8,128)(2,1)S(1)} %copy-done.7), custom_call_target="tpu_custom_call" | custom-call | flops 67108864 | bytes 1048576 | tf_op jit(solution)/shard_map/pallas_call | solution.py:288
  6.0 0.0 copy-start.8
  6.1 2.5 %collective-permute-start.4 = (bf16[512,128]{1,0:T(8,128)(2,1)S(1)}, bf16[512,128]{1,0:T(8,128)(2,1)S(1)}, u32[]{:S(2)}, u32[]{:S(2)}) collective-permute-start(bf16[512,128]{1,0:T(8,128)(2,1)S(1)} %get-tuple-element.29), channel_id=1, source_target_pairs={{0,12},{1,13},{2,14},{3,15},{4,8},{5,9},{6,10},{7,11},{8,4},{9,5},... | collective-permute-start | bytes 393224 | tf_op jit(solution)/shard_map/ppermute | solution.py:284
  8.6 0.2 collective-permute-start.3
  8.8 0.0 copy-done.4
  8.8 0.0 copy-done.5
  8.8 0.0 copy-done.8
  8.8 1.0 %shard_map.115 = (bf16[512,128]{1,0:T(8,128)(2,1)S(1)}, bf16[512,128]{1,0:T(8,128)(2,1)S(1)}, f32[24,128]{1,0:T(8,128)S(1)}) custom-call(s32[5]{0:T(128)S(1)} %copy-done.8, bf16[1024,128]{1,0:T(8,128)(2,1)S(1)} %shard_map.113.normed_ref, bf16[128,128]{1,0:T(8,128)(2,1)S(1)} %copy-done.4, bf16[128,128]{1,0:T(8,128)(2,1)S(1)} %copy-done.5, ...), custom_call_target="tpu_custom_call" | custom-call | flops 33554432 | bytes 1048576 | tf_op jit(solution)/shard_map/pallas_call | solution.py:288
  9.8 0.9 %collective-permute-done.1.x_ref = bf16[16,64,128]{2,1,0:T(8,128)(2,1)S(1)} collective-permute-done((bf16[16,64,128]{2,1,0:T(8,128)(2,1)}, bf16[16,64,128]{2,1,0:T(8,128)(2,1)S(1)}, u32[]{:S(2)}, u32[]{:S(2)}) %collective-permute-start.1) | collective-permute-done | bytes 262176 | tf_op jit(solution)/shard_map/ppermute | solution.py:284
  10.7 1.1 %shard_map.117 = (bf16[512,128]{1,0:T(8,128)(2,1)S(1)}, bf16[512,128]{1,0:T(8,128)(2,1)S(1)}) custom-call(f32[24,128]{1,0:T(8,128)S(1)} %get-tuple-element.20.masks_ref, bf16[16,64,128]{2,1,0:T(8,128)(2,1)S(1)} %collective-permute-done.1.x_ref, bf16[128,128]{1,0:T(8,128)(2,1)S(1)} %copy-done.4, bf16[128,128]{1,0:T(8,128)(2,1)S(1)} %copy-done.5, ...), custom_call_target="tpu_custom_call" | custom-call | flops 67108864 | bytes 1048576 | tf_op jit(solution)/shard_map/pallas_call | solution.py:288
  11.8 0.1 collective-permute-start.2
  11.9 0.5 %collective-permute-start = (bf16[512,128]{1,0:T(8,128)(2,1)S(1)}, bf16[512,128]{1,0:T(8,128)(2,1)S(1)}, u32[]{:S(2)}, u32[]{:S(2)}) collective-permute-start(bf16[512,128]{1,0:T(8,128)(2,1)S(1)} %get-tuple-element.26), channel_id=1, source_target_pairs={{0,2},{1,3},{2,0},{3,1},{4,6},{5,7},{6,4},{7,5},{8,10},{9,11},{10,... | collective-permute-start | bytes 393224 | tf_op jit(solution)/shard_map/ppermute | solution.py:284
  12.4 4.1 %collective-permute-done.4.cross_ref.cross = bf16[512,128]{1,0:T(8,128)(2,1)S(1)} collective-permute-done((bf16[512,128]{1,0:T(8,128)(2,1)S(1)}, bf16[512,128]{1,0:T(8,128)(2,1)S(1)}, u32[]{:S(2)}, u32[]{:S(2)}) %collective-permute-start.4) | collective-permute-done | bytes 131104 | tf_op jit(solution)/shard_map/ppermute | solution.py:284
  16.5 3.9 %collective-permute-done.3.far_ref.far = bf16[512,128]{1,0:T(8,128)(2,1)S(1)} collective-permute-done((bf16[512,128]{1,0:T(8,128)(2,1)S(1)}, bf16[512,128]{1,0:T(8,128)(2,1)S(1)}, u32[]{:S(2)}, u32[]{:S(2)}) %collective-permute-start.3) | collective-permute-done | bytes 131104 | tf_op jit(solution)/shard_map/ppermute | solution.py:284
  20.4 0.0 collective-permute-done.2.ready_ref.near_over
  20.4 0.1 collective-permute-start.5
  20.5 0.0 collective-permute-done.core
  20.5 1.3 %collective-permute-done.5.both_over = bf16[512,128]{1,0:T(8,128)(2,1)S(1)} collective-permute-done((bf16[512,128]{1,0:T(8,128)(2,1)S(1)}, bf16[512,128]{1,0:T(8,128)(2,1)S(1)}, u32[]{:S(2)}, u32[]{:S(2)}) %collective-permute-start.5) | collective-permute-done | bytes 131104 | tf_op jit(solution)/shard_map/ppermute | solution.py:284
  21.8 0.0 copy-start.10
  21.8 0.0 copy-start.9
  21.8 0.0 copy-start.1
  21.8 0.5 %shard_map.119 = (bf16[512,128]{1,0:T(8,128)(2,1)S(1)}, bf16[512,128]{1,0:T(8,128)(2,1)S(1)}, bf16[512,128]{1,0:T(8,128)(2,1)S(1)}, bf16[512,128]{1,0:T(8,128)(2,1)S(1)}) custom-call(f32[24,128]{1,0:T(8,128)S(1)} %get-tuple-element.20.masks_ref, bf16[512,128]{1,0:T(8,128)(2,1)S(1)} %get-tuple-element.25.own, bf16[512,128]{1,0:T(8,128)(2,1)S(1)} %collective-permute-done.core, ...), custom_call_target="tpu_custom_call" | custom-call | flops 16777216 | bytes 1048576 | tf_op jit(solution)/shard_map/pallas_call | solution.py:288
  22.3 1.6 %collective-permute-start.6 = (bf16[512,128]{1,0:T(8,128)(2,1)S(1)}, bf16[512,128]{1,0:T(8,128)(2,1)S(1)}, u32[]{:S(2)}, u32[]{:S(2)}) collective-permute-start(bf16[512,128]{1,0:T(8,128)(2,1)S(1)} %get-tuple-element.31), channel_id=1, source_target_pairs={{0,1},{1,0},{2,3},{3,2},{4,5},{5,4},{6,7},{7,6},{8,9},{9,8},{10,11... | collective-permute-start | bytes 393224 | tf_op jit(solution)/shard_map/ppermute | solution.py:284
  23.9 0.0 copy-start.3
  23.9 0.0 copy-start.2
  23.9 0.0 collective-permute-start.7
  23.9 2.0 %collective-permute-start.8 = (bf16[512,128]{1,0:T(8,128)(2,1)S(1)}, bf16[512,128]{1,0:T(8,128)(2,1)S(1)}, u32[]{:S(2)}, u32[]{:S(2)}) collective-permute-start(bf16[512,128]{1,0:T(8,128)(2,1)S(1)} %get-tuple-element.33), channel_id=1, source_target_pairs={{0,5},{1,4},{2,7},{3,6},{4,1},{5,0},{6,3},{7,2},{8,13},{9,12},{10,... | collective-permute-start | bytes 393224 | tf_op jit(solution)/shard_map/ppermute | solution.py:284
  25.9 0.0 collective-permute-start.9
  25.9 2.1 %collective-permute-done.6.refs_1_ = bf16[512,128]{1,0:T(8,128)(2,1)S(1)} collective-permute-done((bf16[512,128]{1,0:T(8,128)(2,1)S(1)}, bf16[512,128]{1,0:T(8,128)(2,1)S(1)}, u32[]{:S(2)}, u32[]{:S(2)}) %collective-permute-start.6) | collective-permute-done | bytes 131104 | tf_op jit(solution)/shard_map/ppermute | solution.py:284
  28.0 0.0 collective-permute-start.10
  28.0 2.3 %collective-permute-done.7.refs_2_ = bf16[512,128]{1,0:T(8,128)(2,1)S(1)} collective-permute-done((bf16[512,128]{1,0:T(8,128)(2,1)S(1)}, bf16[512,128]{1,0:T(8,128)(2,1)S(1)}, u32[]{:S(2)}, u32[]{:S(2)}) %collective-permute-start.7) | collective-permute-done | bytes 131104 | tf_op jit(solution)/shard_map/ppermute | solution.py:284
  30.3 0.0 collective-permute-start.11
  30.3 1.7 %collective-permute-done.8.refs_3_ = bf16[512,128]{1,0:T(8,128)(2,1)S(1)} collective-permute-done((bf16[512,128]{1,0:T(8,128)(2,1)S(1)}, bf16[512,128]{1,0:T(8,128)(2,1)S(1)}, u32[]{:S(2)}, u32[]{:S(2)}) %collective-permute-start.8) | collective-permute-done | bytes 131104 | tf_op jit(solution)/shard_map/ppermute | solution.py:284
  32.0 0.0 collective-permute-start.12
  32.0 0.0 copy-done.10
  32.0 0.1 reshape.7.bins_ref
  32.0 0.0 copy-done.9
  32.0 0.1 copy.12.dw_ref
  32.2 0.0 copy-done.1
  32.2 0.0 copy-done.3
  32.2 0.0 copy-done.2
  32.2 0.4 shard_map.116
  32.5 0.0 collective-permute-done.9.refs_4_
  32.6 0.0 collective-permute-done.10.refs_5_
  32.6 0.0 collective-permute-done.11.refs_6_
  32.6 0.7 %collective-permute-done.12.refs_7_ = bf16[512,128]{1,0:T(8,128)(2,1)S(1)} collective-permute-done((bf16[512,128]{1,0:T(8,128)(2,1)S(1)}, bf16[512,128]{1,0:T(8,128)(2,1)S(1)}, u32[]{:S(2)}, u32[]{:S(2)}) %collective-permute-start.12) | collective-permute-done | bytes 131104 | tf_op jit(solution)/shard_map/ppermute | solution.py:284
  33.3 1.5 %shard_map.120 = (bf16[128,1024]{1,0:T(8,128)(2,1)S(1)}, f32[16,8,128]{2,1,0:T(8,128)}) custom-call(f32[24,128]{1,0:T(8,128)S(1)} %get-tuple-element.20.masks_ref, f32[128,1024]{1,0:T(8,128)S(1)} %get-tuple-element.21.x_ref, f32[128,1024]{1,0:T(8,128)S(1)} %get-tuple-element.22.gate_ref, s32[8,128]{1,0:T(8,128)S(1)} %reshape.7.bins_ref, ...), custom_call_target="tpu_custom_call" | custom-call | flops 100663296 | bytes 1048576 | tf_op jit(solution)/shard_map/pallas_call | solution.py:288
  34.9 4.9 %all-to-all-start = ((f32[16,8,128]{2,1,0:T(8,128)}), f32[16,8,128]{2,1,0:T(8,128)S(1)}, u32[]{:S(2)}, u32[]{:S(2)}) async-start(f32[16,8,128]{2,1,0:T(8,128)} %get-tuple-element.35), calls=%async_computation | async-start | bytes 131072 | tf_op jit(solution)/shard_map/all_to_all | solution.py:403
  39.8 0.8 %shard_map.121 = bf16[16,64,128]{2,1,0:T(8,128)(2,1)} custom-call(bf16[128,1024]{1,0:T(8,128)(2,1)S(1)} %get-tuple-element.34.turned_ref), custom_call_target="tpu_custom_call" | custom-call | flops 67108864 | bytes 1048576 | tf_op jit(solution)/shard_map/pallas_call | solution.py:288
  40.6 5.8 %all-to-all-done = f32[16,8,128]{2,1,0:T(8,128)S(1)} async-done(((f32[16,8,128]{2,1,0:T(8,128)}), f32[16,8,128]{2,1,0:T(8,128)S(1)}, u32[]{:S(2)}, u32[]{:S(2)}) %all-to-all-start) | async-done | bytes 65568 | tf_op jit(solution)/shard_map/all_to_all | solution.py:403
  46.5 0.5 %slice.3 = f32[1,1]{1,0:T(1,128)} slice(f32[8,128]{1,0:T(8,128)S(1)} %reduce_sum.9), slice={[0:1], [0:1]} | slice | bytes 8 | tf_op jit(solution)/shard_map/slice | solution.py:404
  (2 shorter events, 0.0 us)
Async XLA Ops:
  0.6 10.1 %collective-permute-start.1 = (bf16[16,64,128]{2,1,0:T(8,128)(2,1)}, bf16[16,64,128]{2,1,0:T(8,128)(2,1)S(1)}, u32[]{:S(2)}, u32[]{:S(2)}) collective-permute-start(bf16[16,64,128]{2,1,0:T(8,128)(2,1)} %x_ref.3), channel_id=1, source_target_pairs={{0,4},{1,5},{2,6},{3,7},{4,0},{5,1},{6,2},{7,3},{8,12},{9,13},{10,... | collective-permute-start | bytes 786440 | tf_op jit(solution)/shard_map/ppermute | solution.py:284
  3.7 1.0 %copy-start = (bf16[16,64,128]{2,1,0:T(8,128)(2,1)S(1)}, bf16[16,64,128]{2,1,0:T(8,128)(2,1)}, u32[]{:S(2)}) copy-start(bf16[16,64,128]{2,1,0:T(8,128)(2,1)} %x_ref.3) | copy-start | bytes 786436
  4.7 0.8 %copy-start.6 = (bf16[128,128]{1,0:T(8,128)(2,1)S(1)}, bf16[128,128]{1,0:T(8,128)(2,1)}, u32[]{:S(2)}) copy-start(bf16[128,128]{1,0:T(8,128)(2,1)} %rw_ref.1) | copy-start | bytes 98308
  4.7 0.8 %copy-start.7 = (bf16[128,128]{1,0:T(8,128)(2,1)S(1)}, bf16[128,128]{1,0:T(8,128)(2,1)}, u32[]{:S(2)}) copy-start(bf16[128,128]{1,0:T(8,128)(2,1)} %rg_ref.1) | copy-start | bytes 98308
  5.5 3.3 %copy-start.4 = (bf16[128,128]{1,0:T(8,128)(2,1)S(1)}, bf16[128,128]{1,0:T(8,128)(2,1)}, u32[]{:S(2)}) copy-start(bf16[128,128]{1,0:T(8,128)(2,1)} %lw_ref.1) | copy-start | bytes 98308
  5.5 3.3 %copy-start.5 = (bf16[128,128]{1,0:T(8,128)(2,1)S(1)}, bf16[128,128]{1,0:T(8,128)(2,1)}, u32[]{:S(2)}) copy-start(bf16[128,128]{1,0:T(8,128)(2,1)} %lg_ref.1) | copy-start | bytes 98308
  6.0 2.8 %copy-start.8 = (s32[5]{0:T(128)S(1)}, s32[5]{0:T(128)}, u32[]{:S(2)}) copy-start(s32[5]{0:T(128)} %lens_ref.1) | copy-start | bytes 64
  6.1 10.4 %collective-permute-start.4 = (bf16[512,128]{1,0:T(8,128)(2,1)S(1)}, bf16[512,128]{1,0:T(8,128)(2,1)S(1)}, u32[]{:S(2)}, u32[]{:S(2)}) collective-permute-start(bf16[512,128]{1,0:T(8,128)(2,1)S(1)} %get-tuple-element.29), channel_id=1, source_target_pairs={{0,12},{1,13},{2,14},{3,15},{4,8},{5,9},{6,10},{7,11},{8,4},{9,5},... | collective-permute-start | bytes 393224 | tf_op jit(solution)/shard_map/ppermute | solution.py:284
  8.6 11.8 %collective-permute-start.3 = (bf16[512,128]{1,0:T(8,128)(2,1)S(1)}, bf16[512,128]{1,0:T(8,128)(2,1)S(1)}, u32[]{:S(2)}, u32[]{:S(2)}) collective-permute-start(bf16[512,128]{1,0:T(8,128)(2,1)S(1)} %get-tuple-element.19.stay_ref), channel_id=1, source_target_pairs={{0,8},{1,9},{2,10},{3,11},{4,12},{5,13},{6,14},{7,15},{8,0},{9,1},... | collective-permute-start | bytes 393224 | tf_op jit(solution)/shard_map/ppermute | solution.py:284
  11.8 8.5 %collective-permute-start.2 = (bf16[512,128]{1,0:T(8,128)(2,1)S(1)}, bf16[512,128]{1,0:T(8,128)(2,1)S(1)}, u32[]{:S(2)}, u32[]{:S(2)}) collective-permute-start(bf16[512,128]{1,0:T(8,128)(2,1)S(1)} %get-tuple-element.28), channel_id=1, source_target_pairs={{0,2},{1,3},{2,0},{3,1},{4,6},{5,7},{6,4},{7,5},{8,10},{9,11},{10,... | collective-permute-start | bytes 393224 | tf_op jit(solution)/shard_map/ppermute | solution.py:284
  11.9 8.6 %collective-permute-start = (bf16[512,128]{1,0:T(8,128)(2,1)S(1)}, bf16[512,128]{1,0:T(8,128)(2,1)S(1)}, u32[]{:S(2)}, u32[]{:S(2)}) collective-permute-start(bf16[512,128]{1,0:T(8,128)(2,1)S(1)} %get-tuple-element.26), channel_id=1, source_target_pairs={{0,2},{1,3},{2,0},{3,1},{4,6},{5,7},{6,4},{7,5},{8,10},{9,11},{10,... | collective-permute-start | bytes 393224 | tf_op jit(solution)/shard_map/ppermute | solution.py:284
  20.4 1.4 %collective-permute-start.5 = (bf16[512,128]{1,0:T(8,128)(2,1)S(1)}, bf16[512,128]{1,0:T(8,128)(2,1)S(1)}, u32[]{:S(2)}, u32[]{:S(2)}) collective-permute-start(bf16[512,128]{1,0:T(8,128)(2,1)S(1)} %shard_map.118), channel_id=1, source_target_pairs={{0,2},{1,3},{2,0},{3,1},{4,6},{5,7},{6,4},{7,5},{8,10},{9,11},{10,... | collective-permute-start | bytes 393224 | tf_op jit(solution)/shard_map/ppermute | solution.py:284
  21.8 10.2 %copy-start.10 = (s32[16,64]{1,0:T(8,128)S(1)}, s32[16,64]{1,0:T(8,128)}, u32[]{:S(2)}) copy-start(s32[16,64]{1,0:T(8,128)} %param.11) | copy-start | bytes 12292
  21.8 10.2 %copy-start.9 = (bf16[128,64]{0,1:T(8,128)(2,1)S(1)}, bf16[128,64]{0,1:T(8,128)(2,1)}, u32[]{:S(2)}) copy-start(bf16[128,64]{0,1:T(8,128)(2,1)} %param.19) | copy-start | bytes 49156
  21.8 10.4 %copy-start.1 = (bf16[16,64,128]{2,1,0:T(8,128)(2,1)S(1)}, bf16[16,64,128]{2,1,0:T(8,128)(2,1)}, u32[]{:S(2)}) copy-start(bf16[16,64,128]{2,1,0:T(8,128)(2,1)} %x_ref.3) | copy-start | bytes 786436
  22.3 5.6 %collective-permute-start.6 = (bf16[512,128]{1,0:T(8,128)(2,1)S(1)}, bf16[512,128]{1,0:T(8,128)(2,1)S(1)}, u32[]{:S(2)}, u32[]{:S(2)}) collective-permute-start(bf16[512,128]{1,0:T(8,128)(2,1)S(1)} %get-tuple-element.31), channel_id=1, source_target_pairs={{0,1},{1,0},{2,3},{3,2},{4,5},{5,4},{6,7},{7,6},{8,9},{9,8},{10,11... | collective-permute-start | bytes 393224 | tf_op jit(solution)/shard_map/ppermute | solution.py:284
  23.9 8.3 %copy-start.3 = (bf16[128,128]{1,0:T(8,128)(2,1)S(1)}, bf16[128,128]{1,0:T(8,128)(2,1)}, u32[]{:S(2)}) copy-start(bf16[128,128]{1,0:T(8,128)(2,1)} %ow_ref.1) | copy-start | bytes 98308
  23.9 8.3 %copy-start.2 = (bf16[128,128]{1,0:T(8,128)(2,1)S(1)}, bf16[128,128]{1,0:T(8,128)(2,1)}, u32[]{:S(2)}) copy-start(bf16[128,128]{1,0:T(8,128)(2,1)} %gw_ref.1) | copy-start | bytes 98308
  23.9 6.4 %collective-permute-start.7 = (bf16[512,128]{1,0:T(8,128)(2,1)S(1)}, bf16[512,128]{1,0:T(8,128)(2,1)S(1)}, u32[]{:S(2)}, u32[]{:S(2)}) collective-permute-start(bf16[512,128]{1,0:T(8,128)(2,1)S(1)} %get-tuple-element.32), channel_id=1, source_target_pairs={{0,4},{1,5},{2,6},{3,7},{4,0},{5,1},{6,2},{7,3},{8,12},{9,13},{10,... | collective-permute-start | bytes 393224 | tf_op jit(solution)/shard_map/ppermute | solution.py:284
  23.9 8.0 %collective-permute-start.8 = (bf16[512,128]{1,0:T(8,128)(2,1)S(1)}, bf16[512,128]{1,0:T(8,128)(2,1)S(1)}, u32[]{:S(2)}, u32[]{:S(2)}) collective-permute-start(bf16[512,128]{1,0:T(8,128)(2,1)S(1)} %get-tuple-element.33), channel_id=1, source_target_pairs={{0,5},{1,4},{2,7},{3,6},{4,1},{5,0},{6,3},{7,2},{8,13},{9,12},{10,... | collective-permute-start | bytes 393224 | tf_op jit(solution)/shard_map/ppermute | solution.py:284
  25.9 6.6 %collective-permute-start.9 = (bf16[512,128]{1,0:T(8,128)(2,1)S(1)}, bf16[512,128]{1,0:T(8,128)(2,1)S(1)}, u32[]{:S(2)}, u32[]{:S(2)}) collective-permute-start(bf16[512,128]{1,0:T(8,128)(2,1)S(1)} %get-tuple-element.30.refs_0_), channel_id=1, source_target_pairs={{0,2},{1,3},{2,0},{3,1},{4,6},{5,7},{6,4},{7,5},{8,10},{9,11},{10,... | collective-permute-start | bytes 393224 | tf_op jit(solution)/shard_map/ppermute | solution.py:284
  28.0 4.6 %collective-permute-start.10 = (bf16[512,128]{1,0:T(8,128)(2,1)S(1)}, bf16[512,128]{1,0:T(8,128)(2,1)S(1)}, u32[]{:S(2)}, u32[]{:S(2)}) collective-permute-start(bf16[512,128]{1,0:T(8,128)(2,1)S(1)} %collective-permute-done.6.refs_1_), channel_id=1, source_target_pairs={{0,2},{1,3},{2,0},{3,1},{4,6},{5,7},{6,4},{7,5},{8,10},{9,11},{10,... | collective-permute-start | bytes 393224 | tf_op jit(solution)/shard_map/ppermute | solution.py:284
  30.3 2.3 %collective-permute-start.11 = (bf16[512,128]{1,0:T(8,128)(2,1)S(1)}, bf16[512,128]{1,0:T(8,128)(2,1)S(1)}, u32[]{:S(2)}, u32[]{:S(2)}) collective-permute-start(bf16[512,128]{1,0:T(8,128)(2,1)S(1)} %collective-permute-done.7.refs_2_), channel_id=1, source_target_pairs={{0,2},{1,3},{2,0},{3,1},{4,6},{5,7},{6,4},{7,5},{8,10},{9,11},{10,... | collective-permute-start | bytes 393224 | tf_op jit(solution)/shard_map/ppermute | solution.py:284
  32.0 1.3 %collective-permute-start.12 = (bf16[512,128]{1,0:T(8,128)(2,1)S(1)}, bf16[512,128]{1,0:T(8,128)(2,1)S(1)}, u32[]{:S(2)}, u32[]{:S(2)}) collective-permute-start(bf16[512,128]{1,0:T(8,128)(2,1)S(1)} %collective-permute-done.8.refs_3_), channel_id=1, source_target_pairs={{0,2},{1,3},{2,0},{3,1},{4,6},{5,7},{6,4},{7,5},{8,10},{9,11},{10,... | collective-permute-start | bytes 393224 | tf_op jit(solution)/shard_map/ppermute | solution.py:284
  34.9 11.6 %all-to-all-start = ((f32[16,8,128]{2,1,0:T(8,128)}), f32[16,8,128]{2,1,0:T(8,128)S(1)}, u32[]{:S(2)}, u32[]{:S(2)}) async-start(f32[16,8,128]{2,1,0:T(8,128)} %get-tuple-element.35), calls=%async_computation | async-start | bytes 131072 | tf_op jit(solution)/shard_map/all_to_all | solution.py:403

commit v11 on v10

--- a/solution.py
+++ b/solution.py
@@ -7,6 +7,7 @@
 
 AXES = ("row", "col")
 OWNERS = 4
+DIAGONAL_FIRST = (3, 1, 2, 0)
 VMEM = pl.BlockSpec(memory_space=pltpu.VMEM)
 SMEM = pl.BlockSpec(memory_space=pltpu.SMEM)
 PARAMS = pltpu.CompilerParams(vmem_limit_bytes=24 * 1024 * 1024)
@@ -222,7 +223,9 @@
 
 
 def finish_kernel(masks_ref, x_ref, gate_ref, bins_ref, ow_ref, dw_ref, *refs):
-    parts, overs = refs[:OWNERS], refs[OWNERS : 2 * OWNERS]
+    parts, overs = [
+        [refs[first + DIAGONAL_FIRST.index(d)] for d in range(OWNERS)] for first in (0, OWNERS)
+    ]
     out_ref, loss_ref, held = refs[2 * OWNERS :]
     channels = x_ref.shape[0]
     size, width = parts[0].shape[0] // 2, parts[0].shape[1]
@@ -369,8 +372,8 @@
         args=(masks, own, core, near, near_over, far, cross, both_over),
         flops=8 * size * 2 * tile_rows * 2 * width,
     )
-    parts = [parts[0]] + [
-        exchange(parts[d], places, d // 2 * over_z + d % 2 * over_x) for d in range(1, OWNERS)
+    parts = [
+        exchange(parts[d], places, d // 2 * over_z + d % 2 * over_x) if d else parts[0] for d in DIAGONAL_FIRST
     ]
     parts += [exchange(value, places, over_core) for value in parts]
     gate, x_turned, out_turned, dist_turned = call(

time: 47.3 us -> 46.4 us (0.981)
  starting transfers between devices: 15 us -> 14.3 us
    all_to_all x1, starting transfers between devices: 4.95 us -> 4.27 us  [by_kernels(): loss = lax.all_to_all(loss, AXES, 0, 0, tiled=True)]
  transfers between devices with their start and end apart: 14 -> 14, of which waited for: 9 -> 10; matrix products, arithmetic and copies ran while one was open for 0% -> 0% of each run, Pallas kernels for 9% -> 9%
where the time goes in v11:
time: 46.4 us; the launch traced here: 46.1 us
  waiting for transfers between devices  22.6 us (49%)
  starting transfers between devices  14.3 us (31%)
  Pallas kernels  6.31 us (14%)
  local copies, waits for them, and re-layouts  2.13 us (5%)
  between operations  0.79 us (2%)
    ppermute x13, waiting for transfers between devices, exchange(): return lax.ppermute(value, AXES, [(at, at ^ mask) for at in range(places)])  16.7 us
    ppermute x13, starting transfers between devices, exchange(): return lax.ppermute(value, AXES, [(at, at ^ mask) for at in range(places)])  10 us
    pallas_call x9, Pallas kernels, call(): pl.pallas_call(kernel, out_shape=outs, in_specs=specs if specs is not Non...  6.31 us
    all_to_all x1, waiting for transfers between devices, by_kernels(): loss = lax.all_to_all(loss, AXES, 0, 0, tiled=True)  5.83 us
    all_to_all x1, starting transfers between devices, by_kernels(): loss = lax.all_to_all(loss, AXES, 0, 0, tiled=True)  4.27 us
    unnamed x23, local copies, waits for them, and re-layouts  1.54 us
  transfers between devices with their start and end apart: 14, of which 10 were waited for; matrix products, arithmetic and copies ran while one was open for 0% of the time, Pallas kernels for 9%

profile of v11, /device:TPU:0, one launch (start us, length us, event | category | flops | bytes accessed | tf_op | source)
XLA Modules:
  0.0 46.1 jit_solution(10335157407888545798)
XLA Ops:
  0.6 3.1 %collective-permute-start.1 = (bf16[16,64,128]{2,1,0:T(8,128)(2,1)}, bf16[16,64,128]{2,1,0:T(8,128)(2,1)S(1)}, u32[]{:S(2)}, u32[]{:S(2)}) collective-permute-start(bf16[16,64,128]{2,1,0:T(8,128)(2,1)} %x_ref.3), channel_id=1, source_target_pairs={{0,4},{1,5},{2,6},{3,7},{4,0},{5,1},{6,2},{7,3},{8,12},{9,13},{10,... | collective-permute-start | bytes 786440 | tf_op jit(solution)/shard_map/ppermute | solution.py:287
  3.7 0.0 copy-start
  3.7 1.0 %copy-done = bf16[16,64,128]{2,1,0:T(8,128)(2,1)S(1)} copy-done((bf16[16,64,128]{2,1,0:T(8,128)(2,1)S(1)}, bf16[16,64,128]{2,1,0:T(8,128)(2,1)}, u32[]{:S(2)}) %copy-start) | copy-done | bytes 262168
  4.7 0.0 copy-start.6
  4.7 0.0 copy-start.7
  4.7 0.4 shard_map.113.normed_ref
  5.1 0.4 copy-done.6
  5.5 0.0 copy-done.7
  5.5 0.0 copy-start.4
  5.5 0.0 copy-start.5
  5.5 0.6 %shard_map.114 = (bf16[512,128]{1,0:T(8,128)(2,1)S(1)}, bf16[512,128]{1,0:T(8,128)(2,1)S(1)}) custom-call(bf16[1024,128]{1,0:T(8,128)(2,1)S(1)} %shard_map.113.normed_ref, bf16[128,128]{1,0:T(8,128)(2,1)S(1)} %copy-done.6, bf16[128,128]{1,0:T(8,128)(2,1)S(1)} %copy-done.7), custom_call_target="tpu_custom_call" | custom-call | flops 67108864 | bytes 1048576 | tf_op jit(solution)/shard_map/pallas_call | solution.py:291
  6.0 0.0 copy-start.8
  6.1 2.5 %collective-permute-start.4 = (bf16[512,128]{1,0:T(8,128)(2,1)S(1)}, bf16[512,128]{1,0:T(8,128)(2,1)S(1)}, u32[]{:S(2)}, u32[]{:S(2)}) collective-permute-start(bf16[512,128]{1,0:T(8,128)(2,1)S(1)} %get-tuple-element.29), channel_id=1, source_target_pairs={{0,12},{1,13},{2,14},{3,15},{4,8},{5,9},{6,10},{7,11},{8,4},{9,5},... | collective-permute-start | bytes 393224 | tf_op jit(solution)/shard_map/ppermute | solution.py:287
  8.6 0.2 collective-permute-start.3
  8.8 0.0 copy-done.4
  8.8 0.0 copy-done.5
  8.8 0.0 copy-done.8
  8.8 1.0 %shard_map.115 = (bf16[512,128]{1,0:T(8,128)(2,1)S(1)}, bf16[512,128]{1,0:T(8,128)(2,1)S(1)}, f32[24,128]{1,0:T(8,128)S(1)}) custom-call(s32[5]{0:T(128)S(1)} %copy-done.8, bf16[1024,128]{1,0:T(8,128)(2,1)S(1)} %shard_map.113.normed_ref, bf16[128,128]{1,0:T(8,128)(2,1)S(1)} %copy-done.4, bf16[128,128]{1,0:T(8,128)(2,1)S(1)} %copy-done.5, ...), custom_call_target="tpu_custom_call" | custom-call | flops 33554432 | bytes 1048576 | tf_op jit(solution)/shard_map/pallas_call | solution.py:291
  9.8 0.9 %collective-permute-done.1.x_ref = bf16[16,64,128]{2,1,0:T(8,128)(2,1)S(1)} collective-permute-done((bf16[16,64,128]{2,1,0:T(8,128)(2,1)}, bf16[16,64,128]{2,1,0:T(8,128)(2,1)S(1)}, u32[]{:S(2)}, u32[]{:S(2)}) %collective-permute-start.1) | collective-permute-done | bytes 262176 | tf_op jit(solution)/shard_map/ppermute | solution.py:287
  10.7 1.1 %shard_map.117 = (bf16[512,128]{1,0:T(8,128)(2,1)S(1)}, bf16[512,128]{1,0:T(8,128)(2,1)S(1)}) custom-call(f32[24,128]{1,0:T(8,128)S(1)} %get-tuple-element.20.masks_ref, bf16[16,64,128]{2,1,0:T(8,128)(2,1)S(1)} %collective-permute-done.1.x_ref, bf16[128,128]{1,0:T(8,128)(2,1)S(1)} %copy-done.4, bf16[128,128]{1,0:T(8,128)(2,1)S(1)} %copy-done.5, ...), custom_call_target="tpu_custom_call" | custom-call | flops 67108864 | bytes 1048576 | tf_op jit(solution)/shard_map/pallas_call | solution.py:291
  11.8 0.1 collective-permute-start.2
  11.9 0.5 %collective-permute-start = (bf16[512,128]{1,0:T(8,128)(2,1)S(1)}, bf16[512,128]{1,0:T(8,128)(2,1)S(1)}, u32[]{:S(2)}, u32[]{:S(2)}) collective-permute-start(bf16[512,128]{1,0:T(8,128)(2,1)S(1)} %get-tuple-element.26), channel_id=1, source_target_pairs={{0,2},{1,3},{2,0},{3,1},{4,6},{5,7},{6,4},{7,5},{8,10},{9,11},{10,... | collective-permute-start | bytes 393224 | tf_op jit(solution)/shard_map/ppermute | solution.py:287
  12.4 4.1 %collective-permute-done.4.cross_ref.cross = bf16[512,128]{1,0:T(8,128)(2,1)S(1)} collective-permute-done((bf16[512,128]{1,0:T(8,128)(2,1)S(1)}, bf16[512,128]{1,0:T(8,128)(2,1)S(1)}, u32[]{:S(2)}, u32[]{:S(2)}) %collective-permute-start.4) | collective-permute-done | bytes 131104 | tf_op jit(solution)/shard_map/ppermute | solution.py:287
  16.5 3.9 %collective-permute-done.3.far_ref.far = bf16[512,128]{1,0:T(8,128)(2,1)S(1)} collective-permute-done((bf16[512,128]{1,0:T(8,128)(2,1)S(1)}, bf16[512,128]{1,0:T(8,128)(2,1)S(1)}, u32[]{:S(2)}, u32[]{:S(2)}) %collective-permute-start.3) | collective-permute-done | bytes 131104 | tf_op jit(solution)/shard_map/ppermute | solution.py:287
  20.4 0.0 collective-permute-done.2.ready_ref.near_over
  20.4 0.1 collective-permute-start.5
  20.5 0.0 collective-permute-done.core
  20.5 1.3 %collective-permute-done.5.both_over = bf16[512,128]{1,0:T(8,128)(2,1)S(1)} collective-permute-done((bf16[512,128]{1,0:T(8,128)(2,1)S(1)}, bf16[512,128]{1,0:T(8,128)(2,1)S(1)}, u32[]{:S(2)}, u32[]{:S(2)}) %collective-permute-start.5) | collective-permute-done | bytes 131104 | tf_op jit(solution)/shard_map/ppermute | solution.py:287
  21.8 0.0 copy-start.10
  21.8 0.0 copy-start.9
  21.8 0.0 copy-start.1
  21.8 0.5 %shard_map.119 = (bf16[512,128]{1,0:T(8,128)(2,1)S(1)}, bf16[512,128]{1,0:T(8,128)(2,1)S(1)}, bf16[512,128]{1,0:T(8,128)(2,1)S(1)}, bf16[512,128]{1,0:T(8,128)(2,1)S(1)}) custom-call(f32[24,128]{1,0:T(8,128)S(1)} %get-tuple-element.20.masks_ref, bf16[512,128]{1,0:T(8,128)(2,1)S(1)} %get-tuple-element.25.own, bf16[512,128]{1,0:T(8,128)(2,1)S(1)} %collective-permute-done.core, ...), custom_call_target="tpu_custom_call" | custom-call | flops 16777216 | bytes 1048576 | tf_op jit(solution)/shard_map/pallas_call | solution.py:291
  22.3 0.8 %collective-permute-start.6 = (bf16[512,128]{1,0:T(8,128)(2,1)S(1)}, bf16[512,128]{1,0:T(8,128)(2,1)S(1)}, u32[]{:S(2)}, u32[]{:S(2)}) collective-permute-start(bf16[512,128]{1,0:T(8,128)(2,1)S(1)} %get-tuple-element.30), channel_id=1, source_target_pairs={{0,5},{1,4},{2,7},{3,6},{4,1},{5,0},{6,3},{7,2},{8,13},{9,12},{10,... | collective-permute-start | bytes 393224 | tf_op jit(solution)/shard_map/ppermute | solution.py:287
  23.2 0.0 copy-start.3
  23.2 0.0 copy-start.2
  23.2 0.8 %collective-permute-start.7 = (bf16[512,128]{1,0:T(8,128)(2,1)S(1)}, bf16[512,128]{1,0:T(8,128)(2,1)S(1)}, u32[]{:S(2)}, u32[]{:S(2)}) collective-permute-start(bf16[512,128]{1,0:T(8,128)(2,1)S(1)} %get-tuple-element.31), channel_id=1, source_target_pairs={{0,1},{1,0},{2,3},{3,2},{4,5},{5,4},{6,7},{7,6},{8,9},{9,8},{10,11... | collective-permute-start | bytes 393224 | tf_op jit(solution)/shard_map/ppermute | solution.py:287
  24.0 1.9 %collective-permute-start.8 = (bf16[512,128]{1,0:T(8,128)(2,1)S(1)}, bf16[512,128]{1,0:T(8,128)(2,1)S(1)}, u32[]{:S(2)}, u32[]{:S(2)}) collective-permute-start(bf16[512,128]{1,0:T(8,128)(2,1)S(1)} %get-tuple-element.32), channel_id=1, source_target_pairs={{0,4},{1,5},{2,6},{3,7},{4,0},{5,1},{6,2},{7,3},{8,12},{9,13},{10,... | collective-permute-start | bytes 393224 | tf_op jit(solution)/shard_map/ppermute | solution.py:287
  25.9 0.0 collective-permute-start.12
  25.9 3.8 %collective-permute-done.6.refs_0_ = bf16[512,128]{1,0:T(8,128)(2,1)S(1)} collective-permute-done((bf16[512,128]{1,0:T(8,128)(2,1)S(1)}, bf16[512,128]{1,0:T(8,128)(2,1)S(1)}, u32[]{:S(2)}, u32[]{:S(2)}) %collective-permute-start.6) | collective-permute-done | bytes 131104 | tf_op jit(solution)/shard_map/ppermute | solution.py:287
  29.7 0.0 collective-permute-start.9
  29.7 1.5 %collective-permute-done.7.refs_1_ = bf16[512,128]{1,0:T(8,128)(2,1)S(1)} collective-permute-done((bf16[512,128]{1,0:T(8,128)(2,1)S(1)}, bf16[512,128]{1,0:T(8,128)(2,1)S(1)}, u32[]{:S(2)}, u32[]{:S(2)}) %collective-permute-start.7) | collective-permute-done | bytes 131104 | tf_op jit(solution)/shard_map/ppermute | solution.py:287
  31.2 0.0 collective-permute-start.10
  31.2 0.5 %collective-permute-done.8.refs_2_ = bf16[512,128]{1,0:T(8,128)(2,1)S(1)} collective-permute-done((bf16[512,128]{1,0:T(8,128)(2,1)S(1)}, bf16[512,128]{1,0:T(8,128)(2,1)S(1)}, u32[]{:S(2)}, u32[]{:S(2)}) %collective-permute-start.8) | collective-permute-done | bytes 131104 | tf_op jit(solution)/shard_map/ppermute | solution.py:287
  31.7 0.0 collective-permute-start.11
  31.8 0.0 copy-done.10
  31.8 0.1 reshape.7.bins_ref
  31.8 0.0 copy-done.9
  31.8 0.1 copy.12.dw_ref
  31.9 0.0 copy-done.1
  32.0 0.0 copy-done.3
  32.0 0.0 copy-done.2
  32.0 0.4 shard_map.116
  32.3 0.0 collective-permute-done.12.refs_7_
  32.4 0.0 collective-permute-done.9.refs_4_
  32.4 0.2 collective-permute-done.10.refs_5_
  32.6 0.5 %collective-permute-done.11.refs_6_ = bf16[512,128]{1,0:T(8,128)(2,1)S(1)} collective-permute-done((bf16[512,128]{1,0:T(8,128)(2,1)S(1)}, bf16[512,128]{1,0:T(8,128)(2,1)S(1)}, u32[]{:S(2)}, u32[]{:S(2)}) %collective-permute-start.11) | collective-permute-done | bytes 131104 | tf_op jit(solution)/shard_map/ppermute | solution.py:287
  33.1 1.5 %shard_map.120 = (bf16[128,1024]{1,0:T(8,128)(2,1)S(1)}, f32[16,8,128]{2,1,0:T(8,128)}) custom-call(f32[24,128]{1,0:T(8,128)S(1)} %get-tuple-element.20.masks_ref, f32[128,1024]{1,0:T(8,128)S(1)} %get-tuple-element.21.x_ref, f32[128,1024]{1,0:T(8,128)S(1)} %get-tuple-element.22.gate_ref, s32[8,128]{1,0:T(8,128)S(1)} %reshape.7.bins_ref, ...), custom_call_target="tpu_custom_call" | custom-call | flops 100663296 | bytes 1048576 | tf_op jit(solution)/shard_map/pallas_call | solution.py:291
  34.6 4.3 %all-to-all-start = ((f32[16,8,128]{2,1,0:T(8,128)}), f32[16,8,128]{2,1,0:T(8,128)S(1)}, u32[]{:S(2)}, u32[]{:S(2)}) async-start(f32[16,8,128]{2,1,0:T(8,128)} %get-tuple-element.35), calls=%async_computation | async-start | bytes 131072 | tf_op jit(solution)/shard_map/all_to_all | solution.py:406
  38.9 0.8 %shard_map.121 = bf16[16,64,128]{2,1,0:T(8,128)(2,1)} custom-call(bf16[128,1024]{1,0:T(8,128)(2,1)S(1)} %get-tuple-element.34.turned_ref), custom_call_target="tpu_custom_call" | custom-call | flops 67108864 | bytes 1048576 | tf_op jit(solution)/shard_map/pallas_call | solution.py:291
  39.8 5.8 %all-to-all-done = f32[16,8,128]{2,1,0:T(8,128)S(1)} async-done(((f32[16,8,128]{2,1,0:T(8,128)}), f32[16,8,128]{2,1,0:T(8,128)S(1)}, u32[]{:S(2)}, u32[]{:S(2)}) %all-to-all-start) | async-done | bytes 65568 | tf_op jit(solution)/shard_map/all_to_all | solution.py:406
  45.6 0.5 %slice.3 = f32[1,1]{1,0:T(1,128)} slice(f32[8,128]{1,0:T(8,128)S(1)} %reduce_sum.9), slice={[0:1], [0:1]} | slice | bytes 8 | tf_op jit(solution)/shard_map/slice | solution.py:407
  (2 shorter events, 0.0 us)
Async XLA Ops:
  0.6 10.1 %collective-permute-start.1 = (bf16[16,64,128]{2,1,0:T(8,128)(2,1)}, bf16[16,64,128]{2,1,0:T(8,128)(2,1)S(1)}, u32[]{:S(2)}, u32[]{:S(2)}) collective-permute-start(bf16[16,64,128]{2,1,0:T(8,128)(2,1)} %x_ref.3), channel_id=1, source_target_pairs={{0,4},{1,5},{2,6},{3,7},{4,0},{5,1},{6,2},{7,3},{8,12},{9,13},{10,... | collective-permute-start | bytes 786440 | tf_op jit(solution)/shard_map/ppermute | solution.py:287
  3.7 1.0 %copy-start = (bf16[16,64,128]{2,1,0:T(8,128)(2,1)S(1)}, bf16[16,64,128]{2,1,0:T(8,128)(2,1)}, u32[]{:S(2)}) copy-start(bf16[16,64,128]{2,1,0:T(8,128)(2,1)} %x_ref.3) | copy-start | bytes 786436
  4.7 0.8 %copy-start.6 = (bf16[128,128]{1,0:T(8,128)(2,1)S(1)}, bf16[128,128]{1,0:T(8,128)(2,1)}, u32[]{:S(2)}) copy-start(bf16[128,128]{1,0:T(8,128)(2,1)} %rw_ref.1) | copy-start | bytes 98308
  4.7 0.8 %copy-start.7 = (bf16[128,128]{1,0:T(8,128)(2,1)S(1)}, bf16[128,128]{1,0:T(8,128)(2,1)}, u32[]{:S(2)}) copy-start(bf16[128,128]{1,0:T(8,128)(2,1)} %rg_ref.1) | copy-start | bytes 98308
  5.5 3.3 %copy-start.4 = (bf16[128,128]{1,0:T(8,128)(2,1)S(1)}, bf16[128,128]{1,0:T(8,128)(2,1)}, u32[]{:S(2)}) copy-start(bf16[128,128]{1,0:T(8,128)(2,1)} %lw_ref.1) | copy-start | bytes 98308
  5.5 3.3 %copy-start.5 = (bf16[128,128]{1,0:T(8,128)(2,1)S(1)}, bf16[128,128]{1,0:T(8,128)(2,1)}, u32[]{:S(2)}) copy-start(bf16[128,128]{1,0:T(8,128)(2,1)} %lg_ref.1) | copy-start | bytes 98308
  6.0 2.8 %copy-start.8 = (s32[5]{0:T(128)S(1)}, s32[5]{0:T(128)}, u32[]{:S(2)}) copy-start(s32[5]{0:T(128)} %lens_ref.1) | copy-start | bytes 64
  6.1 10.4 %collective-permute-start.4 = (bf16[512,128]{1,0:T(8,128)(2,1)S(1)}, bf16[512,128]{1,0:T(8,128)(2,1)S(1)}, u32[]{:S(2)}, u32[]{:S(2)}) collective-permute-start(bf16[512,128]{1,0:T(8,128)(2,1)S(1)} %get-tuple-element.29), channel_id=1, source_target_pairs={{0,12},{1,13},{2,14},{3,15},{4,8},{5,9},{6,10},{7,11},{8,4},{9,5},... | collective-permute-start | bytes 393224 | tf_op jit(solution)/shard_map/ppermute | solution.py:287
  8.6 11.8 %collective-permute-start.3 = (bf16[512,128]{1,0:T(8,128)(2,1)S(1)}, bf16[512,128]{1,0:T(8,128)(2,1)S(1)}, u32[]{:S(2)}, u32[]{:S(2)}) collective-permute-start(bf16[512,128]{1,0:T(8,128)(2,1)S(1)} %get-tuple-element.19.stay_ref), channel_id=1, source_target_pairs={{0,8},{1,9},{2,10},{3,11},{4,12},{5,13},{6,14},{7,15},{8,0},{9,1},... | collective-permute-start | bytes 393224 | tf_op jit(solution)/shard_map/ppermute | solution.py:287
  11.8 8.5 %collective-permute-start.2 = (bf16[512,128]{1,0:T(8,128)(2,1)S(1)}, bf16[512,128]{1,0:T(8,128)(2,1)S(1)}, u32[]{:S(2)}, u32[]{:S(2)}) collective-permute-start(bf16[512,128]{1,0:T(8,128)(2,1)S(1)} %get-tuple-element.28), channel_id=1, source_target_pairs={{0,2},{1,3},{2,0},{3,1},{4,6},{5,7},{6,4},{7,5},{8,10},{9,11},{10,... | collective-permute-start | bytes 393224 | tf_op jit(solution)/shard_map/ppermute | solution.py:287
  11.9 8.6 %collective-permute-start = (bf16[512,128]{1,0:T(8,128)(2,1)S(1)}, bf16[512,128]{1,0:T(8,128)(2,1)S(1)}, u32[]{:S(2)}, u32[]{:S(2)}) collective-permute-start(bf16[512,128]{1,0:T(8,128)(2,1)S(1)} %get-tuple-element.26), channel_id=1, source_target_pairs={{0,2},{1,3},{2,0},{3,1},{4,6},{5,7},{6,4},{7,5},{8,10},{9,11},{10,... | collective-permute-start | bytes 393224 | tf_op jit(solution)/shard_map/ppermute | solution.py:287
  20.4 1.4 %collective-permute-start.5 = (bf16[512,128]{1,0:T(8,128)(2,1)S(1)}, bf16[512,128]{1,0:T(8,128)(2,1)S(1)}, u32[]{:S(2)}, u32[]{:S(2)}) collective-permute-start(bf16[512,128]{1,0:T(8,128)(2,1)S(1)} %shard_map.118), channel_id=1, source_target_pairs={{0,2},{1,3},{2,0},{3,1},{4,6},{5,7},{6,4},{7,5},{8,10},{9,11},{10,... | collective-permute-start | bytes 393224 | tf_op jit(solution)/shard_map/ppermute | solution.py:287
  21.8 10.0 %copy-start.10 = (s32[16,64]{1,0:T(8,128)S(1)}, s32[16,64]{1,0:T(8,128)}, u32[]{:S(2)}) copy-start(s32[16,64]{1,0:T(8,128)} %param.11) | copy-start | bytes 12292
  21.8 10.0 %copy-start.9 = (bf16[128,64]{0,1:T(8,128)(2,1)S(1)}, bf16[128,64]{0,1:T(8,128)(2,1)}, u32[]{:S(2)}) copy-start(bf16[128,64]{0,1:T(8,128)(2,1)} %param.19) | copy-start | bytes 49156
  21.8 10.2 %copy-start.1 = (bf16[16,64,128]{2,1,0:T(8,128)(2,1)S(1)}, bf16[16,64,128]{2,1,0:T(8,128)(2,1)}, u32[]{:S(2)}) copy-start(bf16[16,64,128]{2,1,0:T(8,128)(2,1)} %x_ref.3) | copy-start | bytes 786436
  22.3 7.4 %collective-permute-start.6 = (bf16[512,128]{1,0:T(8,128)(2,1)S(1)}, bf16[512,128]{1,0:T(8,128)(2,1)S(1)}, u32[]{:S(2)}, u32[]{:S(2)}) collective-permute-start(bf16[512,128]{1,0:T(8,128)(2,1)S(1)} %get-tuple-element.30), channel_id=1, source_target_pairs={{0,5},{1,4},{2,7},{3,6},{4,1},{5,0},{6,3},{7,2},{8,13},{9,12},{10,... | collective-permute-start | bytes 393224 | tf_op jit(solution)/shard_map/ppermute | solution.py:287
  23.2 8.8 %copy-start.3 = (bf16[128,128]{1,0:T(8,128)(2,1)S(1)}, bf16[128,128]{1,0:T(8,128)(2,1)}, u32[]{:S(2)}) copy-start(bf16[128,128]{1,0:T(8,128)(2,1)} %ow_ref.1) | copy-start | bytes 98308
  23.2 8.8 %copy-start.2 = (bf16[128,128]{1,0:T(8,128)(2,1)S(1)}, bf16[128,128]{1,0:T(8,128)(2,1)}, u32[]{:S(2)}) copy-start(bf16[128,128]{1,0:T(8,128)(2,1)} %gw_ref.1) | copy-start | bytes 98308
  23.2 8.1 %collective-permute-start.7 = (bf16[512,128]{1,0:T(8,128)(2,1)S(1)}, bf16[512,128]{1,0:T(8,128)(2,1)S(1)}, u32[]{:S(2)}, u32[]{:S(2)}) collective-permute-start(bf16[512,128]{1,0:T(8,128)(2,1)S(1)} %get-tuple-element.31), channel_id=1, source_target_pairs={{0,1},{1,0},{2,3},{3,2},{4,5},{5,4},{6,7},{7,6},{8,9},{9,8},{10,11... | collective-permute-start | bytes 393224 | tf_op jit(solution)/shard_map/ppermute | solution.py:287
  24.0 7.7 %collective-permute-start.8 = (bf16[512,128]{1,0:T(8,128)(2,1)S(1)}, bf16[512,128]{1,0:T(8,128)(2,1)S(1)}, u32[]{:S(2)}, u32[]{:S(2)}) collective-permute-start(bf16[512,128]{1,0:T(8,128)(2,1)S(1)} %get-tuple-element.32), channel_id=1, source_target_pairs={{0,4},{1,5},{2,6},{3,7},{4,0},{5,1},{6,2},{7,3},{8,12},{9,13},{10,... | collective-permute-start | bytes 393224 | tf_op jit(solution)/shard_map/ppermute | solution.py:287
  25.9 6.4 %collective-permute-start.12 = (bf16[512,128]{1,0:T(8,128)(2,1)S(1)}, bf16[512,128]{1,0:T(8,128)(2,1)S(1)}, u32[]{:S(2)}, u32[]{:S(2)}) collective-permute-start(bf16[512,128]{1,0:T(8,128)(2,1)S(1)} %get-tuple-element.33.refs_3_), channel_id=1, source_target_pairs={{0,2},{1,3},{2,0},{3,1},{4,6},{5,7},{6,4},{7,5},{8,10},{9,11},{10,... | collective-permute-start | bytes 393224 | tf_op jit(solution)/shard_map/ppermute | solution.py:287
  29.7 2.7 %collective-permute-start.9 = (bf16[512,128]{1,0:T(8,128)(2,1)S(1)}, bf16[512,128]{1,0:T(8,128)(2,1)S(1)}, u32[]{:S(2)}, u32[]{:S(2)}) collective-permute-start(bf16[512,128]{1,0:T(8,128)(2,1)S(1)} %collective-permute-done.6.refs_0_), channel_id=1, source_target_pairs={{0,2},{1,3},{2,0},{3,1},{4,6},{5,7},{6,4},{7,5},{8,10},{9,11},{10,... | collective-permute-start | bytes 393224 | tf_op jit(solution)/shard_map/ppermute | solution.py:287
  31.2 1.3 %collective-permute-start.10 = (bf16[512,128]{1,0:T(8,128)(2,1)S(1)}, bf16[512,128]{1,0:T(8,128)(2,1)S(1)}, u32[]{:S(2)}, u32[]{:S(2)}) collective-permute-start(bf16[512,128]{1,0:T(8,128)(2,1)S(1)} %collective-permute-done.7.refs_1_), channel_id=1, source_target_pairs={{0,2},{1,3},{2,0},{3,1},{4,6},{5,7},{6,4},{7,5},{8,10},{9,11},{10,... | collective-permute-start | bytes 393224 | tf_op jit(solution)/shard_map/ppermute | solution.py:287
  31.7 1.3 %collective-permute-start.11 = (bf16[512,128]{1,0:T(8,128)(2,1)S(1)}, bf16[512,128]{1,0:T(8,128)(2,1)S(1)}, u32[]{:S(2)}, u32[]{:S(2)}) collective-permute-start(bf16[512,128]{1,0:T(8,128)(2,1)S(1)} %collective-permute-done.8.refs_2_), channel_id=1, source_target_pairs={{0,2},{1,3},{2,0},{3,1},{4,6},{5,7},{6,4},{7,5},{8,10},{9,11},{10,... | collective-permute-start | bytes 393224 | tf_op jit(solution)/shard_map/ppermute | solution.py:287
  34.6 11.0 %all-to-all-start = ((f32[16,8,128]{2,1,0:T(8,128)}), f32[16,8,128]{2,1,0:T(8,128)S(1)}, u32[]{:S(2)}, u32[]{:S(2)}) async-start(f32[16,8,128]{2,1,0:T(8,128)} %get-tuple-element.35), calls=%async_computation | async-start | bytes 131072 | tf_op jit(solution)/shard_map/all_to_all | solution.py:406

commit v12 on v11

--- a/solution.py
+++ b/solution.py
@@ -273,7 +273,7 @@
         loss = loss + masks_ref[first // 2 : first // 2 + 1] * (log_total - picked)
     last = masks_ref.shape[0] - 1
     loss = jnp.sum(loss * masks_ref[last : last + 1], axis=1, keepdims=True)
-    loss_ref[...] = jnp.broadcast_to(loss[None], loss_ref.shape)
+    loss_ref[...] = jnp.broadcast_to(loss, loss_ref.shape)
 
 
 def turn_back_kernel(turned_ref, out_ref):
@@ -389,7 +389,7 @@
     )
     pair_out, loss = call(
         finish_kernel,
-        [struct((channels, spots), bf16), struct((places, 8, 128), f32)],
+        [struct((channels, spots), bf16), struct((8, 128), f32)],
         [held],
         args=(
             masks,
@@ -403,8 +403,13 @@
         flops=6 * spots * channels * channels,
     )
     pair_out = call(turn_back_kernel, struct(pair_repr.shape, bf16), args=(pair_out,), flops=1 << 26)
-    loss = lax.all_to_all(loss, AXES, 0, 0, tiled=True)
-    return (pair_out, jnp.sum(loss, axis=0)[0, :1])
+    loss = loss + exchange(loss, places, over_core)
+    diagonal, beside, near_loss = [
+        exchange(loss, places, mask) for mask in (over_z + over_x, over_x, over_z)
+    ]
+    loss = (diagonal + near_loss) + (beside + loss)
+    loss = loss + exchange(loss, places, over_half)
+    return (pair_out, loss[0, :1])
 
 
 def by_all_to_all(

time: 46.4 us -> 46.1 us (level)
  starting transfers between devices: 14.3 us -> 16.3 us
  waiting for transfers between devices: 22.6 us -> 21 us
  Pallas kernels: 6.31 us -> 5.69 us
    ppermute x13 -> x18, starting transfers between devices: 10 us -> 16.3 us  [exchange(): return lax.ppermute(value, AXES, [(at, at ^ mask) for at in range(places)])]
    all_to_all x1 -> x0, waiting for transfers between devices: 5.83 us -> none  [by_kernels(): loss = lax.all_to_all(loss, AXES, 0, 0, tiled=True)]
    all_to_all x1 -> x0, starting transfers between devices: 4.27 us -> none  [by_kernels(): loss = lax.all_to_all(loss, AXES, 0, 0, tiled=True)]
    ppermute x13 -> x18, waiting for transfers between devices: 16.7 us -> 21 us  [exchange(): return lax.ppermute(value, AXES, [(at, at ^ mask) for at in range(places)])]
    pallas_call x9, Pallas kernels: 6.31 us -> 5.69 us  [call(): pl.pallas_call(kernel, out_shape=outs, in_specs=specs if specs is not Non...]
  transfers between devices with their start and end apart: 14 -> 18, of which waited for: 10 -> 12; matrix products, arithmetic and copies ran while one was open for 0% -> 0% of each run, Pallas kernels for 9% -> 9%
where the time goes in v12:
time: 46.1 us; the launch traced here: 45.9 us
  waiting for transfers between devices  21 us (46%)
  starting transfers between devices  16.3 us (35%)
  Pallas kernels  5.69 us (12%)
  local copies, waits for them, and re-layouts  2.13 us (5%)
  between operations  0.79 us (2%)
    ppermute x18, waiting for transfers between devices, exchange(): return lax.ppermute(value, AXES, [(at, at ^ mask) for at in range(places)])  21 us
    ppermute x18, starting transfers between devices, exchange(): return lax.ppermute(value, AXES, [(at, at ^ mask) for at in range(places)])  16.3 us
    pallas_call x9, Pallas kernels, call(): pl.pallas_call(kernel, out_shape=outs, in_specs=specs if specs is not Non...  5.69 us
    unnamed x23, local copies, waits for them, and re-layouts  1.54 us
  transfers between devices with their start and end apart: 18, of which 12 were waited for; matrix products, arithmetic and copies ran while one was open for 0% of the time, Pallas kernels for 9%

profile of v12, /device:TPU:0, one launch (start us, length us, event | category | flops | bytes accessed | tf_op | source)
XLA Modules:
  0.0 45.9 jit_solution(176095039555734224)
XLA Ops:
  0.6 3.1 %collective-permute-start.1 = (bf16[16,64,128]{2,1,0:T(8,128)(2,1)}, bf16[16,64,128]{2,1,0:T(8,128)(2,1)S(1)}, u32[]{:S(2)}, u32[]{:S(2)}) collective-permute-start(bf16[16,64,128]{2,1,0:T(8,128)(2,1)} %x_ref.3), channel_id=1, source_target_pairs={{0,4},{1,5},{2,6},{3,7},{4,0},{5,1},{6,2},{7,3},{8,12},{9,13},{10,... | collective-permute-start | bytes 786440 | tf_op jit(solution)/shard_map/ppermute | solution.py:287
  3.7 0.0 copy-start
  3.7 1.0 %copy-done = bf16[16,64,128]{2,1,0:T(8,128)(2,1)S(1)} copy-done((bf16[16,64,128]{2,1,0:T(8,128)(2,1)S(1)}, bf16[16,64,128]{2,1,0:T(8,128)(2,1)}, u32[]{:S(2)}) %copy-start) | copy-done | bytes 262168
  4.7 0.0 copy-start.7
  4.7 0.4 shard_map.113.normed_ref
  5.1 0.4 copy-done.6
  5.5 0.0 copy-done.7
  5.5 0.0 copy-start.4
  5.5 0.0 copy-start.5
  5.5 0.6 %shard_map.114 = (bf16[512,128]{1,0:T(8,128)(2,1)S(1)}, bf16[512,128]{1,0:T(8,128)(2,1)S(1)}) custom-call(bf16[1024,128]{1,0:T(8,128)(2,1)S(1)} %shard_map.113.normed_ref, bf16[128,128]{1,0:T(8,128)(2,1)S(1)} %copy-done.6, bf16[128,128]{1,0:T(8,128)(2,1)S(1)} %copy-done.7), custom_call_target="tpu_custom_call" | custom-call | flops 67108864 | bytes 1048576 | tf_op jit(solution)/shard_map/pallas_call | solution.py:291
  6.0 0.0 copy-start.8
  6.1 2.7 %collective-permute-start.3 = (bf16[512,128]{1,0:T(8,128)(2,1)S(1)}, bf16[512,128]{1,0:T(8,128)(2,1)S(1)}, u32[]{:S(2)}, u32[]{:S(2)}) collective-permute-start(bf16[512,128]{1,0:T(8,128)(2,1)S(1)} %get-tuple-element.19.stay_ref), channel_id=1, source_target_pairs={{0,8},{1,9},{2,10},{3,11},{4,12},{5,13},{6,14},{7,15},{8,0},{9,1},... | collective-permute-start | bytes 393224 | tf_op jit(solution)/shard_map/ppermute | solution.py:287
  8.7 0.0 collective-permute-start.4
  8.7 0.0 copy-done.4
  8.7 0.0 copy-done.5
  8.7 0.0 copy-done.8
  8.7 1.0 %shard_map.115 = (bf16[512,128]{1,0:T(8,128)(2,1)S(1)}, bf16[512,128]{1,0:T(8,128)(2,1)S(1)}, f32[24,128]{1,0:T(8,128)S(1)}) custom-call(s32[5]{0:T(128)S(1)} %copy-done.8, bf16[1024,128]{1,0:T(8,128)(2,1)S(1)} %shard_map.113.normed_ref, bf16[128,128]{1,0:T(8,128)(2,1)S(1)} %copy-done.4, bf16[128,128]{1,0:T(8,128)(2,1)S(1)} %copy-done.5, ...), custom_call_target="tpu_custom_call" | custom-call | flops 33554432 | bytes 1048576 | tf_op jit(solution)/shard_map/pallas_call | solution.py:291
  9.8 2.4 %collective-permute-done.1.x_ref = bf16[16,64,128]{2,1,0:T(8,128)(2,1)S(1)} collective-permute-done((bf16[16,64,128]{2,1,0:T(8,128)(2,1)}, bf16[16,64,128]{2,1,0:T(8,128)(2,1)S(1)}, u32[]{:S(2)}, u32[]{:S(2)}) %collective-permute-start.1) | collective-permute-done | bytes 262176 | tf_op jit(solution)/shard_map/ppermute | solution.py:287
  12.2 1.1 %shard_map.117 = (bf16[512,128]{1,0:T(8,128)(2,1)S(1)}, bf16[512,128]{1,0:T(8,128)(2,1)S(1)}) custom-call(f32[24,128]{1,0:T(8,128)S(1)} %get-tuple-element.20.masks_ref, bf16[16,64,128]{2,1,0:T(8,128)(2,1)S(1)} %collective-permute-done.1.x_ref, bf16[128,128]{1,0:T(8,128)(2,1)S(1)} %copy-done.4, bf16[128,128]{1,0:T(8,128)(2,1)S(1)} %copy-done.5, ...), custom_call_target="tpu_custom_call" | custom-call | flops 67108864 | bytes 1048576 | tf_op jit(solution)/shard_map/pallas_call | solution.py:291
  13.3 0.1 collective-permute-start.2
  13.3 0.5 %collective-permute-start = (bf16[512,128]{1,0:T(8,128)(2,1)S(1)}, bf16[512,128]{1,0:T(8,128)(2,1)S(1)}, u32[]{:S(2)}, u32[]{:S(2)}) collective-permute-start(bf16[512,128]{1,0:T(8,128)(2,1)S(1)} %get-tuple-element.26), channel_id=1, source_target_pairs={{0,2},{1,3},{2,0},{3,1},{4,6},{5,7},{6,4},{7,5},{8,10},{9,11},{10,... | collective-permute-start | bytes 393224 | tf_op jit(solution)/shard_map/ppermute | solution.py:287
  13.8 5.2 %collective-permute-done.3.far_ref.far = bf16[512,128]{1,0:T(8,128)(2,1)S(1)} collective-permute-done((bf16[512,128]{1,0:T(8,128)(2,1)S(1)}, bf16[512,128]{1,0:T(8,128)(2,1)S(1)}, u32[]{:S(2)}, u32[]{:S(2)}) %collective-permute-start.3) | collective-permute-done | bytes 131104 | tf_op jit(solution)/shard_map/ppermute | solution.py:287
  19.1 0.0 collective-permute-done.4.cross_ref.cross
  19.1 0.0 collective-permute-done.2.ready_ref.near_over
  19.1 0.1 collective-permute-start.5
  19.2 0.0 collective-permute-done.core
  19.2 1.3 %collective-permute-done.5.both_over = bf16[512,128]{1,0:T(8,128)(2,1)S(1)} collective-permute-done((bf16[512,128]{1,0:T(8,128)(2,1)S(1)}, bf16[512,128]{1,0:T(8,128)(2,1)S(1)}, u32[]{:S(2)}, u32[]{:S(2)}) %collective-permute-start.5) | collective-permute-done | bytes 131104 | tf_op jit(solution)/shard_map/ppermute | solution.py:287
  20.5 0.0 copy-start.9
  20.5 0.5 %shard_map.119 = (bf16[512,128]{1,0:T(8,128)(2,1)S(1)}, bf16[512,128]{1,0:T(8,128)(2,1)S(1)}, bf16[512,128]{1,0:T(8,128)(2,1)S(1)}, bf16[512,128]{1,0:T(8,128)(2,1)S(1)}) custom-call(f32[24,128]{1,0:T(8,128)S(1)} %get-tuple-element.20.masks_ref, bf16[512,128]{1,0:T(8,128)(2,1)S(1)} %get-tuple-element.25.own, bf16[512,128]{1,0:T(8,128)(2,1)S(1)} %collective-permute-done.core, ...), custom_call_target="tpu_custom_call" | custom-call | flops 16777216 | bytes 1048576 | tf_op jit(solution)/shard_map/pallas_call | solution.py:291
  21.0 1.6 %collective-permute-start.7 = (bf16[512,128]{1,0:T(8,128)(2,1)S(1)}, bf16[512,128]{1,0:T(8,128)(2,1)S(1)}, u32[]{:S(2)}, u32[]{:S(2)}) collective-permute-start(bf16[512,128]{1,0:T(8,128)(2,1)S(1)} %get-tuple-element.31), channel_id=1, source_target_pairs={{0,1},{1,0},{2,3},{3,2},{4,5},{5,4},{6,7},{7,6},{8,9},{9,8},{10,11... | collective-permute-start | bytes 393224 | tf_op jit(solution)/shard_map/ppermute | solution.py:287
  22.6 2.0 %collective-permute-start.8 = (bf16[512,128]{1,0:T(8,128)(2,1)S(1)}, bf16[512,128]{1,0:T(8,128)(2,1)S(1)}, u32[]{:S(2)}, u32[]{:S(2)}) collective-permute-start(bf16[512,128]{1,0:T(8,128)(2,1)S(1)} %get-tuple-element.32), channel_id=1, source_target_pairs={{0,4},{1,5},{2,6},{3,7},{4,0},{5,1},{6,2},{7,3},{8,12},{9,13},{10,... | collective-permute-start | bytes 393224 | tf_op jit(solution)/shard_map/ppermute | solution.py:287
  24.6 0.0 collective-permute-start.6
  24.6 0.0 collective-permute-start.12
  24.6 2.1 %collective-permute-done.7.refs_1_ = bf16[512,128]{1,0:T(8,128)(2,1)S(1)} collective-permute-done((bf16[512,128]{1,0:T(8,128)(2,1)S(1)}, bf16[512,128]{1,0:T(8,128)(2,1)S(1)}, u32[]{:S(2)}, u32[]{:S(2)}) %collective-permute-start.7) | collective-permute-done | bytes 131104 | tf_op jit(solution)/shard_map/ppermute | solution.py:287
  26.7 0.0 collective-permute-start.10
  26.7 2.3 %collective-permute-done.8.refs_2_ = bf16[512,128]{1,0:T(8,128)(2,1)S(1)} collective-permute-done((bf16[512,128]{1,0:T(8,128)(2,1)S(1)}, bf16[512,128]{1,0:T(8,128)(2,1)S(1)}, u32[]{:S(2)}, u32[]{:S(2)}) %collective-permute-start.8) | collective-permute-done | bytes 131104 | tf_op jit(solution)/shard_map/ppermute | solution.py:287
  29.0 0.0 collective-permute-start.11
  29.0 1.9 %collective-permute-done.6.refs_0_ = bf16[512,128]{1,0:T(8,128)(2,1)S(1)} collective-permute-done((bf16[512,128]{1,0:T(8,128)(2,1)S(1)}, bf16[512,128]{1,0:T(8,128)(2,1)S(1)}, u32[]{:S(2)}, u32[]{:S(2)}) %collective-permute-start.6) | collective-permute-done | bytes 131104 | tf_op jit(solution)/shard_map/ppermute | solution.py:287
  30.9 0.0 collective-permute-start.9
  30.9 0.0 copy-done.9
  30.9 0.1 copy.12.dw_ref
  31.0 0.0 copy-done.10
  31.0 0.1 reshape.7.bins_ref
  31.1 0.0 copy-done.1
  31.1 0.0 copy-done.3
  31.1 0.0 copy-done.2
  31.1 0.4 shard_map.116
  31.4 0.0 collective-permute-done.12.refs_7_
  31.5 0.0 collective-permute-done.10.refs_5_
  31.5 0.0 collective-permute-done.11.refs_6_
  31.5 0.7 %collective-permute-done.9.refs_4_ = bf16[512,128]{1,0:T(8,128)(2,1)S(1)} collective-permute-done((bf16[512,128]{1,0:T(8,128)(2,1)S(1)}, bf16[512,128]{1,0:T(8,128)(2,1)S(1)}, u32[]{:S(2)}, u32[]{:S(2)}) %collective-permute-start.9) | collective-permute-done | bytes 131104 | tf_op jit(solution)/shard_map/ppermute | solution.py:287
  32.2 0.9 %shard_map.120 = (bf16[128,1024]{1,0:T(8,128)(2,1)S(1)}, f32[8,128]{1,0:T(8,128)S(1)}) custom-call(f32[24,128]{1,0:T(8,128)S(1)} %get-tuple-element.20.masks_ref, f32[128,1024]{1,0:T(8,128)S(1)} %get-tuple-element.21.x_ref, f32[128,1024]{1,0:T(8,128)S(1)} %get-tuple-element.22.gate_ref, s32[8,128]{1,0:T(8,128)S(1)} %reshape.7.bins_ref, ...), custom_call_target="tpu_custom_call" | custom-call | flops 100663296 | bytes 1048576 | tf_op jit(solution)/shard_map/pallas_call | solution.py:291
  33.1 0.2 collective-permute-start.13
  33.3 1.0 %collective-permute-done.13 = f32[8,128]{1,0:T(8,128)S(1)} collective-permute-done((f32[8,128]{1,0:T(8,128)S(1)}, f32[8,128]{1,0:T(8,128)S(1)}, u32[]{:S(2)}, u32[]{:S(2)}) %collective-permute-start.13) | collective-permute-done | bytes 4128 | tf_op jit(solution)/shard_map/ppermute | solution.py:287
  34.3 2.7 %collective-permute-start.14 = (f32[8,128]{1,0:T(8,128)S(1)}, f32[8,128]{1,0:T(8,128)S(1)}, u32[]{:S(2)}, u32[]{:S(2)}) collective-permute-start(f32[8,128]{1,0:T(8,128)S(1)} %add.15), channel_id=1, source_target_pairs={{0,5},{1,4},{2,7},{3,6},{4,1},{5,0},{6,3},{7,2},{8,13},{9,12},{10,... | collective-permute-start | bytes 12296 | tf_op jit(solution)/shard_map/ppermute | solution.py:287
  37.0 0.3 collective-permute-start.15
  37.3 0.5 %collective-permute-start.16 = (f32[8,128]{1,0:T(8,128)S(1)}, f32[8,128]{1,0:T(8,128)S(1)}, u32[]{:S(2)}, u32[]{:S(2)}) collective-permute-start(f32[8,128]{1,0:T(8,128)S(1)} %add.15), channel_id=1, source_target_pairs={{0,1},{1,0},{2,3},{3,2},{4,5},{5,4},{6,7},{7,6},{8,9},{9,8},{10,11... | collective-permute-start | bytes 12296 | tf_op jit(solution)/shard_map/ppermute | solution.py:287
  37.8 1.0 %collective-permute-done.14 = f32[8,128]{1,0:T(8,128)S(1)} collective-permute-done((f32[8,128]{1,0:T(8,128)S(1)}, f32[8,128]{1,0:T(8,128)S(1)}, u32[]{:S(2)}, u32[]{:S(2)}) %collective-permute-start.14) | collective-permute-done | bytes 4128 | tf_op jit(solution)/shard_map/ppermute | solution.py:287
  38.8 1.8 %collective-permute-done.15 = f32[8,128]{1,0:T(8,128)S(1)} collective-permute-done((f32[8,128]{1,0:T(8,128)S(1)}, f32[8,128]{1,0:T(8,128)S(1)}, u32[]{:S(2)}, u32[]{:S(2)}) %collective-permute-start.15) | collective-permute-done | bytes 4128 | tf_op jit(solution)/shard_map/ppermute | solution.py:287
  40.6 0.3 collective-permute-done.16
  40.9 2.8 %collective-permute-start.17 = (f32[8,128]{1,0:T(8,128)S(1)}, f32[8,128]{1,0:T(8,128)S(1)}, u32[]{:S(2)}, u32[]{:S(2)}) collective-permute-start(f32[8,128]{1,0:T(8,128)S(1)} %add_add_fusion), channel_id=1, source_target_pairs={{0,8},{1,9},{2,10},{3,11},{4,12},{5,13},{6,14},{7,15},{8,0},{9,1},... | collective-permute-start | bytes 12296 | tf_op jit(solution)/shard_map/ppermute | solution.py:287
  43.6 0.8 %shard_map.121 = bf16[16,64,128]{2,1,0:T(8,128)(2,1)} custom-call(bf16[128,1024]{1,0:T(8,128)(2,1)S(1)} %get-tuple-element.34.turned_ref), custom_call_target="tpu_custom_call" | custom-call | flops 67108864 | bytes 1048576 | tf_op jit(solution)/shard_map/pallas_call | solution.py:291
  44.5 0.9 %collective-permute-done.17 = f32[8,128]{1,0:T(8,128)S(1)} collective-permute-done((f32[8,128]{1,0:T(8,128)S(1)}, f32[8,128]{1,0:T(8,128)S(1)}, u32[]{:S(2)}, u32[]{:S(2)}) %collective-permute-start.17) | collective-permute-done | bytes 4128 | tf_op jit(solution)/shard_map/ppermute | solution.py:287
  45.4 0.5 %slice.3 = f32[1,1]{1,0:T(1,128)} slice(f32[8,128]{1,0:T(8,128)S(1)} %add.19), slice={[0:1], [0:1]} | slice | bytes 8 | tf_op jit(solution)/shard_map/slice | solution.py:412
  (9 shorter events, 0.0 us)
Async XLA Ops:
  0.6 11.6 %collective-permute-start.1 = (bf16[16,64,128]{2,1,0:T(8,128)(2,1)}, bf16[16,64,128]{2,1,0:T(8,128)(2,1)S(1)}, u32[]{:S(2)}, u32[]{:S(2)}) collective-permute-start(bf16[16,64,128]{2,1,0:T(8,128)(2,1)} %x_ref.3), channel_id=1, source_target_pairs={{0,4},{1,5},{2,6},{3,7},{4,0},{5,1},{6,2},{7,3},{8,12},{9,13},{10,... | collective-permute-start | bytes 786440 | tf_op jit(solution)/shard_map/ppermute | solution.py:287
  3.7 1.0 %copy-start = (bf16[16,64,128]{2,1,0:T(8,128)(2,1)S(1)}, bf16[16,64,128]{2,1,0:T(8,128)(2,1)}, u32[]{:S(2)}) copy-start(bf16[16,64,128]{2,1,0:T(8,128)(2,1)} %x_ref.3) | copy-start | bytes 786436
  4.7 0.8 %copy-start.6 = (bf16[128,128]{1,0:T(8,128)(2,1)S(1)}, bf16[128,128]{1,0:T(8,128)(2,1)}, u32[]{:S(2)}) copy-start(bf16[128,128]{1,0:T(8,128)(2,1)} %rw_ref.1) | copy-start | bytes 98308
  4.7 0.8 %copy-start.7 = (bf16[128,128]{1,0:T(8,128)(2,1)S(1)}, bf16[128,128]{1,0:T(8,128)(2,1)}, u32[]{:S(2)}) copy-start(bf16[128,128]{1,0:T(8,128)(2,1)} %rg_ref.1) | copy-start | bytes 98308
  5.5 3.2 %copy-start.4 = (bf16[128,128]{1,0:T(8,128)(2,1)S(1)}, bf16[128,128]{1,0:T(8,128)(2,1)}, u32[]{:S(2)}) copy-start(bf16[128,128]{1,0:T(8,128)(2,1)} %lw_ref.1) | copy-start | bytes 98308
  5.5 3.2 %copy-start.5 = (bf16[128,128]{1,0:T(8,128)(2,1)S(1)}, bf16[128,128]{1,0:T(8,128)(2,1)}, u32[]{:S(2)}) copy-start(bf16[128,128]{1,0:T(8,128)(2,1)} %lg_ref.1) | copy-start | bytes 98308
  6.0 2.7 %copy-start.8 = (s32[5]{0:T(128)S(1)}, s32[5]{0:T(128)}, u32[]{:S(2)}) copy-start(s32[5]{0:T(128)} %lens_ref.1) | copy-start | bytes 64
  6.1 13.0 %collective-permute-start.3 = (bf16[512,128]{1,0:T(8,128)(2,1)S(1)}, bf16[512,128]{1,0:T(8,128)(2,1)S(1)}, u32[]{:S(2)}, u32[]{:S(2)}) collective-permute-start(bf16[512,128]{1,0:T(8,128)(2,1)S(1)} %get-tuple-element.19.stay_ref), channel_id=1, source_target_pairs={{0,8},{1,9},{2,10},{3,11},{4,12},{5,13},{6,14},{7,15},{8,0},{9,1},... | collective-permute-start | bytes 393224 | tf_op jit(solution)/shard_map/ppermute | solution.py:287
  8.7 10.3 %collective-permute-start.4 = (bf16[512,128]{1,0:T(8,128)(2,1)S(1)}, bf16[512,128]{1,0:T(8,128)(2,1)S(1)}, u32[]{:S(2)}, u32[]{:S(2)}) collective-permute-start(bf16[512,128]{1,0:T(8,128)(2,1)S(1)} %get-tuple-element.29), channel_id=1, source_target_pairs={{0,12},{1,13},{2,14},{3,15},{4,8},{5,9},{6,10},{7,11},{8,4},{9,5},... | collective-permute-start | bytes 393224 | tf_op jit(solution)/shard_map/ppermute | solution.py:287
  13.3 5.8 %collective-permute-start.2 = (bf16[512,128]{1,0:T(8,128)(2,1)S(1)}, bf16[512,128]{1,0:T(8,128)(2,1)S(1)}, u32[]{:S(2)}, u32[]{:S(2)}) collective-permute-start(bf16[512,128]{1,0:T(8,128)(2,1)S(1)} %get-tuple-element.28), channel_id=1, source_target_pairs={{0,2},{1,3},{2,0},{3,1},{4,6},{5,7},{6,4},{7,5},{8,10},{9,11},{10,... | collective-permute-start | bytes 393224 | tf_op jit(solution)/shard_map/ppermute | solution.py:287
  13.3 5.8 %collective-permute-start = (bf16[512,128]{1,0:T(8,128)(2,1)S(1)}, bf16[512,128]{1,0:T(8,128)(2,1)S(1)}, u32[]{:S(2)}, u32[]{:S(2)}) collective-permute-start(bf16[512,128]{1,0:T(8,128)(2,1)S(1)} %get-tuple-element.26), channel_id=1, source_target_pairs={{0,2},{1,3},{2,0},{3,1},{4,6},{5,7},{6,4},{7,5},{8,10},{9,11},{10,... | collective-permute-start | bytes 393224 | tf_op jit(solution)/shard_map/ppermute | solution.py:287
  19.1 1.4 %collective-permute-start.5 = (bf16[512,128]{1,0:T(8,128)(2,1)S(1)}, bf16[512,128]{1,0:T(8,128)(2,1)S(1)}, u32[]{:S(2)}, u32[]{:S(2)}) collective-permute-start(bf16[512,128]{1,0:T(8,128)(2,1)S(1)} %shard_map.118), channel_id=1, source_target_pairs={{0,2},{1,3},{2,0},{3,1},{4,6},{5,7},{6,4},{7,5},{8,10},{9,11},{10,... | collective-permute-start | bytes 393224 | tf_op jit(solution)/shard_map/ppermute | solution.py:287
  20.5 10.4 %copy-start.9 = (bf16[128,64]{0,1:T(8,128)(2,1)S(1)}, bf16[128,64]{0,1:T(8,128)(2,1)}, u32[]{:S(2)}) copy-start(bf16[128,64]{0,1:T(8,128)(2,1)} %param.19) | copy-start | bytes 49156
  20.5 10.5 %copy-start.10 = (s32[16,64]{1,0:T(8,128)S(1)}, s32[16,64]{1,0:T(8,128)}, u32[]{:S(2)}) copy-start(s32[16,64]{1,0:T(8,128)} %param.11) | copy-start | bytes 12292
  20.5 10.6 %copy-start.1 = (bf16[16,64,128]{2,1,0:T(8,128)(2,1)S(1)}, bf16[16,64,128]{2,1,0:T(8,128)(2,1)}, u32[]{:S(2)}) copy-start(bf16[16,64,128]{2,1,0:T(8,128)(2,1)} %x_ref.3) | copy-start | bytes 786436
  21.0 5.6 %collective-permute-start.7 = (bf16[512,128]{1,0:T(8,128)(2,1)S(1)}, bf16[512,128]{1,0:T(8,128)(2,1)S(1)}, u32[]{:S(2)}, u32[]{:S(2)}) collective-permute-start(bf16[512,128]{1,0:T(8,128)(2,1)S(1)} %get-tuple-element.31), channel_id=1, source_target_pairs={{0,1},{1,0},{2,3},{3,2},{4,5},{5,4},{6,7},{7,6},{8,9},{9,8},{10,11... | collective-permute-start | bytes 393224 | tf_op jit(solution)/shard_map/ppermute | solution.py:287
  22.6 8.5 %copy-start.3 = (bf16[128,128]{1,0:T(8,128)(2,1)S(1)}, bf16[128,128]{1,0:T(8,128)(2,1)}, u32[]{:S(2)}) copy-start(bf16[128,128]{1,0:T(8,128)(2,1)} %ow_ref.1) | copy-start | bytes 98308
  22.6 8.5 %copy-start.2 = (bf16[128,128]{1,0:T(8,128)(2,1)S(1)}, bf16[128,128]{1,0:T(8,128)(2,1)}, u32[]{:S(2)}) copy-start(bf16[128,128]{1,0:T(8,128)(2,1)} %gw_ref.1) | copy-start | bytes 98308
  22.6 6.4 %collective-permute-start.8 = (bf16[512,128]{1,0:T(8,128)(2,1)S(1)}, bf16[512,128]{1,0:T(8,128)(2,1)S(1)}, u32[]{:S(2)}, u32[]{:S(2)}) collective-permute-start(bf16[512,128]{1,0:T(8,128)(2,1)S(1)} %get-tuple-element.32), channel_id=1, source_target_pairs={{0,4},{1,5},{2,6},{3,7},{4,0},{5,1},{6,2},{7,3},{8,12},{9,13},{10,... | collective-permute-start | bytes 393224 | tf_op jit(solution)/shard_map/ppermute | solution.py:287
  24.6 6.3 %collective-permute-start.6 = (bf16[512,128]{1,0:T(8,128)(2,1)S(1)}, bf16[512,128]{1,0:T(8,128)(2,1)S(1)}, u32[]{:S(2)}, u32[]{:S(2)}) collective-permute-start(bf16[512,128]{1,0:T(8,128)(2,1)S(1)} %get-tuple-element.30), channel_id=1, source_target_pairs={{0,5},{1,4},{2,7},{3,6},{4,1},{5,0},{6,3},{7,2},{8,13},{9,12},{10,... | collective-permute-start | bytes 393224 | tf_op jit(solution)/shard_map/ppermute | solution.py:287
  24.6 6.9 %collective-permute-start.12 = (bf16[512,128]{1,0:T(8,128)(2,1)S(1)}, bf16[512,128]{1,0:T(8,128)(2,1)S(1)}, u32[]{:S(2)}, u32[]{:S(2)}) collective-permute-start(bf16[512,128]{1,0:T(8,128)(2,1)S(1)} %get-tuple-element.33.refs_3_), channel_id=1, source_target_pairs={{0,2},{1,3},{2,0},{3,1},{4,6},{5,7},{6,4},{7,5},{8,10},{9,11},{10,... | collective-permute-start | bytes 393224 | tf_op jit(solution)/shard_map/ppermute | solution.py:287
  26.7 4.8 %collective-permute-start.10 = (bf16[512,128]{1,0:T(8,128)(2,1)S(1)}, bf16[512,128]{1,0:T(8,128)(2,1)S(1)}, u32[]{:S(2)}, u32[]{:S(2)}) collective-permute-start(bf16[512,128]{1,0:T(8,128)(2,1)S(1)} %collective-permute-done.7.refs_1_), channel_id=1, source_target_pairs={{0,2},{1,3},{2,0},{3,1},{4,6},{5,7},{6,4},{7,5},{8,10},{9,11},{10,... | collective-permute-start | bytes 393224 | tf_op jit(solution)/shard_map/ppermute | solution.py:287
  29.0 2.5 %collective-permute-start.11 = (bf16[512,128]{1,0:T(8,128)(2,1)S(1)}, bf16[512,128]{1,0:T(8,128)(2,1)S(1)}, u32[]{:S(2)}, u32[]{:S(2)}) collective-permute-start(bf16[512,128]{1,0:T(8,128)(2,1)S(1)} %collective-permute-done.8.refs_2_), channel_id=1, source_target_pairs={{0,2},{1,3},{2,0},{3,1},{4,6},{5,7},{6,4},{7,5},{8,10},{9,11},{10,... | collective-permute-start | bytes 393224 | tf_op jit(solution)/shard_map/ppermute | solution.py:287
  30.9 1.3 %collective-permute-start.9 = (bf16[512,128]{1,0:T(8,128)(2,1)S(1)}, bf16[512,128]{1,0:T(8,128)(2,1)S(1)}, u32[]{:S(2)}, u32[]{:S(2)}) collective-permute-start(bf16[512,128]{1,0:T(8,128)(2,1)S(1)} %collective-permute-done.6.refs_0_), channel_id=1, source_target_pairs={{0,2},{1,3},{2,0},{3,1},{4,6},{5,7},{6,4},{7,5},{8,10},{9,11},{10,... | collective-permute-start | bytes 393224 | tf_op jit(solution)/shard_map/ppermute | solution.py:287
  33.1 1.2 %collective-permute-start.13 = (f32[8,128]{1,0:T(8,128)S(1)}, f32[8,128]{1,0:T(8,128)S(1)}, u32[]{:S(2)}, u32[]{:S(2)}) collective-permute-start(f32[8,128]{1,0:T(8,128)S(1)} %get-tuple-element.35), channel_id=1, source_target_pairs={{0,2},{1,3},{2,0},{3,1},{4,6},{5,7},{6,4},{7,5},{8,10},{9,11},{10,... | collective-permute-start | bytes 12296 | tf_op jit(solution)/shard_map/ppermute | solution.py:287
  34.3 4.5 %collective-permute-start.14 = (f32[8,128]{1,0:T(8,128)S(1)}, f32[8,128]{1,0:T(8,128)S(1)}, u32[]{:S(2)}, u32[]{:S(2)}) collective-permute-start(f32[8,128]{1,0:T(8,128)S(1)} %add.15), channel_id=1, source_target_pairs={{0,5},{1,4},{2,7},{3,6},{4,1},{5,0},{6,3},{7,2},{8,13},{9,12},{10,... | collective-permute-start | bytes 12296 | tf_op jit(solution)/shard_map/ppermute | solution.py:287
  37.0 3.6 %collective-permute-start.15 = (f32[8,128]{1,0:T(8,128)S(1)}, f32[8,128]{1,0:T(8,128)S(1)}, u32[]{:S(2)}, u32[]{:S(2)}) collective-permute-start(f32[8,128]{1,0:T(8,128)S(1)} %add.15), channel_id=1, source_target_pairs={{0,4},{1,5},{2,6},{3,7},{4,0},{5,1},{6,2},{7,3},{8,12},{9,13},{10,... | collective-permute-start | bytes 12296 | tf_op jit(solution)/shard_map/ppermute | solution.py:287
  37.3 3.6 %collective-permute-start.16 = (f32[8,128]{1,0:T(8,128)S(1)}, f32[8,128]{1,0:T(8,128)S(1)}, u32[]{:S(2)}, u32[]{:S(2)}) collective-permute-start(f32[8,128]{1,0:T(8,128)S(1)} %add.15), channel_id=1, source_target_pairs={{0,1},{1,0},{2,3},{3,2},{4,5},{5,4},{6,7},{7,6},{8,9},{9,8},{10,11... | collective-permute-start | bytes 12296 | tf_op jit(solution)/shard_map/ppermute | solution.py:287
  40.9 4.5 %collective-permute-start.17 = (f32[8,128]{1,0:T(8,128)S(1)}, f32[8,128]{1,0:T(8,128)S(1)}, u32[]{:S(2)}, u32[]{:S(2)}) collective-permute-start(f32[8,128]{1,0:T(8,128)S(1)} %add_add_fusion), channel_id=1, source_target_pairs={{0,8},{1,9},{2,10},{3,11},{4,12},{5,13},{6,14},{7,15},{8,0},{9,1},... | collective-permute-start | bytes 12296 | tf_op jit(solution)/shard_map/ppermute | solution.py:287

commit v13 on v12

--- a/solution.py
+++ b/solution.py
@@ -7,7 +7,7 @@
 
 AXES = ("row", "col")
 OWNERS = 4
-DIAGONAL_FIRST = (3, 1, 2, 0)
+DIAGONAL_FIRST = (0, 3, 1, 2)
 VMEM = pl.BlockSpec(memory_space=pltpu.VMEM)
 SMEM = pl.BlockSpec(memory_space=pltpu.SMEM)
 PARAMS = pltpu.CompilerParams(vmem_limit_bytes=24 * 1024 * 1024)

time: 46.1 us -> 45.8 us (level)
  waiting for transfers between devices: 21 us -> 20.5 us
    ppermute x18, waiting for transfers between devices: 21 us -> 20.5 us  [exchange(): return lax.ppermute(value, AXES, [(at, at ^ mask) for at in range(places)])]
where the time goes in v13:
time: 45.8 us; the launch traced here: 45.6 us
  waiting for transfers between devices  20.5 us (45%)
  starting transfers between devices  16.5 us (36%)
  Pallas kernels  5.69 us (12%)
  local copies, waits for them, and re-layouts  2.13 us (5%)
  between operations  0.78 us (2%)
    ppermute x18, waiting for transfers between devices, exchange(): return lax.ppermute(value, AXES, [(at, at ^ mask) for at in range(places)])  20.5 us
    ppermute x18, starting transfers between devices, exchange(): return lax.ppermute(value, AXES, [(at, at ^ mask) for at in range(places)])  16.5 us
    pallas_call x9, Pallas kernels, call(): pl.pallas_call(kernel, out_shape=outs, in_specs=specs if specs is not Non...  5.69 us
    unnamed x23, local copies, waits for them, and re-layouts  1.54 us
  transfers between devices with their start and end apart: 18, of which 12 were waited for; matrix products, arithmetic and copies ran while one was open for 0% of the time, Pallas kernels for 9%

profile of v13, /device:TPU:0, one launch (start us, length us, event | category | flops | bytes accessed | tf_op | source)
XLA Modules:
  0.0 45.6 jit_solution(7454126945712202692)
XLA Ops:
  0.6 3.1 %collective-permute-start.1 = (bf16[16,64,128]{2,1,0:T(8,128)(2,1)}, bf16[16,64,128]{2,1,0:T(8,128)(2,1)S(1)}, u32[]{:S(2)}, u32[]{:S(2)}) collective-permute-start(bf16[16,64,128]{2,1,0:T(8,128)(2,1)} %x_ref.3), channel_id=1, source_target_pairs={{0,4},{1,5},{2,6},{3,7},{4,0},{5,1},{6,2},{7,3},{8,12},{9,13},{10,... | collective-permute-start | bytes 786440 | tf_op jit(solution)/shard_map/ppermute | solution.py:287
  3.7 0.0 copy-start
  3.7 1.0 %copy-done = bf16[16,64,128]{2,1,0:T(8,128)(2,1)S(1)} copy-done((bf16[16,64,128]{2,1,0:T(8,128)(2,1)S(1)}, bf16[16,64,128]{2,1,0:T(8,128)(2,1)}, u32[]{:S(2)}) %copy-start) | copy-done | bytes 262168
  4.7 0.0 copy-start.6
  4.7 0.4 shard_map.113.normed_ref
  5.1 0.4 copy-done.6
  5.5 0.0 copy-done.7
  5.5 0.0 copy-start.4
  5.5 0.0 copy-start.5
  5.5 0.6 %shard_map.114 = (bf16[512,128]{1,0:T(8,128)(2,1)S(1)}, bf16[512,128]{1,0:T(8,128)(2,1)S(1)}) custom-call(bf16[1024,128]{1,0:T(8,128)(2,1)S(1)} %shard_map.113.normed_ref, bf16[128,128]{1,0:T(8,128)(2,1)S(1)} %copy-done.6, bf16[128,128]{1,0:T(8,128)(2,1)S(1)} %copy-done.7), custom_call_target="tpu_custom_call" | custom-call | flops 67108864 | bytes 1048576 | tf_op jit(solution)/shard_map/pallas_call | solution.py:291
  6.0 0.0 copy-start.8
  6.1 2.7 %collective-permute-start.3 = (bf16[512,128]{1,0:T(8,128)(2,1)S(1)}, bf16[512,128]{1,0:T(8,128)(2,1)S(1)}, u32[]{:S(2)}, u32[]{:S(2)}) collective-permute-start(bf16[512,128]{1,0:T(8,128)(2,1)S(1)} %get-tuple-element.19.stay_ref), channel_id=1, source_target_pairs={{0,8},{1,9},{2,10},{3,11},{4,12},{5,13},{6,14},{7,15},{8,0},{9,1},... | collective-permute-start | bytes 393224 | tf_op jit(solution)/shard_map/ppermute | solution.py:287
  8.7 0.0 collective-permute-start.4
  8.7 0.0 copy-done.4
  8.7 0.0 copy-done.5
  8.7 0.0 copy-done.8
  8.7 1.0 %shard_map.115 = (bf16[512,128]{1,0:T(8,128)(2,1)S(1)}, bf16[512,128]{1,0:T(8,128)(2,1)S(1)}, f32[24,128]{1,0:T(8,128)S(1)}) custom-call(s32[5]{0:T(128)S(1)} %copy-done.8, bf16[1024,128]{1,0:T(8,128)(2,1)S(1)} %shard_map.113.normed_ref, bf16[128,128]{1,0:T(8,128)(2,1)S(1)} %copy-done.4, bf16[128,128]{1,0:T(8,128)(2,1)S(1)} %copy-done.5, ...), custom_call_target="tpu_custom_call" | custom-call | flops 33554432 | bytes 1048576 | tf_op jit(solution)/shard_map/pallas_call | solution.py:291
  9.8 2.4 %collective-permute-done.1.x_ref = bf16[16,64,128]{2,1,0:T(8,128)(2,1)S(1)} collective-permute-done((bf16[16,64,128]{2,1,0:T(8,128)(2,1)}, bf16[16,64,128]{2,1,0:T(8,128)(2,1)S(1)}, u32[]{:S(2)}, u32[]{:S(2)}) %collective-permute-start.1) | collective-permute-done | bytes 262176 | tf_op jit(solution)/shard_map/ppermute | solution.py:287
  12.2 1.1 %shard_map.117 = (bf16[512,128]{1,0:T(8,128)(2,1)S(1)}, bf16[512,128]{1,0:T(8,128)(2,1)S(1)}) custom-call(f32[24,128]{1,0:T(8,128)S(1)} %get-tuple-element.20.masks_ref, bf16[16,64,128]{2,1,0:T(8,128)(2,1)S(1)} %collective-permute-done.1.x_ref, bf16[128,128]{1,0:T(8,128)(2,1)S(1)} %copy-done.4, bf16[128,128]{1,0:T(8,128)(2,1)S(1)} %copy-done.5, ...), custom_call_target="tpu_custom_call" | custom-call | flops 67108864 | bytes 1048576 | tf_op jit(solution)/shard_map/pallas_call | solution.py:291
  13.3 0.1 collective-permute-start.2
  13.3 0.5 %collective-permute-start = (bf16[512,128]{1,0:T(8,128)(2,1)S(1)}, bf16[512,128]{1,0:T(8,128)(2,1)S(1)}, u32[]{:S(2)}, u32[]{:S(2)}) collective-permute-start(bf16[512,128]{1,0:T(8,128)(2,1)S(1)} %get-tuple-element.26), channel_id=1, source_target_pairs={{0,2},{1,3},{2,0},{3,1},{4,6},{5,7},{6,4},{7,5},{8,10},{9,11},{10,... | collective-permute-start | bytes 393224 | tf_op jit(solution)/shard_map/ppermute | solution.py:287
  13.8 5.2 %collective-permute-done.3.far_ref.far = bf16[512,128]{1,0:T(8,128)(2,1)S(1)} collective-permute-done((bf16[512,128]{1,0:T(8,128)(2,1)S(1)}, bf16[512,128]{1,0:T(8,128)(2,1)S(1)}, u32[]{:S(2)}, u32[]{:S(2)}) %collective-permute-start.3) | collective-permute-done | bytes 131104 | tf_op jit(solution)/shard_map/ppermute | solution.py:287
  19.1 0.0 collective-permute-done.4.cross_ref.cross
  19.1 0.0 collective-permute-done.2.ready_ref.near_over
  19.1 0.1 collective-permute-start.5
  19.2 0.0 collective-permute-done.core
  19.2 1.3 %collective-permute-done.5.both_over = bf16[512,128]{1,0:T(8,128)(2,1)S(1)} collective-permute-done((bf16[512,128]{1,0:T(8,128)(2,1)S(1)}, bf16[512,128]{1,0:T(8,128)(2,1)S(1)}, u32[]{:S(2)}, u32[]{:S(2)}) %collective-permute-start.5) | collective-permute-done | bytes 131104 | tf_op jit(solution)/shard_map/ppermute | solution.py:287
  20.5 0.0 copy-start.9
  20.5 0.5 %shard_map.119 = (bf16[512,128]{1,0:T(8,128)(2,1)S(1)}, bf16[512,128]{1,0:T(8,128)(2,1)S(1)}, bf16[512,128]{1,0:T(8,128)(2,1)S(1)}, bf16[512,128]{1,0:T(8,128)(2,1)S(1)}) custom-call(f32[24,128]{1,0:T(8,128)S(1)} %get-tuple-element.20.masks_ref, bf16[512,128]{1,0:T(8,128)(2,1)S(1)} %get-tuple-element.25.own, bf16[512,128]{1,0:T(8,128)(2,1)S(1)} %collective-permute-done.core, ...), custom_call_target="tpu_custom_call" | custom-call | flops 16777216 | bytes 1048576 | tf_op jit(solution)/shard_map/pallas_call | solution.py:291
  21.0 3.0 %collective-permute-start.6 = (bf16[512,128]{1,0:T(8,128)(2,1)S(1)}, bf16[512,128]{1,0:T(8,128)(2,1)S(1)}, u32[]{:S(2)}, u32[]{:S(2)}) collective-permute-start(bf16[512,128]{1,0:T(8,128)(2,1)S(1)} %get-tuple-element.31), channel_id=1, source_target_pairs={{0,5},{1,4},{2,7},{3,6},{4,1},{5,0},{6,3},{7,2},{8,13},{9,12},{10,... | collective-permute-start | bytes 393224 | tf_op jit(solution)/shard_map/ppermute | solution.py:287
  24.0 0.5 %collective-permute-start.7 = (bf16[512,128]{1,0:T(8,128)(2,1)S(1)}, bf16[512,128]{1,0:T(8,128)(2,1)S(1)}, u32[]{:S(2)}, u32[]{:S(2)}) collective-permute-start(bf16[512,128]{1,0:T(8,128)(2,1)S(1)} %get-tuple-element.32), channel_id=1, source_target_pairs={{0,1},{1,0},{2,3},{3,2},{4,5},{5,4},{6,7},{7,6},{8,9},{9,8},{10,11... | collective-permute-start | bytes 393224 | tf_op jit(solution)/shard_map/ppermute | solution.py:287
  24.5 0.1 collective-permute-start.8
  24.7 0.0 collective-permute-start.9
  24.7 3.2 %collective-permute-done.6.refs_1_ = bf16[512,128]{1,0:T(8,128)(2,1)S(1)} collective-permute-done((bf16[512,128]{1,0:T(8,128)(2,1)S(1)}, bf16[512,128]{1,0:T(8,128)(2,1)S(1)}, u32[]{:S(2)}, u32[]{:S(2)}) %collective-permute-start.6) | collective-permute-done | bytes 131104 | tf_op jit(solution)/shard_map/ppermute | solution.py:287
  27.9 0.0 collective-permute-start.10
  27.9 2.7 %collective-permute-done.7.refs_2_ = bf16[512,128]{1,0:T(8,128)(2,1)S(1)} collective-permute-done((bf16[512,128]{1,0:T(8,128)(2,1)S(1)}, bf16[512,128]{1,0:T(8,128)(2,1)S(1)}, u32[]{:S(2)}, u32[]{:S(2)}) %collective-permute-start.7) | collective-permute-done | bytes 131104 | tf_op jit(solution)/shard_map/ppermute | solution.py:287
  30.6 0.0 collective-permute-start.11
  30.6 0.0 collective-permute-done.8.refs_3_
  30.6 0.5 %collective-permute-start.12 = (bf16[512,128]{1,0:T(8,128)(2,1)S(1)}, bf16[512,128]{1,0:T(8,128)(2,1)S(1)}, u32[]{:S(2)}, u32[]{:S(2)}) collective-permute-start(bf16[512,128]{1,0:T(8,128)(2,1)S(1)} %collective-permute-done.8.refs_3_), channel_id=1, source_target_pairs={{0,2},{1,3},{2,0},{3,1},{4,6},{5,7},{6,4},{7,5},{8,10},{9,11},{10,... | collective-permute-start | bytes 393224 | tf_op jit(solution)/shard_map/ppermute | solution.py:287
  31.1 0.0 copy-done.9
  31.1 0.1 copy.12.dw_ref
  31.3 0.0 copy-done.10
  31.3 0.1 reshape.7.bins_ref
  31.3 0.0 copy-done.1
  31.3 0.0 copy-done.3
  31.3 0.0 copy-done.2
  31.3 0.4 shard_map.116
  31.7 0.0 collective-permute-done.9.refs_4_
  31.7 0.0 collective-permute-done.10.refs_5_
  31.7 0.2 collective-permute-done.11.refs_6_
  32.0 0.2 collective-permute-done.12.refs_7_
  32.2 0.9 %shard_map.120 = (bf16[128,1024]{1,0:T(8,128)(2,1)S(1)}, f32[8,128]{1,0:T(8,128)S(1)}) custom-call(f32[24,128]{1,0:T(8,128)S(1)} %get-tuple-element.20.masks_ref, f32[128,1024]{1,0:T(8,128)S(1)} %get-tuple-element.21.x_ref, f32[128,1024]{1,0:T(8,128)S(1)} %get-tuple-element.22.gate_ref, s32[8,128]{1,0:T(8,128)S(1)} %reshape.7.bins_ref, ...), custom_call_target="tpu_custom_call" | custom-call | flops 100663296 | bytes 1048576 | tf_op jit(solution)/shard_map/pallas_call | solution.py:291
  33.1 0.3 collective-permute-start.13
  33.4 0.8 %collective-permute-done.13 = f32[8,128]{1,0:T(8,128)S(1)} collective-permute-done((f32[8,128]{1,0:T(8,128)S(1)}, f32[8,128]{1,0:T(8,128)S(1)}, u32[]{:S(2)}, u32[]{:S(2)}) %collective-permute-start.13) | collective-permute-done | bytes 4128 | tf_op jit(solution)/shard_map/ppermute | solution.py:287
  34.3 1.8 %collective-permute-start.14 = (f32[8,128]{1,0:T(8,128)S(1)}, f32[8,128]{1,0:T(8,128)S(1)}, u32[]{:S(2)}, u32[]{:S(2)}) collective-permute-start(f32[8,128]{1,0:T(8,128)S(1)} %add.15), channel_id=1, source_target_pairs={{0,5},{1,4},{2,7},{3,6},{4,1},{5,0},{6,3},{7,2},{8,13},{9,12},{10,... | collective-permute-start | bytes 12296 | tf_op jit(solution)/shard_map/ppermute | solution.py:287
  36.1 0.9 %collective-permute-start.15 = (f32[8,128]{1,0:T(8,128)S(1)}, f32[8,128]{1,0:T(8,128)S(1)}, u32[]{:S(2)}, u32[]{:S(2)}) collective-permute-start(f32[8,128]{1,0:T(8,128)S(1)} %add.15), channel_id=1, source_target_pairs={{0,4},{1,5},{2,6},{3,7},{4,0},{5,1},{6,2},{7,3},{8,12},{9,13},{10,... | collective-permute-start | bytes 12296 | tf_op jit(solution)/shard_map/ppermute | solution.py:287
  37.0 0.8 %collective-permute-start.16 = (f32[8,128]{1,0:T(8,128)S(1)}, f32[8,128]{1,0:T(8,128)S(1)}, u32[]{:S(2)}, u32[]{:S(2)}) collective-permute-start(f32[8,128]{1,0:T(8,128)S(1)} %add.15), channel_id=1, source_target_pairs={{0,1},{1,0},{2,3},{3,2},{4,5},{5,4},{6,7},{7,6},{8,9},{9,8},{10,11... | collective-permute-start | bytes 12296 | tf_op jit(solution)/shard_map/ppermute | solution.py:287
  37.7 1.0 %collective-permute-done.14 = f32[8,128]{1,0:T(8,128)S(1)} collective-permute-done((f32[8,128]{1,0:T(8,128)S(1)}, f32[8,128]{1,0:T(8,128)S(1)}, u32[]{:S(2)}, u32[]{:S(2)}) %collective-permute-start.14) | collective-permute-done | bytes 4128 | tf_op jit(solution)/shard_map/ppermute | solution.py:287
  38.8 0.9 %collective-permute-done.15 = f32[8,128]{1,0:T(8,128)S(1)} collective-permute-done((f32[8,128]{1,0:T(8,128)S(1)}, f32[8,128]{1,0:T(8,128)S(1)}, u32[]{:S(2)}, u32[]{:S(2)}) %collective-permute-start.15) | collective-permute-done | bytes 4128 | tf_op jit(solution)/shard_map/ppermute | solution.py:287
  39.7 0.9 %collective-permute-done.16 = f32[8,128]{1,0:T(8,128)S(1)} collective-permute-done((f32[8,128]{1,0:T(8,128)S(1)}, f32[8,128]{1,0:T(8,128)S(1)}, u32[]{:S(2)}, u32[]{:S(2)}) %collective-permute-start.16) | collective-permute-done | bytes 4128 | tf_op jit(solution)/shard_map/ppermute | solution.py:287
  40.6 2.2 %collective-permute-start.17 = (f32[8,128]{1,0:T(8,128)S(1)}, f32[8,128]{1,0:T(8,128)S(1)}, u32[]{:S(2)}, u32[]{:S(2)}) collective-permute-start(f32[8,128]{1,0:T(8,128)S(1)} %add_add_fusion), channel_id=1, source_target_pairs={{0,8},{1,9},{2,10},{3,11},{4,12},{5,13},{6,14},{7,15},{8,0},{9,1},... | collective-permute-start | bytes 12296 | tf_op jit(solution)/shard_map/ppermute | solution.py:287
  42.7 0.8 %shard_map.121 = bf16[16,64,128]{2,1,0:T(8,128)(2,1)} custom-call(bf16[128,1024]{1,0:T(8,128)(2,1)S(1)} %get-tuple-element.34.turned_ref), custom_call_target="tpu_custom_call" | custom-call | flops 67108864 | bytes 1048576 | tf_op jit(solution)/shard_map/pallas_call | solution.py:291
  43.6 1.5 %collective-permute-done.17 = f32[8,128]{1,0:T(8,128)S(1)} collective-permute-done((f32[8,128]{1,0:T(8,128)S(1)}, f32[8,128]{1,0:T(8,128)S(1)}, u32[]{:S(2)}, u32[]{:S(2)}) %collective-permute-start.17) | collective-permute-done | bytes 4128 | tf_op jit(solution)/shard_map/ppermute | solution.py:287
  45.1 0.5 %slice.3 = f32[1,1]{1,0:T(1,128)} slice(f32[8,128]{1,0:T(8,128)S(1)} %add.19), slice={[0:1], [0:1]} | slice | bytes 8 | tf_op jit(solution)/shard_map/slice | solution.py:412
  (9 shorter events, 0.0 us)
Async XLA Ops:
  0.6 11.6 %collective-permute-start.1 = (bf16[16,64,128]{2,1,0:T(8,128)(2,1)}, bf16[16,64,128]{2,1,0:T(8,128)(2,1)S(1)}, u32[]{:S(2)}, u32[]{:S(2)}) collective-permute-start(bf16[16,64,128]{2,1,0:T(8,128)(2,1)} %x_ref.3), channel_id=1, source_target_pairs={{0,4},{1,5},{2,6},{3,7},{4,0},{5,1},{6,2},{7,3},{8,12},{9,13},{10,... | collective-permute-start | bytes 786440 | tf_op jit(solution)/shard_map/ppermute | solution.py:287
  3.7 1.0 %copy-start = (bf16[16,64,128]{2,1,0:T(8,128)(2,1)S(1)}, bf16[16,64,128]{2,1,0:T(8,128)(2,1)}, u32[]{:S(2)}) copy-start(bf16[16,64,128]{2,1,0:T(8,128)(2,1)} %x_ref.3) | copy-start | bytes 786436
  4.7 0.8 %copy-start.6 = (bf16[128,128]{1,0:T(8,128)(2,1)S(1)}, bf16[128,128]{1,0:T(8,128)(2,1)}, u32[]{:S(2)}) copy-start(bf16[128,128]{1,0:T(8,128)(2,1)} %rw_ref.1) | copy-start | bytes 98308
  4.7 0.8 %copy-start.7 = (bf16[128,128]{1,0:T(8,128)(2,1)S(1)}, bf16[128,128]{1,0:T(8,128)(2,1)}, u32[]{:S(2)}) copy-start(bf16[128,128]{1,0:T(8,128)(2,1)} %rg_ref.1) | copy-start | bytes 98308
  5.5 3.2 %copy-start.4 = (bf16[128,128]{1,0:T(8,128)(2,1)S(1)}, bf16[128,128]{1,0:T(8,128)(2,1)}, u32[]{:S(2)}) copy-start(bf16[128,128]{1,0:T(8,128)(2,1)} %lw_ref.1) | copy-start | bytes 98308
  5.5 3.2 %copy-start.5 = (bf16[128,128]{1,0:T(8,128)(2,1)S(1)}, bf16[128,128]{1,0:T(8,128)(2,1)}, u32[]{:S(2)}) copy-start(bf16[128,128]{1,0:T(8,128)(2,1)} %lg_ref.1) | copy-start | bytes 98308
  6.0 2.7 %copy-start.8 = (s32[5]{0:T(128)S(1)}, s32[5]{0:T(128)}, u32[]{:S(2)}) copy-start(s32[5]{0:T(128)} %lens_ref.1) | copy-start | bytes 64
  6.1 13.0 %collective-permute-start.3 = (bf16[512,128]{1,0:T(8,128)(2,1)S(1)}, bf16[512,128]{1,0:T(8,128)(2,1)S(1)}, u32[]{:S(2)}, u32[]{:S(2)}) collective-permute-start(bf16[512,128]{1,0:T(8,128)(2,1)S(1)} %get-tuple-element.19.stay_ref), channel_id=1, source_target_pairs={{0,8},{1,9},{2,10},{3,11},{4,12},{5,13},{6,14},{7,15},{8,0},{9,1},... | collective-permute-start | bytes 393224 | tf_op jit(solution)/shard_map/ppermute | solution.py:287
  8.7 10.3 %collective-permute-start.4 = (bf16[512,128]{1,0:T(8,128)(2,1)S(1)}, bf16[512,128]{1,0:T(8,128)(2,1)S(1)}, u32[]{:S(2)}, u32[]{:S(2)}) collective-permute-start(bf16[512,128]{1,0:T(8,128)(2,1)S(1)} %get-tuple-element.29), channel_id=1, source_target_pairs={{0,12},{1,13},{2,14},{3,15},{4,8},{5,9},{6,10},{7,11},{8,4},{9,5},... | collective-permute-start | bytes 393224 | tf_op jit(solution)/shard_map/ppermute | solution.py:287
  13.3 5.8 %collective-permute-start.2 = (bf16[512,128]{1,0:T(8,128)(2,1)S(1)}, bf16[512,128]{1,0:T(8,128)(2,1)S(1)}, u32[]{:S(2)}, u32[]{:S(2)}) collective-permute-start(bf16[512,128]{1,0:T(8,128)(2,1)S(1)} %get-tuple-element.28), channel_id=1, source_target_pairs={{0,2},{1,3},{2,0},{3,1},{4,6},{5,7},{6,4},{7,5},{8,10},{9,11},{10,... | collective-permute-start | bytes 393224 | tf_op jit(solution)/shard_map/ppermute | solution.py:287
  13.3 5.8 %collective-permute-start = (bf16[512,128]{1,0:T(8,128)(2,1)S(1)}, bf16[512,128]{1,0:T(8,128)(2,1)S(1)}, u32[]{:S(2)}, u32[]{:S(2)}) collective-permute-start(bf16[512,128]{1,0:T(8,128)(2,1)S(1)} %get-tuple-element.26), channel_id=1, source_target_pairs={{0,2},{1,3},{2,0},{3,1},{4,6},{5,7},{6,4},{7,5},{8,10},{9,11},{10,... | collective-permute-start | bytes 393224 | tf_op jit(solution)/shard_map/ppermute | solution.py:287
  19.1 1.4 %collective-permute-start.5 = (bf16[512,128]{1,0:T(8,128)(2,1)S(1)}, bf16[512,128]{1,0:T(8,128)(2,1)S(1)}, u32[]{:S(2)}, u32[]{:S(2)}) collective-permute-start(bf16[512,128]{1,0:T(8,128)(2,1)S(1)} %shard_map.118), channel_id=1, source_target_pairs={{0,2},{1,3},{2,0},{3,1},{4,6},{5,7},{6,4},{7,5},{8,10},{9,11},{10,... | collective-permute-start | bytes 393224 | tf_op jit(solution)/shard_map/ppermute | solution.py:287
  20.5 10.6 %copy-start.9 = (bf16[128,64]{0,1:T(8,128)(2,1)S(1)}, bf16[128,64]{0,1:T(8,128)(2,1)}, u32[]{:S(2)}) copy-start(bf16[128,64]{0,1:T(8,128)(2,1)} %param.19) | copy-start | bytes 49156
  20.5 10.8 %copy-start.10 = (s32[16,64]{1,0:T(8,128)S(1)}, s32[16,64]{1,0:T(8,128)}, u32[]{:S(2)}) copy-start(s32[16,64]{1,0:T(8,128)} %param.11) | copy-start | bytes 12292
  20.5 10.8 %copy-start.1 = (bf16[16,64,128]{2,1,0:T(8,128)(2,1)S(1)}, bf16[16,64,128]{2,1,0:T(8,128)(2,1)}, u32[]{:S(2)}) copy-start(bf16[16,64,128]{2,1,0:T(8,128)(2,1)} %x_ref.3) | copy-start | bytes 786436
  21.0 6.9 %collective-permute-start.6 = (bf16[512,128]{1,0:T(8,128)(2,1)S(1)}, bf16[512,128]{1,0:T(8,128)(2,1)S(1)}, u32[]{:S(2)}, u32[]{:S(2)}) collective-permute-start(bf16[512,128]{1,0:T(8,128)(2,1)S(1)} %get-tuple-element.31), channel_id=1, source_target_pairs={{0,5},{1,4},{2,7},{3,6},{4,1},{5,0},{6,3},{7,2},{8,13},{9,12},{10,... | collective-permute-start | bytes 393224 | tf_op jit(solution)/shard_map/ppermute | solution.py:287
  24.0 7.3 %copy-start.3 = (bf16[128,128]{1,0:T(8,128)(2,1)S(1)}, bf16[128,128]{1,0:T(8,128)(2,1)}, u32[]{:S(2)}) copy-start(bf16[128,128]{1,0:T(8,128)(2,1)} %ow_ref.1) | copy-start | bytes 98308
  24.0 7.3 %copy-start.2 = (bf16[128,128]{1,0:T(8,128)(2,1)S(1)}, bf16[128,128]{1,0:T(8,128)(2,1)}, u32[]{:S(2)}) copy-start(bf16[128,128]{1,0:T(8,128)(2,1)} %gw_ref.1) | copy-start | bytes 98308
  24.0 6.6 %collective-permute-start.7 = (bf16[512,128]{1,0:T(8,128)(2,1)S(1)}, bf16[512,128]{1,0:T(8,128)(2,1)S(1)}, u32[]{:S(2)}, u32[]{:S(2)}) collective-permute-start(bf16[512,128]{1,0:T(8,128)(2,1)S(1)} %get-tuple-element.32), channel_id=1, source_target_pairs={{0,1},{1,0},{2,3},{3,2},{4,5},{5,4},{6,7},{7,6},{8,9},{9,8},{10,11... | collective-permute-start | bytes 393224 | tf_op jit(solution)/shard_map/ppermute | solution.py:287
  24.5 6.1 %collective-permute-start.8 = (bf16[512,128]{1,0:T(8,128)(2,1)S(1)}, bf16[512,128]{1,0:T(8,128)(2,1)S(1)}, u32[]{:S(2)}, u32[]{:S(2)}) collective-permute-start(bf16[512,128]{1,0:T(8,128)(2,1)S(1)} %get-tuple-element.33), channel_id=1, source_target_pairs={{0,4},{1,5},{2,6},{3,7},{4,0},{5,1},{6,2},{7,3},{8,12},{9,13},{10,... | collective-permute-start | bytes 393224 | tf_op jit(solution)/shard_map/ppermute | solution.py:287
  24.7 7.0 %collective-permute-start.9 = (bf16[512,128]{1,0:T(8,128)(2,1)S(1)}, bf16[512,128]{1,0:T(8,128)(2,1)S(1)}, u32[]{:S(2)}, u32[]{:S(2)}) collective-permute-start(bf16[512,128]{1,0:T(8,128)(2,1)S(1)} %get-tuple-element.30.refs_0_), channel_id=1, source_target_pairs={{0,2},{1,3},{2,0},{3,1},{4,6},{5,7},{6,4},{7,5},{8,10},{9,11},{10,... | collective-permute-start | bytes 393224 | tf_op jit(solution)/shard_map/ppermute | solution.py:287
  27.9 3.8 %collective-permute-start.10 = (bf16[512,128]{1,0:T(8,128)(2,1)S(1)}, bf16[512,128]{1,0:T(8,128)(2,1)S(1)}, u32[]{:S(2)}, u32[]{:S(2)}) collective-permute-start(bf16[512,128]{1,0:T(8,128)(2,1)S(1)} %collective-permute-done.6.refs_1_), channel_id=1, source_target_pairs={{0,2},{1,3},{2,0},{3,1},{4,6},{5,7},{6,4},{7,5},{8,10},{9,11},{10,... | collective-permute-start | bytes 393224 | tf_op jit(solution)/shard_map/ppermute | solution.py:287
  30.6 1.3 %collective-permute-start.11 = (bf16[512,128]{1,0:T(8,128)(2,1)S(1)}, bf16[512,128]{1,0:T(8,128)(2,1)S(1)}, u32[]{:S(2)}, u32[]{:S(2)}) collective-permute-start(bf16[512,128]{1,0:T(8,128)(2,1)S(1)} %collective-permute-done.7.refs_2_), channel_id=1, source_target_pairs={{0,2},{1,3},{2,0},{3,1},{4,6},{5,7},{6,4},{7,5},{8,10},{9,11},{10,... | collective-permute-start | bytes 393224 | tf_op jit(solution)/shard_map/ppermute | solution.py:287
  30.6 1.5 %collective-permute-start.12 = (bf16[512,128]{1,0:T(8,128)(2,1)S(1)}, bf16[512,128]{1,0:T(8,128)(2,1)S(1)}, u32[]{:S(2)}, u32[]{:S(2)}) collective-permute-start(bf16[512,128]{1,0:T(8,128)(2,1)S(1)} %collective-permute-done.8.refs_3_), channel_id=1, source_target_pairs={{0,2},{1,3},{2,0},{3,1},{4,6},{5,7},{6,4},{7,5},{8,10},{9,11},{10,... | collective-permute-start | bytes 393224 | tf_op jit(solution)/shard_map/ppermute | solution.py:287
  33.1 1.2 %collective-permute-start.13 = (f32[8,128]{1,0:T(8,128)S(1)}, f32[8,128]{1,0:T(8,128)S(1)}, u32[]{:S(2)}, u32[]{:S(2)}) collective-permute-start(f32[8,128]{1,0:T(8,128)S(1)} %get-tuple-element.35), channel_id=1, source_target_pairs={{0,2},{1,3},{2,0},{3,1},{4,6},{5,7},{6,4},{7,5},{8,10},{9,11},{10,... | collective-permute-start | bytes 12296 | tf_op jit(solution)/shard_map/ppermute | solution.py:287
  34.3 4.5 %collective-permute-start.14 = (f32[8,128]{1,0:T(8,128)S(1)}, f32[8,128]{1,0:T(8,128)S(1)}, u32[]{:S(2)}, u32[]{:S(2)}) collective-permute-start(f32[8,128]{1,0:T(8,128)S(1)} %add.15), channel_id=1, source_target_pairs={{0,5},{1,4},{2,7},{3,6},{4,1},{5,0},{6,3},{7,2},{8,13},{9,12},{10,... | collective-permute-start | bytes 12296 | tf_op jit(solution)/shard_map/ppermute | solution.py:287
  36.1 3.6 %collective-permute-start.15 = (f32[8,128]{1,0:T(8,128)S(1)}, f32[8,128]{1,0:T(8,128)S(1)}, u32[]{:S(2)}, u32[]{:S(2)}) collective-permute-start(f32[8,128]{1,0:T(8,128)S(1)} %add.15), channel_id=1, source_target_pairs={{0,4},{1,5},{2,6},{3,7},{4,0},{5,1},{6,2},{7,3},{8,12},{9,13},{10,... | collective-permute-start | bytes 12296 | tf_op jit(solution)/shard_map/ppermute | solution.py:287
  37.0 3.6 %collective-permute-start.16 = (f32[8,128]{1,0:T(8,128)S(1)}, f32[8,128]{1,0:T(8,128)S(1)}, u32[]{:S(2)}, u32[]{:S(2)}) collective-permute-start(f32[8,128]{1,0:T(8,128)S(1)} %add.15), channel_id=1, source_target_pairs={{0,1},{1,0},{2,3},{3,2},{4,5},{5,4},{6,7},{7,6},{8,9},{9,8},{10,11... | collective-permute-start | bytes 12296 | tf_op jit(solution)/shard_map/ppermute | solution.py:287
  40.6 4.5 %collective-permute-start.17 = (f32[8,128]{1,0:T(8,128)S(1)}, f32[8,128]{1,0:T(8,128)S(1)}, u32[]{:S(2)}, u32[]{:S(2)}) collective-permute-start(f32[8,128]{1,0:T(8,128)S(1)} %add_add_fusion), channel_id=1, source_target_pairs={{0,8},{1,9},{2,10},{3,11},{4,12},{5,13},{6,14},{7,15},{8,0},{9,1},... | collective-permute-start | bytes 12296 | tf_op jit(solution)/shard_map/ppermute | solution.py:287

commit v14 on v13

--- a/solution.py
+++ b/solution.py
@@ -403,12 +403,14 @@
         flops=6 * spots * channels * channels,
     )
     pair_out = call(turn_back_kernel, struct(pair_repr.shape, bf16), args=(pair_out,), flops=1 << 26)
-    loss = loss + exchange(loss, places, over_core)
     diagonal, beside, near_loss = [
         exchange(loss, places, mask) for mask in (over_z + over_x, over_x, over_z)
     ]
     loss = (diagonal + near_loss) + (beside + loss)
-    loss = loss + exchange(loss, places, over_half)
+    half, half_over, sibling = [
+        exchange(loss, places, mask) for mask in (over_half, over_half + over_core, over_core)
+    ]
+    loss = (half + half_over) + (sibling + loss)
     return (pair_out, loss[0, :1])
 
 

time: 45.8 us -> 46.3 us (1.011)
  starting transfers between devices: 16.5 us -> 17.1 us
    ppermute x18 -> x19, starting transfers between devices: 16.5 us -> 17.1 us  [exchange(): return lax.ppermute(value, AXES, [(at, at ^ mask) for at in range(places)])]
    ppermute x18 -> x19, waiting for transfers between devices: 20.5 us -> 20.4 us  [exchange(): return lax.ppermute(value, AXES, [(at, at ^ mask) for at in range(places)])]
  transfers between devices with their start and end apart: 18 -> 19, of which waited for: 12 -> 12; matrix products, arithmetic and copies ran while one was open for 0% -> 0% of each run, Pallas kernels for 9% -> 9%
where the time goes in v14:
time: 46.3 us; the launch traced here: 46 us
  waiting for transfers between devices  20.4 us (44%)
  starting transfers between devices  17.1 us (37%)
  Pallas kernels  5.69 us (12%)
  local copies, waits for them, and re-layouts  2.13 us (5%)
  between operations  0.78 us (2%)
    ppermute x19, waiting for transfers between devices, exchange(): return lax.ppermute(value, AXES, [(at, at ^ mask) for at in range(places)])  20.4 us
    ppermute x19, starting transfers between devices, exchange(): return lax.ppermute(value, AXES, [(at, at ^ mask) for at in range(places)])  17.1 us
    pallas_call x9, Pallas kernels, call(): pl.pallas_call(kernel, out_shape=outs, in_specs=specs if specs is not Non...  5.69 us
    unnamed x23, local copies, waits for them, and re-layouts  1.54 us
  transfers between devices with their start and end apart: 19, of which 12 were waited for; matrix products, arithmetic and copies ran while one was open for 0% of the time, Pallas kernels for 9%

profile of v14, /device:TPU:0, one launch (start us, length us, event | category | flops | bytes accessed | tf_op | source)
XLA Modules:
  0.0 46.0 jit_solution(7258932912797808741)
XLA Ops:
  0.6 3.1 %collective-permute-start.1 = (bf16[16,64,128]{2,1,0:T(8,128)(2,1)}, bf16[16,64,128]{2,1,0:T(8,128)(2,1)S(1)}, u32[]{:S(2)}, u32[]{:S(2)}) collective-permute-start(bf16[16,64,128]{2,1,0:T(8,128)(2,1)} %x_ref.3), channel_id=1, source_target_pairs={{0,4},{1,5},{2,6},{3,7},{4,0},{5,1},{6,2},{7,3},{8,12},{9,13},{10,... | collective-permute-start | bytes 786440 | tf_op jit(solution)/shard_map/ppermute | solution.py:287
  3.7 0.0 copy-start
  3.7 1.0 %copy-done = bf16[16,64,128]{2,1,0:T(8,128)(2,1)S(1)} copy-done((bf16[16,64,128]{2,1,0:T(8,128)(2,1)S(1)}, bf16[16,64,128]{2,1,0:T(8,128)(2,1)}, u32[]{:S(2)}) %copy-start) | copy-done | bytes 262168
  4.7 0.0 copy-start.6
  4.7 0.0 copy-start.7
  4.7 0.4 shard_map.113.normed_ref
  5.1 0.4 copy-done.6
  5.5 0.0 copy-done.7
  5.5 0.6 %shard_map.114 = (bf16[512,128]{1,0:T(8,128)(2,1)S(1)}, bf16[512,128]{1,0:T(8,128)(2,1)S(1)}) custom-call(bf16[1024,128]{1,0:T(8,128)(2,1)S(1)} %shard_map.113.normed_ref, bf16[128,128]{1,0:T(8,128)(2,1)S(1)} %copy-done.6, bf16[128,128]{1,0:T(8,128)(2,1)S(1)} %copy-done.7), custom_call_target="tpu_custom_call" | custom-call | flops 67108864 | bytes 1048576 | tf_op jit(solution)/shard_map/pallas_call | solution.py:291
  6.0 0.0 copy-start.8
  6.1 2.7 %collective-permute-start.3 = (bf16[512,128]{1,0:T(8,128)(2,1)S(1)}, bf16[512,128]{1,0:T(8,128)(2,1)S(1)}, u32[]{:S(2)}, u32[]{:S(2)}) collective-permute-start(bf16[512,128]{1,0:T(8,128)(2,1)S(1)} %get-tuple-element.19.stay_ref), channel_id=1, source_target_pairs={{0,8},{1,9},{2,10},{3,11},{4,12},{5,13},{6,14},{7,15},{8,0},{9,1},... | collective-permute-start | bytes 393224 | tf_op jit(solution)/shard_map/ppermute | solution.py:287
  8.7 0.0 collective-permute-start.4
  8.7 0.0 copy-done.4
  8.7 0.0 copy-done.5
  8.7 0.0 copy-done.8
  8.7 1.0 %shard_map.115 = (bf16[512,128]{1,0:T(8,128)(2,1)S(1)}, bf16[512,128]{1,0:T(8,128)(2,1)S(1)}, f32[24,128]{1,0:T(8,128)S(1)}) custom-call(s32[5]{0:T(128)S(1)} %copy-done.8, bf16[1024,128]{1,0:T(8,128)(2,1)S(1)} %shard_map.113.normed_ref, bf16[128,128]{1,0:T(8,128)(2,1)S(1)} %copy-done.4, bf16[128,128]{1,0:T(8,128)(2,1)S(1)} %copy-done.5, ...), custom_call_target="tpu_custom_call" | custom-call | flops 33554432 | bytes 1048576 | tf_op jit(solution)/shard_map/pallas_call | solution.py:291
  9.8 2.4 %collective-permute-done.1.x_ref = bf16[16,64,128]{2,1,0:T(8,128)(2,1)S(1)} collective-permute-done((bf16[16,64,128]{2,1,0:T(8,128)(2,1)}, bf16[16,64,128]{2,1,0:T(8,128)(2,1)S(1)}, u32[]{:S(2)}, u32[]{:S(2)}) %collective-permute-start.1) | collective-permute-done | bytes 262176 | tf_op jit(solution)/shard_map/ppermute | solution.py:287
  12.2 1.1 %shard_map.117 = (bf16[512,128]{1,0:T(8,128)(2,1)S(1)}, bf16[512,128]{1,0:T(8,128)(2,1)S(1)}) custom-call(f32[24,128]{1,0:T(8,128)S(1)} %get-tuple-element.20.masks_ref, bf16[16,64,128]{2,1,0:T(8,128)(2,1)S(1)} %collective-permute-done.1.x_ref, bf16[128,128]{1,0:T(8,128)(2,1)S(1)} %copy-done.4, bf16[128,128]{1,0:T(8,128)(2,1)S(1)} %copy-done.5, ...), custom_call_target="tpu_custom_call" | custom-call | flops 67108864 | bytes 1048576 | tf_op jit(solution)/shard_map/pallas_call | solution.py:291
  13.3 0.1 collective-permute-start.2
  13.3 0.5 %collective-permute-start = (bf16[512,128]{1,0:T(8,128)(2,1)S(1)}, bf16[512,128]{1,0:T(8,128)(2,1)S(1)}, u32[]{:S(2)}, u32[]{:S(2)}) collective-permute-start(bf16[512,128]{1,0:T(8,128)(2,1)S(1)} %get-tuple-element.26), channel_id=1, source_target_pairs={{0,2},{1,3},{2,0},{3,1},{4,6},{5,7},{6,4},{7,5},{8,10},{9,11},{10,... | collective-permute-start | bytes 393224 | tf_op jit(solution)/shard_map/ppermute | solution.py:287
  13.8 5.2 %collective-permute-done.3.far_ref.far = bf16[512,128]{1,0:T(8,128)(2,1)S(1)} collective-permute-done((bf16[512,128]{1,0:T(8,128)(2,1)S(1)}, bf16[512,128]{1,0:T(8,128)(2,1)S(1)}, u32[]{:S(2)}, u32[]{:S(2)}) %collective-permute-start.3) | collective-permute-done | bytes 131104 | tf_op jit(solution)/shard_map/ppermute | solution.py:287
  19.1 0.0 collective-permute-done.4.cross_ref.cross
  19.1 0.0 collective-permute-done.2.ready_ref.near_over
  19.1 0.1 collective-permute-start.5
  19.2 0.0 collective-permute-done.core
  19.2 1.3 %collective-permute-done.5.both_over = bf16[512,128]{1,0:T(8,128)(2,1)S(1)} collective-permute-done((bf16[512,128]{1,0:T(8,128)(2,1)S(1)}, bf16[512,128]{1,0:T(8,128)(2,1)S(1)}, u32[]{:S(2)}, u32[]{:S(2)}) %collective-permute-start.5) | collective-permute-done | bytes 131104 | tf_op jit(solution)/shard_map/ppermute | solution.py:287
  20.5 0.5 %shard_map.119 = (bf16[512,128]{1,0:T(8,128)(2,1)S(1)}, bf16[512,128]{1,0:T(8,128)(2,1)S(1)}, bf16[512,128]{1,0:T(8,128)(2,1)S(1)}, bf16[512,128]{1,0:T(8,128)(2,1)S(1)}) custom-call(f32[24,128]{1,0:T(8,128)S(1)} %get-tuple-element.20.masks_ref, bf16[512,128]{1,0:T(8,128)(2,1)S(1)} %get-tuple-element.25.own, bf16[512,128]{1,0:T(8,128)(2,1)S(1)} %collective-permute-done.core, ...), custom_call_target="tpu_custom_call" | custom-call | flops 16777216 | bytes 1048576 | tf_op jit(solution)/shard_map/pallas_call | solution.py:291
  21.0 3.0 %collective-permute-start.6 = (bf16[512,128]{1,0:T(8,128)(2,1)S(1)}, bf16[512,128]{1,0:T(8,128)(2,1)S(1)}, u32[]{:S(2)}, u32[]{:S(2)}) collective-permute-start(bf16[512,128]{1,0:T(8,128)(2,1)S(1)} %get-tuple-element.31), channel_id=1, source_target_pairs={{0,5},{1,4},{2,7},{3,6},{4,1},{5,0},{6,3},{7,2},{8,13},{9,12},{10,... | collective-permute-start | bytes 393224 | tf_op jit(solution)/shard_map/ppermute | solution.py:287
  24.0 0.5 %collective-permute-start.7 = (bf16[512,128]{1,0:T(8,128)(2,1)S(1)}, bf16[512,128]{1,0:T(8,128)(2,1)S(1)}, u32[]{:S(2)}, u32[]{:S(2)}) collective-permute-start(bf16[512,128]{1,0:T(8,128)(2,1)S(1)} %get-tuple-element.32), channel_id=1, source_target_pairs={{0,1},{1,0},{2,3},{3,2},{4,5},{5,4},{6,7},{7,6},{8,9},{9,8},{10,11... | collective-permute-start | bytes 393224 | tf_op jit(solution)/shard_map/ppermute | solution.py:287
  24.5 0.1 collective-permute-start.8
  24.7 0.0 collective-permute-start.9
  24.7 3.2 %collective-permute-done.6.refs_1_ = bf16[512,128]{1,0:T(8,128)(2,1)S(1)} collective-permute-done((bf16[512,128]{1,0:T(8,128)(2,1)S(1)}, bf16[512,128]{1,0:T(8,128)(2,1)S(1)}, u32[]{:S(2)}, u32[]{:S(2)}) %collective-permute-start.6) | collective-permute-done | bytes 131104 | tf_op jit(solution)/shard_map/ppermute | solution.py:287
  27.9 0.0 collective-permute-start.10
  27.9 2.7 %collective-permute-done.7.refs_2_ = bf16[512,128]{1,0:T(8,128)(2,1)S(1)} collective-permute-done((bf16[512,128]{1,0:T(8,128)(2,1)S(1)}, bf16[512,128]{1,0:T(8,128)(2,1)S(1)}, u32[]{:S(2)}, u32[]{:S(2)}) %collective-permute-start.7) | collective-permute-done | bytes 131104 | tf_op jit(solution)/shard_map/ppermute | solution.py:287
  30.6 0.0 collective-permute-start.11
  30.6 0.0 collective-permute-done.8.refs_3_
  30.6 0.5 %collective-permute-start.12 = (bf16[512,128]{1,0:T(8,128)(2,1)S(1)}, bf16[512,128]{1,0:T(8,128)(2,1)S(1)}, u32[]{:S(2)}, u32[]{:S(2)}) collective-permute-start(bf16[512,128]{1,0:T(8,128)(2,1)S(1)} %collective-permute-done.8.refs_3_), channel_id=1, source_target_pairs={{0,2},{1,3},{2,0},{3,1},{4,6},{5,7},{6,4},{7,5},{8,10},{9,11},{10,... | collective-permute-start | bytes 393224 | tf_op jit(solution)/shard_map/ppermute | solution.py:287
  31.1 0.0 copy-done.9
  31.1 0.1 copy.12.dw_ref
  31.3 0.0 copy-done.10
  31.3 0.1 reshape.7.bins_ref
  31.3 0.0 copy-done.1
  31.3 0.0 copy-done.3
  31.3 0.0 copy-done.2
  31.3 0.4 shard_map.116
  31.7 0.0 collective-permute-done.9.refs_4_
  31.7 0.0 collective-permute-done.10.refs_5_
  31.7 0.2 collective-permute-done.11.refs_6_
  32.0 0.2 collective-permute-done.12.refs_7_
  32.2 0.9 %shard_map.120 = (bf16[128,1024]{1,0:T(8,128)(2,1)S(1)}, f32[8,128]{1,0:T(8,128)S(1)}) custom-call(f32[24,128]{1,0:T(8,128)S(1)} %get-tuple-element.20.masks_ref, f32[128,1024]{1,0:T(8,128)S(1)} %get-tuple-element.21.x_ref, f32[128,1024]{1,0:T(8,128)S(1)} %get-tuple-element.22.gate_ref, s32[8,128]{1,0:T(8,128)S(1)} %reshape.7.bins_ref, ...), custom_call_target="tpu_custom_call" | custom-call | flops 100663296 | bytes 1048576 | tf_op jit(solution)/shard_map/pallas_call | solution.py:291
  33.1 1.9 %collective-permute-start.13 = (f32[8,128]{1,0:T(8,128)S(1)}, f32[8,128]{1,0:T(8,128)S(1)}, u32[]{:S(2)}, u32[]{:S(2)}) collective-permute-start(f32[8,128]{1,0:T(8,128)S(1)} %get-tuple-element.35), channel_id=1, source_target_pairs={{0,5},{1,4},{2,7},{3,6},{4,1},{5,0},{6,3},{7,2},{8,13},{9,12},{10,... | collective-permute-start | bytes 12296 | tf_op jit(solution)/shard_map/ppermute | solution.py:287
  34.9 0.9 %collective-permute-start.14 = (f32[8,128]{1,0:T(8,128)S(1)}, f32[8,128]{1,0:T(8,128)S(1)}, u32[]{:S(2)}, u32[]{:S(2)}) collective-permute-start(f32[8,128]{1,0:T(8,128)S(1)} %get-tuple-element.35), channel_id=1, source_target_pairs={{0,4},{1,5},{2,6},{3,7},{4,0},{5,1},{6,2},{7,3},{8,12},{9,13},{10,... | collective-permute-start | bytes 12296 | tf_op jit(solution)/shard_map/ppermute | solution.py:287
  35.8 0.8 %collective-permute-start.15 = (f32[8,128]{1,0:T(8,128)S(1)}, f32[8,128]{1,0:T(8,128)S(1)}, u32[]{:S(2)}, u32[]{:S(2)}) collective-permute-start(f32[8,128]{1,0:T(8,128)S(1)} %get-tuple-element.35), channel_id=1, source_target_pairs={{0,1},{1,0},{2,3},{3,2},{4,5},{5,4},{6,7},{7,6},{8,9},{9,8},{10,11... | collective-permute-start | bytes 12296 | tf_op jit(solution)/shard_map/ppermute | solution.py:287
  36.6 1.0 %collective-permute-done.13 = f32[8,128]{1,0:T(8,128)S(1)} collective-permute-done((f32[8,128]{1,0:T(8,128)S(1)}, f32[8,128]{1,0:T(8,128)S(1)}, u32[]{:S(2)}, u32[]{:S(2)}) %collective-permute-start.13) | collective-permute-done | bytes 4128 | tf_op jit(solution)/shard_map/ppermute | solution.py:287
  37.6 0.9 %collective-permute-done.14 = f32[8,128]{1,0:T(8,128)S(1)} collective-permute-done((f32[8,128]{1,0:T(8,128)S(1)}, f32[8,128]{1,0:T(8,128)S(1)}, u32[]{:S(2)}, u32[]{:S(2)}) %collective-permute-start.14) | collective-permute-done | bytes 4128 | tf_op jit(solution)/shard_map/ppermute | solution.py:287
  38.5 0.9 %collective-permute-done.15 = f32[8,128]{1,0:T(8,128)S(1)} collective-permute-done((f32[8,128]{1,0:T(8,128)S(1)}, f32[8,128]{1,0:T(8,128)S(1)}, u32[]{:S(2)}, u32[]{:S(2)}) %collective-permute-start.15) | collective-permute-done | bytes 4128 | tf_op jit(solution)/shard_map/ppermute | solution.py:287
  39.4 2.2 %collective-permute-start.16 = (f32[8,128]{1,0:T(8,128)S(1)}, f32[8,128]{1,0:T(8,128)S(1)}, u32[]{:S(2)}, u32[]{:S(2)}) collective-permute-start(f32[8,128]{1,0:T(8,128)S(1)} %add_add_fusion.1), channel_id=1, source_target_pairs={{0,8},{1,9},{2,10},{3,11},{4,12},{5,13},{6,14},{7,15},{8,0},{9,1},... | collective-permute-start | bytes 12296 | tf_op jit(solution)/shard_map/ppermute | solution.py:287
  41.6 0.0 collective-permute-start.17
  41.6 0.9 %collective-permute-start.18 = (f32[8,128]{1,0:T(8,128)S(1)}, f32[8,128]{1,0:T(8,128)S(1)}, u32[]{:S(2)}, u32[]{:S(2)}) collective-permute-start(f32[8,128]{1,0:T(8,128)S(1)} %add_add_fusion.1), channel_id=1, source_target_pairs={{0,2},{1,3},{2,0},{3,1},{4,6},{5,7},{6,4},{7,5},{8,10},{9,11},{10,... | collective-permute-start | bytes 12296 | tf_op jit(solution)/shard_map/ppermute | solution.py:287
  42.4 0.8 %shard_map.121 = bf16[16,64,128]{2,1,0:T(8,128)(2,1)} custom-call(bf16[128,1024]{1,0:T(8,128)(2,1)S(1)} %get-tuple-element.34.turned_ref), custom_call_target="tpu_custom_call" | custom-call | flops 67108864 | bytes 1048576 | tf_op jit(solution)/shard_map/pallas_call | solution.py:291
  43.3 0.6 %collective-permute-done.16 = f32[8,128]{1,0:T(8,128)S(1)} collective-permute-done((f32[8,128]{1,0:T(8,128)S(1)}, f32[8,128]{1,0:T(8,128)S(1)}, u32[]{:S(2)}, u32[]{:S(2)}) %collective-permute-start.16) | collective-permute-done | bytes 4128 | tf_op jit(solution)/shard_map/ppermute | solution.py:287
  43.9 1.6 %collective-permute-done.17 = f32[8,128]{1,0:T(8,128)S(1)} collective-permute-done((f32[8,128]{1,0:T(8,128)S(1)}, f32[8,128]{1,0:T(8,128)S(1)}, u32[]{:S(2)}, u32[]{:S(2)}) %collective-permute-start.17) | collective-permute-done | bytes 4128 | tf_op jit(solution)/shard_map/ppermute | solution.py:287
  45.5 0.0 collective-permute-done.18
  45.5 0.5 %slice.3 = f32[1,1]{1,0:T(1,128)} slice(f32[8,128]{1,0:T(8,128)S(1)} %add_add_fusion), slice={[0:1], [0:1]} | slice | bytes 8 | tf_op jit(solution)/shard_map/slice | solution.py:414
  (10 shorter events, 0.0 us)
Async XLA Ops:
  0.6 11.6 %collective-permute-start.1 = (bf16[16,64,128]{2,1,0:T(8,128)(2,1)}, bf16[16,64,128]{2,1,0:T(8,128)(2,1)S(1)}, u32[]{:S(2)}, u32[]{:S(2)}) collective-permute-start(bf16[16,64,128]{2,1,0:T(8,128)(2,1)} %x_ref.3), channel_id=1, source_target_pairs={{0,4},{1,5},{2,6},{3,7},{4,0},{5,1},{6,2},{7,3},{8,12},{9,13},{10,... | collective-permute-start | bytes 786440 | tf_op jit(solution)/shard_map/ppermute | solution.py:287
  3.7 1.0 %copy-start = (bf16[16,64,128]{2,1,0:T(8,128)(2,1)S(1)}, bf16[16,64,128]{2,1,0:T(8,128)(2,1)}, u32[]{:S(2)}) copy-start(bf16[16,64,128]{2,1,0:T(8,128)(2,1)} %x_ref.3) | copy-start | bytes 786436
  4.7 0.8 %copy-start.6 = (bf16[128,128]{1,0:T(8,128)(2,1)S(1)}, bf16[128,128]{1,0:T(8,128)(2,1)}, u32[]{:S(2)}) copy-start(bf16[128,128]{1,0:T(8,128)(2,1)} %rw_ref.1) | copy-start | bytes 98308
  4.7 0.8 %copy-start.7 = (bf16[128,128]{1,0:T(8,128)(2,1)S(1)}, bf16[128,128]{1,0:T(8,128)(2,1)}, u32[]{:S(2)}) copy-start(bf16[128,128]{1,0:T(8,128)(2,1)} %rg_ref.1) | copy-start | bytes 98308
  5.5 3.2 %copy-start.4 = (bf16[128,128]{1,0:T(8,128)(2,1)S(1)}, bf16[128,128]{1,0:T(8,128)(2,1)}, u32[]{:S(2)}) copy-start(bf16[128,128]{1,0:T(8,128)(2,1)} %lw_ref.1) | copy-start | bytes 98308
  5.5 3.2 %copy-start.5 = (bf16[128,128]{1,0:T(8,128)(2,1)S(1)}, bf16[128,128]{1,0:T(8,128)(2,1)}, u32[]{:S(2)}) copy-start(bf16[128,128]{1,0:T(8,128)(2,1)} %lg_ref.1) | copy-start | bytes 98308
  6.0 2.7 %copy-start.8 = (s32[5]{0:T(128)S(1)}, s32[5]{0:T(128)}, u32[]{:S(2)}) copy-start(s32[5]{0:T(128)} %lens_ref.1) | copy-start | bytes 64
  6.1 13.0 %collective-permute-start.3 = (bf16[512,128]{1,0:T(8,128)(2,1)S(1)}, bf16[512,128]{1,0:T(8,128)(2,1)S(1)}, u32[]{:S(2)}, u32[]{:S(2)}) collective-permute-start(bf16[512,128]{1,0:T(8,128)(2,1)S(1)} %get-tuple-element.19.stay_ref), channel_id=1, source_target_pairs={{0,8},{1,9},{2,10},{3,11},{4,12},{5,13},{6,14},{7,15},{8,0},{9,1},... | collective-permute-start | bytes 393224 | tf_op jit(solution)/shard_map/ppermute | solution.py:287
  8.7 10.3 %collective-permute-start.4 = (bf16[512,128]{1,0:T(8,128)(2,1)S(1)}, bf16[512,128]{1,0:T(8,128)(2,1)S(1)}, u32[]{:S(2)}, u32[]{:S(2)}) collective-permute-start(bf16[512,128]{1,0:T(8,128)(2,1)S(1)} %get-tuple-element.29), channel_id=1, source_target_pairs={{0,12},{1,13},{2,14},{3,15},{4,8},{5,9},{6,10},{7,11},{8,4},{9,5},... | collective-permute-start | bytes 393224 | tf_op jit(solution)/shard_map/ppermute | solution.py:287
  13.3 5.8 %collective-permute-start.2 = (bf16[512,128]{1,0:T(8,128)(2,1)S(1)}, bf16[512,128]{1,0:T(8,128)(2,1)S(1)}, u32[]{:S(2)}, u32[]{:S(2)}) collective-permute-start(bf16[512,128]{1,0:T(8,128)(2,1)S(1)} %get-tuple-element.28), channel_id=1, source_target_pairs={{0,2},{1,3},{2,0},{3,1},{4,6},{5,7},{6,4},{7,5},{8,10},{9,11},{10,... | collective-permute-start | bytes 393224 | tf_op jit(solution)/shard_map/ppermute | solution.py:287
  13.3 5.8 %collective-permute-start = (bf16[512,128]{1,0:T(8,128)(2,1)S(1)}, bf16[512,128]{1,0:T(8,128)(2,1)S(1)}, u32[]{:S(2)}, u32[]{:S(2)}) collective-permute-start(bf16[512,128]{1,0:T(8,128)(2,1)S(1)} %get-tuple-element.26), channel_id=1, source_target_pairs={{0,2},{1,3},{2,0},{3,1},{4,6},{5,7},{6,4},{7,5},{8,10},{9,11},{10,... | collective-permute-start | bytes 393224 | tf_op jit(solution)/shard_map/ppermute | solution.py:287
  19.1 1.4 %collective-permute-start.5 = (bf16[512,128]{1,0:T(8,128)(2,1)S(1)}, bf16[512,128]{1,0:T(8,128)(2,1)S(1)}, u32[]{:S(2)}, u32[]{:S(2)}) collective-permute-start(bf16[512,128]{1,0:T(8,128)(2,1)S(1)} %shard_map.118), channel_id=1, source_target_pairs={{0,2},{1,3},{2,0},{3,1},{4,6},{5,7},{6,4},{7,5},{8,10},{9,11},{10,... | collective-permute-start | bytes 393224 | tf_op jit(solution)/shard_map/ppermute | solution.py:287
  20.5 10.6 %copy-start.9 = (bf16[128,64]{0,1:T(8,128)(2,1)S(1)}, bf16[128,64]{0,1:T(8,128)(2,1)}, u32[]{:S(2)}) copy-start(bf16[128,64]{0,1:T(8,128)(2,1)} %param.19) | copy-start | bytes 49156
  20.5 10.8 %copy-start.10 = (s32[16,64]{1,0:T(8,128)S(1)}, s32[16,64]{1,0:T(8,128)}, u32[]{:S(2)}) copy-start(s32[16,64]{1,0:T(8,128)} %param.11) | copy-start | bytes 12292
  20.5 10.8 %copy-start.1 = (bf16[16,64,128]{2,1,0:T(8,128)(2,1)S(1)}, bf16[16,64,128]{2,1,0:T(8,128)(2,1)}, u32[]{:S(2)}) copy-start(bf16[16,64,128]{2,1,0:T(8,128)(2,1)} %x_ref.3) | copy-start | bytes 786436
  21.0 6.9 %collective-permute-start.6 = (bf16[512,128]{1,0:T(8,128)(2,1)S(1)}, bf16[512,128]{1,0:T(8,128)(2,1)S(1)}, u32[]{:S(2)}, u32[]{:S(2)}) collective-permute-start(bf16[512,128]{1,0:T(8,128)(2,1)S(1)} %get-tuple-element.31), channel_id=1, source_target_pairs={{0,5},{1,4},{2,7},{3,6},{4,1},{5,0},{6,3},{7,2},{8,13},{9,12},{10,... | collective-permute-start | bytes 393224 | tf_op jit(solution)/shard_map/ppermute | solution.py:287
  24.0 7.3 %copy-start.3 = (bf16[128,128]{1,0:T(8,128)(2,1)S(1)}, bf16[128,128]{1,0:T(8,128)(2,1)}, u32[]{:S(2)}) copy-start(bf16[128,128]{1,0:T(8,128)(2,1)} %ow_ref.1) | copy-start | bytes 98308
  24.0 7.3 %copy-start.2 = (bf16[128,128]{1,0:T(8,128)(2,1)S(1)}, bf16[128,128]{1,0:T(8,128)(2,1)}, u32[]{:S(2)}) copy-start(bf16[128,128]{1,0:T(8,128)(2,1)} %gw_ref.1) | copy-start | bytes 98308
  24.0 6.6 %collective-permute-start.7 = (bf16[512,128]{1,0:T(8,128)(2,1)S(1)}, bf16[512,128]{1,0:T(8,128)(2,1)S(1)}, u32[]{:S(2)}, u32[]{:S(2)}) collective-permute-start(bf16[512,128]{1,0:T(8,128)(2,1)S(1)} %get-tuple-element.32), channel_id=1, source_target_pairs={{0,1},{1,0},{2,3},{3,2},{4,5},{5,4},{6,7},{7,6},{8,9},{9,8},{10,11... | collective-permute-start | bytes 393224 | tf_op jit(solution)/shard_map/ppermute | solution.py:287
  24.5 6.1 %collective-permute-start.8 = (bf16[512,128]{1,0:T(8,128)(2,1)S(1)}, bf16[512,128]{1,0:T(8,128)(2,1)S(1)}, u32[]{:S(2)}, u32[]{:S(2)}) collective-permute-start(bf16[512,128]{1,0:T(8,128)(2,1)S(1)} %get-tuple-element.33), channel_id=1, source_target_pairs={{0,4},{1,5},{2,6},{3,7},{4,0},{5,1},{6,2},{7,3},{8,12},{9,13},{10,... | collective-permute-start | bytes 393224 | tf_op jit(solution)/shard_map/ppermute | solution.py:287
  24.7 7.0 %collective-permute-start.9 = (bf16[512,128]{1,0:T(8,128)(2,1)S(1)}, bf16[512,128]{1,0:T(8,128)(2,1)S(1)}, u32[]{:S(2)}, u32[]{:S(2)}) collective-permute-start(bf16[512,128]{1,0:T(8,128)(2,1)S(1)} %get-tuple-element.30.refs_0_), channel_id=1, source_target_pairs={{0,2},{1,3},{2,0},{3,1},{4,6},{5,7},{6,4},{7,5},{8,10},{9,11},{10,... | collective-permute-start | bytes 393224 | tf_op jit(solution)/shard_map/ppermute | solution.py:287
  27.9 3.8 %collective-permute-start.10 = (bf16[512,128]{1,0:T(8,128)(2,1)S(1)}, bf16[512,128]{1,0:T(8,128)(2,1)S(1)}, u32[]{:S(2)}, u32[]{:S(2)}) collective-permute-start(bf16[512,128]{1,0:T(8,128)(2,1)S(1)} %collective-permute-done.6.refs_1_), channel_id=1, source_target_pairs={{0,2},{1,3},{2,0},{3,1},{4,6},{5,7},{6,4},{7,5},{8,10},{9,11},{10,... | collective-permute-start | bytes 393224 | tf_op jit(solution)/shard_map/ppermute | solution.py:287
  30.6 1.3 %collective-permute-start.11 = (bf16[512,128]{1,0:T(8,128)(2,1)S(1)}, bf16[512,128]{1,0:T(8,128)(2,1)S(1)}, u32[]{:S(2)}, u32[]{:S(2)}) collective-permute-start(bf16[512,128]{1,0:T(8,128)(2,1)S(1)} %collective-permute-done.7.refs_2_), channel_id=1, source_target_pairs={{0,2},{1,3},{2,0},{3,1},{4,6},{5,7},{6,4},{7,5},{8,10},{9,11},{10,... | collective-permute-start | bytes 393224 | tf_op jit(solution)/shard_map/ppermute | solution.py:287
  30.6 1.5 %collective-permute-start.12 = (bf16[512,128]{1,0:T(8,128)(2,1)S(1)}, bf16[512,128]{1,0:T(8,128)(2,1)S(1)}, u32[]{:S(2)}, u32[]{:S(2)}) collective-permute-start(bf16[512,128]{1,0:T(8,128)(2,1)S(1)} %collective-permute-done.8.refs_3_), channel_id=1, source_target_pairs={{0,2},{1,3},{2,0},{3,1},{4,6},{5,7},{6,4},{7,5},{8,10},{9,11},{10,... | collective-permute-start | bytes 393224 | tf_op jit(solution)/shard_map/ppermute | solution.py:287
  33.1 4.5 %collective-permute-start.13 = (f32[8,128]{1,0:T(8,128)S(1)}, f32[8,128]{1,0:T(8,128)S(1)}, u32[]{:S(2)}, u32[]{:S(2)}) collective-permute-start(f32[8,128]{1,0:T(8,128)S(1)} %get-tuple-element.35), channel_id=1, source_target_pairs={{0,5},{1,4},{2,7},{3,6},{4,1},{5,0},{6,3},{7,2},{8,13},{9,12},{10,... | collective-permute-start | bytes 12296 | tf_op jit(solution)/shard_map/ppermute | solution.py:287
  34.9 3.6 %collective-permute-start.14 = (f32[8,128]{1,0:T(8,128)S(1)}, f32[8,128]{1,0:T(8,128)S(1)}, u32[]{:S(2)}, u32[]{:S(2)}) collective-permute-start(f32[8,128]{1,0:T(8,128)S(1)} %get-tuple-element.35), channel_id=1, source_target_pairs={{0,4},{1,5},{2,6},{3,7},{4,0},{5,1},{6,2},{7,3},{8,12},{9,13},{10,... | collective-permute-start | bytes 12296 | tf_op jit(solution)/shard_map/ppermute | solution.py:287
  35.8 3.6 %collective-permute-start.15 = (f32[8,128]{1,0:T(8,128)S(1)}, f32[8,128]{1,0:T(8,128)S(1)}, u32[]{:S(2)}, u32[]{:S(2)}) collective-permute-start(f32[8,128]{1,0:T(8,128)S(1)} %get-tuple-element.35), channel_id=1, source_target_pairs={{0,1},{1,0},{2,3},{3,2},{4,5},{5,4},{6,7},{7,6},{8,9},{9,8},{10,11... | collective-permute-start | bytes 12296 | tf_op jit(solution)/shard_map/ppermute | solution.py:287
  39.4 4.5 %collective-permute-start.16 = (f32[8,128]{1,0:T(8,128)S(1)}, f32[8,128]{1,0:T(8,128)S(1)}, u32[]{:S(2)}, u32[]{:S(2)}) collective-permute-start(f32[8,128]{1,0:T(8,128)S(1)} %add_add_fusion.1), channel_id=1, source_target_pairs={{0,8},{1,9},{2,10},{3,11},{4,12},{5,13},{6,14},{7,15},{8,0},{9,1},... | collective-permute-start | bytes 12296 | tf_op jit(solution)/shard_map/ppermute | solution.py:287
  41.6 3.9 %collective-permute-start.17 = (f32[8,128]{1,0:T(8,128)S(1)}, f32[8,128]{1,0:T(8,128)S(1)}, u32[]{:S(2)}, u32[]{:S(2)}) collective-permute-start(f32[8,128]{1,0:T(8,128)S(1)} %add_add_fusion.1), channel_id=1, source_target_pairs={{0,10},{1,11},{2,8},{3,9},{4,14},{5,15},{6,12},{7,13},{8,2},{9,3},... | collective-permute-start | bytes 12296 | tf_op jit(solution)/shard_map/ppermute | solution.py:287
  41.6 3.9 %collective-permute-start.18 = (f32[8,128]{1,0:T(8,128)S(1)}, f32[8,128]{1,0:T(8,128)S(1)}, u32[]{:S(2)}, u32[]{:S(2)}) collective-permute-start(f32[8,128]{1,0:T(8,128)S(1)} %add_add_fusion.1), channel_id=1, source_target_pairs={{0,2},{1,3},{2,0},{3,1},{4,6},{5,7},{6,4},{7,5},{8,10},{9,11},{10,... | collective-permute-start | bytes 12296 | tf_op jit(solution)/shard_map/ppermute | solution.py:287

commit v15 on v13

--- a/solution.py
+++ b/solution.py
@@ -404,11 +404,11 @@
     )
     pair_out = call(turn_back_kernel, struct(pair_repr.shape, bf16), args=(pair_out,), flops=1 << 26)
     loss = loss + exchange(loss, places, over_core)
-    diagonal, beside, near_loss = [
-        exchange(loss, places, mask) for mask in (over_z + over_x, over_x, over_z)
+    loss = loss + exchange(loss, places, over_x)
+    cross_loss, half, near_loss = [
+        exchange(loss, places, mask) for mask in (over_half + over_z, over_half, over_z)
     ]
-    loss = (diagonal + near_loss) + (beside + loss)
-    loss = loss + exchange(loss, places, over_half)
+    loss = (cross_loss + half) + (near_loss + loss)
     return (pair_out, loss[0, :1])
 
 

time: 45.8 us -> 45.6 us (level)
  transfers between devices with their start and end apart: 18 -> 18, of which waited for: 12 -> 11; matrix products, arithmetic and copies ran while one was open for 0% -> 0% of each run, Pallas kernels for 9% -> 9%
where the time goes in v15:
time: 45.6 us; the launch traced here: 45.4 us
  waiting for transfers between devices  20.3 us (45%)
  starting transfers between devices  16.5 us (36%)
  Pallas kernels  5.69 us (12%)
  local copies, waits for them, and re-layouts  2.13 us (5%)
  between operations  0.78 us (2%)
    ppermute x18, waiting for transfers between devices, exchange(): return lax.ppermute(value, AXES, [(at, at ^ mask) for at in range(places)])  20.3 us
    ppermute x18, starting transfers between devices, exchange(): return lax.ppermute(value, AXES, [(at, at ^ mask) for at in range(places)])  16.5 us
    pallas_call x9, Pallas kernels, call(): pl.pallas_call(kernel, out_shape=outs, in_specs=specs if specs is not Non...  5.69 us
    unnamed x23, local copies, waits for them, and re-layouts  1.54 us
  transfers between devices with their start and end apart: 18, of which 11 were waited for; matrix products, arithmetic and copies ran while one was open for 0% of the time, Pallas kernels for 9%

profile of v15, /device:TPU:0, one launch (start us, length us, event | category | flops | bytes accessed | tf_op | source)
XLA Modules:
  0.0 45.4 jit_solution(17781647075129934431)
XLA Ops:
  0.6 3.1 %collective-permute-start.1 = (bf16[16,64,128]{2,1,0:T(8,128)(2,1)}, bf16[16,64,128]{2,1,0:T(8,128)(2,1)S(1)}, u32[]{:S(2)}, u32[]{:S(2)}) collective-permute-start(bf16[16,64,128]{2,1,0:T(8,128)(2,1)} %x_ref.3), channel_id=1, source_target_pairs={{0,4},{1,5},{2,6},{3,7},{4,0},{5,1},{6,2},{7,3},{8,12},{9,13},{10,... | collective-permute-start | bytes 786440 | tf_op jit(solution)/shard_map/ppermute | solution.py:287
  3.7 0.0 copy-start
  3.7 1.0 %copy-done = bf16[16,64,128]{2,1,0:T(8,128)(2,1)S(1)} copy-done((bf16[16,64,128]{2,1,0:T(8,128)(2,1)S(1)}, bf16[16,64,128]{2,1,0:T(8,128)(2,1)}, u32[]{:S(2)}) %copy-start) | copy-done | bytes 262168
  4.7 0.0 copy-start.7
  4.7 0.4 shard_map.113.normed_ref
  5.1 0.4 copy-done.6
  5.5 0.0 copy-done.7
  5.5 0.0 copy-start.4
  5.5 0.0 copy-start.5
  5.5 0.6 %shard_map.114 = (bf16[512,128]{1,0:T(8,128)(2,1)S(1)}, bf16[512,128]{1,0:T(8,128)(2,1)S(1)}) custom-call(bf16[1024,128]{1,0:T(8,128)(2,1)S(1)} %shard_map.113.normed_ref, bf16[128,128]{1,0:T(8,128)(2,1)S(1)} %copy-done.6, bf16[128,128]{1,0:T(8,128)(2,1)S(1)} %copy-done.7), custom_call_target="tpu_custom_call" | custom-call | flops 67108864 | bytes 1048576 | tf_op jit(solution)/shard_map/pallas_call | solution.py:291
  6.0 0.0 copy-start.8
  6.1 2.7 %collective-permute-start.3 = (bf16[512,128]{1,0:T(8,128)(2,1)S(1)}, bf16[512,128]{1,0:T(8,128)(2,1)S(1)}, u32[]{:S(2)}, u32[]{:S(2)}) collective-permute-start(bf16[512,128]{1,0:T(8,128)(2,1)S(1)} %get-tuple-element.19.stay_ref), channel_id=1, source_target_pairs={{0,8},{1,9},{2,10},{3,11},{4,12},{5,13},{6,14},{7,15},{8,0},{9,1},... | collective-permute-start | bytes 393224 | tf_op jit(solution)/shard_map/ppermute | solution.py:287
  8.7 0.0 collective-permute-start.4
  8.7 0.0 copy-done.4
  8.7 0.0 copy-done.5
  8.7 0.0 copy-done.8
  8.7 1.0 %shard_map.115 = (bf16[512,128]{1,0:T(8,128)(2,1)S(1)}, bf16[512,128]{1,0:T(8,128)(2,1)S(1)}, f32[24,128]{1,0:T(8,128)S(1)}) custom-call(s32[5]{0:T(128)S(1)} %copy-done.8, bf16[1024,128]{1,0:T(8,128)(2,1)S(1)} %shard_map.113.normed_ref, bf16[128,128]{1,0:T(8,128)(2,1)S(1)} %copy-done.4, bf16[128,128]{1,0:T(8,128)(2,1)S(1)} %copy-done.5, ...), custom_call_target="tpu_custom_call" | custom-call | flops 33554432 | bytes 1048576 | tf_op jit(solution)/shard_map/pallas_call | solution.py:291
  9.8 2.4 %collective-permute-done.1.x_ref = bf16[16,64,128]{2,1,0:T(8,128)(2,1)S(1)} collective-permute-done((bf16[16,64,128]{2,1,0:T(8,128)(2,1)}, bf16[16,64,128]{2,1,0:T(8,128)(2,1)S(1)}, u32[]{:S(2)}, u32[]{:S(2)}) %collective-permute-start.1) | collective-permute-done | bytes 262176 | tf_op jit(solution)/shard_map/ppermute | solution.py:287
  12.2 1.1 %shard_map.117 = (bf16[512,128]{1,0:T(8,128)(2,1)S(1)}, bf16[512,128]{1,0:T(8,128)(2,1)S(1)}) custom-call(f32[24,128]{1,0:T(8,128)S(1)} %get-tuple-element.20.masks_ref, bf16[16,64,128]{2,1,0:T(8,128)(2,1)S(1)} %collective-permute-done.1.x_ref, bf16[128,128]{1,0:T(8,128)(2,1)S(1)} %copy-done.4, bf16[128,128]{1,0:T(8,128)(2,1)S(1)} %copy-done.5, ...), custom_call_target="tpu_custom_call" | custom-call | flops 67108864 | bytes 1048576 | tf_op jit(solution)/shard_map/pallas_call | solution.py:291
  13.3 0.1 collective-permute-start.2
  13.3 0.5 %collective-permute-start = (bf16[512,128]{1,0:T(8,128)(2,1)S(1)}, bf16[512,128]{1,0:T(8,128)(2,1)S(1)}, u32[]{:S(2)}, u32[]{:S(2)}) collective-permute-start(bf16[512,128]{1,0:T(8,128)(2,1)S(1)} %get-tuple-element.26), channel_id=1, source_target_pairs={{0,2},{1,3},{2,0},{3,1},{4,6},{5,7},{6,4},{7,5},{8,10},{9,11},{10,... | collective-permute-start | bytes 393224 | tf_op jit(solution)/shard_map/ppermute | solution.py:287
  13.8 5.2 %collective-permute-done.3.far_ref.far = bf16[512,128]{1,0:T(8,128)(2,1)S(1)} collective-permute-done((bf16[512,128]{1,0:T(8,128)(2,1)S(1)}, bf16[512,128]{1,0:T(8,128)(2,1)S(1)}, u32[]{:S(2)}, u32[]{:S(2)}) %collective-permute-start.3) | collective-permute-done | bytes 131104 | tf_op jit(solution)/shard_map/ppermute | solution.py:287
  19.1 0.0 collective-permute-done.4.cross_ref.cross
  19.1 0.0 collective-permute-done.2.ready_ref.near_over
  19.1 0.1 collective-permute-start.5
  19.2 0.0 collective-permute-done.core
  19.2 1.3 %collective-permute-done.5.both_over = bf16[512,128]{1,0:T(8,128)(2,1)S(1)} collective-permute-done((bf16[512,128]{1,0:T(8,128)(2,1)S(1)}, bf16[512,128]{1,0:T(8,128)(2,1)S(1)}, u32[]{:S(2)}, u32[]{:S(2)}) %collective-permute-start.5) | collective-permute-done | bytes 131104 | tf_op jit(solution)/shard_map/ppermute | solution.py:287
  20.5 0.0 copy-start.9
  20.5 0.5 %shard_map.119 = (bf16[512,128]{1,0:T(8,128)(2,1)S(1)}, bf16[512,128]{1,0:T(8,128)(2,1)S(1)}, bf16[512,128]{1,0:T(8,128)(2,1)S(1)}, bf16[512,128]{1,0:T(8,128)(2,1)S(1)}) custom-call(f32[24,128]{1,0:T(8,128)S(1)} %get-tuple-element.20.masks_ref, bf16[512,128]{1,0:T(8,128)(2,1)S(1)} %get-tuple-element.25.own, bf16[512,128]{1,0:T(8,128)(2,1)S(1)} %collective-permute-done.core, ...), custom_call_target="tpu_custom_call" | custom-call | flops 16777216 | bytes 1048576 | tf_op jit(solution)/shard_map/pallas_call | solution.py:291
  21.0 3.0 %collective-permute-start.6 = (bf16[512,128]{1,0:T(8,128)(2,1)S(1)}, bf16[512,128]{1,0:T(8,128)(2,1)S(1)}, u32[]{:S(2)}, u32[]{:S(2)}) collective-permute-start(bf16[512,128]{1,0:T(8,128)(2,1)S(1)} %get-tuple-element.31), channel_id=1, source_target_pairs={{0,5},{1,4},{2,7},{3,6},{4,1},{5,0},{6,3},{7,2},{8,13},{9,12},{10,... | collective-permute-start | bytes 393224 | tf_op jit(solution)/shard_map/ppermute | solution.py:287
  24.0 0.5 %collective-permute-start.7 = (bf16[512,128]{1,0:T(8,128)(2,1)S(1)}, bf16[512,128]{1,0:T(8,128)(2,1)S(1)}, u32[]{:S(2)}, u32[]{:S(2)}) collective-permute-start(bf16[512,128]{1,0:T(8,128)(2,1)S(1)} %get-tuple-element.32), channel_id=1, source_target_pairs={{0,1},{1,0},{2,3},{3,2},{4,5},{5,4},{6,7},{7,6},{8,9},{9,8},{10,11... | collective-permute-start | bytes 393224 | tf_op jit(solution)/shard_map/ppermute | solution.py:287
  24.5 0.1 collective-permute-start.8
  24.7 0.0 collective-permute-start.9
  24.7 3.2 %collective-permute-done.6.refs_1_ = bf16[512,128]{1,0:T(8,128)(2,1)S(1)} collective-permute-done((bf16[512,128]{1,0:T(8,128)(2,1)S(1)}, bf16[512,128]{1,0:T(8,128)(2,1)S(1)}, u32[]{:S(2)}, u32[]{:S(2)}) %collective-permute-start.6) | collective-permute-done | bytes 131104 | tf_op jit(solution)/shard_map/ppermute | solution.py:287
  27.9 0.0 collective-permute-start.10
  27.9 2.7 %collective-permute-done.7.refs_2_ = bf16[512,128]{1,0:T(8,128)(2,1)S(1)} collective-permute-done((bf16[512,128]{1,0:T(8,128)(2,1)S(1)}, bf16[512,128]{1,0:T(8,128)(2,1)S(1)}, u32[]{:S(2)}, u32[]{:S(2)}) %collective-permute-start.7) | collective-permute-done | bytes 131104 | tf_op jit(solution)/shard_map/ppermute | solution.py:287
  30.6 0.0 collective-permute-start.11
  30.6 0.0 collective-permute-done.8.refs_3_
  30.6 0.5 %collective-permute-start.12 = (bf16[512,128]{1,0:T(8,128)(2,1)S(1)}, bf16[512,128]{1,0:T(8,128)(2,1)S(1)}, u32[]{:S(2)}, u32[]{:S(2)}) collective-permute-start(bf16[512,128]{1,0:T(8,128)(2,1)S(1)} %collective-permute-done.8.refs_3_), channel_id=1, source_target_pairs={{0,2},{1,3},{2,0},{3,1},{4,6},{5,7},{6,4},{7,5},{8,10},{9,11},{10,... | collective-permute-start | bytes 393224 | tf_op jit(solution)/shard_map/ppermute | solution.py:287
  31.1 0.0 copy-done.9
  31.1 0.1 copy.12.dw_ref
  31.3 0.0 copy-done.10
  31.3 0.1 reshape.7.bins_ref
  31.3 0.0 copy-done.1
  31.3 0.0 copy-done.3
  31.3 0.0 copy-done.2
  31.3 0.4 shard_map.116
  31.7 0.0 collective-permute-done.9.refs_4_
  31.7 0.0 collective-permute-done.10.refs_5_
  31.7 0.2 collective-permute-done.11.refs_6_
  32.0 0.2 collective-permute-done.12.refs_7_
  32.2 0.9 %shard_map.120 = (bf16[128,1024]{1,0:T(8,128)(2,1)S(1)}, f32[8,128]{1,0:T(8,128)S(1)}) custom-call(f32[24,128]{1,0:T(8,128)S(1)} %get-tuple-element.20.masks_ref, f32[128,1024]{1,0:T(8,128)S(1)} %get-tuple-element.21.x_ref, f32[128,1024]{1,0:T(8,128)S(1)} %get-tuple-element.22.gate_ref, s32[8,128]{1,0:T(8,128)S(1)} %reshape.7.bins_ref, ...), custom_call_target="tpu_custom_call" | custom-call | flops 100663296 | bytes 1048576 | tf_op jit(solution)/shard_map/pallas_call | solution.py:291
  33.1 0.3 collective-permute-start.13
  33.4 0.8 %collective-permute-done.13 = f32[8,128]{1,0:T(8,128)S(1)} collective-permute-done((f32[8,128]{1,0:T(8,128)S(1)}, f32[8,128]{1,0:T(8,128)S(1)}, u32[]{:S(2)}, u32[]{:S(2)}) %collective-permute-start.13) | collective-permute-done | bytes 4128 | tf_op jit(solution)/shard_map/ppermute | solution.py:287
  34.3 1.2 %collective-permute-start.14 = (f32[8,128]{1,0:T(8,128)S(1)}, f32[8,128]{1,0:T(8,128)S(1)}, u32[]{:S(2)}, u32[]{:S(2)}) collective-permute-start(f32[8,128]{1,0:T(8,128)S(1)} %add.15), channel_id=1, source_target_pairs={{0,1},{1,0},{2,3},{3,2},{4,5},{5,4},{6,7},{7,6},{8,9},{9,8},{10,11... | collective-permute-start | bytes 12296 | tf_op jit(solution)/shard_map/ppermute | solution.py:287
  35.5 2.4 %collective-permute-done.14 = f32[8,128]{1,0:T(8,128)S(1)} collective-permute-done((f32[8,128]{1,0:T(8,128)S(1)}, f32[8,128]{1,0:T(8,128)S(1)}, u32[]{:S(2)}, u32[]{:S(2)}) %collective-permute-start.14) | collective-permute-done | bytes 4128 | tf_op jit(solution)/shard_map/ppermute | solution.py:287
  37.9 2.5 %collective-permute-start.15 = (f32[8,128]{1,0:T(8,128)S(1)}, f32[8,128]{1,0:T(8,128)S(1)}, u32[]{:S(2)}, u32[]{:S(2)}) collective-permute-start(f32[8,128]{1,0:T(8,128)S(1)} %add.16), channel_id=1, source_target_pairs={{0,12},{1,13},{2,14},{3,15},{4,8},{5,9},{6,10},{7,11},{8,4},{9,5},... | collective-permute-start | bytes 12296 | tf_op jit(solution)/shard_map/ppermute | solution.py:287
  40.3 0.6 %collective-permute-start.16 = (f32[8,128]{1,0:T(8,128)S(1)}, f32[8,128]{1,0:T(8,128)S(1)}, u32[]{:S(2)}, u32[]{:S(2)}) collective-permute-start(f32[8,128]{1,0:T(8,128)S(1)} %add.16), channel_id=1, source_target_pairs={{0,8},{1,9},{2,10},{3,11},{4,12},{5,13},{6,14},{7,15},{8,0},{9,1},... | collective-permute-start | bytes 12296 | tf_op jit(solution)/shard_map/ppermute | solution.py:287
  40.9 1.3 %collective-permute-start.17 = (f32[8,128]{1,0:T(8,128)S(1)}, f32[8,128]{1,0:T(8,128)S(1)}, u32[]{:S(2)}, u32[]{:S(2)}) collective-permute-start(f32[8,128]{1,0:T(8,128)S(1)} %add.16), channel_id=1, source_target_pairs={{0,4},{1,5},{2,6},{3,7},{4,0},{5,1},{6,2},{7,3},{8,12},{9,13},{10,... | collective-permute-start | bytes 12296 | tf_op jit(solution)/shard_map/ppermute | solution.py:287
  42.3 0.8 %shard_map.121 = bf16[16,64,128]{2,1,0:T(8,128)(2,1)} custom-call(bf16[128,1024]{1,0:T(8,128)(2,1)S(1)} %get-tuple-element.34.turned_ref), custom_call_target="tpu_custom_call" | custom-call | flops 67108864 | bytes 1048576 | tf_op jit(solution)/shard_map/pallas_call | solution.py:291
  43.1 0.2 collective-permute-done.15
  43.3 1.6 %collective-permute-done.16 = f32[8,128]{1,0:T(8,128)S(1)} collective-permute-done((f32[8,128]{1,0:T(8,128)S(1)}, f32[8,128]{1,0:T(8,128)S(1)}, u32[]{:S(2)}, u32[]{:S(2)}) %collective-permute-start.16) | collective-permute-done | bytes 4128 | tf_op jit(solution)/shard_map/ppermute | solution.py:287
  44.8 0.0 collective-permute-done.17
  44.9 0.5 %slice.3 = f32[1,1]{1,0:T(1,128)} slice(f32[8,128]{1,0:T(8,128)S(1)} %add_add_fusion), slice={[0:1], [0:1]} | slice | bytes 8 | tf_op jit(solution)/shard_map/slice | solution.py:412
  (9 shorter events, 0.0 us)
Async XLA Ops:
  0.6 11.6 %collective-permute-start.1 = (bf16[16,64,128]{2,1,0:T(8,128)(2,1)}, bf16[16,64,128]{2,1,0:T(8,128)(2,1)S(1)}, u32[]{:S(2)}, u32[]{:S(2)}) collective-permute-start(bf16[16,64,128]{2,1,0:T(8,128)(2,1)} %x_ref.3), channel_id=1, source_target_pairs={{0,4},{1,5},{2,6},{3,7},{4,0},{5,1},{6,2},{7,3},{8,12},{9,13},{10,... | collective-permute-start | bytes 786440 | tf_op jit(solution)/shard_map/ppermute | solution.py:287
  3.7 1.0 %copy-start = (bf16[16,64,128]{2,1,0:T(8,128)(2,1)S(1)}, bf16[16,64,128]{2,1,0:T(8,128)(2,1)}, u32[]{:S(2)}) copy-start(bf16[16,64,128]{2,1,0:T(8,128)(2,1)} %x_ref.3) | copy-start | bytes 786436
  4.7 0.8 %copy-start.6 = (bf16[128,128]{1,0:T(8,128)(2,1)S(1)}, bf16[128,128]{1,0:T(8,128)(2,1)}, u32[]{:S(2)}) copy-start(bf16[128,128]{1,0:T(8,128)(2,1)} %rw_ref.1) | copy-start | bytes 98308
  4.7 0.8 %copy-start.7 = (bf16[128,128]{1,0:T(8,128)(2,1)S(1)}, bf16[128,128]{1,0:T(8,128)(2,1)}, u32[]{:S(2)}) copy-start(bf16[128,128]{1,0:T(8,128)(2,1)} %rg_ref.1) | copy-start | bytes 98308
  5.5 3.2 %copy-start.4 = (bf16[128,128]{1,0:T(8,128)(2,1)S(1)}, bf16[128,128]{1,0:T(8,128)(2,1)}, u32[]{:S(2)}) copy-start(bf16[128,128]{1,0:T(8,128)(2,1)} %lw_ref.1) | copy-start | bytes 98308
  5.5 3.2 %copy-start.5 = (bf16[128,128]{1,0:T(8,128)(2,1)S(1)}, bf16[128,128]{1,0:T(8,128)(2,1)}, u32[]{:S(2)}) copy-start(bf16[128,128]{1,0:T(8,128)(2,1)} %lg_ref.1) | copy-start | bytes 98308
  6.0 2.7 %copy-start.8 = (s32[5]{0:T(128)S(1)}, s32[5]{0:T(128)}, u32[]{:S(2)}) copy-start(s32[5]{0:T(128)} %lens_ref.1) | copy-start | bytes 64
  6.1 13.0 %collective-permute-start.3 = (bf16[512,128]{1,0:T(8,128)(2,1)S(1)}, bf16[512,128]{1,0:T(8,128)(2,1)S(1)}, u32[]{:S(2)}, u32[]{:S(2)}) collective-permute-start(bf16[512,128]{1,0:T(8,128)(2,1)S(1)} %get-tuple-element.19.stay_ref), channel_id=1, source_target_pairs={{0,8},{1,9},{2,10},{3,11},{4,12},{5,13},{6,14},{7,15},{8,0},{9,1},... | collective-permute-start | bytes 393224 | tf_op jit(solution)/shard_map/ppermute | solution.py:287
  8.7 10.3 %collective-permute-start.4 = (bf16[512,128]{1,0:T(8,128)(2,1)S(1)}, bf16[512,128]{1,0:T(8,128)(2,1)S(1)}, u32[]{:S(2)}, u32[]{:S(2)}) collective-permute-start(bf16[512,128]{1,0:T(8,128)(2,1)S(1)} %get-tuple-element.29), channel_id=1, source_target_pairs={{0,12},{1,13},{2,14},{3,15},{4,8},{5,9},{6,10},{7,11},{8,4},{9,5},... | collective-permute-start | bytes 393224 | tf_op jit(solution)/shard_map/ppermute | solution.py:287
  13.3 5.8 %collective-permute-start.2 = (bf16[512,128]{1,0:T(8,128)(2,1)S(1)}, bf16[512,128]{1,0:T(8,128)(2,1)S(1)}, u32[]{:S(2)}, u32[]{:S(2)}) collective-permute-start(bf16[512,128]{1,0:T(8,128)(2,1)S(1)} %get-tuple-element.28), channel_id=1, source_target_pairs={{0,2},{1,3},{2,0},{3,1},{4,6},{5,7},{6,4},{7,5},{8,10},{9,11},{10,... | collective-permute-start | bytes 393224 | tf_op jit(solution)/shard_map/ppermute | solution.py:287
  13.3 5.8 %collective-permute-start = (bf16[512,128]{1,0:T(8,128)(2,1)S(1)}, bf16[512,128]{1,0:T(8,128)(2,1)S(1)}, u32[]{:S(2)}, u32[]{:S(2)}) collective-permute-start(bf16[512,128]{1,0:T(8,128)(2,1)S(1)} %get-tuple-element.26), channel_id=1, source_target_pairs={{0,2},{1,3},{2,0},{3,1},{4,6},{5,7},{6,4},{7,5},{8,10},{9,11},{10,... | collective-permute-start | bytes 393224 | tf_op jit(solution)/shard_map/ppermute | solution.py:287
  19.1 1.4 %collective-permute-start.5 = (bf16[512,128]{1,0:T(8,128)(2,1)S(1)}, bf16[512,128]{1,0:T(8,128)(2,1)S(1)}, u32[]{:S(2)}, u32[]{:S(2)}) collective-permute-start(bf16[512,128]{1,0:T(8,128)(2,1)S(1)} %shard_map.118), channel_id=1, source_target_pairs={{0,2},{1,3},{2,0},{3,1},{4,6},{5,7},{6,4},{7,5},{8,10},{9,11},{10,... | collective-permute-start | bytes 393224 | tf_op jit(solution)/shard_map/ppermute | solution.py:287
  20.5 10.6 %copy-start.9 = (bf16[128,64]{0,1:T(8,128)(2,1)S(1)}, bf16[128,64]{0,1:T(8,128)(2,1)}, u32[]{:S(2)}) copy-start(bf16[128,64]{0,1:T(8,128)(2,1)} %param.19) | copy-start | bytes 49156
  20.5 10.8 %copy-start.10 = (s32[16,64]{1,0:T(8,128)S(1)}, s32[16,64]{1,0:T(8,128)}, u32[]{:S(2)}) copy-start(s32[16,64]{1,0:T(8,128)} %param.11) | copy-start | bytes 12292
  20.5 10.8 %copy-start.1 = (bf16[16,64,128]{2,1,0:T(8,128)(2,1)S(1)}, bf16[16,64,128]{2,1,0:T(8,128)(2,1)}, u32[]{:S(2)}) copy-start(bf16[16,64,128]{2,1,0:T(8,128)(2,1)} %x_ref.3) | copy-start | bytes 786436
  21.0 6.9 %collective-permute-start.6 = (bf16[512,128]{1,0:T(8,128)(2,1)S(1)}, bf16[512,128]{1,0:T(8,128)(2,1)S(1)}, u32[]{:S(2)}, u32[]{:S(2)}) collective-permute-start(bf16[512,128]{1,0:T(8,128)(2,1)S(1)} %get-tuple-element.31), channel_id=1, source_target_pairs={{0,5},{1,4},{2,7},{3,6},{4,1},{5,0},{6,3},{7,2},{8,13},{9,12},{10,... | collective-permute-start | bytes 393224 | tf_op jit(solution)/shard_map/ppermute | solution.py:287
  24.0 7.3 %copy-start.3 = (bf16[128,128]{1,0:T(8,128)(2,1)S(1)}, bf16[128,128]{1,0:T(8,128)(2,1)}, u32[]{:S(2)}) copy-start(bf16[128,128]{1,0:T(8,128)(2,1)} %ow_ref.1) | copy-start | bytes 98308
  24.0 7.3 %copy-start.2 = (bf16[128,128]{1,0:T(8,128)(2,1)S(1)}, bf16[128,128]{1,0:T(8,128)(2,1)}, u32[]{:S(2)}) copy-start(bf16[128,128]{1,0:T(8,128)(2,1)} %gw_ref.1) | copy-start | bytes 98308
  24.0 6.6 %collective-permute-start.7 = (bf16[512,128]{1,0:T(8,128)(2,1)S(1)}, bf16[512,128]{1,0:T(8,128)(2,1)S(1)}, u32[]{:S(2)}, u32[]{:S(2)}) collective-permute-start(bf16[512,128]{1,0:T(8,128)(2,1)S(1)} %get-tuple-element.32), channel_id=1, source_target_pairs={{0,1},{1,0},{2,3},{3,2},{4,5},{5,4},{6,7},{7,6},{8,9},{9,8},{10,11... | collective-permute-start | bytes 393224 | tf_op jit(solution)/shard_map/ppermute | solution.py:287
  24.5 6.1 %collective-permute-start.8 = (bf16[512,128]{1,0:T(8,128)(2,1)S(1)}, bf16[512,128]{1,0:T(8,128)(2,1)S(1)}, u32[]{:S(2)}, u32[]{:S(2)}) collective-permute-start(bf16[512,128]{1,0:T(8,128)(2,1)S(1)} %get-tuple-element.33), channel_id=1, source_target_pairs={{0,4},{1,5},{2,6},{3,7},{4,0},{5,1},{6,2},{7,3},{8,12},{9,13},{10,... | collective-permute-start | bytes 393224 | tf_op jit(solution)/shard_map/ppermute | solution.py:287
  24.7 7.0 %collective-permute-start.9 = (bf16[512,128]{1,0:T(8,128)(2,1)S(1)}, bf16[512,128]{1,0:T(8,128)(2,1)S(1)}, u32[]{:S(2)}, u32[]{:S(2)}) collective-permute-start(bf16[512,128]{1,0:T(8,128)(2,1)S(1)} %get-tuple-element.30.refs_0_), channel_id=1, source_target_pairs={{0,2},{1,3},{2,0},{3,1},{4,6},{5,7},{6,4},{7,5},{8,10},{9,11},{10,... | collective-permute-start | bytes 393224 | tf_op jit(solution)/shard_map/ppermute | solution.py:287
  27.9 3.8 %collective-permute-start.10 = (bf16[512,128]{1,0:T(8,128)(2,1)S(1)}, bf16[512,128]{1,0:T(8,128)(2,1)S(1)}, u32[]{:S(2)}, u32[]{:S(2)}) collective-permute-start(bf16[512,128]{1,0:T(8,128)(2,1)S(1)} %collective-permute-done.6.refs_1_), channel_id=1, source_target_pairs={{0,2},{1,3},{2,0},{3,1},{4,6},{5,7},{6,4},{7,5},{8,10},{9,11},{10,... | collective-permute-start | bytes 393224 | tf_op jit(solution)/shard_map/ppermute | solution.py:287
  30.6 1.3 %collective-permute-start.11 = (bf16[512,128]{1,0:T(8,128)(2,1)S(1)}, bf16[512,128]{1,0:T(8,128)(2,1)S(1)}, u32[]{:S(2)}, u32[]{:S(2)}) collective-permute-start(bf16[512,128]{1,0:T(8,128)(2,1)S(1)} %collective-permute-done.7.refs_2_), channel_id=1, source_target_pairs={{0,2},{1,3},{2,0},{3,1},{4,6},{5,7},{6,4},{7,5},{8,10},{9,11},{10,... | collective-permute-start | bytes 393224 | tf_op jit(solution)/shard_map/ppermute | solution.py:287
  30.6 1.5 %collective-permute-start.12 = (bf16[512,128]{1,0:T(8,128)(2,1)S(1)}, bf16[512,128]{1,0:T(8,128)(2,1)S(1)}, u32[]{:S(2)}, u32[]{:S(2)}) collective-permute-start(bf16[512,128]{1,0:T(8,128)(2,1)S(1)} %collective-permute-done.8.refs_3_), channel_id=1, source_target_pairs={{0,2},{1,3},{2,0},{3,1},{4,6},{5,7},{6,4},{7,5},{8,10},{9,11},{10,... | collective-permute-start | bytes 393224 | tf_op jit(solution)/shard_map/ppermute | solution.py:287
  33.1 1.2 %collective-permute-start.13 = (f32[8,128]{1,0:T(8,128)S(1)}, f32[8,128]{1,0:T(8,128)S(1)}, u32[]{:S(2)}, u32[]{:S(2)}) collective-permute-start(f32[8,128]{1,0:T(8,128)S(1)} %get-tuple-element.35), channel_id=1, source_target_pairs={{0,2},{1,3},{2,0},{3,1},{4,6},{5,7},{6,4},{7,5},{8,10},{9,11},{10,... | collective-permute-start | bytes 12296 | tf_op jit(solution)/shard_map/ppermute | solution.py:287
  34.3 3.6 %collective-permute-start.14 = (f32[8,128]{1,0:T(8,128)S(1)}, f32[8,128]{1,0:T(8,128)S(1)}, u32[]{:S(2)}, u32[]{:S(2)}) collective-permute-start(f32[8,128]{1,0:T(8,128)S(1)} %add.15), channel_id=1, source_target_pairs={{0,1},{1,0},{2,3},{3,2},{4,5},{5,4},{6,7},{7,6},{8,9},{9,8},{10,11... | collective-permute-start | bytes 12296 | tf_op jit(solution)/shard_map/ppermute | solution.py:287
  37.9 5.4 %collective-permute-start.15 = (f32[8,128]{1,0:T(8,128)S(1)}, f32[8,128]{1,0:T(8,128)S(1)}, u32[]{:S(2)}, u32[]{:S(2)}) collective-permute-start(f32[8,128]{1,0:T(8,128)S(1)} %add.16), channel_id=1, source_target_pairs={{0,12},{1,13},{2,14},{3,15},{4,8},{5,9},{6,10},{7,11},{8,4},{9,5},... | collective-permute-start | bytes 12296 | tf_op jit(solution)/shard_map/ppermute | solution.py:287
  40.3 4.5 %collective-permute-start.16 = (f32[8,128]{1,0:T(8,128)S(1)}, f32[8,128]{1,0:T(8,128)S(1)}, u32[]{:S(2)}, u32[]{:S(2)}) collective-permute-start(f32[8,128]{1,0:T(8,128)S(1)} %add.16), channel_id=1, source_target_pairs={{0,8},{1,9},{2,10},{3,11},{4,12},{5,13},{6,14},{7,15},{8,0},{9,1},... | collective-permute-start | bytes 12296 | tf_op jit(solution)/shard_map/ppermute | solution.py:287
  40.9 3.9 %collective-permute-start.17 = (f32[8,128]{1,0:T(8,128)S(1)}, f32[8,128]{1,0:T(8,128)S(1)}, u32[]{:S(2)}, u32[]{:S(2)}) collective-permute-start(f32[8,128]{1,0:T(8,128)S(1)} %add.16), channel_id=1, source_target_pairs={{0,4},{1,5},{2,6},{3,7},{4,0},{5,1},{6,2},{7,3},{8,12},{9,13},{10,... | collective-permute-start | bytes 12296 | tf_op jit(solution)/shard_map/ppermute | solution.py:287

commit v16 on v15

--- a/solution.py
+++ b/solution.py
@@ -7,7 +7,7 @@
 
 AXES = ("row", "col")
 OWNERS = 4
-DIAGONAL_FIRST = (0, 3, 1, 2)
+DIAGONAL_FIRST = (0, 3, 2, 1)
 VMEM = pl.BlockSpec(memory_space=pltpu.VMEM)
 SMEM = pl.BlockSpec(memory_space=pltpu.SMEM)
 PARAMS = pltpu.CompilerParams(vmem_limit_bytes=24 * 1024 * 1024)

time: 45.6 us -> 45.4 us (level)
  transfers between devices with their start and end apart: 18 -> 18, of which waited for: 11 -> 12; matrix products, arithmetic and copies ran while one was open for 0% -> 0% of each run, Pallas kernels for 9% -> 9%
where the time goes in v16:
time: 45.4 us; the launch traced here: 45.2 us
  waiting for transfers between devices  20.4 us (45%)
  starting transfers between devices  16.2 us (36%)
  Pallas kernels  5.69 us (13%)
  local copies, waits for them, and re-layouts  2.13 us (5%)
  between operations  0.78 us (2%)
    ppermute x18, waiting for transfers between devices, exchange(): return lax.ppermute(value, AXES, [(at, at ^ mask) for at in range(places)])  20.4 us
    ppermute x18, starting transfers between devices, exchange(): return lax.ppermute(value, AXES, [(at, at ^ mask) for at in range(places)])  16.2 us
    pallas_call x9, Pallas kernels, call(): pl.pallas_call(kernel, out_shape=outs, in_specs=specs if specs is not Non...  5.69 us
    unnamed x23, local copies, waits for them, and re-layouts  1.54 us
  transfers between devices with their start and end apart: 18, of which 12 were waited for; matrix products, arithmetic and copies ran while one was open for 0% of the time, Pallas kernels for 9%

profile of v16, /device:TPU:0, one launch (start us, length us, event | category | flops | bytes accessed | tf_op | source)
XLA Modules:
  0.0 45.2 jit_solution(1849289832524651590)
XLA Ops:
  0.6 3.1 %collective-permute-start.1 = (bf16[16,64,128]{2,1,0:T(8,128)(2,1)}, bf16[16,64,128]{2,1,0:T(8,128)(2,1)S(1)}, u32[]{:S(2)}, u32[]{:S(2)}) collective-permute-start(bf16[16,64,128]{2,1,0:T(8,128)(2,1)} %x_ref.3), channel_id=1, source_target_pairs={{0,4},{1,5},{2,6},{3,7},{4,0},{5,1},{6,2},{7,3},{8,12},{9,13},{10,... | collective-permute-start | bytes 786440 | tf_op jit(solution)/shard_map/ppermute | solution.py:287
  3.7 0.0 copy-start
  3.7 1.0 %copy-done = bf16[16,64,128]{2,1,0:T(8,128)(2,1)S(1)} copy-done((bf16[16,64,128]{2,1,0:T(8,128)(2,1)S(1)}, bf16[16,64,128]{2,1,0:T(8,128)(2,1)}, u32[]{:S(2)}) %copy-start) | copy-done | bytes 262168
  4.7 0.0 copy-start.6
  4.7 0.0 copy-start.7
  4.7 0.4 shard_map.113.normed_ref
  5.1 0.4 copy-done.6
  5.5 0.0 copy-done.7
  5.5 0.0 copy-start.4
  5.5 0.0 copy-start.5
  5.5 0.6 %shard_map.114 = (bf16[512,128]{1,0:T(8,128)(2,1)S(1)}, bf16[512,128]{1,0:T(8,128)(2,1)S(1)}) custom-call(bf16[1024,128]{1,0:T(8,128)(2,1)S(1)} %shard_map.113.normed_ref, bf16[128,128]{1,0:T(8,128)(2,1)S(1)} %copy-done.6, bf16[128,128]{1,0:T(8,128)(2,1)S(1)} %copy-done.7), custom_call_target="tpu_custom_call" | custom-call | flops 67108864 | bytes 1048576 | tf_op jit(solution)/shard_map/pallas_call | solution.py:291
  6.0 0.0 copy-start.8
  6.1 2.7 %collective-permute-start.3 = (bf16[512,128]{1,0:T(8,128)(2,1)S(1)}, bf16[512,128]{1,0:T(8,128)(2,1)S(1)}, u32[]{:S(2)}, u32[]{:S(2)}) collective-permute-start(bf16[512,128]{1,0:T(8,128)(2,1)S(1)} %get-tuple-element.19.stay_ref), channel_id=1, source_target_pairs={{0,8},{1,9},{2,10},{3,11},{4,12},{5,13},{6,14},{7,15},{8,0},{9,1},... | collective-permute-start | bytes 393224 | tf_op jit(solution)/shard_map/ppermute | solution.py:287
  8.7 0.0 collective-permute-start.4
  8.7 0.0 copy-done.4
  8.7 0.0 copy-done.5
  8.7 0.0 copy-done.8
  8.7 1.0 %shard_map.115 = (bf16[512,128]{1,0:T(8,128)(2,1)S(1)}, bf16[512,128]{1,0:T(8,128)(2,1)S(1)}, f32[24,128]{1,0:T(8,128)S(1)}) custom-call(s32[5]{0:T(128)S(1)} %copy-done.8, bf16[1024,128]{1,0:T(8,128)(2,1)S(1)} %shard_map.113.normed_ref, bf16[128,128]{1,0:T(8,128)(2,1)S(1)} %copy-done.4, bf16[128,128]{1,0:T(8,128)(2,1)S(1)} %copy-done.5, ...), custom_call_target="tpu_custom_call" | custom-call | flops 33554432 | bytes 1048576 | tf_op jit(solution)/shard_map/pallas_call | solution.py:291
  9.8 2.4 %collective-permute-done.1.x_ref = bf16[16,64,128]{2,1,0:T(8,128)(2,1)S(1)} collective-permute-done((bf16[16,64,128]{2,1,0:T(8,128)(2,1)}, bf16[16,64,128]{2,1,0:T(8,128)(2,1)S(1)}, u32[]{:S(2)}, u32[]{:S(2)}) %collective-permute-start.1) | collective-permute-done | bytes 262176 | tf_op jit(solution)/shard_map/ppermute | solution.py:287
  12.2 1.1 %shard_map.117 = (bf16[512,128]{1,0:T(8,128)(2,1)S(1)}, bf16[512,128]{1,0:T(8,128)(2,1)S(1)}) custom-call(f32[24,128]{1,0:T(8,128)S(1)} %get-tuple-element.20.masks_ref, bf16[16,64,128]{2,1,0:T(8,128)(2,1)S(1)} %collective-permute-done.1.x_ref, bf16[128,128]{1,0:T(8,128)(2,1)S(1)} %copy-done.4, bf16[128,128]{1,0:T(8,128)(2,1)S(1)} %copy-done.5, ...), custom_call_target="tpu_custom_call" | custom-call | flops 67108864 | bytes 1048576 | tf_op jit(solution)/shard_map/pallas_call | solution.py:291
  13.3 0.1 collective-permute-start.2
  13.3 0.5 %collective-permute-start = (bf16[512,128]{1,0:T(8,128)(2,1)S(1)}, bf16[512,128]{1,0:T(8,128)(2,1)S(1)}, u32[]{:S(2)}, u32[]{:S(2)}) collective-permute-start(bf16[512,128]{1,0:T(8,128)(2,1)S(1)} %get-tuple-element.26), channel_id=1, source_target_pairs={{0,2},{1,3},{2,0},{3,1},{4,6},{5,7},{6,4},{7,5},{8,10},{9,11},{10,... | collective-permute-start | bytes 393224 | tf_op jit(solution)/shard_map/ppermute | solution.py:287
  13.8 5.2 %collective-permute-done.3.far_ref.far = bf16[512,128]{1,0:T(8,128)(2,1)S(1)} collective-permute-done((bf16[512,128]{1,0:T(8,128)(2,1)S(1)}, bf16[512,128]{1,0:T(8,128)(2,1)S(1)}, u32[]{:S(2)}, u32[]{:S(2)}) %collective-permute-start.3) | collective-permute-done | bytes 131104 | tf_op jit(solution)/shard_map/ppermute | solution.py:287
  19.1 0.0 collective-permute-done.4.cross_ref.cross
  19.1 0.0 collective-permute-done.2.ready_ref.near_over
  19.1 0.1 collective-permute-start.5
  19.2 0.0 collective-permute-done.core
  19.2 1.3 %collective-permute-done.5.both_over = bf16[512,128]{1,0:T(8,128)(2,1)S(1)} collective-permute-done((bf16[512,128]{1,0:T(8,128)(2,1)S(1)}, bf16[512,128]{1,0:T(8,128)(2,1)S(1)}, u32[]{:S(2)}, u32[]{:S(2)}) %collective-permute-start.5) | collective-permute-done | bytes 131104 | tf_op jit(solution)/shard_map/ppermute | solution.py:287
  20.5 0.5 %shard_map.119 = (bf16[512,128]{1,0:T(8,128)(2,1)S(1)}, bf16[512,128]{1,0:T(8,128)(2,1)S(1)}, bf16[512,128]{1,0:T(8,128)(2,1)S(1)}, bf16[512,128]{1,0:T(8,128)(2,1)S(1)}) custom-call(f32[24,128]{1,0:T(8,128)S(1)} %get-tuple-element.20.masks_ref, bf16[512,128]{1,0:T(8,128)(2,1)S(1)} %get-tuple-element.25.own, bf16[512,128]{1,0:T(8,128)(2,1)S(1)} %collective-permute-done.core, ...), custom_call_target="tpu_custom_call" | custom-call | flops 16777216 | bytes 1048576 | tf_op jit(solution)/shard_map/pallas_call | solution.py:291
  21.0 3.0 %collective-permute-start.6 = (bf16[512,128]{1,0:T(8,128)(2,1)S(1)}, bf16[512,128]{1,0:T(8,128)(2,1)S(1)}, u32[]{:S(2)}, u32[]{:S(2)}) collective-permute-start(bf16[512,128]{1,0:T(8,128)(2,1)S(1)} %get-tuple-element.31), channel_id=1, source_target_pairs={{0,5},{1,4},{2,7},{3,6},{4,1},{5,0},{6,3},{7,2},{8,13},{9,12},{10,... | collective-permute-start | bytes 393224 | tf_op jit(solution)/shard_map/ppermute | solution.py:287
  24.0 0.1 collective-permute-start.7
  24.1 0.6 %collective-permute-start.8 = (bf16[512,128]{1,0:T(8,128)(2,1)S(1)}, bf16[512,128]{1,0:T(8,128)(2,1)S(1)}, u32[]{:S(2)}, u32[]{:S(2)}) collective-permute-start(bf16[512,128]{1,0:T(8,128)(2,1)S(1)} %get-tuple-element.33), channel_id=1, source_target_pairs={{0,1},{1,0},{2,3},{3,2},{4,5},{5,4},{6,7},{7,6},{8,9},{9,8},{10,11... | collective-permute-start | bytes 393224 | tf_op jit(solution)/shard_map/ppermute | solution.py:287
  24.7 0.0 collective-permute-start.9
  24.7 3.6 %collective-permute-done.6.refs_1_ = bf16[512,128]{1,0:T(8,128)(2,1)S(1)} collective-permute-done((bf16[512,128]{1,0:T(8,128)(2,1)S(1)}, bf16[512,128]{1,0:T(8,128)(2,1)S(1)}, u32[]{:S(2)}, u32[]{:S(2)}) %collective-permute-start.6) | collective-permute-done | bytes 131104 | tf_op jit(solution)/shard_map/ppermute | solution.py:287
  28.3 0.0 collective-permute-start.10
  28.3 2.1 %collective-permute-done.7.refs_2_ = bf16[512,128]{1,0:T(8,128)(2,1)S(1)} collective-permute-done((bf16[512,128]{1,0:T(8,128)(2,1)S(1)}, bf16[512,128]{1,0:T(8,128)(2,1)S(1)}, u32[]{:S(2)}, u32[]{:S(2)}) %collective-permute-start.7) | collective-permute-done | bytes 131104 | tf_op jit(solution)/shard_map/ppermute | solution.py:287
  30.4 0.0 collective-permute-start.11
  30.4 0.2 collective-permute-done.8.refs_3_
  30.6 0.3 collective-permute-start.12
  30.9 0.0 copy-done.9
  30.9 0.1 copy.12.dw_ref
  31.0 0.0 copy-done.10
  31.0 0.1 reshape.7.bins_ref
  31.1 0.0 copy-done.1
  31.1 0.0 copy-done.3
  31.1 0.0 copy-done.2
  31.1 0.4 shard_map.116
  31.5 0.0 collective-permute-done.9.refs_4_
  31.5 0.0 collective-permute-done.10.refs_5_
  31.5 0.2 collective-permute-done.11.refs_6_
  31.7 0.2 collective-permute-done.12.refs_7_
  32.0 0.9 %shard_map.120 = (bf16[128,1024]{1,0:T(8,128)(2,1)S(1)}, f32[8,128]{1,0:T(8,128)S(1)}) custom-call(f32[24,128]{1,0:T(8,128)S(1)} %get-tuple-element.20.masks_ref, f32[128,1024]{1,0:T(8,128)S(1)} %get-tuple-element.21.x_ref, f32[128,1024]{1,0:T(8,128)S(1)} %get-tuple-element.22.gate_ref, s32[8,128]{1,0:T(8,128)S(1)} %reshape.7.bins_ref, ...), custom_call_target="tpu_custom_call" | custom-call | flops 100663296 | bytes 1048576 | tf_op jit(solution)/shard_map/pallas_call | solution.py:291
  32.9 0.3 collective-permute-start.13
  33.2 0.9 %collective-permute-done.13 = f32[8,128]{1,0:T(8,128)S(1)} collective-permute-done((f32[8,128]{1,0:T(8,128)S(1)}, f32[8,128]{1,0:T(8,128)S(1)}, u32[]{:S(2)}, u32[]{:S(2)}) %collective-permute-start.13) | collective-permute-done | bytes 4128 | tf_op jit(solution)/shard_map/ppermute | solution.py:287
  34.1 1.2 %collective-permute-start.14 = (f32[8,128]{1,0:T(8,128)S(1)}, f32[8,128]{1,0:T(8,128)S(1)}, u32[]{:S(2)}, u32[]{:S(2)}) collective-permute-start(f32[8,128]{1,0:T(8,128)S(1)} %add.15), channel_id=1, source_target_pairs={{0,1},{1,0},{2,3},{3,2},{4,5},{5,4},{6,7},{7,6},{8,9},{9,8},{10,11... | collective-permute-start | bytes 12296 | tf_op jit(solution)/shard_map/ppermute | solution.py:287
  35.3 2.4 %collective-permute-done.14 = f32[8,128]{1,0:T(8,128)S(1)} collective-permute-done((f32[8,128]{1,0:T(8,128)S(1)}, f32[8,128]{1,0:T(8,128)S(1)}, u32[]{:S(2)}, u32[]{:S(2)}) %collective-permute-start.14) | collective-permute-done | bytes 4128 | tf_op jit(solution)/shard_map/ppermute | solution.py:287
  37.7 2.5 %collective-permute-start.15 = (f32[8,128]{1,0:T(8,128)S(1)}, f32[8,128]{1,0:T(8,128)S(1)}, u32[]{:S(2)}, u32[]{:S(2)}) collective-permute-start(f32[8,128]{1,0:T(8,128)S(1)} %add.16), channel_id=1, source_target_pairs={{0,12},{1,13},{2,14},{3,15},{4,8},{5,9},{6,10},{7,11},{8,4},{9,5},... | collective-permute-start | bytes 12296 | tf_op jit(solution)/shard_map/ppermute | solution.py:287
  40.2 0.9 %collective-permute-start.16 = (f32[8,128]{1,0:T(8,128)S(1)}, f32[8,128]{1,0:T(8,128)S(1)}, u32[]{:S(2)}, u32[]{:S(2)}) collective-permute-start(f32[8,128]{1,0:T(8,128)S(1)} %add.16), channel_id=1, source_target_pairs={{0,8},{1,9},{2,10},{3,11},{4,12},{5,13},{6,14},{7,15},{8,0},{9,1},... | collective-permute-start | bytes 12296 | tf_op jit(solution)/shard_map/ppermute | solution.py:287
  41.1 1.0 %collective-permute-start.17 = (f32[8,128]{1,0:T(8,128)S(1)}, f32[8,128]{1,0:T(8,128)S(1)}, u32[]{:S(2)}, u32[]{:S(2)}) collective-permute-start(f32[8,128]{1,0:T(8,128)S(1)} %add.16), channel_id=1, source_target_pairs={{0,4},{1,5},{2,6},{3,7},{4,0},{5,1},{6,2},{7,3},{8,12},{9,13},{10,... | collective-permute-start | bytes 12296 | tf_op jit(solution)/shard_map/ppermute | solution.py:287
  42.1 0.8 %shard_map.121 = bf16[16,64,128]{2,1,0:T(8,128)(2,1)} custom-call(bf16[128,1024]{1,0:T(8,128)(2,1)S(1)} %get-tuple-element.34.turned_ref), custom_call_target="tpu_custom_call" | custom-call | flops 67108864 | bytes 1048576 | tf_op jit(solution)/shard_map/pallas_call | solution.py:291
  42.9 0.2 collective-permute-done.15
  43.1 1.6 %collective-permute-done.16 = f32[8,128]{1,0:T(8,128)S(1)} collective-permute-done((f32[8,128]{1,0:T(8,128)S(1)}, f32[8,128]{1,0:T(8,128)S(1)}, u32[]{:S(2)}, u32[]{:S(2)}) %collective-permute-start.16) | collective-permute-done | bytes 4128 | tf_op jit(solution)/shard_map/ppermute | solution.py:287
  44.7 0.0 collective-permute-done.17
  44.7 0.5 %slice.3 = f32[1,1]{1,0:T(1,128)} slice(f32[8,128]{1,0:T(8,128)S(1)} %add_add_fusion), slice={[0:1], [0:1]} | slice | bytes 8 | tf_op jit(solution)/shard_map/slice | solution.py:412
  (9 shorter events, 0.0 us)
Async XLA Ops:
  0.6 11.6 %collective-permute-start.1 = (bf16[16,64,128]{2,1,0:T(8,128)(2,1)}, bf16[16,64,128]{2,1,0:T(8,128)(2,1)S(1)}, u32[]{:S(2)}, u32[]{:S(2)}) collective-permute-start(bf16[16,64,128]{2,1,0:T(8,128)(2,1)} %x_ref.3), channel_id=1, source_target_pairs={{0,4},{1,5},{2,6},{3,7},{4,0},{5,1},{6,2},{7,3},{8,12},{9,13},{10,... | collective-permute-start | bytes 786440 | tf_op jit(solution)/shard_map/ppermute | solution.py:287
  3.7 1.0 %copy-start = (bf16[16,64,128]{2,1,0:T(8,128)(2,1)S(1)}, bf16[16,64,128]{2,1,0:T(8,128)(2,1)}, u32[]{:S(2)}) copy-start(bf16[16,64,128]{2,1,0:T(8,128)(2,1)} %x_ref.3) | copy-start | bytes 786436
  4.7 0.8 %copy-start.6 = (bf16[128,128]{1,0:T(8,128)(2,1)S(1)}, bf16[128,128]{1,0:T(8,128)(2,1)}, u32[]{:S(2)}) copy-start(bf16[128,128]{1,0:T(8,128)(2,1)} %rw_ref.1) | copy-start | bytes 98308
  4.7 0.8 %copy-start.7 = (bf16[128,128]{1,0:T(8,128)(2,1)S(1)}, bf16[128,128]{1,0:T(8,128)(2,1)}, u32[]{:S(2)}) copy-start(bf16[128,128]{1,0:T(8,128)(2,1)} %rg_ref.1) | copy-start | bytes 98308
  5.5 3.2 %copy-start.4 = (bf16[128,128]{1,0:T(8,128)(2,1)S(1)}, bf16[128,128]{1,0:T(8,128)(2,1)}, u32[]{:S(2)}) copy-start(bf16[128,128]{1,0:T(8,128)(2,1)} %lw_ref.1) | copy-start | bytes 98308
  5.5 3.2 %copy-start.5 = (bf16[128,128]{1,0:T(8,128)(2,1)S(1)}, bf16[128,128]{1,0:T(8,128)(2,1)}, u32[]{:S(2)}) copy-start(bf16[128,128]{1,0:T(8,128)(2,1)} %lg_ref.1) | copy-start | bytes 98308
  6.0 2.7 %copy-start.8 = (s32[5]{0:T(128)S(1)}, s32[5]{0:T(128)}, u32[]{:S(2)}) copy-start(s32[5]{0:T(128)} %lens_ref.1) | copy-start | bytes 64
  6.1 13.0 %collective-permute-start.3 = (bf16[512,128]{1,0:T(8,128)(2,1)S(1)}, bf16[512,128]{1,0:T(8,128)(2,1)S(1)}, u32[]{:S(2)}, u32[]{:S(2)}) collective-permute-start(bf16[512,128]{1,0:T(8,128)(2,1)S(1)} %get-tuple-element.19.stay_ref), channel_id=1, source_target_pairs={{0,8},{1,9},{2,10},{3,11},{4,12},{5,13},{6,14},{7,15},{8,0},{9,1},... | collective-permute-start | bytes 393224 | tf_op jit(solution)/shard_map/ppermute | solution.py:287
  8.7 10.3 %collective-permute-start.4 = (bf16[512,128]{1,0:T(8,128)(2,1)S(1)}, bf16[512,128]{1,0:T(8,128)(2,1)S(1)}, u32[]{:S(2)}, u32[]{:S(2)}) collective-permute-start(bf16[512,128]{1,0:T(8,128)(2,1)S(1)} %get-tuple-element.29), channel_id=1, source_target_pairs={{0,12},{1,13},{2,14},{3,15},{4,8},{5,9},{6,10},{7,11},{8,4},{9,5},... | collective-permute-start | bytes 393224 | tf_op jit(solution)/shard_map/ppermute | solution.py:287
  13.3 5.8 %collective-permute-start.2 = (bf16[512,128]{1,0:T(8,128)(2,1)S(1)}, bf16[512,128]{1,0:T(8,128)(2,1)S(1)}, u32[]{:S(2)}, u32[]{:S(2)}) collective-permute-start(bf16[512,128]{1,0:T(8,128)(2,1)S(1)} %get-tuple-element.28), channel_id=1, source_target_pairs={{0,2},{1,3},{2,0},{3,1},{4,6},{5,7},{6,4},{7,5},{8,10},{9,11},{10,... | collective-permute-start | bytes 393224 | tf_op jit(solution)/shard_map/ppermute | solution.py:287
  13.3 5.8 %collective-permute-start = (bf16[512,128]{1,0:T(8,128)(2,1)S(1)}, bf16[512,128]{1,0:T(8,128)(2,1)S(1)}, u32[]{:S(2)}, u32[]{:S(2)}) collective-permute-start(bf16[512,128]{1,0:T(8,128)(2,1)S(1)} %get-tuple-element.26), channel_id=1, source_target_pairs={{0,2},{1,3},{2,0},{3,1},{4,6},{5,7},{6,4},{7,5},{8,10},{9,11},{10,... | collective-permute-start | bytes 393224 | tf_op jit(solution)/shard_map/ppermute | solution.py:287
  19.1 1.4 %collective-permute-start.5 = (bf16[512,128]{1,0:T(8,128)(2,1)S(1)}, bf16[512,128]{1,0:T(8,128)(2,1)S(1)}, u32[]{:S(2)}, u32[]{:S(2)}) collective-permute-start(bf16[512,128]{1,0:T(8,128)(2,1)S(1)} %shard_map.118), channel_id=1, source_target_pairs={{0,2},{1,3},{2,0},{3,1},{4,6},{5,7},{6,4},{7,5},{8,10},{9,11},{10,... | collective-permute-start | bytes 393224 | tf_op jit(solution)/shard_map/ppermute | solution.py:287
  20.5 10.4 %copy-start.9 = (bf16[128,64]{0,1:T(8,128)(2,1)S(1)}, bf16[128,64]{0,1:T(8,128)(2,1)}, u32[]{:S(2)}) copy-start(bf16[128,64]{0,1:T(8,128)(2,1)} %param.19) | copy-start | bytes 49156
  20.5 10.5 %copy-start.10 = (s32[16,64]{1,0:T(8,128)S(1)}, s32[16,64]{1,0:T(8,128)}, u32[]{:S(2)}) copy-start(s32[16,64]{1,0:T(8,128)} %param.11) | copy-start | bytes 12292
  20.5 10.6 %copy-start.1 = (bf16[16,64,128]{2,1,0:T(8,128)(2,1)S(1)}, bf16[16,64,128]{2,1,0:T(8,128)(2,1)}, u32[]{:S(2)}) copy-start(bf16[16,64,128]{2,1,0:T(8,128)(2,1)} %x_ref.3) | copy-start | bytes 786436
  21.0 7.3 %collective-permute-start.6 = (bf16[512,128]{1,0:T(8,128)(2,1)S(1)}, bf16[512,128]{1,0:T(8,128)(2,1)S(1)}, u32[]{:S(2)}, u32[]{:S(2)}) collective-permute-start(bf16[512,128]{1,0:T(8,128)(2,1)S(1)} %get-tuple-element.31), channel_id=1, source_target_pairs={{0,5},{1,4},{2,7},{3,6},{4,1},{5,0},{6,3},{7,2},{8,13},{9,12},{10,... | collective-permute-start | bytes 393224 | tf_op jit(solution)/shard_map/ppermute | solution.py:287
  24.0 7.1 %copy-start.3 = (bf16[128,128]{1,0:T(8,128)(2,1)S(1)}, bf16[128,128]{1,0:T(8,128)(2,1)}, u32[]{:S(2)}) copy-start(bf16[128,128]{1,0:T(8,128)(2,1)} %ow_ref.1) | copy-start | bytes 98308
  24.0 7.1 %copy-start.2 = (bf16[128,128]{1,0:T(8,128)(2,1)S(1)}, bf16[128,128]{1,0:T(8,128)(2,1)}, u32[]{:S(2)}) copy-start(bf16[128,128]{1,0:T(8,128)(2,1)} %gw_ref.1) | copy-start | bytes 98308
  24.0 6.4 %collective-permute-start.7 = (bf16[512,128]{1,0:T(8,128)(2,1)S(1)}, bf16[512,128]{1,0:T(8,128)(2,1)S(1)}, u32[]{:S(2)}, u32[]{:S(2)}) collective-permute-start(bf16[512,128]{1,0:T(8,128)(2,1)S(1)} %get-tuple-element.32), channel_id=1, source_target_pairs={{0,4},{1,5},{2,6},{3,7},{4,0},{5,1},{6,2},{7,3},{8,12},{9,13},{10,... | collective-permute-start | bytes 393224 | tf_op jit(solution)/shard_map/ppermute | solution.py:287
  24.1 6.6 %collective-permute-start.8 = (bf16[512,128]{1,0:T(8,128)(2,1)S(1)}, bf16[512,128]{1,0:T(8,128)(2,1)S(1)}, u32[]{:S(2)}, u32[]{:S(2)}) collective-permute-start(bf16[512,128]{1,0:T(8,128)(2,1)S(1)} %get-tuple-element.33), channel_id=1, source_target_pairs={{0,1},{1,0},{2,3},{3,2},{4,5},{5,4},{6,7},{7,6},{8,9},{9,8},{10,11... | collective-permute-start | bytes 393224 | tf_op jit(solution)/shard_map/ppermute | solution.py:287
  24.7 6.8 %collective-permute-start.9 = (bf16[512,128]{1,0:T(8,128)(2,1)S(1)}, bf16[512,128]{1,0:T(8,128)(2,1)S(1)}, u32[]{:S(2)}, u32[]{:S(2)}) collective-permute-start(bf16[512,128]{1,0:T(8,128)(2,1)S(1)} %get-tuple-element.30.refs_0_), channel_id=1, source_target_pairs={{0,2},{1,3},{2,0},{3,1},{4,6},{5,7},{6,4},{7,5},{8,10},{9,11},{10,... | collective-permute-start | bytes 393224 | tf_op jit(solution)/shard_map/ppermute | solution.py:287
  28.3 3.2 %collective-permute-start.10 = (bf16[512,128]{1,0:T(8,128)(2,1)S(1)}, bf16[512,128]{1,0:T(8,128)(2,1)S(1)}, u32[]{:S(2)}, u32[]{:S(2)}) collective-permute-start(bf16[512,128]{1,0:T(8,128)(2,1)S(1)} %collective-permute-done.6.refs_1_), channel_id=1, source_target_pairs={{0,2},{1,3},{2,0},{3,1},{4,6},{5,7},{6,4},{7,5},{8,10},{9,11},{10,... | collective-permute-start | bytes 393224 | tf_op jit(solution)/shard_map/ppermute | solution.py:287
  30.4 1.3 %collective-permute-start.11 = (bf16[512,128]{1,0:T(8,128)(2,1)S(1)}, bf16[512,128]{1,0:T(8,128)(2,1)S(1)}, u32[]{:S(2)}, u32[]{:S(2)}) collective-permute-start(bf16[512,128]{1,0:T(8,128)(2,1)S(1)} %collective-permute-done.7.refs_2_), channel_id=1, source_target_pairs={{0,2},{1,3},{2,0},{3,1},{4,6},{5,7},{6,4},{7,5},{8,10},{9,11},{10,... | collective-permute-start | bytes 393224 | tf_op jit(solution)/shard_map/ppermute | solution.py:287
  30.6 1.3 %collective-permute-start.12 = (bf16[512,128]{1,0:T(8,128)(2,1)S(1)}, bf16[512,128]{1,0:T(8,128)(2,1)S(1)}, u32[]{:S(2)}, u32[]{:S(2)}) collective-permute-start(bf16[512,128]{1,0:T(8,128)(2,1)S(1)} %collective-permute-done.8.refs_3_), channel_id=1, source_target_pairs={{0,2},{1,3},{2,0},{3,1},{4,6},{5,7},{6,4},{7,5},{8,10},{9,11},{10,... | collective-permute-start | bytes 393224 | tf_op jit(solution)/shard_map/ppermute | solution.py:287
  32.9 1.2 %collective-permute-start.13 = (f32[8,128]{1,0:T(8,128)S(1)}, f32[8,128]{1,0:T(8,128)S(1)}, u32[]{:S(2)}, u32[]{:S(2)}) collective-permute-start(f32[8,128]{1,0:T(8,128)S(1)} %get-tuple-element.35), channel_id=1, source_target_pairs={{0,2},{1,3},{2,0},{3,1},{4,6},{5,7},{6,4},{7,5},{8,10},{9,11},{10,... | collective-permute-start | bytes 12296 | tf_op jit(solution)/shard_map/ppermute | solution.py:287
  34.1 3.6 %collective-permute-start.14 = (f32[8,128]{1,0:T(8,128)S(1)}, f32[8,128]{1,0:T(8,128)S(1)}, u32[]{:S(2)}, u32[]{:S(2)}) collective-permute-start(f32[8,128]{1,0:T(8,128)S(1)} %add.15), channel_id=1, source_target_pairs={{0,1},{1,0},{2,3},{3,2},{4,5},{5,4},{6,7},{7,6},{8,9},{9,8},{10,11... | collective-permute-start | bytes 12296 | tf_op jit(solution)/shard_map/ppermute | solution.py:287
  37.7 5.4 %collective-permute-start.15 = (f32[8,128]{1,0:T(8,128)S(1)}, f32[8,128]{1,0:T(8,128)S(1)}, u32[]{:S(2)}, u32[]{:S(2)}) collective-permute-start(f32[8,128]{1,0:T(8,128)S(1)} %add.16), channel_id=1, source_target_pairs={{0,12},{1,13},{2,14},{3,15},{4,8},{5,9},{6,10},{7,11},{8,4},{9,5},... | collective-permute-start | bytes 12296 | tf_op jit(solution)/shard_map/ppermute | solution.py:287
  40.2 4.5 %collective-permute-start.16 = (f32[8,128]{1,0:T(8,128)S(1)}, f32[8,128]{1,0:T(8,128)S(1)}, u32[]{:S(2)}, u32[]{:S(2)}) collective-permute-start(f32[8,128]{1,0:T(8,128)S(1)} %add.16), channel_id=1, source_target_pairs={{0,8},{1,9},{2,10},{3,11},{4,12},{5,13},{6,14},{7,15},{8,0},{9,1},... | collective-permute-start | bytes 12296 | tf_op jit(solution)/shard_map/ppermute | solution.py:287
  41.1 3.6 %collective-permute-start.17 = (f32[8,128]{1,0:T(8,128)S(1)}, f32[8,128]{1,0:T(8,128)S(1)}, u32[]{:S(2)}, u32[]{:S(2)}) collective-permute-start(f32[8,128]{1,0:T(8,128)S(1)} %add.16), channel_id=1, source_target_pairs={{0,4},{1,5},{2,6},{3,7},{4,0},{5,1},{6,2},{7,3},{8,12},{9,13},{10,... | collective-permute-start | bytes 12296 | tf_op jit(solution)/shard_map/ppermute | solution.py:287

commit v17 on v16

--- a/solution.py
+++ b/solution.py
@@ -403,8 +403,8 @@
         flops=6 * spots * channels * channels,
     )
     pair_out = call(turn_back_kernel, struct(pair_repr.shape, bf16), args=(pair_out,), flops=1 << 26)
+    loss = loss + exchange(loss, places, over_x)
     loss = loss + exchange(loss, places, over_core)
-    loss = loss + exchange(loss, places, over_x)
     cross_loss, half, near_loss = [
         exchange(loss, places, mask) for mask in (over_half + over_z, over_half, over_z)
     ]

time: 45.4 us -> 45.4 us (level)
  no operation moved by 1% of the time
where the time goes in v17:
time: 45.4 us; the launch traced here: 45.2 us
  waiting for transfers between devices  20.7 us (46%)
  starting transfers between devices  15.9 us (35%)
  Pallas kernels  5.69 us (13%)
  local copies, waits for them, and re-layouts  2.13 us (5%)
  between operations  0.78 us (2%)
    ppermute x18, waiting for transfers between devices, exchange(): return lax.ppermute(value, AXES, [(at, at ^ mask) for at in range(places)])  20.7 us
    ppermute x18, starting transfers between devices, exchange(): return lax.ppermute(value, AXES, [(at, at ^ mask) for at in range(places)])  15.9 us
    pallas_call x9, Pallas kernels, call(): pl.pallas_call(kernel, out_shape=outs, in_specs=specs if specs is not Non...  5.69 us
    unnamed x23, local copies, waits for them, and re-layouts  1.54 us
  transfers between devices with their start and end apart: 18, of which 12 were waited for; matrix products, arithmetic and copies ran while one was open for 0% of the time, Pallas kernels for 9%

profile of v17, /device:TPU:0, one launch (start us, length us, event | category | flops | bytes accessed | tf_op | source)
XLA Modules:
  0.0 45.2 jit_solution(7767102052114421817)
XLA Ops:
  0.6 3.1 %collective-permute-start.1 = (bf16[16,64,128]{2,1,0:T(8,128)(2,1)}, bf16[16,64,128]{2,1,0:T(8,128)(2,1)S(1)}, u32[]{:S(2)}, u32[]{:S(2)}) collective-permute-start(bf16[16,64,128]{2,1,0:T(8,128)(2,1)} %x_ref.3), channel_id=1, source_target_pairs={{0,4},{1,5},{2,6},{3,7},{4,0},{5,1},{6,2},{7,3},{8,12},{9,13},{10,... | collective-permute-start | bytes 786440 | tf_op jit(solution)/shard_map/ppermute | solution.py:287
  3.7 0.0 copy-start
  3.7 1.0 %copy-done = bf16[16,64,128]{2,1,0:T(8,128)(2,1)S(1)} copy-done((bf16[16,64,128]{2,1,0:T(8,128)(2,1)S(1)}, bf16[16,64,128]{2,1,0:T(8,128)(2,1)}, u32[]{:S(2)}) %copy-start) | copy-done | bytes 262168
  4.7 0.0 copy-start.6
  4.7 0.0 copy-start.7
  4.7 0.4 shard_map.113.normed_ref
  5.1 0.4 copy-done.6
  5.5 0.0 copy-done.7
  5.5 0.0 copy-start.4
  5.5 0.0 copy-start.5
  5.5 0.6 %shard_map.114 = (bf16[512,128]{1,0:T(8,128)(2,1)S(1)}, bf16[512,128]{1,0:T(8,128)(2,1)S(1)}) custom-call(bf16[1024,128]{1,0:T(8,128)(2,1)S(1)} %shard_map.113.normed_ref, bf16[128,128]{1,0:T(8,128)(2,1)S(1)} %copy-done.6, bf16[128,128]{1,0:T(8,128)(2,1)S(1)} %copy-done.7), custom_call_target="tpu_custom_call" | custom-call | flops 67108864 | bytes 1048576 | tf_op jit(solution)/shard_map/pallas_call | solution.py:291
  6.0 0.0 copy-start.8
  6.1 2.7 %collective-permute-start.3 = (bf16[512,128]{1,0:T(8,128)(2,1)S(1)}, bf16[512,128]{1,0:T(8,128)(2,1)S(1)}, u32[]{:S(2)}, u32[]{:S(2)}) collective-permute-start(bf16[512,128]{1,0:T(8,128)(2,1)S(1)} %get-tuple-element.19.stay_ref), channel_id=1, source_target_pairs={{0,8},{1,9},{2,10},{3,11},{4,12},{5,13},{6,14},{7,15},{8,0},{9,1},... | collective-permute-start | bytes 393224 | tf_op jit(solution)/shard_map/ppermute | solution.py:287
  8.7 0.0 collective-permute-start.4
  8.7 0.0 copy-done.4
  8.7 0.0 copy-done.5
  8.7 0.0 copy-done.8
  8.7 1.0 %shard_map.115 = (bf16[512,128]{1,0:T(8,128)(2,1)S(1)}, bf16[512,128]{1,0:T(8,128)(2,1)S(1)}, f32[24,128]{1,0:T(8,128)S(1)}) custom-call(s32[5]{0:T(128)S(1)} %copy-done.8, bf16[1024,128]{1,0:T(8,128)(2,1)S(1)} %shard_map.113.normed_ref, bf16[128,128]{1,0:T(8,128)(2,1)S(1)} %copy-done.4, bf16[128,128]{1,0:T(8,128)(2,1)S(1)} %copy-done.5, ...), custom_call_target="tpu_custom_call" | custom-call | flops 33554432 | bytes 1048576 | tf_op jit(solution)/shard_map/pallas_call | solution.py:291
  9.8 2.4 %collective-permute-done.1.x_ref = bf16[16,64,128]{2,1,0:T(8,128)(2,1)S(1)} collective-permute-done((bf16[16,64,128]{2,1,0:T(8,128)(2,1)}, bf16[16,64,128]{2,1,0:T(8,128)(2,1)S(1)}, u32[]{:S(2)}, u32[]{:S(2)}) %collective-permute-start.1) | collective-permute-done | bytes 262176 | tf_op jit(solution)/shard_map/ppermute | solution.py:287
  12.2 1.1 %shard_map.117 = (bf16[512,128]{1,0:T(8,128)(2,1)S(1)}, bf16[512,128]{1,0:T(8,128)(2,1)S(1)}) custom-call(f32[24,128]{1,0:T(8,128)S(1)} %get-tuple-element.20.masks_ref, bf16[16,64,128]{2,1,0:T(8,128)(2,1)S(1)} %collective-permute-done.1.x_ref, bf16[128,128]{1,0:T(8,128)(2,1)S(1)} %copy-done.4, bf16[128,128]{1,0:T(8,128)(2,1)S(1)} %copy-done.5, ...), custom_call_target="tpu_custom_call" | custom-call | flops 67108864 | bytes 1048576 | tf_op jit(solution)/shard_map/pallas_call | solution.py:291
  13.3 0.1 collective-permute-start.2
  13.3 0.5 %collective-permute-start = (bf16[512,128]{1,0:T(8,128)(2,1)S(1)}, bf16[512,128]{1,0:T(8,128)(2,1)S(1)}, u32[]{:S(2)}, u32[]{:S(2)}) collective-permute-start(bf16[512,128]{1,0:T(8,128)(2,1)S(1)} %get-tuple-element.26), channel_id=1, source_target_pairs={{0,2},{1,3},{2,0},{3,1},{4,6},{5,7},{6,4},{7,5},{8,10},{9,11},{10,... | collective-permute-start | bytes 393224 | tf_op jit(solution)/shard_map/ppermute | solution.py:287
  13.8 5.2 %collective-permute-done.3.far_ref.far = bf16[512,128]{1,0:T(8,128)(2,1)S(1)} collective-permute-done((bf16[512,128]{1,0:T(8,128)(2,1)S(1)}, bf16[512,128]{1,0:T(8,128)(2,1)S(1)}, u32[]{:S(2)}, u32[]{:S(2)}) %collective-permute-start.3) | collective-permute-done | bytes 131104 | tf_op jit(solution)/shard_map/ppermute | solution.py:287
  19.1 0.0 collective-permute-done.4.cross_ref.cross
  19.1 0.0 collective-permute-done.2.ready_ref.near_over
  19.1 0.1 collective-permute-start.5
  19.2 0.0 collective-permute-done.core
  19.2 1.3 %collective-permute-done.5.both_over = bf16[512,128]{1,0:T(8,128)(2,1)S(1)} collective-permute-done((bf16[512,128]{1,0:T(8,128)(2,1)S(1)}, bf16[512,128]{1,0:T(8,128)(2,1)S(1)}, u32[]{:S(2)}, u32[]{:S(2)}) %collective-permute-start.5) | collective-permute-done | bytes 131104 | tf_op jit(solution)/shard_map/ppermute | solution.py:287
  20.5 0.5 %shard_map.119 = (bf16[512,128]{1,0:T(8,128)(2,1)S(1)}, bf16[512,128]{1,0:T(8,128)(2,1)S(1)}, bf16[512,128]{1,0:T(8,128)(2,1)S(1)}, bf16[512,128]{1,0:T(8,128)(2,1)S(1)}) custom-call(f32[24,128]{1,0:T(8,128)S(1)} %get-tuple-element.20.masks_ref, bf16[512,128]{1,0:T(8,128)(2,1)S(1)} %get-tuple-element.25.own, bf16[512,128]{1,0:T(8,128)(2,1)S(1)} %collective-permute-done.core, ...), custom_call_target="tpu_custom_call" | custom-call | flops 16777216 | bytes 1048576 | tf_op jit(solution)/shard_map/pallas_call | solution.py:291
  21.0 3.0 %collective-permute-start.6 = (bf16[512,128]{1,0:T(8,128)(2,1)S(1)}, bf16[512,128]{1,0:T(8,128)(2,1)S(1)}, u32[]{:S(2)}, u32[]{:S(2)}) collective-permute-start(bf16[512,128]{1,0:T(8,128)(2,1)S(1)} %get-tuple-element.31), channel_id=1, source_target_pairs={{0,5},{1,4},{2,7},{3,6},{4,1},{5,0},{6,3},{7,2},{8,13},{9,12},{10,... | collective-permute-start | bytes 393224 | tf_op jit(solution)/shard_map/ppermute | solution.py:287
  24.0 0.1 collective-permute-start.7
  24.1 0.6 %collective-permute-start.8 = (bf16[512,128]{1,0:T(8,128)(2,1)S(1)}, bf16[512,128]{1,0:T(8,128)(2,1)S(1)}, u32[]{:S(2)}, u32[]{:S(2)}) collective-permute-start(bf16[512,128]{1,0:T(8,128)(2,1)S(1)} %get-tuple-element.33), channel_id=1, source_target_pairs={{0,1},{1,0},{2,3},{3,2},{4,5},{5,4},{6,7},{7,6},{8,9},{9,8},{10,11... | collective-permute-start | bytes 393224 | tf_op jit(solution)/shard_map/ppermute | solution.py:287
  24.7 0.0 collective-permute-start.9
  24.7 3.6 %collective-permute-done.6.refs_1_ = bf16[512,128]{1,0:T(8,128)(2,1)S(1)} collective-permute-done((bf16[512,128]{1,0:T(8,128)(2,1)S(1)}, bf16[512,128]{1,0:T(8,128)(2,1)S(1)}, u32[]{:S(2)}, u32[]{:S(2)}) %collective-permute-start.6) | collective-permute-done | bytes 131104 | tf_op jit(solution)/shard_map/ppermute | solution.py:287
  28.3 0.0 collective-permute-start.10
  28.3 2.1 %collective-permute-done.7.refs_2_ = bf16[512,128]{1,0:T(8,128)(2,1)S(1)} collective-permute-done((bf16[512,128]{1,0:T(8,128)(2,1)S(1)}, bf16[512,128]{1,0:T(8,128)(2,1)S(1)}, u32[]{:S(2)}, u32[]{:S(2)}) %collective-permute-start.7) | collective-permute-done | bytes 131104 | tf_op jit(solution)/shard_map/ppermute | solution.py:287
  30.4 0.0 collective-permute-start.11
  30.4 0.2 collective-permute-done.8.refs_3_
  30.6 0.3 collective-permute-start.12
  30.9 0.0 copy-done.9
  30.9 0.1 copy.12.dw_ref
  31.0 0.0 copy-done.10
  31.0 0.1 reshape.7.bins_ref
  31.1 0.0 copy-done.1
  31.1 0.0 copy-done.3
  31.1 0.0 copy-done.2
  31.1 0.4 shard_map.116
  31.5 0.0 collective-permute-done.9.refs_4_
  31.5 0.0 collective-permute-done.10.refs_5_
  31.5 0.2 collective-permute-done.11.refs_6_
  31.7 0.2 collective-permute-done.12.refs_7_
  32.0 0.9 %shard_map.120 = (bf16[128,1024]{1,0:T(8,128)(2,1)S(1)}, f32[8,128]{1,0:T(8,128)S(1)}) custom-call(f32[24,128]{1,0:T(8,128)S(1)} %get-tuple-element.20.masks_ref, f32[128,1024]{1,0:T(8,128)S(1)} %get-tuple-element.21.x_ref, f32[128,1024]{1,0:T(8,128)S(1)} %get-tuple-element.22.gate_ref, s32[8,128]{1,0:T(8,128)S(1)} %reshape.7.bins_ref, ...), custom_call_target="tpu_custom_call" | custom-call | flops 100663296 | bytes 1048576 | tf_op jit(solution)/shard_map/pallas_call | solution.py:291
  32.9 1.2 %collective-permute-start.13 = (f32[8,128]{1,0:T(8,128)S(1)}, f32[8,128]{1,0:T(8,128)S(1)}, u32[]{:S(2)}, u32[]{:S(2)}) collective-permute-start(f32[8,128]{1,0:T(8,128)S(1)} %get-tuple-element.35), channel_id=1, source_target_pairs={{0,1},{1,0},{2,3},{3,2},{4,5},{5,4},{6,7},{7,6},{8,9},{9,8},{10,11... | collective-permute-start | bytes 12296 | tf_op jit(solution)/shard_map/ppermute | solution.py:287
  34.1 2.4 %collective-permute-done.13 = f32[8,128]{1,0:T(8,128)S(1)} collective-permute-done((f32[8,128]{1,0:T(8,128)S(1)}, f32[8,128]{1,0:T(8,128)S(1)}, u32[]{:S(2)}, u32[]{:S(2)}) %collective-permute-start.13) | collective-permute-done | bytes 4128 | tf_op jit(solution)/shard_map/ppermute | solution.py:287
  36.5 0.0 collective-permute-start.14
  36.5 1.2 %collective-permute-done.14 = f32[8,128]{1,0:T(8,128)S(1)} collective-permute-done((f32[8,128]{1,0:T(8,128)S(1)}, f32[8,128]{1,0:T(8,128)S(1)}, u32[]{:S(2)}, u32[]{:S(2)}) %collective-permute-start.14) | collective-permute-done | bytes 4128 | tf_op jit(solution)/shard_map/ppermute | solution.py:287
  37.7 2.5 %collective-permute-start.15 = (f32[8,128]{1,0:T(8,128)S(1)}, f32[8,128]{1,0:T(8,128)S(1)}, u32[]{:S(2)}, u32[]{:S(2)}) collective-permute-start(f32[8,128]{1,0:T(8,128)S(1)} %add.16), channel_id=1, source_target_pairs={{0,12},{1,13},{2,14},{3,15},{4,8},{5,9},{6,10},{7,11},{8,4},{9,5},... | collective-permute-start | bytes 12296 | tf_op jit(solution)/shard_map/ppermute | solution.py:287
  40.2 0.9 %collective-permute-start.16 = (f32[8,128]{1,0:T(8,128)S(1)}, f32[8,128]{1,0:T(8,128)S(1)}, u32[]{:S(2)}, u32[]{:S(2)}) collective-permute-start(f32[8,128]{1,0:T(8,128)S(1)} %add.16), channel_id=1, source_target_pairs={{0,8},{1,9},{2,10},{3,11},{4,12},{5,13},{6,14},{7,15},{8,0},{9,1},... | collective-permute-start | bytes 12296 | tf_op jit(solution)/shard_map/ppermute | solution.py:287
  41.1 1.0 %collective-permute-start.17 = (f32[8,128]{1,0:T(8,128)S(1)}, f32[8,128]{1,0:T(8,128)S(1)}, u32[]{:S(2)}, u32[]{:S(2)}) collective-permute-start(f32[8,128]{1,0:T(8,128)S(1)} %add.16), channel_id=1, source_target_pairs={{0,4},{1,5},{2,6},{3,7},{4,0},{5,1},{6,2},{7,3},{8,12},{9,13},{10,... | collective-permute-start | bytes 12296 | tf_op jit(solution)/shard_map/ppermute | solution.py:287
  42.1 0.8 %shard_map.121 = bf16[16,64,128]{2,1,0:T(8,128)(2,1)} custom-call(bf16[128,1024]{1,0:T(8,128)(2,1)S(1)} %get-tuple-element.34.turned_ref), custom_call_target="tpu_custom_call" | custom-call | flops 67108864 | bytes 1048576 | tf_op jit(solution)/shard_map/pallas_call | solution.py:291
  42.9 0.2 collective-permute-done.15
  43.1 1.6 %collective-permute-done.16 = f32[8,128]{1,0:T(8,128)S(1)} collective-permute-done((f32[8,128]{1,0:T(8,128)S(1)}, f32[8,128]{1,0:T(8,128)S(1)}, u32[]{:S(2)}, u32[]{:S(2)}) %collective-permute-start.16) | collective-permute-done | bytes 4128 | tf_op jit(solution)/shard_map/ppermute | solution.py:287
  44.7 0.0 collective-permute-done.17
  44.7 0.5 %slice.3 = f32[1,1]{1,0:T(1,128)} slice(f32[8,128]{1,0:T(8,128)S(1)} %add_add_fusion), slice={[0:1], [0:1]} | slice | bytes 8 | tf_op jit(solution)/shard_map/slice | solution.py:412
  (9 shorter events, 0.0 us)
Async XLA Ops:
  0.6 11.6 %collective-permute-start.1 = (bf16[16,64,128]{2,1,0:T(8,128)(2,1)}, bf16[16,64,128]{2,1,0:T(8,128)(2,1)S(1)}, u32[]{:S(2)}, u32[]{:S(2)}) collective-permute-start(bf16[16,64,128]{2,1,0:T(8,128)(2,1)} %x_ref.3), channel_id=1, source_target_pairs={{0,4},{1,5},{2,6},{3,7},{4,0},{5,1},{6,2},{7,3},{8,12},{9,13},{10,... | collective-permute-start | bytes 786440 | tf_op jit(solution)/shard_map/ppermute | solution.py:287
  3.7 1.0 %copy-start = (bf16[16,64,128]{2,1,0:T(8,128)(2,1)S(1)}, bf16[16,64,128]{2,1,0:T(8,128)(2,1)}, u32[]{:S(2)}) copy-start(bf16[16,64,128]{2,1,0:T(8,128)(2,1)} %x_ref.3) | copy-start | bytes 786436
  4.7 0.8 %copy-start.6 = (bf16[128,128]{1,0:T(8,128)(2,1)S(1)}, bf16[128,128]{1,0:T(8,128)(2,1)}, u32[]{:S(2)}) copy-start(bf16[128,128]{1,0:T(8,128)(2,1)} %rw_ref.1) | copy-start | bytes 98308
  4.7 0.8 %copy-start.7 = (bf16[128,128]{1,0:T(8,128)(2,1)S(1)}, bf16[128,128]{1,0:T(8,128)(2,1)}, u32[]{:S(2)}) copy-start(bf16[128,128]{1,0:T(8,128)(2,1)} %rg_ref.1) | copy-start | bytes 98308
  5.5 3.2 %copy-start.4 = (bf16[128,128]{1,0:T(8,128)(2,1)S(1)}, bf16[128,128]{1,0:T(8,128)(2,1)}, u32[]{:S(2)}) copy-start(bf16[128,128]{1,0:T(8,128)(2,1)} %lw_ref.1) | copy-start | bytes 98308
  5.5 3.2 %copy-start.5 = (bf16[128,128]{1,0:T(8,128)(2,1)S(1)}, bf16[128,128]{1,0:T(8,128)(2,1)}, u32[]{:S(2)}) copy-start(bf16[128,128]{1,0:T(8,128)(2,1)} %lg_ref.1) | copy-start | bytes 98308
  6.0 2.7 %copy-start.8 = (s32[5]{0:T(128)S(1)}, s32[5]{0:T(128)}, u32[]{:S(2)}) copy-start(s32[5]{0:T(128)} %lens_ref.1) | copy-start | bytes 64
  6.1 13.0 %collective-permute-start.3 = (bf16[512,128]{1,0:T(8,128)(2,1)S(1)}, bf16[512,128]{1,0:T(8,128)(2,1)S(1)}, u32[]{:S(2)}, u32[]{:S(2)}) collective-permute-start(bf16[512,128]{1,0:T(8,128)(2,1)S(1)} %get-tuple-element.19.stay_ref), channel_id=1, source_target_pairs={{0,8},{1,9},{2,10},{3,11},{4,12},{5,13},{6,14},{7,15},{8,0},{9,1},... | collective-permute-start | bytes 393224 | tf_op jit(solution)/shard_map/ppermute | solution.py:287
  8.7 10.3 %collective-permute-start.4 = (bf16[512,128]{1,0:T(8,128)(2,1)S(1)}, bf16[512,128]{1,0:T(8,128)(2,1)S(1)}, u32[]{:S(2)}, u32[]{:S(2)}) collective-permute-start(bf16[512,128]{1,0:T(8,128)(2,1)S(1)} %get-tuple-element.29), channel_id=1, source_target_pairs={{0,12},{1,13},{2,14},{3,15},{4,8},{5,9},{6,10},{7,11},{8,4},{9,5},... | collective-permute-start | bytes 393224 | tf_op jit(solution)/shard_map/ppermute | solution.py:287
  13.3 5.8 %collective-permute-start.2 = (bf16[512,128]{1,0:T(8,128)(2,1)S(1)}, bf16[512,128]{1,0:T(8,128)(2,1)S(1)}, u32[]{:S(2)}, u32[]{:S(2)}) collective-permute-start(bf16[512,128]{1,0:T(8,128)(2,1)S(1)} %get-tuple-element.28), channel_id=1, source_target_pairs={{0,2},{1,3},{2,0},{3,1},{4,6},{5,7},{6,4},{7,5},{8,10},{9,11},{10,... | collective-permute-start | bytes 393224 | tf_op jit(solution)/shard_map/ppermute | solution.py:287
  13.3 5.8 %collective-permute-start = (bf16[512,128]{1,0:T(8,128)(2,1)S(1)}, bf16[512,128]{1,0:T(8,128)(2,1)S(1)}, u32[]{:S(2)}, u32[]{:S(2)}) collective-permute-start(bf16[512,128]{1,0:T(8,128)(2,1)S(1)} %get-tuple-element.26), channel_id=1, source_target_pairs={{0,2},{1,3},{2,0},{3,1},{4,6},{5,7},{6,4},{7,5},{8,10},{9,11},{10,... | collective-permute-start | bytes 393224 | tf_op jit(solution)/shard_map/ppermute | solution.py:287
  19.1 1.4 %collective-permute-start.5 = (bf16[512,128]{1,0:T(8,128)(2,1)S(1)}, bf16[512,128]{1,0:T(8,128)(2,1)S(1)}, u32[]{:S(2)}, u32[]{:S(2)}) collective-permute-start(bf16[512,128]{1,0:T(8,128)(2,1)S(1)} %shard_map.118), channel_id=1, source_target_pairs={{0,2},{1,3},{2,0},{3,1},{4,6},{5,7},{6,4},{7,5},{8,10},{9,11},{10,... | collective-permute-start | bytes 393224 | tf_op jit(solution)/shard_map/ppermute | solution.py:287
  20.5 10.4 %copy-start.9 = (bf16[128,64]{0,1:T(8,128)(2,1)S(1)}, bf16[128,64]{0,1:T(8,128)(2,1)}, u32[]{:S(2)}) copy-start(bf16[128,64]{0,1:T(8,128)(2,1)} %param.19) | copy-start | bytes 49156
  20.5 10.5 %copy-start.10 = (s32[16,64]{1,0:T(8,128)S(1)}, s32[16,64]{1,0:T(8,128)}, u32[]{:S(2)}) copy-start(s32[16,64]{1,0:T(8,128)} %param.11) | copy-start | bytes 12292
  20.5 10.6 %copy-start.1 = (bf16[16,64,128]{2,1,0:T(8,128)(2,1)S(1)}, bf16[16,64,128]{2,1,0:T(8,128)(2,1)}, u32[]{:S(2)}) copy-start(bf16[16,64,128]{2,1,0:T(8,128)(2,1)} %x_ref.3) | copy-start | bytes 786436
  21.0 7.3 %collective-permute-start.6 = (bf16[512,128]{1,0:T(8,128)(2,1)S(1)}, bf16[512,128]{1,0:T(8,128)(2,1)S(1)}, u32[]{:S(2)}, u32[]{:S(2)}) collective-permute-start(bf16[512,128]{1,0:T(8,128)(2,1)S(1)} %get-tuple-element.31), channel_id=1, source_target_pairs={{0,5},{1,4},{2,7},{3,6},{4,1},{5,0},{6,3},{7,2},{8,13},{9,12},{10,... | collective-permute-start | bytes 393224 | tf_op jit(solution)/shard_map/ppermute | solution.py:287
  24.0 7.1 %copy-start.3 = (bf16[128,128]{1,0:T(8,128)(2,1)S(1)}, bf16[128,128]{1,0:T(8,128)(2,1)}, u32[]{:S(2)}) copy-start(bf16[128,128]{1,0:T(8,128)(2,1)} %ow_ref.1) | copy-start | bytes 98308
  24.0 7.1 %copy-start.2 = (bf16[128,128]{1,0:T(8,128)(2,1)S(1)}, bf16[128,128]{1,0:T(8,128)(2,1)}, u32[]{:S(2)}) copy-start(bf16[128,128]{1,0:T(8,128)(2,1)} %gw_ref.1) | copy-start | bytes 98308
  24.0 6.4 %collective-permute-start.7 = (bf16[512,128]{1,0:T(8,128)(2,1)S(1)}, bf16[512,128]{1,0:T(8,128)(2,1)S(1)}, u32[]{:S(2)}, u32[]{:S(2)}) collective-permute-start(bf16[512,128]{1,0:T(8,128)(2,1)S(1)} %get-tuple-element.32), channel_id=1, source_target_pairs={{0,4},{1,5},{2,6},{3,7},{4,0},{5,1},{6,2},{7,3},{8,12},{9,13},{10,... | collective-permute-start | bytes 393224 | tf_op jit(solution)/shard_map/ppermute | solution.py:287
  24.1 6.6 %collective-permute-start.8 = (bf16[512,128]{1,0:T(8,128)(2,1)S(1)}, bf16[512,128]{1,0:T(8,128)(2,1)S(1)}, u32[]{:S(2)}, u32[]{:S(2)}) collective-permute-start(bf16[512,128]{1,0:T(8,128)(2,1)S(1)} %get-tuple-element.33), channel_id=1, source_target_pairs={{0,1},{1,0},{2,3},{3,2},{4,5},{5,4},{6,7},{7,6},{8,9},{9,8},{10,11... | collective-permute-start | bytes 393224 | tf_op jit(solution)/shard_map/ppermute | solution.py:287
  24.7 6.8 %collective-permute-start.9 = (bf16[512,128]{1,0:T(8,128)(2,1)S(1)}, bf16[512,128]{1,0:T(8,128)(2,1)S(1)}, u32[]{:S(2)}, u32[]{:S(2)}) collective-permute-start(bf16[512,128]{1,0:T(8,128)(2,1)S(1)} %get-tuple-element.30.refs_0_), channel_id=1, source_target_pairs={{0,2},{1,3},{2,0},{3,1},{4,6},{5,7},{6,4},{7,5},{8,10},{9,11},{10,... | collective-permute-start | bytes 393224 | tf_op jit(solution)/shard_map/ppermute | solution.py:287
  28.3 3.2 %collective-permute-start.10 = (bf16[512,128]{1,0:T(8,128)(2,1)S(1)}, bf16[512,128]{1,0:T(8,128)(2,1)S(1)}, u32[]{:S(2)}, u32[]{:S(2)}) collective-permute-start(bf16[512,128]{1,0:T(8,128)(2,1)S(1)} %collective-permute-done.6.refs_1_), channel_id=1, source_target_pairs={{0,2},{1,3},{2,0},{3,1},{4,6},{5,7},{6,4},{7,5},{8,10},{9,11},{10,... | collective-permute-start | bytes 393224 | tf_op jit(solution)/shard_map/ppermute | solution.py:287
  30.4 1.3 %collective-permute-start.11 = (bf16[512,128]{1,0:T(8,128)(2,1)S(1)}, bf16[512,128]{1,0:T(8,128)(2,1)S(1)}, u32[]{:S(2)}, u32[]{:S(2)}) collective-permute-start(bf16[512,128]{1,0:T(8,128)(2,1)S(1)} %collective-permute-done.7.refs_2_), channel_id=1, source_target_pairs={{0,2},{1,3},{2,0},{3,1},{4,6},{5,7},{6,4},{7,5},{8,10},{9,11},{10,... | collective-permute-start | bytes 393224 | tf_op jit(solution)/shard_map/ppermute | solution.py:287
  30.6 1.3 %collective-permute-start.12 = (bf16[512,128]{1,0:T(8,128)(2,1)S(1)}, bf16[512,128]{1,0:T(8,128)(2,1)S(1)}, u32[]{:S(2)}, u32[]{:S(2)}) collective-permute-start(bf16[512,128]{1,0:T(8,128)(2,1)S(1)} %collective-permute-done.8.refs_3_), channel_id=1, source_target_pairs={{0,2},{1,3},{2,0},{3,1},{4,6},{5,7},{6,4},{7,5},{8,10},{9,11},{10,... | collective-permute-start | bytes 393224 | tf_op jit(solution)/shard_map/ppermute | solution.py:287
  32.9 3.6 %collective-permute-start.13 = (f32[8,128]{1,0:T(8,128)S(1)}, f32[8,128]{1,0:T(8,128)S(1)}, u32[]{:S(2)}, u32[]{:S(2)}) collective-permute-start(f32[8,128]{1,0:T(8,128)S(1)} %get-tuple-element.35), channel_id=1, source_target_pairs={{0,1},{1,0},{2,3},{3,2},{4,5},{5,4},{6,7},{7,6},{8,9},{9,8},{10,11... | collective-permute-start | bytes 12296 | tf_op jit(solution)/shard_map/ppermute | solution.py:287
  36.5 1.2 %collective-permute-start.14 = (f32[8,128]{1,0:T(8,128)S(1)}, f32[8,128]{1,0:T(8,128)S(1)}, u32[]{:S(2)}, u32[]{:S(2)}) collective-permute-start(f32[8,128]{1,0:T(8,128)S(1)} %add.15), channel_id=1, source_target_pairs={{0,2},{1,3},{2,0},{3,1},{4,6},{5,7},{6,4},{7,5},{8,10},{9,11},{10,... | collective-permute-start | bytes 12296 | tf_op jit(solution)/shard_map/ppermute | solution.py:287
  37.7 5.4 %collective-permute-start.15 = (f32[8,128]{1,0:T(8,128)S(1)}, f32[8,128]{1,0:T(8,128)S(1)}, u32[]{:S(2)}, u32[]{:S(2)}) collective-permute-start(f32[8,128]{1,0:T(8,128)S(1)} %add.16), channel_id=1, source_target_pairs={{0,12},{1,13},{2,14},{3,15},{4,8},{5,9},{6,10},{7,11},{8,4},{9,5},... | collective-permute-start | bytes 12296 | tf_op jit(solution)/shard_map/ppermute | solution.py:287
  40.2 4.5 %collective-permute-start.16 = (f32[8,128]{1,0:T(8,128)S(1)}, f32[8,128]{1,0:T(8,128)S(1)}, u32[]{:S(2)}, u32[]{:S(2)}) collective-permute-start(f32[8,128]{1,0:T(8,128)S(1)} %add.16), channel_id=1, source_target_pairs={{0,8},{1,9},{2,10},{3,11},{4,12},{5,13},{6,14},{7,15},{8,0},{9,1},... | collective-permute-start | bytes 12296 | tf_op jit(solution)/shard_map/ppermute | solution.py:287
  41.1 3.6 %collective-permute-start.17 = (f32[8,128]{1,0:T(8,128)S(1)}, f32[8,128]{1,0:T(8,128)S(1)}, u32[]{:S(2)}, u32[]{:S(2)}) collective-permute-start(f32[8,128]{1,0:T(8,128)S(1)} %add.16), channel_id=1, source_target_pairs={{0,4},{1,5},{2,6},{3,7},{4,0},{5,1},{6,2},{7,3},{8,12},{9,13},{10,... | collective-permute-start | bytes 12296 | tf_op jit(solution)/shard_map/ppermute | solution.py:287

commit v18 on v17

--- a/solution.py
+++ b/solution.py
@@ -403,8 +403,10 @@
         flops=6 * spots * channels * channels,
     )
     pair_out = call(turn_back_kernel, struct(pair_repr.shape, bf16), args=(pair_out,), flops=1 << 26)
-    loss = loss + exchange(loss, places, over_x)
-    loss = loss + exchange(loss, places, over_core)
+    beside, beside_over, sibling = [
+        exchange(loss, places, mask) for mask in (over_x, over_x + over_core, over_core)
+    ]
+    loss = (beside + beside_over) + (sibling + loss)
     cross_loss, half, near_loss = [
         exchange(loss, places, mask) for mask in (over_half + over_z, over_half, over_z)
     ]

time: 45.4 us -> 45 us (level)
  waiting for transfers between devices: 20.7 us -> 19.3 us
  starting transfers between devices: 15.9 us -> 16.9 us
    ppermute x18 -> x19, waiting for transfers between devices: 20.7 us -> 19.3 us  [exchange(): return lax.ppermute(value, AXES, [(at, at ^ mask) for at in range(places)])]
    ppermute x18 -> x19, starting transfers between devices: 15.9 us -> 16.9 us  [exchange(): return lax.ppermute(value, AXES, [(at, at ^ mask) for at in range(places)])]
  transfers between devices with their start and end apart: 18 -> 19, of which waited for: 12 -> 13; matrix products, arithmetic and copies ran while one was open for 0% -> 0% of each run, Pallas kernels for 9% -> 9%
where the time goes in v18:
time: 45 us; the launch traced here: 44.8 us
  waiting for transfers between devices  19.3 us (43%)
  starting transfers between devices  16.9 us (38%)
  Pallas kernels  5.69 us (13%)
  local copies, waits for them, and re-layouts  2.13 us (5%)
  between operations  0.78 us (2%)
    ppermute x19, waiting for transfers between devices, exchange(): return lax.ppermute(value, AXES, [(at, at ^ mask) for at in range(places)])  19.3 us
    ppermute x19, starting transfers between devices, exchange(): return lax.ppermute(value, AXES, [(at, at ^ mask) for at in range(places)])  16.9 us
    pallas_call x9, Pallas kernels, call(): pl.pallas_call(kernel, out_shape=outs, in_specs=specs if specs is not Non...  5.69 us
    unnamed x23, local copies, waits for them, and re-layouts  1.54 us
  transfers between devices with their start and end apart: 19, of which 13 were waited for; matrix products, arithmetic and copies ran while one was open for 0% of the time, Pallas kernels for 9%

profile of v18, /device:TPU:0, one launch (start us, length us, event | category | flops | bytes accessed | tf_op | source)
XLA Modules:
  0.0 44.8 jit_solution(13261635292213043301)
XLA Ops:
  0.6 3.1 %collective-permute-start.1 = (bf16[16,64,128]{2,1,0:T(8,128)(2,1)}, bf16[16,64,128]{2,1,0:T(8,128)(2,1)S(1)}, u32[]{:S(2)}, u32[]{:S(2)}) collective-permute-start(bf16[16,64,128]{2,1,0:T(8,128)(2,1)} %x_ref.3), channel_id=1, source_target_pairs={{0,4},{1,5},{2,6},{3,7},{4,0},{5,1},{6,2},{7,3},{8,12},{9,13},{10,... | collective-permute-start | bytes 786440 | tf_op jit(solution)/shard_map/ppermute | solution.py:287
  3.7 0.0 copy-start
  3.7 1.0 %copy-done = bf16[16,64,128]{2,1,0:T(8,128)(2,1)S(1)} copy-done((bf16[16,64,128]{2,1,0:T(8,128)(2,1)S(1)}, bf16[16,64,128]{2,1,0:T(8,128)(2,1)}, u32[]{:S(2)}) %copy-start) | copy-done | bytes 262168
  4.7 0.0 copy-start.6
  4.7 0.0 copy-start.7
  4.7 0.4 shard_map.113.normed_ref
  5.1 0.4 copy-done.6
  5.5 0.0 copy-done.7
  5.5 0.6 %shard_map.114 = (bf16[512,128]{1,0:T(8,128)(2,1)S(1)}, bf16[512,128]{1,0:T(8,128)(2,1)S(1)}) custom-call(bf16[1024,128]{1,0:T(8,128)(2,1)S(1)} %shard_map.113.normed_ref, bf16[128,128]{1,0:T(8,128)(2,1)S(1)} %copy-done.6, bf16[128,128]{1,0:T(8,128)(2,1)S(1)} %copy-done.7), custom_call_target="tpu_custom_call" | custom-call | flops 67108864 | bytes 1048576 | tf_op jit(solution)/shard_map/pallas_call | solution.py:291
  6.0 0.0 copy-start.8
  6.1 2.7 %collective-permute-start.3 = (bf16[512,128]{1,0:T(8,128)(2,1)S(1)}, bf16[512,128]{1,0:T(8,128)(2,1)S(1)}, u32[]{:S(2)}, u32[]{:S(2)}) collective-permute-start(bf16[512,128]{1,0:T(8,128)(2,1)S(1)} %get-tuple-element.19.stay_ref), channel_id=1, source_target_pairs={{0,8},{1,9},{2,10},{3,11},{4,12},{5,13},{6,14},{7,15},{8,0},{9,1},... | collective-permute-start | bytes 393224 | tf_op jit(solution)/shard_map/ppermute | solution.py:287
  8.7 0.0 collective-permute-start.4
  8.7 0.0 copy-done.4
  8.7 0.0 copy-done.5
  8.7 0.0 copy-done.8
  8.7 1.0 %shard_map.115 = (bf16[512,128]{1,0:T(8,128)(2,1)S(1)}, bf16[512,128]{1,0:T(8,128)(2,1)S(1)}, f32[24,128]{1,0:T(8,128)S(1)}) custom-call(s32[5]{0:T(128)S(1)} %copy-done.8, bf16[1024,128]{1,0:T(8,128)(2,1)S(1)} %shard_map.113.normed_ref, bf16[128,128]{1,0:T(8,128)(2,1)S(1)} %copy-done.4, bf16[128,128]{1,0:T(8,128)(2,1)S(1)} %copy-done.5, ...), custom_call_target="tpu_custom_call" | custom-call | flops 33554432 | bytes 1048576 | tf_op jit(solution)/shard_map/pallas_call | solution.py:291
  9.8 2.4 %collective-permute-done.1.x_ref = bf16[16,64,128]{2,1,0:T(8,128)(2,1)S(1)} collective-permute-done((bf16[16,64,128]{2,1,0:T(8,128)(2,1)}, bf16[16,64,128]{2,1,0:T(8,128)(2,1)S(1)}, u32[]{:S(2)}, u32[]{:S(2)}) %collective-permute-start.1) | collective-permute-done | bytes 262176 | tf_op jit(solution)/shard_map/ppermute | solution.py:287
  12.2 1.1 %shard_map.117 = (bf16[512,128]{1,0:T(8,128)(2,1)S(1)}, bf16[512,128]{1,0:T(8,128)(2,1)S(1)}) custom-call(f32[24,128]{1,0:T(8,128)S(1)} %get-tuple-element.20.masks_ref, bf16[16,64,128]{2,1,0:T(8,128)(2,1)S(1)} %collective-permute-done.1.x_ref, bf16[128,128]{1,0:T(8,128)(2,1)S(1)} %copy-done.4, bf16[128,128]{1,0:T(8,128)(2,1)S(1)} %copy-done.5, ...), custom_call_target="tpu_custom_call" | custom-call | flops 67108864 | bytes 1048576 | tf_op jit(solution)/shard_map/pallas_call | solution.py:291
  13.3 0.1 collective-permute-start.2
  13.3 0.5 %collective-permute-start = (bf16[512,128]{1,0:T(8,128)(2,1)S(1)}, bf16[512,128]{1,0:T(8,128)(2,1)S(1)}, u32[]{:S(2)}, u32[]{:S(2)}) collective-permute-start(bf16[512,128]{1,0:T(8,128)(2,1)S(1)} %get-tuple-element.26), channel_id=1, source_target_pairs={{0,2},{1,3},{2,0},{3,1},{4,6},{5,7},{6,4},{7,5},{8,10},{9,11},{10,... | collective-permute-start | bytes 393224 | tf_op jit(solution)/shard_map/ppermute | solution.py:287
  13.8 5.2 %collective-permute-done.3.far_ref.far = bf16[512,128]{1,0:T(8,128)(2,1)S(1)} collective-permute-done((bf16[512,128]{1,0:T(8,128)(2,1)S(1)}, bf16[512,128]{1,0:T(8,128)(2,1)S(1)}, u32[]{:S(2)}, u32[]{:S(2)}) %collective-permute-start.3) | collective-permute-done | bytes 131104 | tf_op jit(solution)/shard_map/ppermute | solution.py:287
  19.1 0.0 collective-permute-done.4.cross_ref.cross
  19.1 0.0 collective-permute-done.2.ready_ref.near_over
  19.1 0.1 collective-permute-start.5
  19.2 0.0 collective-permute-done.core
  19.2 1.3 %collective-permute-done.5.both_over = bf16[512,128]{1,0:T(8,128)(2,1)S(1)} collective-permute-done((bf16[512,128]{1,0:T(8,128)(2,1)S(1)}, bf16[512,128]{1,0:T(8,128)(2,1)S(1)}, u32[]{:S(2)}, u32[]{:S(2)}) %collective-permute-start.5) | collective-permute-done | bytes 131104 | tf_op jit(solution)/shard_map/ppermute | solution.py:287
  20.5 0.5 %shard_map.119 = (bf16[512,128]{1,0:T(8,128)(2,1)S(1)}, bf16[512,128]{1,0:T(8,128)(2,1)S(1)}, bf16[512,128]{1,0:T(8,128)(2,1)S(1)}, bf16[512,128]{1,0:T(8,128)(2,1)S(1)}) custom-call(f32[24,128]{1,0:T(8,128)S(1)} %get-tuple-element.20.masks_ref, bf16[512,128]{1,0:T(8,128)(2,1)S(1)} %get-tuple-element.25.own, bf16[512,128]{1,0:T(8,128)(2,1)S(1)} %collective-permute-done.core, ...), custom_call_target="tpu_custom_call" | custom-call | flops 16777216 | bytes 1048576 | tf_op jit(solution)/shard_map/pallas_call | solution.py:291
  21.0 3.0 %collective-permute-start.6 = (bf16[512,128]{1,0:T(8,128)(2,1)S(1)}, bf16[512,128]{1,0:T(8,128)(2,1)S(1)}, u32[]{:S(2)}, u32[]{:S(2)}) collective-permute-start(bf16[512,128]{1,0:T(8,128)(2,1)S(1)} %get-tuple-element.31), channel_id=1, source_target_pairs={{0,5},{1,4},{2,7},{3,6},{4,1},{5,0},{6,3},{7,2},{8,13},{9,12},{10,... | collective-permute-start | bytes 393224 | tf_op jit(solution)/shard_map/ppermute | solution.py:287
  24.0 0.1 collective-permute-start.7
  24.1 0.6 %collective-permute-start.8 = (bf16[512,128]{1,0:T(8,128)(2,1)S(1)}, bf16[512,128]{1,0:T(8,128)(2,1)S(1)}, u32[]{:S(2)}, u32[]{:S(2)}) collective-permute-start(bf16[512,128]{1,0:T(8,128)(2,1)S(1)} %get-tuple-element.33), channel_id=1, source_target_pairs={{0,1},{1,0},{2,3},{3,2},{4,5},{5,4},{6,7},{7,6},{8,9},{9,8},{10,11... | collective-permute-start | bytes 393224 | tf_op jit(solution)/shard_map/ppermute | solution.py:287
  24.7 0.0 collective-permute-start.9
  24.7 3.6 %collective-permute-done.6.refs_1_ = bf16[512,128]{1,0:T(8,128)(2,1)S(1)} collective-permute-done((bf16[512,128]{1,0:T(8,128)(2,1)S(1)}, bf16[512,128]{1,0:T(8,128)(2,1)S(1)}, u32[]{:S(2)}, u32[]{:S(2)}) %collective-permute-start.6) | collective-permute-done | bytes 131104 | tf_op jit(solution)/shard_map/ppermute | solution.py:287
  28.3 0.0 collective-permute-start.10
  28.3 2.1 %collective-permute-done.7.refs_2_ = bf16[512,128]{1,0:T(8,128)(2,1)S(1)} collective-permute-done((bf16[512,128]{1,0:T(8,128)(2,1)S(1)}, bf16[512,128]{1,0:T(8,128)(2,1)S(1)}, u32[]{:S(2)}, u32[]{:S(2)}) %collective-permute-start.7) | collective-permute-done | bytes 131104 | tf_op jit(solution)/shard_map/ppermute | solution.py:287
  30.4 0.0 collective-permute-start.11
  30.4 0.2 collective-permute-done.8.refs_3_
  30.6 0.3 collective-permute-start.12
  30.9 0.0 copy-done.9
  30.9 0.1 copy.12.dw_ref
  31.0 0.0 copy-done.10
  31.0 0.1 reshape.7.bins_ref
  31.1 0.0 copy-done.1
  31.1 0.0 copy-done.3
  31.1 0.0 copy-done.2
  31.1 0.4 shard_map.116
  31.5 0.0 collective-permute-done.9.refs_4_
  31.5 0.0 collective-permute-done.10.refs_5_
  31.5 0.2 collective-permute-done.11.refs_6_
  31.7 0.2 collective-permute-done.12.refs_7_
  32.0 0.9 %shard_map.120 = (bf16[128,1024]{1,0:T(8,128)(2,1)S(1)}, f32[8,128]{1,0:T(8,128)S(1)}) custom-call(f32[24,128]{1,0:T(8,128)S(1)} %get-tuple-element.20.masks_ref, f32[128,1024]{1,0:T(8,128)S(1)} %get-tuple-element.21.x_ref, f32[128,1024]{1,0:T(8,128)S(1)} %get-tuple-element.22.gate_ref, s32[8,128]{1,0:T(8,128)S(1)} %reshape.7.bins_ref, ...), custom_call_target="tpu_custom_call" | custom-call | flops 100663296 | bytes 1048576 | tf_op jit(solution)/shard_map/pallas_call | solution.py:291
  32.9 1.2 %collective-permute-start.13 = (f32[8,128]{1,0:T(8,128)S(1)}, f32[8,128]{1,0:T(8,128)S(1)}, u32[]{:S(2)}, u32[]{:S(2)}) collective-permute-start(f32[8,128]{1,0:T(8,128)S(1)} %get-tuple-element.35), channel_id=1, source_target_pairs={{0,1},{1,0},{2,3},{3,2},{4,5},{5,4},{6,7},{7,6},{8,9},{9,8},{10,11... | collective-permute-start | bytes 12296 | tf_op jit(solution)/shard_map/ppermute | solution.py:287
  34.1 0.4 collective-permute-start.14
  34.5 0.5 %collective-permute-start.15 = (f32[8,128]{1,0:T(8,128)S(1)}, f32[8,128]{1,0:T(8,128)S(1)}, u32[]{:S(2)}, u32[]{:S(2)}) collective-permute-start(f32[8,128]{1,0:T(8,128)S(1)} %get-tuple-element.35), channel_id=1, source_target_pairs={{0,2},{1,3},{2,0},{3,1},{4,6},{5,7},{6,4},{7,5},{8,10},{9,11},{10,... | collective-permute-start | bytes 12296 | tf_op jit(solution)/shard_map/ppermute | solution.py:287
  35.0 1.5 %collective-permute-done.13 = f32[8,128]{1,0:T(8,128)S(1)} collective-permute-done((f32[8,128]{1,0:T(8,128)S(1)}, f32[8,128]{1,0:T(8,128)S(1)}, u32[]{:S(2)}, u32[]{:S(2)}) %collective-permute-start.13) | collective-permute-done | bytes 4128 | tf_op jit(solution)/shard_map/ppermute | solution.py:287
  36.5 0.7 %collective-permute-done.14 = f32[8,128]{1,0:T(8,128)S(1)} collective-permute-done((f32[8,128]{1,0:T(8,128)S(1)}, f32[8,128]{1,0:T(8,128)S(1)}, u32[]{:S(2)}, u32[]{:S(2)}) %collective-permute-start.14) | collective-permute-done | bytes 4128 | tf_op jit(solution)/shard_map/ppermute | solution.py:287
  37.2 0.0 collective-permute-done.15
  37.2 2.4 %collective-permute-start.16 = (f32[8,128]{1,0:T(8,128)S(1)}, f32[8,128]{1,0:T(8,128)S(1)}, u32[]{:S(2)}, u32[]{:S(2)}) collective-permute-start(f32[8,128]{1,0:T(8,128)S(1)} %add_add_fusion.1), channel_id=1, source_target_pairs={{0,12},{1,13},{2,14},{3,15},{4,8},{5,9},{6,10},{7,11},{8,4},{9,5},... | collective-permute-start | bytes 12296 | tf_op jit(solution)/shard_map/ppermute | solution.py:287
  39.6 1.1 %collective-permute-start.17 = (f32[8,128]{1,0:T(8,128)S(1)}, f32[8,128]{1,0:T(8,128)S(1)}, u32[]{:S(2)}, u32[]{:S(2)}) collective-permute-start(f32[8,128]{1,0:T(8,128)S(1)} %add_add_fusion.1), channel_id=1, source_target_pairs={{0,8},{1,9},{2,10},{3,11},{4,12},{5,13},{6,14},{7,15},{8,0},{9,1},... | collective-permute-start | bytes 12296 | tf_op jit(solution)/shard_map/ppermute | solution.py:287
  40.7 1.0 %collective-permute-start.18 = (f32[8,128]{1,0:T(8,128)S(1)}, f32[8,128]{1,0:T(8,128)S(1)}, u32[]{:S(2)}, u32[]{:S(2)}) collective-permute-start(f32[8,128]{1,0:T(8,128)S(1)} %add_add_fusion.1), channel_id=1, source_target_pairs={{0,4},{1,5},{2,6},{3,7},{4,0},{5,1},{6,2},{7,3},{8,12},{9,13},{10,... | collective-permute-start | bytes 12296 | tf_op jit(solution)/shard_map/ppermute | solution.py:287
  41.6 0.8 %shard_map.121 = bf16[16,64,128]{2,1,0:T(8,128)(2,1)} custom-call(bf16[128,1024]{1,0:T(8,128)(2,1)S(1)} %get-tuple-element.34.turned_ref), custom_call_target="tpu_custom_call" | custom-call | flops 67108864 | bytes 1048576 | tf_op jit(solution)/shard_map/pallas_call | solution.py:291
  42.5 0.2 collective-permute-done.16
  42.6 1.4 %collective-permute-done.17 = f32[8,128]{1,0:T(8,128)S(1)} collective-permute-done((f32[8,128]{1,0:T(8,128)S(1)}, f32[8,128]{1,0:T(8,128)S(1)}, u32[]{:S(2)}, u32[]{:S(2)}) %collective-permute-start.17) | collective-permute-done | bytes 4128 | tf_op jit(solution)/shard_map/ppermute | solution.py:287
  44.1 0.2 collective-permute-done.18
  44.3 0.5 %slice.3 = f32[1,1]{1,0:T(1,128)} slice(f32[8,128]{1,0:T(8,128)S(1)} %add_add_fusion), slice={[0:1], [0:1]} | slice | bytes 8 | tf_op jit(solution)/shard_map/slice | solution.py:414
  (10 shorter events, 0.0 us)
Async XLA Ops:
  0.6 11.6 %collective-permute-start.1 = (bf16[16,64,128]{2,1,0:T(8,128)(2,1)}, bf16[16,64,128]{2,1,0:T(8,128)(2,1)S(1)}, u32[]{:S(2)}, u32[]{:S(2)}) collective-permute-start(bf16[16,64,128]{2,1,0:T(8,128)(2,1)} %x_ref.3), channel_id=1, source_target_pairs={{0,4},{1,5},{2,6},{3,7},{4,0},{5,1},{6,2},{7,3},{8,12},{9,13},{10,... | collective-permute-start | bytes 786440 | tf_op jit(solution)/shard_map/ppermute | solution.py:287
  3.7 1.0 %copy-start = (bf16[16,64,128]{2,1,0:T(8,128)(2,1)S(1)}, bf16[16,64,128]{2,1,0:T(8,128)(2,1)}, u32[]{:S(2)}) copy-start(bf16[16,64,128]{2,1,0:T(8,128)(2,1)} %x_ref.3) | copy-start | bytes 786436
  4.7 0.8 %copy-start.6 = (bf16[128,128]{1,0:T(8,128)(2,1)S(1)}, bf16[128,128]{1,0:T(8,128)(2,1)}, u32[]{:S(2)}) copy-start(bf16[128,128]{1,0:T(8,128)(2,1)} %rw_ref.1) | copy-start | bytes 98308
  4.7 0.8 %copy-start.7 = (bf16[128,128]{1,0:T(8,128)(2,1)S(1)}, bf16[128,128]{1,0:T(8,128)(2,1)}, u32[]{:S(2)}) copy-start(bf16[128,128]{1,0:T(8,128)(2,1)} %rg_ref.1) | copy-start | bytes 98308
  5.5 3.2 %copy-start.4 = (bf16[128,128]{1,0:T(8,128)(2,1)S(1)}, bf16[128,128]{1,0:T(8,128)(2,1)}, u32[]{:S(2)}) copy-start(bf16[128,128]{1,0:T(8,128)(2,1)} %lw_ref.1) | copy-start | bytes 98308
  5.5 3.2 %copy-start.5 = (bf16[128,128]{1,0:T(8,128)(2,1)S(1)}, bf16[128,128]{1,0:T(8,128)(2,1)}, u32[]{:S(2)}) copy-start(bf16[128,128]{1,0:T(8,128)(2,1)} %lg_ref.1) | copy-start | bytes 98308
  6.0 2.7 %copy-start.8 = (s32[5]{0:T(128)S(1)}, s32[5]{0:T(128)}, u32[]{:S(2)}) copy-start(s32[5]{0:T(128)} %lens_ref.1) | copy-start | bytes 64
  6.1 13.0 %collective-permute-start.3 = (bf16[512,128]{1,0:T(8,128)(2,1)S(1)}, bf16[512,128]{1,0:T(8,128)(2,1)S(1)}, u32[]{:S(2)}, u32[]{:S(2)}) collective-permute-start(bf16[512,128]{1,0:T(8,128)(2,1)S(1)} %get-tuple-element.19.stay_ref), channel_id=1, source_target_pairs={{0,8},{1,9},{2,10},{3,11},{4,12},{5,13},{6,14},{7,15},{8,0},{9,1},... | collective-permute-start | bytes 393224 | tf_op jit(solution)/shard_map/ppermute | solution.py:287
  8.7 10.3 %collective-permute-start.4 = (bf16[512,128]{1,0:T(8,128)(2,1)S(1)}, bf16[512,128]{1,0:T(8,128)(2,1)S(1)}, u32[]{:S(2)}, u32[]{:S(2)}) collective-permute-start(bf16[512,128]{1,0:T(8,128)(2,1)S(1)} %get-tuple-element.29), channel_id=1, source_target_pairs={{0,12},{1,13},{2,14},{3,15},{4,8},{5,9},{6,10},{7,11},{8,4},{9,5},... | collective-permute-start | bytes 393224 | tf_op jit(solution)/shard_map/ppermute | solution.py:287
  13.3 5.8 %collective-permute-start.2 = (bf16[512,128]{1,0:T(8,128)(2,1)S(1)}, bf16[512,128]{1,0:T(8,128)(2,1)S(1)}, u32[]{:S(2)}, u32[]{:S(2)}) collective-permute-start(bf16[512,128]{1,0:T(8,128)(2,1)S(1)} %get-tuple-element.28), channel_id=1, source_target_pairs={{0,2},{1,3},{2,0},{3,1},{4,6},{5,7},{6,4},{7,5},{8,10},{9,11},{10,... | collective-permute-start | bytes 393224 | tf_op jit(solution)/shard_map/ppermute | solution.py:287
  13.3 5.8 %collective-permute-start = (bf16[512,128]{1,0:T(8,128)(2,1)S(1)}, bf16[512,128]{1,0:T(8,128)(2,1)S(1)}, u32[]{:S(2)}, u32[]{:S(2)}) collective-permute-start(bf16[512,128]{1,0:T(8,128)(2,1)S(1)} %get-tuple-element.26), channel_id=1, source_target_pairs={{0,2},{1,3},{2,0},{3,1},{4,6},{5,7},{6,4},{7,5},{8,10},{9,11},{10,... | collective-permute-start | bytes 393224 | tf_op jit(solution)/shard_map/ppermute | solution.py:287
  19.1 1.4 %collective-permute-start.5 = (bf16[512,128]{1,0:T(8,128)(2,1)S(1)}, bf16[512,128]{1,0:T(8,128)(2,1)S(1)}, u32[]{:S(2)}, u32[]{:S(2)}) collective-permute-start(bf16[512,128]{1,0:T(8,128)(2,1)S(1)} %shard_map.118), channel_id=1, source_target_pairs={{0,2},{1,3},{2,0},{3,1},{4,6},{5,7},{6,4},{7,5},{8,10},{9,11},{10,... | collective-permute-start | bytes 393224 | tf_op jit(solution)/shard_map/ppermute | solution.py:287
  20.5 10.4 %copy-start.9 = (bf16[128,64]{0,1:T(8,128)(2,1)S(1)}, bf16[128,64]{0,1:T(8,128)(2,1)}, u32[]{:S(2)}) copy-start(bf16[128,64]{0,1:T(8,128)(2,1)} %param.19) | copy-start | bytes 49156
  20.5 10.5 %copy-start.10 = (s32[16,64]{1,0:T(8,128)S(1)}, s32[16,64]{1,0:T(8,128)}, u32[]{:S(2)}) copy-start(s32[16,64]{1,0:T(8,128)} %param.11) | copy-start | bytes 12292
  20.5 10.6 %copy-start.1 = (bf16[16,64,128]{2,1,0:T(8,128)(2,1)S(1)}, bf16[16,64,128]{2,1,0:T(8,128)(2,1)}, u32[]{:S(2)}) copy-start(bf16[16,64,128]{2,1,0:T(8,128)(2,1)} %x_ref.3) | copy-start | bytes 786436
  21.0 7.3 %collective-permute-start.6 = (bf16[512,128]{1,0:T(8,128)(2,1)S(1)}, bf16[512,128]{1,0:T(8,128)(2,1)S(1)}, u32[]{:S(2)}, u32[]{:S(2)}) collective-permute-start(bf16[512,128]{1,0:T(8,128)(2,1)S(1)} %get-tuple-element.31), channel_id=1, source_target_pairs={{0,5},{1,4},{2,7},{3,6},{4,1},{5,0},{6,3},{7,2},{8,13},{9,12},{10,... | collective-permute-start | bytes 393224 | tf_op jit(solution)/shard_map/ppermute | solution.py:287
  24.0 7.1 %copy-start.3 = (bf16[128,128]{1,0:T(8,128)(2,1)S(1)}, bf16[128,128]{1,0:T(8,128)(2,1)}, u32[]{:S(2)}) copy-start(bf16[128,128]{1,0:T(8,128)(2,1)} %ow_ref.1) | copy-start | bytes 98308
  24.0 7.1 %copy-start.2 = (bf16[128,128]{1,0:T(8,128)(2,1)S(1)}, bf16[128,128]{1,0:T(8,128)(2,1)}, u32[]{:S(2)}) copy-start(bf16[128,128]{1,0:T(8,128)(2,1)} %gw_ref.1) | copy-start | bytes 98308
  24.0 6.4 %collective-permute-start.7 = (bf16[512,128]{1,0:T(8,128)(2,1)S(1)}, bf16[512,128]{1,0:T(8,128)(2,1)S(1)}, u32[]{:S(2)}, u32[]{:S(2)}) collective-permute-start(bf16[512,128]{1,0:T(8,128)(2,1)S(1)} %get-tuple-element.32), channel_id=1, source_target_pairs={{0,4},{1,5},{2,6},{3,7},{4,0},{5,1},{6,2},{7,3},{8,12},{9,13},{10,... | collective-permute-start | bytes 393224 | tf_op jit(solution)/shard_map/ppermute | solution.py:287
  24.1 6.6 %collective-permute-start.8 = (bf16[512,128]{1,0:T(8,128)(2,1)S(1)}, bf16[512,128]{1,0:T(8,128)(2,1)S(1)}, u32[]{:S(2)}, u32[]{:S(2)}) collective-permute-start(bf16[512,128]{1,0:T(8,128)(2,1)S(1)} %get-tuple-element.33), channel_id=1, source_target_pairs={{0,1},{1,0},{2,3},{3,2},{4,5},{5,4},{6,7},{7,6},{8,9},{9,8},{10,11... | collective-permute-start | bytes 393224 | tf_op jit(solution)/shard_map/ppermute | solution.py:287
  24.7 6.8 %collective-permute-start.9 = (bf16[512,128]{1,0:T(8,128)(2,1)S(1)}, bf16[512,128]{1,0:T(8,128)(2,1)S(1)}, u32[]{:S(2)}, u32[]{:S(2)}) collective-permute-start(bf16[512,128]{1,0:T(8,128)(2,1)S(1)} %get-tuple-element.30.refs_0_), channel_id=1, source_target_pairs={{0,2},{1,3},{2,0},{3,1},{4,6},{5,7},{6,4},{7,5},{8,10},{9,11},{10,... | collective-permute-start | bytes 393224 | tf_op jit(solution)/shard_map/ppermute | solution.py:287
  28.3 3.2 %collective-permute-start.10 = (bf16[512,128]{1,0:T(8,128)(2,1)S(1)}, bf16[512,128]{1,0:T(8,128)(2,1)S(1)}, u32[]{:S(2)}, u32[]{:S(2)}) collective-permute-start(bf16[512,128]{1,0:T(8,128)(2,1)S(1)} %collective-permute-done.6.refs_1_), channel_id=1, source_target_pairs={{0,2},{1,3},{2,0},{3,1},{4,6},{5,7},{6,4},{7,5},{8,10},{9,11},{10,... | collective-permute-start | bytes 393224 | tf_op jit(solution)/shard_map/ppermute | solution.py:287
  30.4 1.3 %collective-permute-start.11 = (bf16[512,128]{1,0:T(8,128)(2,1)S(1)}, bf16[512,128]{1,0:T(8,128)(2,1)S(1)}, u32[]{:S(2)}, u32[]{:S(2)}) collective-permute-start(bf16[512,128]{1,0:T(8,128)(2,1)S(1)} %collective-permute-done.7.refs_2_), channel_id=1, source_target_pairs={{0,2},{1,3},{2,0},{3,1},{4,6},{5,7},{6,4},{7,5},{8,10},{9,11},{10,... | collective-permute-start | bytes 393224 | tf_op jit(solution)/shard_map/ppermute | solution.py:287
  30.6 1.3 %collective-permute-start.12 = (bf16[512,128]{1,0:T(8,128)(2,1)S(1)}, bf16[512,128]{1,0:T(8,128)(2,1)S(1)}, u32[]{:S(2)}, u32[]{:S(2)}) collective-permute-start(bf16[512,128]{1,0:T(8,128)(2,1)S(1)} %collective-permute-done.8.refs_3_), channel_id=1, source_target_pairs={{0,2},{1,3},{2,0},{3,1},{4,6},{5,7},{6,4},{7,5},{8,10},{9,11},{10,... | collective-permute-start | bytes 393224 | tf_op jit(solution)/shard_map/ppermute | solution.py:287
  32.9 3.6 %collective-permute-start.13 = (f32[8,128]{1,0:T(8,128)S(1)}, f32[8,128]{1,0:T(8,128)S(1)}, u32[]{:S(2)}, u32[]{:S(2)}) collective-permute-start(f32[8,128]{1,0:T(8,128)S(1)} %get-tuple-element.35), channel_id=1, source_target_pairs={{0,1},{1,0},{2,3},{3,2},{4,5},{5,4},{6,7},{7,6},{8,9},{9,8},{10,11... | collective-permute-start | bytes 12296 | tf_op jit(solution)/shard_map/ppermute | solution.py:287
  34.1 3.0 %collective-permute-start.14 = (f32[8,128]{1,0:T(8,128)S(1)}, f32[8,128]{1,0:T(8,128)S(1)}, u32[]{:S(2)}, u32[]{:S(2)}) collective-permute-start(f32[8,128]{1,0:T(8,128)S(1)} %get-tuple-element.35), channel_id=1, source_target_pairs={{0,3},{1,2},{2,1},{3,0},{4,7},{5,6},{6,5},{7,4},{8,11},{9,10},{10,... | collective-permute-start | bytes 12296 | tf_op jit(solution)/shard_map/ppermute | solution.py:287
  34.5 2.6 %collective-permute-start.15 = (f32[8,128]{1,0:T(8,128)S(1)}, f32[8,128]{1,0:T(8,128)S(1)}, u32[]{:S(2)}, u32[]{:S(2)}) collective-permute-start(f32[8,128]{1,0:T(8,128)S(1)} %get-tuple-element.35), channel_id=1, source_target_pairs={{0,2},{1,3},{2,0},{3,1},{4,6},{5,7},{6,4},{7,5},{8,10},{9,11},{10,... | collective-permute-start | bytes 12296 | tf_op jit(solution)/shard_map/ppermute | solution.py:287
  37.2 5.5 %collective-permute-start.16 = (f32[8,128]{1,0:T(8,128)S(1)}, f32[8,128]{1,0:T(8,128)S(1)}, u32[]{:S(2)}, u32[]{:S(2)}) collective-permute-start(f32[8,128]{1,0:T(8,128)S(1)} %add_add_fusion.1), channel_id=1, source_target_pairs={{0,12},{1,13},{2,14},{3,15},{4,8},{5,9},{6,10},{7,11},{8,4},{9,5},... | collective-permute-start | bytes 12296 | tf_op jit(solution)/shard_map/ppermute | solution.py:287
  39.6 4.5 %collective-permute-start.17 = (f32[8,128]{1,0:T(8,128)S(1)}, f32[8,128]{1,0:T(8,128)S(1)}, u32[]{:S(2)}, u32[]{:S(2)}) collective-permute-start(f32[8,128]{1,0:T(8,128)S(1)} %add_add_fusion.1), channel_id=1, source_target_pairs={{0,8},{1,9},{2,10},{3,11},{4,12},{5,13},{6,14},{7,15},{8,0},{9,1},... | collective-permute-start | bytes 12296 | tf_op jit(solution)/shard_map/ppermute | solution.py:287
  40.7 3.6 %collective-permute-start.18 = (f32[8,128]{1,0:T(8,128)S(1)}, f32[8,128]{1,0:T(8,128)S(1)}, u32[]{:S(2)}, u32[]{:S(2)}) collective-permute-start(f32[8,128]{1,0:T(8,128)S(1)} %add_add_fusion.1), channel_id=1, source_target_pairs={{0,4},{1,5},{2,6},{3,7},{4,0},{5,1},{6,2},{7,3},{8,12},{9,13},{10,... | collective-permute-start | bytes 12296 | tf_op jit(solution)/shard_map/ppermute | solution.py:287

commit v19 on v18

--- a/solution.py
+++ b/solution.py
@@ -403,10 +403,10 @@
         flops=6 * spots * channels * channels,
     )
     pair_out = call(turn_back_kernel, struct(pair_repr.shape, bf16), args=(pair_out,), flops=1 << 26)
-    beside, beside_over, sibling = [
-        exchange(loss, places, mask) for mask in (over_x, over_x + over_core, over_core)
+    beside_over, beside, sibling = [
+        exchange(loss, places, mask) for mask in (over_x + over_core, over_x, over_core)
     ]
-    loss = (beside + beside_over) + (sibling + loss)
+    loss = (beside_over + beside) + (sibling + loss)
     cross_loss, half, near_loss = [
         exchange(loss, places, mask) for mask in (over_half + over_z, over_half, over_z)
     ]

time: 45 us -> 45.4 us (level)
  waiting for transfers between devices: 19.3 us -> 19.8 us
    ppermute x19, waiting for transfers between devices: 19.3 us -> 19.8 us  [exchange(): return lax.ppermute(value, AXES, [(at, at ^ mask) for at in range(places)])]
where the time goes in v19:
time: 45.4 us; the launch traced here: 45.1 us
  waiting for transfers between devices  19.8 us (44%)
  starting transfers between devices  16.7 us (37%)
  Pallas kernels  5.69 us (13%)
  local copies, waits for them, and re-layouts  2.13 us (5%)
  between operations  0.78 us (2%)
    ppermute x19, waiting for transfers between devices, exchange(): return lax.ppermute(value, AXES, [(at, at ^ mask) for at in range(places)])  19.8 us
    ppermute x19, starting transfers between devices, exchange(): return lax.ppermute(value, AXES, [(at, at ^ mask) for at in range(places)])  16.7 us
    pallas_call x9, Pallas kernels, call(): pl.pallas_call(kernel, out_shape=outs, in_specs=specs if specs is not Non...  5.69 us
    unnamed x23, local copies, waits for them, and re-layouts  1.54 us
  transfers between devices with their start and end apart: 19, of which 13 were waited for; matrix products, arithmetic and copies ran while one was open for 0% of the time, Pallas kernels for 9%

profile of v19, /device:TPU:0, one launch (start us, length us, event | category | flops | bytes accessed | tf_op | source)
XLA Modules:
  0.0 45.1 jit_solution(13537478589287456554)
XLA Ops:
  0.6 3.1 %collective-permute-start.1 = (bf16[16,64,128]{2,1,0:T(8,128)(2,1)}, bf16[16,64,128]{2,1,0:T(8,128)(2,1)S(1)}, u32[]{:S(2)}, u32[]{:S(2)}) collective-permute-start(bf16[16,64,128]{2,1,0:T(8,128)(2,1)} %x_ref.3), channel_id=1, source_target_pairs={{0,4},{1,5},{2,6},{3,7},{4,0},{5,1},{6,2},{7,3},{8,12},{9,13},{10,... | collective-permute-start | bytes 786440 | tf_op jit(solution)/shard_map/ppermute | solution.py:287
  3.7 0.0 copy-start
  3.7 1.0 %copy-done = bf16[16,64,128]{2,1,0:T(8,128)(2,1)S(1)} copy-done((bf16[16,64,128]{2,1,0:T(8,128)(2,1)S(1)}, bf16[16,64,128]{2,1,0:T(8,128)(2,1)}, u32[]{:S(2)}) %copy-start) | copy-done | bytes 262168
  4.7 0.0 copy-start.6
  4.7 0.0 copy-start.7
  4.7 0.4 shard_map.113.normed_ref
  5.1 0.4 copy-done.6
  5.5 0.0 copy-done.7
  5.5 0.6 %shard_map.114 = (bf16[512,128]{1,0:T(8,128)(2,1)S(1)}, bf16[512,128]{1,0:T(8,128)(2,1)S(1)}) custom-call(bf16[1024,128]{1,0:T(8,128)(2,1)S(1)} %shard_map.113.normed_ref, bf16[128,128]{1,0:T(8,128)(2,1)S(1)} %copy-done.6, bf16[128,128]{1,0:T(8,128)(2,1)S(1)} %copy-done.7), custom_call_target="tpu_custom_call" | custom-call | flops 67108864 | bytes 1048576 | tf_op jit(solution)/shard_map/pallas_call | solution.py:291
  6.0 0.0 copy-start.8
  6.1 2.7 %collective-permute-start.3 = (bf16[512,128]{1,0:T(8,128)(2,1)S(1)}, bf16[512,128]{1,0:T(8,128)(2,1)S(1)}, u32[]{:S(2)}, u32[]{:S(2)}) collective-permute-start(bf16[512,128]{1,0:T(8,128)(2,1)S(1)} %get-tuple-element.19.stay_ref), channel_id=1, source_target_pairs={{0,8},{1,9},{2,10},{3,11},{4,12},{5,13},{6,14},{7,15},{8,0},{9,1},... | collective-permute-start | bytes 393224 | tf_op jit(solution)/shard_map/ppermute | solution.py:287
  8.7 0.0 collective-permute-start.4
  8.7 0.0 copy-done.4
  8.7 0.0 copy-done.5
  8.7 0.0 copy-done.8
  8.7 1.0 %shard_map.115 = (bf16[512,128]{1,0:T(8,128)(2,1)S(1)}, bf16[512,128]{1,0:T(8,128)(2,1)S(1)}, f32[24,128]{1,0:T(8,128)S(1)}) custom-call(s32[5]{0:T(128)S(1)} %copy-done.8, bf16[1024,128]{1,0:T(8,128)(2,1)S(1)} %shard_map.113.normed_ref, bf16[128,128]{1,0:T(8,128)(2,1)S(1)} %copy-done.4, bf16[128,128]{1,0:T(8,128)(2,1)S(1)} %copy-done.5, ...), custom_call_target="tpu_custom_call" | custom-call | flops 33554432 | bytes 1048576 | tf_op jit(solution)/shard_map/pallas_call | solution.py:291
  9.8 2.4 %collective-permute-done.1.x_ref = bf16[16,64,128]{2,1,0:T(8,128)(2,1)S(1)} collective-permute-done((bf16[16,64,128]{2,1,0:T(8,128)(2,1)}, bf16[16,64,128]{2,1,0:T(8,128)(2,1)S(1)}, u32[]{:S(2)}, u32[]{:S(2)}) %collective-permute-start.1) | collective-permute-done | bytes 262176 | tf_op jit(solution)/shard_map/ppermute | solution.py:287
  12.2 1.1 %shard_map.117 = (bf16[512,128]{1,0:T(8,128)(2,1)S(1)}, bf16[512,128]{1,0:T(8,128)(2,1)S(1)}) custom-call(f32[24,128]{1,0:T(8,128)S(1)} %get-tuple-element.20.masks_ref, bf16[16,64,128]{2,1,0:T(8,128)(2,1)S(1)} %collective-permute-done.1.x_ref, bf16[128,128]{1,0:T(8,128)(2,1)S(1)} %copy-done.4, bf16[128,128]{1,0:T(8,128)(2,1)S(1)} %copy-done.5, ...), custom_call_target="tpu_custom_call" | custom-call | flops 67108864 | bytes 1048576 | tf_op jit(solution)/shard_map/pallas_call | solution.py:291
  13.3 0.1 collective-permute-start.2
  13.3 0.5 %collective-permute-start = (bf16[512,128]{1,0:T(8,128)(2,1)S(1)}, bf16[512,128]{1,0:T(8,128)(2,1)S(1)}, u32[]{:S(2)}, u32[]{:S(2)}) collective-permute-start(bf16[512,128]{1,0:T(8,128)(2,1)S(1)} %get-tuple-element.26), channel_id=1, source_target_pairs={{0,2},{1,3},{2,0},{3,1},{4,6},{5,7},{6,4},{7,5},{8,10},{9,11},{10,... | collective-permute-start | bytes 393224 | tf_op jit(solution)/shard_map/ppermute | solution.py:287
  13.8 5.2 %collective-permute-done.3.far_ref.far = bf16[512,128]{1,0:T(8,128)(2,1)S(1)} collective-permute-done((bf16[512,128]{1,0:T(8,128)(2,1)S(1)}, bf16[512,128]{1,0:T(8,128)(2,1)S(1)}, u32[]{:S(2)}, u32[]{:S(2)}) %collective-permute-start.3) | collective-permute-done | bytes 131104 | tf_op jit(solution)/shard_map/ppermute | solution.py:287
  19.1 0.0 collective-permute-done.4.cross_ref.cross
  19.1 0.0 collective-permute-done.2.ready_ref.near_over
  19.1 0.1 collective-permute-start.5
  19.2 0.0 collective-permute-done.core
  19.2 1.3 %collective-permute-done.5.both_over = bf16[512,128]{1,0:T(8,128)(2,1)S(1)} collective-permute-done((bf16[512,128]{1,0:T(8,128)(2,1)S(1)}, bf16[512,128]{1,0:T(8,128)(2,1)S(1)}, u32[]{:S(2)}, u32[]{:S(2)}) %collective-permute-start.5) | collective-permute-done | bytes 131104 | tf_op jit(solution)/shard_map/ppermute | solution.py:287
  20.5 0.5 %shard_map.119 = (bf16[512,128]{1,0:T(8,128)(2,1)S(1)}, bf16[512,128]{1,0:T(8,128)(2,1)S(1)}, bf16[512,128]{1,0:T(8,128)(2,1)S(1)}, bf16[512,128]{1,0:T(8,128)(2,1)S(1)}) custom-call(f32[24,128]{1,0:T(8,128)S(1)} %get-tuple-element.20.masks_ref, bf16[512,128]{1,0:T(8,128)(2,1)S(1)} %get-tuple-element.25.own, bf16[512,128]{1,0:T(8,128)(2,1)S(1)} %collective-permute-done.core, ...), custom_call_target="tpu_custom_call" | custom-call | flops 16777216 | bytes 1048576 | tf_op jit(solution)/shard_map/pallas_call | solution.py:291
  21.0 3.0 %collective-permute-start.6 = (bf16[512,128]{1,0:T(8,128)(2,1)S(1)}, bf16[512,128]{1,0:T(8,128)(2,1)S(1)}, u32[]{:S(2)}, u32[]{:S(2)}) collective-permute-start(bf16[512,128]{1,0:T(8,128)(2,1)S(1)} %get-tuple-element.31), channel_id=1, source_target_pairs={{0,5},{1,4},{2,7},{3,6},{4,1},{5,0},{6,3},{7,2},{8,13},{9,12},{10,... | collective-permute-start | bytes 393224 | tf_op jit(solution)/shard_map/ppermute | solution.py:287
  24.0 0.1 collective-permute-start.7
  24.1 0.6 %collective-permute-start.8 = (bf16[512,128]{1,0:T(8,128)(2,1)S(1)}, bf16[512,128]{1,0:T(8,128)(2,1)S(1)}, u32[]{:S(2)}, u32[]{:S(2)}) collective-permute-start(bf16[512,128]{1,0:T(8,128)(2,1)S(1)} %get-tuple-element.33), channel_id=1, source_target_pairs={{0,1},{1,0},{2,3},{3,2},{4,5},{5,4},{6,7},{7,6},{8,9},{9,8},{10,11... | collective-permute-start | bytes 393224 | tf_op jit(solution)/shard_map/ppermute | solution.py:287
  24.7 0.0 collective-permute-start.9
  24.7 3.6 %collective-permute-done.6.refs_1_ = bf16[512,128]{1,0:T(8,128)(2,1)S(1)} collective-permute-done((bf16[512,128]{1,0:T(8,128)(2,1)S(1)}, bf16[512,128]{1,0:T(8,128)(2,1)S(1)}, u32[]{:S(2)}, u32[]{:S(2)}) %collective-permute-start.6) | collective-permute-done | bytes 131104 | tf_op jit(solution)/shard_map/ppermute | solution.py:287
  28.3 0.0 collective-permute-start.10
  28.3 2.1 %collective-permute-done.7.refs_2_ = bf16[512,128]{1,0:T(8,128)(2,1)S(1)} collective-permute-done((bf16[512,128]{1,0:T(8,128)(2,1)S(1)}, bf16[512,128]{1,0:T(8,128)(2,1)S(1)}, u32[]{:S(2)}, u32[]{:S(2)}) %collective-permute-start.7) | collective-permute-done | bytes 131104 | tf_op jit(solution)/shard_map/ppermute | solution.py:287
  30.4 0.0 collective-permute-start.11
  30.4 0.2 collective-permute-done.8.refs_3_
  30.6 0.3 collective-permute-start.12
  30.9 0.0 copy-done.9
  30.9 0.1 copy.12.dw_ref
  31.0 0.0 copy-done.10
  31.0 0.1 reshape.7.bins_ref
  31.1 0.0 copy-done.1
  31.1 0.0 copy-done.3
  31.1 0.0 copy-done.2
  31.1 0.4 shard_map.116
  31.5 0.0 collective-permute-done.9.refs_4_
  31.5 0.0 collective-permute-done.10.refs_5_
  31.5 0.2 collective-permute-done.11.refs_6_
  31.7 0.2 collective-permute-done.12.refs_7_
  32.0 0.9 %shard_map.120 = (bf16[128,1024]{1,0:T(8,128)(2,1)S(1)}, f32[8,128]{1,0:T(8,128)S(1)}) custom-call(f32[24,128]{1,0:T(8,128)S(1)} %get-tuple-element.20.masks_ref, f32[128,1024]{1,0:T(8,128)S(1)} %get-tuple-element.21.x_ref, f32[128,1024]{1,0:T(8,128)S(1)} %get-tuple-element.22.gate_ref, s32[8,128]{1,0:T(8,128)S(1)} %reshape.7.bins_ref, ...), custom_call_target="tpu_custom_call" | custom-call | flops 100663296 | bytes 1048576 | tf_op jit(solution)/shard_map/pallas_call | solution.py:291
  32.9 1.0 %collective-permute-start.13 = (f32[8,128]{1,0:T(8,128)S(1)}, f32[8,128]{1,0:T(8,128)S(1)}, u32[]{:S(2)}, u32[]{:S(2)}) collective-permute-start(f32[8,128]{1,0:T(8,128)S(1)} %get-tuple-element.35), channel_id=1, source_target_pairs={{0,3},{1,2},{2,1},{3,0},{4,7},{5,6},{6,5},{7,4},{8,11},{9,10},{10,... | collective-permute-start | bytes 12296 | tf_op jit(solution)/shard_map/ppermute | solution.py:287
  33.9 0.9 %collective-permute-start.14 = (f32[8,128]{1,0:T(8,128)S(1)}, f32[8,128]{1,0:T(8,128)S(1)}, u32[]{:S(2)}, u32[]{:S(2)}) collective-permute-start(f32[8,128]{1,0:T(8,128)S(1)} %get-tuple-element.35), channel_id=1, source_target_pairs={{0,1},{1,0},{2,3},{3,2},{4,5},{5,4},{6,7},{7,6},{8,9},{9,8},{10,11... | collective-permute-start | bytes 12296 | tf_op jit(solution)/shard_map/ppermute | solution.py:287
  34.8 0.0 collective-permute-start.15
  34.8 1.1 %collective-permute-done.13 = f32[8,128]{1,0:T(8,128)S(1)} collective-permute-done((f32[8,128]{1,0:T(8,128)S(1)}, f32[8,128]{1,0:T(8,128)S(1)}, u32[]{:S(2)}, u32[]{:S(2)}) %collective-permute-start.13) | collective-permute-done | bytes 4128 | tf_op jit(solution)/shard_map/ppermute | solution.py:287
  35.9 1.6 %collective-permute-done.14 = f32[8,128]{1,0:T(8,128)S(1)} collective-permute-done((f32[8,128]{1,0:T(8,128)S(1)}, f32[8,128]{1,0:T(8,128)S(1)}, u32[]{:S(2)}, u32[]{:S(2)}) %collective-permute-start.14) | collective-permute-done | bytes 4128 | tf_op jit(solution)/shard_map/ppermute | solution.py:287
  37.5 0.0 collective-permute-done.15
  37.5 2.4 %collective-permute-start.16 = (f32[8,128]{1,0:T(8,128)S(1)}, f32[8,128]{1,0:T(8,128)S(1)}, u32[]{:S(2)}, u32[]{:S(2)}) collective-permute-start(f32[8,128]{1,0:T(8,128)S(1)} %add_add_fusion.1), channel_id=1, source_target_pairs={{0,12},{1,13},{2,14},{3,15},{4,8},{5,9},{6,10},{7,11},{8,4},{9,5},... | collective-permute-start | bytes 12296 | tf_op jit(solution)/shard_map/ppermute | solution.py:287
  39.9 1.1 %collective-permute-start.17 = (f32[8,128]{1,0:T(8,128)S(1)}, f32[8,128]{1,0:T(8,128)S(1)}, u32[]{:S(2)}, u32[]{:S(2)}) collective-permute-start(f32[8,128]{1,0:T(8,128)S(1)} %add_add_fusion.1), channel_id=1, source_target_pairs={{0,8},{1,9},{2,10},{3,11},{4,12},{5,13},{6,14},{7,15},{8,0},{9,1},... | collective-permute-start | bytes 12296 | tf_op jit(solution)/shard_map/ppermute | solution.py:287
  41.0 1.0 %collective-permute-start.18 = (f32[8,128]{1,0:T(8,128)S(1)}, f32[8,128]{1,0:T(8,128)S(1)}, u32[]{:S(2)}, u32[]{:S(2)}) collective-permute-start(f32[8,128]{1,0:T(8,128)S(1)} %add_add_fusion.1), channel_id=1, source_target_pairs={{0,4},{1,5},{2,6},{3,7},{4,0},{5,1},{6,2},{7,3},{8,12},{9,13},{10,... | collective-permute-start | bytes 12296 | tf_op jit(solution)/shard_map/ppermute | solution.py:287
  42.0 0.8 %shard_map.121 = bf16[16,64,128]{2,1,0:T(8,128)(2,1)} custom-call(bf16[128,1024]{1,0:T(8,128)(2,1)S(1)} %get-tuple-element.34.turned_ref), custom_call_target="tpu_custom_call" | custom-call | flops 67108864 | bytes 1048576 | tf_op jit(solution)/shard_map/pallas_call | solution.py:291
  42.8 0.2 collective-permute-done.16
  43.0 1.4 %collective-permute-done.17 = f32[8,128]{1,0:T(8,128)S(1)} collective-permute-done((f32[8,128]{1,0:T(8,128)S(1)}, f32[8,128]{1,0:T(8,128)S(1)}, u32[]{:S(2)}, u32[]{:S(2)}) %collective-permute-start.17) | collective-permute-done | bytes 4128 | tf_op jit(solution)/shard_map/ppermute | solution.py:287
  44.4 0.2 collective-permute-done.18
  44.6 0.5 %slice.3 = f32[1,1]{1,0:T(1,128)} slice(f32[8,128]{1,0:T(8,128)S(1)} %add_add_fusion), slice={[0:1], [0:1]} | slice | bytes 8 | tf_op jit(solution)/shard_map/slice | solution.py:414
  (10 shorter events, 0.0 us)
Async XLA Ops:
  0.6 11.6 %collective-permute-start.1 = (bf16[16,64,128]{2,1,0:T(8,128)(2,1)}, bf16[16,64,128]{2,1,0:T(8,128)(2,1)S(1)}, u32[]{:S(2)}, u32[]{:S(2)}) collective-permute-start(bf16[16,64,128]{2,1,0:T(8,128)(2,1)} %x_ref.3), channel_id=1, source_target_pairs={{0,4},{1,5},{2,6},{3,7},{4,0},{5,1},{6,2},{7,3},{8,12},{9,13},{10,... | collective-permute-start | bytes 786440 | tf_op jit(solution)/shard_map/ppermute | solution.py:287
  3.7 1.0 %copy-start = (bf16[16,64,128]{2,1,0:T(8,128)(2,1)S(1)}, bf16[16,64,128]{2,1,0:T(8,128)(2,1)}, u32[]{:S(2)}) copy-start(bf16[16,64,128]{2,1,0:T(8,128)(2,1)} %x_ref.3) | copy-start | bytes 786436
  4.7 0.8 %copy-start.6 = (bf16[128,128]{1,0:T(8,128)(2,1)S(1)}, bf16[128,128]{1,0:T(8,128)(2,1)}, u32[]{:S(2)}) copy-start(bf16[128,128]{1,0:T(8,128)(2,1)} %rw_ref.1) | copy-start | bytes 98308
  4.7 0.8 %copy-start.7 = (bf16[128,128]{1,0:T(8,128)(2,1)S(1)}, bf16[128,128]{1,0:T(8,128)(2,1)}, u32[]{:S(2)}) copy-start(bf16[128,128]{1,0:T(8,128)(2,1)} %rg_ref.1) | copy-start | bytes 98308
  5.5 3.2 %copy-start.4 = (bf16[128,128]{1,0:T(8,128)(2,1)S(1)}, bf16[128,128]{1,0:T(8,128)(2,1)}, u32[]{:S(2)}) copy-start(bf16[128,128]{1,0:T(8,128)(2,1)} %lw_ref.1) | copy-start | bytes 98308
  5.5 3.2 %copy-start.5 = (bf16[128,128]{1,0:T(8,128)(2,1)S(1)}, bf16[128,128]{1,0:T(8,128)(2,1)}, u32[]{:S(2)}) copy-start(bf16[128,128]{1,0:T(8,128)(2,1)} %lg_ref.1) | copy-start | bytes 98308
  6.0 2.7 %copy-start.8 = (s32[5]{0:T(128)S(1)}, s32[5]{0:T(128)}, u32[]{:S(2)}) copy-start(s32[5]{0:T(128)} %lens_ref.1) | copy-start | bytes 64
  6.1 13.0 %collective-permute-start.3 = (bf16[512,128]{1,0:T(8,128)(2,1)S(1)}, bf16[512,128]{1,0:T(8,128)(2,1)S(1)}, u32[]{:S(2)}, u32[]{:S(2)}) collective-permute-start(bf16[512,128]{1,0:T(8,128)(2,1)S(1)} %get-tuple-element.19.stay_ref), channel_id=1, source_target_pairs={{0,8},{1,9},{2,10},{3,11},{4,12},{5,13},{6,14},{7,15},{8,0},{9,1},... | collective-permute-start | bytes 393224 | tf_op jit(solution)/shard_map/ppermute | solution.py:287
  8.7 10.3 %collective-permute-start.4 = (bf16[512,128]{1,0:T(8,128)(2,1)S(1)}, bf16[512,128]{1,0:T(8,128)(2,1)S(1)}, u32[]{:S(2)}, u32[]{:S(2)}) collective-permute-start(bf16[512,128]{1,0:T(8,128)(2,1)S(1)} %get-tuple-element.29), channel_id=1, source_target_pairs={{0,12},{1,13},{2,14},{3,15},{4,8},{5,9},{6,10},{7,11},{8,4},{9,5},... | collective-permute-start | bytes 393224 | tf_op jit(solution)/shard_map/ppermute | solution.py:287
  13.3 5.8 %collective-permute-start.2 = (bf16[512,128]{1,0:T(8,128)(2,1)S(1)}, bf16[512,128]{1,0:T(8,128)(2,1)S(1)}, u32[]{:S(2)}, u32[]{:S(2)}) collective-permute-start(bf16[512,128]{1,0:T(8,128)(2,1)S(1)} %get-tuple-element.28), channel_id=1, source_target_pairs={{0,2},{1,3},{2,0},{3,1},{4,6},{5,7},{6,4},{7,5},{8,10},{9,11},{10,... | collective-permute-start | bytes 393224 | tf_op jit(solution)/shard_map/ppermute | solution.py:287
  13.3 5.8 %collective-permute-start = (bf16[512,128]{1,0:T(8,128)(2,1)S(1)}, bf16[512,128]{1,0:T(8,128)(2,1)S(1)}, u32[]{:S(2)}, u32[]{:S(2)}) collective-permute-start(bf16[512,128]{1,0:T(8,128)(2,1)S(1)} %get-tuple-element.26), channel_id=1, source_target_pairs={{0,2},{1,3},{2,0},{3,1},{4,6},{5,7},{6,4},{7,5},{8,10},{9,11},{10,... | collective-permute-start | bytes 393224 | tf_op jit(solution)/shard_map/ppermute | solution.py:287
  19.1 1.4 %collective-permute-start.5 = (bf16[512,128]{1,0:T(8,128)(2,1)S(1)}, bf16[512,128]{1,0:T(8,128)(2,1)S(1)}, u32[]{:S(2)}, u32[]{:S(2)}) collective-permute-start(bf16[512,128]{1,0:T(8,128)(2,1)S(1)} %shard_map.118), channel_id=1, source_target_pairs={{0,2},{1,3},{2,0},{3,1},{4,6},{5,7},{6,4},{7,5},{8,10},{9,11},{10,... | collective-permute-start | bytes 393224 | tf_op jit(solution)/shard_map/ppermute | solution.py:287
  20.5 10.4 %copy-start.9 = (bf16[128,64]{0,1:T(8,128)(2,1)S(1)}, bf16[128,64]{0,1:T(8,128)(2,1)}, u32[]{:S(2)}) copy-start(bf16[128,64]{0,1:T(8,128)(2,1)} %param.19) | copy-start | bytes 49156
  20.5 10.5 %copy-start.10 = (s32[16,64]{1,0:T(8,128)S(1)}, s32[16,64]{1,0:T(8,128)}, u32[]{:S(2)}) copy-start(s32[16,64]{1,0:T(8,128)} %param.11) | copy-start | bytes 12292
  20.5 10.6 %copy-start.1 = (bf16[16,64,128]{2,1,0:T(8,128)(2,1)S(1)}, bf16[16,64,128]{2,1,0:T(8,128)(2,1)}, u32[]{:S(2)}) copy-start(bf16[16,64,128]{2,1,0:T(8,128)(2,1)} %x_ref.3) | copy-start | bytes 786436
  21.0 7.3 %collective-permute-start.6 = (bf16[512,128]{1,0:T(8,128)(2,1)S(1)}, bf16[512,128]{1,0:T(8,128)(2,1)S(1)}, u32[]{:S(2)}, u32[]{:S(2)}) collective-permute-start(bf16[512,128]{1,0:T(8,128)(2,1)S(1)} %get-tuple-element.31), channel_id=1, source_target_pairs={{0,5},{1,4},{2,7},{3,6},{4,1},{5,0},{6,3},{7,2},{8,13},{9,12},{10,... | collective-permute-start | bytes 393224 | tf_op jit(solution)/shard_map/ppermute | solution.py:287
  24.0 7.1 %copy-start.3 = (bf16[128,128]{1,0:T(8,128)(2,1)S(1)}, bf16[128,128]{1,0:T(8,128)(2,1)}, u32[]{:S(2)}) copy-start(bf16[128,128]{1,0:T(8,128)(2,1)} %ow_ref.1) | copy-start | bytes 98308
  24.0 7.1 %copy-start.2 = (bf16[128,128]{1,0:T(8,128)(2,1)S(1)}, bf16[128,128]{1,0:T(8,128)(2,1)}, u32[]{:S(2)}) copy-start(bf16[128,128]{1,0:T(8,128)(2,1)} %gw_ref.1) | copy-start | bytes 98308
  24.0 6.4 %collective-permute-start.7 = (bf16[512,128]{1,0:T(8,128)(2,1)S(1)}, bf16[512,128]{1,0:T(8,128)(2,1)S(1)}, u32[]{:S(2)}, u32[]{:S(2)}) collective-permute-start(bf16[512,128]{1,0:T(8,128)(2,1)S(1)} %get-tuple-element.32), channel_id=1, source_target_pairs={{0,4},{1,5},{2,6},{3,7},{4,0},{5,1},{6,2},{7,3},{8,12},{9,13},{10,... | collective-permute-start | bytes 393224 | tf_op jit(solution)/shard_map/ppermute | solution.py:287
  24.1 6.6 %collective-permute-start.8 = (bf16[512,128]{1,0:T(8,128)(2,1)S(1)}, bf16[512,128]{1,0:T(8,128)(2,1)S(1)}, u32[]{:S(2)}, u32[]{:S(2)}) collective-permute-start(bf16[512,128]{1,0:T(8,128)(2,1)S(1)} %get-tuple-element.33), channel_id=1, source_target_pairs={{0,1},{1,0},{2,3},{3,2},{4,5},{5,4},{6,7},{7,6},{8,9},{9,8},{10,11... | collective-permute-start | bytes 393224 | tf_op jit(solution)/shard_map/ppermute | solution.py:287
  24.7 6.8 %collective-permute-start.9 = (bf16[512,128]{1,0:T(8,128)(2,1)S(1)}, bf16[512,128]{1,0:T(8,128)(2,1)S(1)}, u32[]{:S(2)}, u32[]{:S(2)}) collective-permute-start(bf16[512,128]{1,0:T(8,128)(2,1)S(1)} %get-tuple-element.30.refs_0_), channel_id=1, source_target_pairs={{0,2},{1,3},{2,0},{3,1},{4,6},{5,7},{6,4},{7,5},{8,10},{9,11},{10,... | collective-permute-start | bytes 393224 | tf_op jit(solution)/shard_map/ppermute | solution.py:287
  28.3 3.2 %collective-permute-start.10 = (bf16[512,128]{1,0:T(8,128)(2,1)S(1)}, bf16[512,128]{1,0:T(8,128)(2,1)S(1)}, u32[]{:S(2)}, u32[]{:S(2)}) collective-permute-start(bf16[512,128]{1,0:T(8,128)(2,1)S(1)} %collective-permute-done.6.refs_1_), channel_id=1, source_target_pairs={{0,2},{1,3},{2,0},{3,1},{4,6},{5,7},{6,4},{7,5},{8,10},{9,11},{10,... | collective-permute-start | bytes 393224 | tf_op jit(solution)/shard_map/ppermute | solution.py:287
  30.4 1.3 %collective-permute-start.11 = (bf16[512,128]{1,0:T(8,128)(2,1)S(1)}, bf16[512,128]{1,0:T(8,128)(2,1)S(1)}, u32[]{:S(2)}, u32[]{:S(2)}) collective-permute-start(bf16[512,128]{1,0:T(8,128)(2,1)S(1)} %collective-permute-done.7.refs_2_), channel_id=1, source_target_pairs={{0,2},{1,3},{2,0},{3,1},{4,6},{5,7},{6,4},{7,5},{8,10},{9,11},{10,... | collective-permute-start | bytes 393224 | tf_op jit(solution)/shard_map/ppermute | solution.py:287
  30.6 1.3 %collective-permute-start.12 = (bf16[512,128]{1,0:T(8,128)(2,1)S(1)}, bf16[512,128]{1,0:T(8,128)(2,1)S(1)}, u32[]{:S(2)}, u32[]{:S(2)}) collective-permute-start(bf16[512,128]{1,0:T(8,128)(2,1)S(1)} %collective-permute-done.8.refs_3_), channel_id=1, source_target_pairs={{0,2},{1,3},{2,0},{3,1},{4,6},{5,7},{6,4},{7,5},{8,10},{9,11},{10,... | collective-permute-start | bytes 393224 | tf_op jit(solution)/shard_map/ppermute | solution.py:287
  32.9 3.0 %collective-permute-start.13 = (f32[8,128]{1,0:T(8,128)S(1)}, f32[8,128]{1,0:T(8,128)S(1)}, u32[]{:S(2)}, u32[]{:S(2)}) collective-permute-start(f32[8,128]{1,0:T(8,128)S(1)} %get-tuple-element.35), channel_id=1, source_target_pairs={{0,3},{1,2},{2,1},{3,0},{4,7},{5,6},{6,5},{7,4},{8,11},{9,10},{10,... | collective-permute-start | bytes 12296 | tf_op jit(solution)/shard_map/ppermute | solution.py:287
  33.9 3.6 %collective-permute-start.14 = (f32[8,128]{1,0:T(8,128)S(1)}, f32[8,128]{1,0:T(8,128)S(1)}, u32[]{:S(2)}, u32[]{:S(2)}) collective-permute-start(f32[8,128]{1,0:T(8,128)S(1)} %get-tuple-element.35), channel_id=1, source_target_pairs={{0,1},{1,0},{2,3},{3,2},{4,5},{5,4},{6,7},{7,6},{8,9},{9,8},{10,11... | collective-permute-start | bytes 12296 | tf_op jit(solution)/shard_map/ppermute | solution.py:287
  34.8 2.7 %collective-permute-start.15 = (f32[8,128]{1,0:T(8,128)S(1)}, f32[8,128]{1,0:T(8,128)S(1)}, u32[]{:S(2)}, u32[]{:S(2)}) collective-permute-start(f32[8,128]{1,0:T(8,128)S(1)} %get-tuple-element.35), channel_id=1, source_target_pairs={{0,2},{1,3},{2,0},{3,1},{4,6},{5,7},{6,4},{7,5},{8,10},{9,11},{10,... | collective-permute-start | bytes 12296 | tf_op jit(solution)/shard_map/ppermute | solution.py:287
  37.5 5.5 %collective-permute-start.16 = (f32[8,128]{1,0:T(8,128)S(1)}, f32[8,128]{1,0:T(8,128)S(1)}, u32[]{:S(2)}, u32[]{:S(2)}) collective-permute-start(f32[8,128]{1,0:T(8,128)S(1)} %add_add_fusion.1), channel_id=1, source_target_pairs={{0,12},{1,13},{2,14},{3,15},{4,8},{5,9},{6,10},{7,11},{8,4},{9,5},... | collective-permute-start | bytes 12296 | tf_op jit(solution)/shard_map/ppermute | solution.py:287
  39.9 4.5 %collective-permute-start.17 = (f32[8,128]{1,0:T(8,128)S(1)}, f32[8,128]{1,0:T(8,128)S(1)}, u32[]{:S(2)}, u32[]{:S(2)}) collective-permute-start(f32[8,128]{1,0:T(8,128)S(1)} %add_add_fusion.1), channel_id=1, source_target_pairs={{0,8},{1,9},{2,10},{3,11},{4,12},{5,13},{6,14},{7,15},{8,0},{9,1},... | collective-permute-start | bytes 12296 | tf_op jit(solution)/shard_map/ppermute | solution.py:287
  41.0 3.6 %collective-permute-start.18 = (f32[8,128]{1,0:T(8,128)S(1)}, f32[8,128]{1,0:T(8,128)S(1)}, u32[]{:S(2)}, u32[]{:S(2)}) collective-permute-start(f32[8,128]{1,0:T(8,128)S(1)} %add_add_fusion.1), channel_id=1, source_target_pairs={{0,4},{1,5},{2,6},{3,7},{4,0},{5,1},{6,2},{7,3},{8,12},{9,13},{10,... | collective-permute-start | bytes 12296 | tf_op jit(solution)/shard_map/ppermute | solution.py:287
